TPU v7x, 32 devices: a whole 2x2x4 slice. The times are simulated.
32 devices in a mesh: grp: 1, tm: 16 (over z, y, core), space: 2 (over x).
Axes of the slice: x: 2, y: 2, z: 4, core: 2. Of those that a mesh axis runs over, the one named last changes fastest.
Arguments:
- tokens: bfloat16 [256, 32, 1152], P('space', ('grp', 'tm')), may hold values from -6 to 6
- modulation: float32 [6, 1152], P('grp'), may hold values from -3 to 3
- qkv_spatial: bfloat16 [1152, 1728], P(None, 'space'), may hold values from -6 to 6
- bias_spatial: float32 [1728], P('space'), may hold values from -3 to 3
- out_spatial: bfloat16 [576, 1152], P('space'), may hold values from -0.25 to 0.25
- outbias_spatial: float32 [1152], replicated, may hold values from -3 to 3
- qkv_temporal: bfloat16 [1152, 1728], P(None, 'space'), may hold values from -6 to 6
- bias_temporal: float32 [1728], P('space'), may hold values from -3 to 3
- out_temporal: bfloat16 [576, 1152], replicated, may hold values from -0.25 to 0.25
- outbias_temporal: float32 [1152], replicated, may hold values from -3 to 3
Outputs:
- result: bfloat16 [256, 32, 1152], P('space', ('grp', 'tm'))
All inputs are finite; a program needn't handle non-finite values.
Results may differ from a plain program's by a relative error of at most 0.025.
Values may be sent and summed in bfloat16 or wider, within the bound.
No kernel may reach another device: no remote copies, remote signals or barrier semaphores. Data moves between devices by JAX's collectives and lax.ppermute only.
A program may use at most 64 MiB of HBM per device.

v0:
```python
import jax
import jax.numpy as jnp
from jax import lax
from jax.sharding import PartitionSpec as P

HD = 72
WIN = 16


def from_behind(array, axis, by):
    devices = lax.axis_size(axis)
    pairs = [(i, i + by) for i in range(devices) if 0 <= i + by < devices]
    return lax.ppermute(array, axis, pairs)


def modulated(values, offset_vec, scaling):
    center = jnp.mean(values, axis=-1, keepdims=True)
    spread = jnp.mean((values - center) ** 2, axis=-1, keepdims=True)
    normed = (values - center) / jnp.sqrt(spread + 1e-06)
    return normed * (1.0 + scaling) + offset_vec


def softmax_rows(scores):
    highest = jnp.max(scores, axis=-1, keepdims=True)
    expon = jnp.exp(scores - highest)
    return (expon / jnp.sum(expon, axis=-1, keepdims=True)).astype(jnp.bfloat16)


def local(
    tokens,
    modulation,
    qkv_spatial,
    bias_spatial,
    out_spatial,
    outbias_spatial,
    qkv_temporal,
    bias_temporal,
    out_temporal,
    outbias_temporal,
):
    patch_dev, frame_dev, model_width = tokens.shape
    qkv_cols = qkv_spatial.shape[1]
    heads_dev = qkv_cols // (3 * HD)
    head_cols = heads_dev * HD
    inv_root = 1.0 / jnp.sqrt(jnp.float32(HD))
    tokens_f = tokens.astype(jnp.float32)
    h_spatial = modulated(tokens_f, modulation[0], modulation[1]).astype(jnp.bfloat16)
    piece = lax.all_gather(h_spatial, "space", axis=0, tiled=True)
    mixed = (
        jnp.dot(piece.reshape(-1, model_width), qkv_spatial, preferred_element_type=jnp.float32)
        + bias_spatial
    )
    qkv_s = mixed.astype(jnp.bfloat16).reshape(piece.shape[0], frame_dev, qkv_cols)
    all_patches = qkv_s.shape[0]
    grouped = qkv_s.reshape(all_patches, frame_dev, heads_dev, 3, HD)
    scores = (
        jnp.einsum(
            "pfhe,qfhe->fhpq",
            grouped[:, :, :, 0],
            grouped[:, :, :, 1],
            preferred_element_type=jnp.float32,
        )
        * inv_root
    )
    probs = softmax_rows(scores)
    o_spatial = jnp.einsum(
        "fhpq,qfhe->pfhe", probs, grouped[:, :, :, 2], preferred_element_type=jnp.float32
    )
    o_spatial = o_spatial.astype(jnp.bfloat16).reshape(all_patches, frame_dev, head_cols)
    full_out = lax.all_gather(out_spatial, "space", axis=0, tiled=True)
    group_count = full_out.shape[0] // head_cols
    grouped_out = full_out.reshape(group_count, head_cols, model_width)
    piece = lax.all_to_all(o_spatial, "space", split_axis=0, concat_axis=2, tiled=True)
    split_cols = piece.reshape(piece.shape[0], piece.shape[1], group_count, head_cols)
    parts = jnp.einsum(
        "pfgc,gcd->pfgd", split_cols, grouped_out, preferred_element_type=jnp.float32
    )
    rounded = lax.optimization_barrier(parts.astype(jnp.bfloat16))
    summed = jnp.sum(rounded.astype(jnp.float32), axis=2)
    mid_rows = (tokens_f + modulation[2] * (summed + outbias_spatial)).astype(jnp.bfloat16)
    h_temporal = modulated(mid_rows.astype(jnp.float32), modulation[3], modulation[4]).astype(
        jnp.bfloat16
    )
    piece = lax.all_gather(h_temporal, "space", axis=0, tiled=True)
    mixed = (
        jnp.dot(piece.reshape(-1, model_width), qkv_temporal, preferred_element_type=jnp.float32)
        + bias_temporal
    )
    qkv_t = mixed.astype(jnp.bfloat16).reshape(piece.shape[0], frame_dev, qkv_cols)
    grouped_t = qkv_t.reshape(all_patches, frame_dev, heads_dev, 3, HD)
    queries = grouped_t[:, :, :, 0]
    key_value = grouped_t[:, :, :, 1:].reshape(all_patches, frame_dev, heads_dev * 2 * HD)
    reach = WIN - 1
    hop_count = (reach + frame_dev - 1) // frame_dev

    def relay_step(step_index, carry):
        moving, stored = carry
        moving = from_behind(moving, "tm", 1)
        stored = lax.dynamic_update_slice_in_dim(
            stored, moving, (hop_count - 1 - step_index) * frame_dev, 1
        )
        return (moving, stored)

    stored_init = jnp.zeros((all_patches, hop_count * frame_dev, key_value.shape[2]), jnp.bfloat16)
    unused, stored = lax.fori_loop(0, hop_count, relay_step, (key_value, stored_init))
    window = jnp.concatenate([stored, key_value], axis=1)
    span_len = reach + frame_dev
    window = window[:, window.shape[1] - span_len :]
    window = window.reshape(all_patches, span_len, heads_dev, 2, HD)
    t_scores = (
        jnp.einsum(
            "pfhe,pjhe->phfj", queries, window[:, :, :, 0], preferred_element_type=jnp.float32
        )
        * inv_root
    )
    first_frame = lax.axis_index("tm") * frame_dev
    query_pos = first_frame + jnp.arange(frame_dev, dtype=jnp.int32)[:, None]
    key_pos = first_frame - reach + jnp.arange(span_len, dtype=jnp.int32)[None, :]
    valid = (key_pos >= 0) & (key_pos <= query_pos) & (key_pos > query_pos - WIN)
    t_scores = jnp.where(valid[None, None], t_scores, jnp.float32(-1e30))
    t_probs = softmax_rows(t_scores)
    o_temporal = jnp.einsum(
        "phfj,pjhe->pfhe", t_probs, window[:, :, :, 1], preferred_element_type=jnp.float32
    )
    o_temporal = o_temporal.astype(jnp.bfloat16).reshape(all_patches, frame_dev, head_cols)
    piece = lax.all_to_all(o_temporal, "space", split_axis=0, concat_axis=2, tiled=True)
    mixed = jnp.dot(
        piece.reshape(-1, piece.shape[2]), out_temporal, preferred_element_type=jnp.float32
    )
    final = mixed.reshape(piece.shape[0], piece.shape[1], model_width)
    return (mid_rows.astype(jnp.float32) + modulation[5] * (final + outbias_temporal)).astype(
        jnp.bfloat16
    )


def solution(mesh):
    return jax.shard_map(
        local,
        mesh=mesh,
        in_specs=(
            P("space", ("grp", "tm"), None),
            P("grp", None),
            P(None, "space"),
            P("space"),
            P("space", None),
            P(),
            P(None, "space"),
            P("space"),
            P(),
            P(),
        ),
        out_specs=P("space", ("grp", "tm"), None),
        check_vma=False,
    )
```

profile of v0, /device:TPU:8, one launch (start us, length us, event | category | flops | bytes accessed | tf_op | source)
XLA Modules:
  0.0 282.0 jit_solution(15972286383642945572)
XLA Ops:
  12.4 23.3 %all-gather.4.cloned.1.call-done = bf16[256,2,1152]{2,0,1:T(8,128)(2,1)} async-done(((bf16[128,2,1152]{2,0,1:T(8,128)(2,1)}), bf16[256,2,1152]{2,0,1:T(8,128)(2,1)}) %all-gather.4.cloned.1.call-update) | async-done | bytes 1179664 | tf_op jit(solution)/shard_map/all_gather | solution.py:48
  35.7 3.5 %copy.39 = bf16[256,2,1152]{2,1,0:T(2,128)(2,1)} copy(bf16[256,2,1152]{2,0,1:T(8,128)(2,1)} %all-gather.4.cloned.1.call-done) | data formatting | bytes 2359296 | tf_op jit(solution)/shard_map/all_gather | solution.py:48
  39.2 3.7 %reshape.164 = bf16[512,1152]{1,0:T(8,128)(2,1)} reshape(bf16[256,2,1152]{2,1,0:T(2,128)(2,1)} %copy.39) | data formatting | bytes 2359296 | tf_op jit(solution)/shard_map/reshape | solution.py:50
  42.9 2.7 add_convert_fusion.1
  46.2 3.8 %reshape_reshape.6 = bf16[256,2,4,3,72]{4,3,2,1,0:T(4,128)(2,1)} reshape(bf16[512,864]{1,0:T(8,128)(2,1)S(1)} %copy.40) | data formatting | bytes 1769472 | tf_op jit(solution)/shard_map/reshape;reshape | solution.py:55
  50.0 6.9 %fusion.60 = (bf16[256,2,4,1,72]{4,3,2,1,0:T(2,128)(2,1)}, bf16[256,2,4,1,72]{4,3,2,1,0:T(2,128)(2,1)}, bf16[256,2,4,1,72]{4,3,2,1,0:T(2,128)(2,1)S(1)}) fusion(bf16[256,2,4,3,72]{4,3,2,1,0:T(4,128)(2,1)} %reshape_reshape.6), kind=kLoop, calls=%fused_computation.73 | loop fusion | bytes 1769472 | tf_op jit(solution)/shard_map/slice | solution.py:67
  56.9 2.3 copy.65
  59.2 2.3 copy.66
  67.0 9.3 %all_to_all.30 = bf16[256,2,288]{2,1,0:T(2,128)(2,1)S(1)} all-to-all(bf16[256,2,288]{2,1,0:T(2,128)(2,1)S(1)} %copy.45), channel_id=1, replica_groups=mesh['grp'=1,'tm'=16,'space'=2] {'space'}, dimensions={0} | all-to-all | bytes 589824 | tf_op jit(solution)/shard_map/all_to_all | solution.py:73
  81.5 22.8 %all-gather.8.cloned.1.call-done = bf16[256,2,1152]{2,0,1:T(8,128)(2,1)} async-done(((bf16[128,2,1152]{2,0,1:T(8,128)(2,1)}), bf16[256,2,1152]{2,0,1:T(8,128)(2,1)}) %all-gather.8.cloned.1.call-update) | async-done | bytes 1179664 | tf_op jit(solution)/shard_map/all_gather | solution.py:84
  104.3 2.5 copy.48
  108.1 3.3 %add_convert_fusion = bf16[512,864]{0,1:T(8,128)(2,1)S(1)} fusion(bf16[512,1152]{1,0:T(8,128)(2,1)} %reshape.167, bf16[1152,864]{0,1:T(8,128)(2,1)} %param.18, f32[864]{0:T(1024)S(1)} %copy-done.8), kind=kOutput, calls=%fused_computation.19 | convolution fusion | flops 1020100608 | bytes 4058496 | tf_op jit(solution)/shard_map/dot_general | solution.py:86
  112.0 3.8 %reshape_reshape.7 = bf16[256,2,4,3,72]{4,3,2,1,0:T(4,128)(2,1)} reshape(bf16[512,864]{1,0:T(8,128)(2,1)S(1)} %copy.49) | data formatting | bytes 1769472 | tf_op jit(solution)/shard_map/reshape;reshape | solution.py:90
  115.8 3.5 %slice.61 = bf16[256,2,4,1,72]{4,3,2,1,0:T(2,128)(2,1)} slice(bf16[256,2,4,3,72]{4,3,2,1,0:T(4,128)(2,1)} %reshape_reshape.7), slice={[0:256], [0:2], [0:4], [0:1], [0:72]} | slice | bytes 589824 | tf_op jit(solution)/shard_map/slice | solution.py:91
  121.5 2.6 broadcast_in_dim.10
  124.1 104.0 %while.15 = (s32[]{:T(128)}, bf16[256,2,576]{0,2,1:T(8,128)(2,1)S(1)}, bf16[256,16,576]{0,2,1:T(8,128)(2,1)}, s32[]{:T(128)}, s32[]{:T(128)}, /*index=5*/s32[]{:T(128)}, s32[]{:T(128)}, s32[]{:T(128)}) while((s32[]{:T(128)}, bf16[256,2,576]{0,2,1:T(8,128)(2,1)S(1)}, bf16[256,16,576]{0,2,1:T(8,128)(2,1)}, s32[]{:T(128)}, s32[]{:T(128)}, ...), condition=%wide.region_8.0_spmd, body=%wide.region_7.0_spmd.sunk | while | flops 7 | bytes 4718779 | solution.py:105
  126.0 10.2 %collective-permute-done = bf16[256,2,576]{0,2,1:T(8,128)(2,1)S(1)} collective-permute-done((bf16[256,2,576]{0,2,1:T(8,128)(2,1)S(1)}, bf16[256,2,576]{0,2,1:T(8,128)(2,1)S(1)}, u32[]{:S(2)}, u32[]{:S(2)}) %collective-permute-start) | collective-permute-done | bytes 589856 | tf_op jit(solution)/shard_map/while/body/eval_jaxpr/ppermute | solution.py:13
  139.0 10.2 %collective-permute-done = bf16[256,2,576]{0,2,1:T(8,128)(2,1)S(1)} collective-permute-done((bf16[256,2,576]{0,2,1:T(8,128)(2,1)S(1)}, bf16[256,2,576]{0,2,1:T(8,128)(2,1)S(1)}, u32[]{:S(2)}, u32[]{:S(2)}) %collective-permute-start) | collective-permute-done | bytes 589856 | tf_op jit(solution)/shard_map/while/body/eval_jaxpr/ppermute | solution.py:13
  152.0 10.2 %collective-permute-done = bf16[256,2,576]{0,2,1:T(8,128)(2,1)S(1)} collective-permute-done((bf16[256,2,576]{0,2,1:T(8,128)(2,1)S(1)}, bf16[256,2,576]{0,2,1:T(8,128)(2,1)S(1)}, u32[]{:S(2)}, u32[]{:S(2)}) %collective-permute-start) | collective-permute-done | bytes 589856 | tf_op jit(solution)/shard_map/while/body/eval_jaxpr/ppermute | solution.py:13
  165.0 10.2 %collective-permute-done = bf16[256,2,576]{0,2,1:T(8,128)(2,1)S(1)} collective-permute-done((bf16[256,2,576]{0,2,1:T(8,128)(2,1)S(1)}, bf16[256,2,576]{0,2,1:T(8,128)(2,1)S(1)}, u32[]{:S(2)}, u32[]{:S(2)}) %collective-permute-start) | collective-permute-done | bytes 589856 | tf_op jit(solution)/shard_map/while/body/eval_jaxpr/ppermute | solution.py:13
  178.0 10.2 %collective-permute-done = bf16[256,2,576]{0,2,1:T(8,128)(2,1)S(1)} collective-permute-done((bf16[256,2,576]{0,2,1:T(8,128)(2,1)S(1)}, bf16[256,2,576]{0,2,1:T(8,128)(2,1)S(1)}, u32[]{:S(2)}, u32[]{:S(2)}) %collective-permute-start) | collective-permute-done | bytes 589856 | tf_op jit(solution)/shard_map/while/body/eval_jaxpr/ppermute | solution.py:13
  191.0 10.2 %collective-permute-done = bf16[256,2,576]{0,2,1:T(8,128)(2,1)S(1)} collective-permute-done((bf16[256,2,576]{0,2,1:T(8,128)(2,1)S(1)}, bf16[256,2,576]{0,2,1:T(8,128)(2,1)S(1)}, u32[]{:S(2)}, u32[]{:S(2)}) %collective-permute-start) | collective-permute-done | bytes 589856 | tf_op jit(solution)/shard_map/while/body/eval_jaxpr/ppermute | solution.py:13
  204.0 10.2 %collective-permute-done = bf16[256,2,576]{0,2,1:T(8,128)(2,1)S(1)} collective-permute-done((bf16[256,2,576]{0,2,1:T(8,128)(2,1)S(1)}, bf16[256,2,576]{0,2,1:T(8,128)(2,1)S(1)}, u32[]{:S(2)}, u32[]{:S(2)}) %collective-permute-start) | collective-permute-done | bytes 589856 | tf_op jit(solution)/shard_map/while/body/eval_jaxpr/ppermute | solution.py:13
  217.0 10.2 %collective-permute-done = bf16[256,2,576]{0,2,1:T(8,128)(2,1)S(1)} collective-permute-done((bf16[256,2,576]{0,2,1:T(8,128)(2,1)S(1)}, bf16[256,2,576]{0,2,1:T(8,128)(2,1)S(1)}, u32[]{:S(2)}, u32[]{:S(2)}) %collective-permute-start) | collective-permute-done | bytes 589856 | tf_op jit(solution)/shard_map/while/body/eval_jaxpr/ppermute | solution.py:13
  228.1 2.7 pad_maximum_fusion
  230.8 2.9 %fusion.59 = (bf16[256,17,4,1,72]{0,4,3,2,1:T(8,128)(2,1)}, bf16[256,17,4,1,72]{0,4,3,2,1:T(8,128)(2,1)}) fusion(bf16[256,17,4,2,72]{0,4,3,2,1:T(8,128)(2,1)S(1)} %bitcast.79), kind=kLoop, calls=%fused_computation.72 | loop fusion | bytes 10027008 | tf_op jit(solution)/shard_map/slice | solution.py:112
  233.7 7.8 %copy.70 = bf16[256,17,4,1,72]{4,1,2,0,3:T(8,128)(2,1)} copy(bf16[256,17,4,1,72]{0,4,3,2,1:T(8,128)(2,1)} %get-tuple-element.87) | data formatting | bytes 5013504
  241.5 8.0 %copy.68 = bf16[256,17,4,1,72]{4,1,2,0,3:T(8,128)(2,1)} copy(bf16[256,17,4,1,72]{0,4,3,2,1:T(8,128)(2,1)} %get-tuple-element.88) | data formatting | bytes 5013504
  249.4 7.4 %fusion.66 = (f32[256,4,2]{2,1,0:T(4,128)S(1)}, f32[256,4,2,17]{3,2,1,0:T(2,128)}) fusion(pred[2,17]{1,0:T(4,128)(4,1)S(1)} %compare_and_fusion, bf16[256,17,4,1,72]{4,1,2,0,3:T(8,128)(2,1)} %copy.70, bf16[256,2,4,1,72]{4,3,2,1,0:T(2,128)(2,1)S(1)} %copy-done.4), kind=kOutput, calls=%fused_computation.75 | convolution fusion | flops 5152784 | bytes 2949154 | tf_op jit(solution)/shard_map/sub | solution.py:25
  256.9 5.1 %fusion.21 = bf16[256,2,4,72]{3,1,2,0:T(2,128)(2,1)S(1)} fusion(bf16[256,17,4,1,72]{4,1,2,0,3:T(8,128)(2,1)} %copy.68, f32[256,4,2,17]{3,2,1,0:T(2,128)} %get-tuple-element.95, f32[256,4,2]{2,1,0:T(4,128)S(1)} %get-tuple-element.94), kind=kOutput, calls=%fused_computation.34 | convolution fusion | flops 5230592 | bytes 2949120 | tf_op jit(solution)/shard_map/phfj,pjhe->pfhe/dot_general | solution.py:122
  263.0 8.3 %all_to_all.31 = bf16[256,2,288]{2,1,0:T(2,128)(2,1)S(1)} all-to-all(bf16[256,2,288]{2,1,0:T(2,128)(2,1)S(1)} %copy.55), channel_id=1, replica_groups=mesh['grp'=1,'tm'=16,'space'=2] {'space'}, dimensions={0} | all-to-all | bytes 589824 | tf_op jit(solution)/shard_map/all_to_all | solution.py:126
  271.8 2.2 fusion.9
  (81 shorter events, 46.5 us)
Async XLA Ops:
  6.5 36.3 %copy-start = (bf16[1152,864]{0,1:T(8,128)(2,1)S(1)}, bf16[1152,864]{0,1:T(8,128)(2,1)}, u32[]{:S(2)}) copy-start(bf16[1152,864]{0,1:T(8,128)(2,1)} %param.14) | copy-start | bytes 5971972
  6.5 3.9 %copy-start.2 = (bf16[128,2,1152]{2,1,0:T(2,128)(2,1)S(1)}, bf16[128,2,1152]{2,1,0:T(2,128)(2,1)}, u32[]{:S(2)}) copy-start(bf16[128,2,1152]{2,1,0:T(2,128)(2,1)} %param.12) | copy-start | bytes 1769476
  6.5 29.1 %all-gather.4.cloned.1.call-start = ((), (), s32[]{:S(2)}) async-start(), calls=%async_computation.2 | async-start | bytes 1769472 | tf_op jit(solution)/shard_map/all_gather | solution.py:48
  11.6 65.2 %all-gather.6.cloned.1.call-start = ((), (), s32[]{:S(2)}) async-start(), calls=%async_computation.3 | async-start | bytes 1990656 | tf_op jit(solution)/shard_map/all_gather | solution.py:70
  12.3 92.0 %all-gather.8.cloned.1.call-start = ((), (), s32[]{:S(2)}) async-start(), calls=%async_computation.4 | async-start | bytes 1769472 | tf_op jit(solution)/shard_map/all_gather | solution.py:84
  39.2 3.7 %copy-start.7 = (f32[864]{0:T(1024)S(1)}, f32[864]{0:T(1024)}, u32[]{:S(2)}) copy-start(f32[864]{0:T(1024)} %param.15) | copy-start | bytes 10372
  79.0 0.7 copy-start.5
  106.8 1.3 copy-start.8
  115.8 3.5 %copy-start.3 = (bf16[256,2,4,3,72]{4,3,2,1,0:T(4,128)(2,1)S(1)}, bf16[256,2,4,3,72]{4,3,2,1,0:T(4,128)(2,1)}, u32[]{:S(2)}) copy-start(bf16[256,2,4,3,72]{4,3,2,1,0:T(4,128)(2,1)} %reshape_reshape.7) | copy-start | bytes 2654212
  124.1 12.1 %collective-permute-start = (bf16[256,2,576]{0,2,1:T(8,128)(2,1)S(1)}, bf16[256,2,576]{0,2,1:T(8,128)(2,1)S(1)}, u32[]{:S(2)}, u32[]{:S(2)}) collective-permute-start(bf16[256,2,576]{0,2,1:T(8,128)(2,1)S(1)} %get-tuple-element.126), channel_id=1, source_target_pairs={{0,2},{2,4},{4,6},{6,8},{8,10},{10,12},{12,14},{14,16},{16,18},{18... | collective-permute-start | bytes 1769480 | tf_op jit(solution)/shard_map/while/body/eval_jaxpr/ppermute | solution.py:13
  137.1 12.1 %collective-permute-start = (bf16[256,2,576]{0,2,1:T(8,128)(2,1)S(1)}, bf16[256,2,576]{0,2,1:T(8,128)(2,1)S(1)}, u32[]{:S(2)}, u32[]{:S(2)}) collective-permute-start(bf16[256,2,576]{0,2,1:T(8,128)(2,1)S(1)} %get-tuple-element.126), channel_id=1, source_target_pairs={{0,2},{2,4},{4,6},{6,8},{8,10},{10,12},{12,14},{14,16},{16,18},{18... | collective-permute-start | bytes 1769480 | tf_op jit(solution)/shard_map/while/body/eval_jaxpr/ppermute | solution.py:13
  150.1 12.1 %collective-permute-start = (bf16[256,2,576]{0,2,1:T(8,128)(2,1)S(1)}, bf16[256,2,576]{0,2,1:T(8,128)(2,1)S(1)}, u32[]{:S(2)}, u32[]{:S(2)}) collective-permute-start(bf16[256,2,576]{0,2,1:T(8,128)(2,1)S(1)} %get-tuple-element.126), channel_id=1, source_target_pairs={{0,2},{2,4},{4,6},{6,8},{8,10},{10,12},{12,14},{14,16},{16,18},{18... | collective-permute-start | bytes 1769480 | tf_op jit(solution)/shard_map/while/body/eval_jaxpr/ppermute | solution.py:13
  163.1 12.1 %collective-permute-start = (bf16[256,2,576]{0,2,1:T(8,128)(2,1)S(1)}, bf16[256,2,576]{0,2,1:T(8,128)(2,1)S(1)}, u32[]{:S(2)}, u32[]{:S(2)}) collective-permute-start(bf16[256,2,576]{0,2,1:T(8,128)(2,1)S(1)} %get-tuple-element.126), channel_id=1, source_target_pairs={{0,2},{2,4},{4,6},{6,8},{8,10},{10,12},{12,14},{14,16},{16,18},{18... | collective-permute-start | bytes 1769480 | tf_op jit(solution)/shard_map/while/body/eval_jaxpr/ppermute | solution.py:13
  176.1 12.1 %collective-permute-start = (bf16[256,2,576]{0,2,1:T(8,128)(2,1)S(1)}, bf16[256,2,576]{0,2,1:T(8,128)(2,1)S(1)}, u32[]{:S(2)}, u32[]{:S(2)}) collective-permute-start(bf16[256,2,576]{0,2,1:T(8,128)(2,1)S(1)} %get-tuple-element.126), channel_id=1, source_target_pairs={{0,2},{2,4},{4,6},{6,8},{8,10},{10,12},{12,14},{14,16},{16,18},{18... | collective-permute-start | bytes 1769480 | tf_op jit(solution)/shard_map/while/body/eval_jaxpr/ppermute | solution.py:13
  189.1 12.1 %collective-permute-start = (bf16[256,2,576]{0,2,1:T(8,128)(2,1)S(1)}, bf16[256,2,576]{0,2,1:T(8,128)(2,1)S(1)}, u32[]{:S(2)}, u32[]{:S(2)}) collective-permute-start(bf16[256,2,576]{0,2,1:T(8,128)(2,1)S(1)} %get-tuple-element.126), channel_id=1, source_target_pairs={{0,2},{2,4},{4,6},{6,8},{8,10},{10,12},{12,14},{14,16},{16,18},{18... | collective-permute-start | bytes 1769480 | tf_op jit(solution)/shard_map/while/body/eval_jaxpr/ppermute | solution.py:13
  202.1 12.1 %collective-permute-start = (bf16[256,2,576]{0,2,1:T(8,128)(2,1)S(1)}, bf16[256,2,576]{0,2,1:T(8,128)(2,1)S(1)}, u32[]{:S(2)}, u32[]{:S(2)}) collective-permute-start(bf16[256,2,576]{0,2,1:T(8,128)(2,1)S(1)} %get-tuple-element.126), channel_id=1, source_target_pairs={{0,2},{2,4},{4,6},{6,8},{8,10},{10,12},{12,14},{14,16},{16,18},{18... | collective-permute-start | bytes 1769480 | tf_op jit(solution)/shard_map/while/body/eval_jaxpr/ppermute | solution.py:13
  215.1 12.1 %collective-permute-start = (bf16[256,2,576]{0,2,1:T(8,128)(2,1)S(1)}, bf16[256,2,576]{0,2,1:T(8,128)(2,1)S(1)}, u32[]{:S(2)}, u32[]{:S(2)}) collective-permute-start(bf16[256,2,576]{0,2,1:T(8,128)(2,1)S(1)} %get-tuple-element.126), channel_id=1, source_target_pairs={{0,2},{2,4},{4,6},{6,8},{8,10},{10,12},{12,14},{14,16},{16,18},{18... | collective-permute-start | bytes 1769480 | tf_op jit(solution)/shard_map/while/body/eval_jaxpr/ppermute | solution.py:13
  241.5 8.0 %copy-start.4 = (bf16[256,2,4,1,72]{4,3,2,1,0:T(2,128)(2,1)S(1)}, bf16[256,2,4,1,72]{4,3,2,1,0:T(2,128)(2,1)}, u32[]{:S(2)}) copy-start(bf16[256,2,4,1,72]{4,3,2,1,0:T(2,128)(2,1)} %slice.61) | copy-start | bytes 884740
  262.0 9.8 %copy-start.6 = (f32[1152]{0:T(1024)S(1)}, f32[1152]{0:T(1024)}, u32[]{:S(2)}) copy-start(f32[1152]{0:T(1024)} %param.21) | copy-start | bytes 13828
  271.8 3.7 %copy-start.1 = (bf16[1152,864]{0,1:T(8,128)(2,1)S(1)}, bf16[1152,864]{0,1:T(8,128)(2,1)}, u32[]{:S(2)}) copy-start(bf16[1152,864]{0,1:T(8,128)(2,1)} %param.14) | copy-start | bytes 5971972
Sparse Core Ops, SparseCore 0:
  11.7 23.9 all-gather.3
  37.2 24.4 all-gather.5
  81.5 22.7 all-gather.7
where the time goes:
time: 283 us; the launch traced here: 282 us
  waiting for transfers between devices  128 us (45%)
  local copies, waits for them, and re-layouts  70.8 us (25%)
  matrix products  27 us (10%)
  blocking collectives  17.5 us (6%)
  starting transfers between devices  15.3 us (5%)
  between operations  13.4 us (5%)
  other arithmetic  9.63 us (3%)
    ppermute x8, waiting for transfers between devices, from_behind(): return lax.ppermute(array, axis, pairs)  81.3 us
    all_gather x1, waiting for transfers between devices, local(): piece = lax.all_gather(h_spatial, 'space', axis=0, tiled=True)  23.3 us
    all_gather x1, waiting for transfers between devices, local(): piece = lax.all_gather(h_temporal, 'space', axis=0, tiled=True)  22.8 us
    unnamed x24, local copies, waits for them, and re-layouts  21.8 us
    ppermute x8, starting transfers between devices, from_behind(): return lax.ppermute(array, axis, pairs)  15.3 us
    sub x2, matrix products, softmax_rows(): expon = jnp.exp(scores - highest)  9.64 us
    all_to_all x1, blocking collectives, local(): lax.all_to_all(o_spatial, 'space', split_axis=0, concat_axis=2, tiled=True)  9.25 us
    all_to_all x1, blocking collectives, local(): lax.all_to_all(o_temporal, 'space', split_axis=0, concat_axis=2, tiled=True)  8.28 us
  transfers between devices with their start and end apart: 11, of which 10 were waited for; matrix products, arithmetic and copies ran while one was open for 11% of the time, Pallas kernels for 0%

commit v1 on v0

v1 whole, which is shorter than its diff:
```python
import functools
import math

import jax
import jax.numpy as jnp
from jax import lax
from jax.experimental import pallas as pl
from jax.experimental.pallas import tpu as pltpu
from jax.sharding import PartitionSpec as P

HD = 72
WIN = 16
BF = jnp.bfloat16
F32 = jnp.float32
EXP2_SCALE = 1.0 / (math.sqrt(HD) * math.log(2.0))

VMEM = pl.BlockSpec(memory_space=pltpu.VMEM)
SMEM = pl.BlockSpec(memory_space=pltpu.SMEM)
PARAMS = pltpu.CompilerParams(vmem_limit_bytes=48 * 1024 * 1024)

NT = (((1,), (1,)), ((), ()))
TN = (((0,), (0,)), ((), ()))


def mm(a, b, dims=(((1,), (0,)), ((), ()))):
    return lax.dot_general(a, b, dims, preferred_element_type=F32)


def modulated(values, offset_vec, scaling):
    center = jnp.mean(values, axis=-1, keepdims=True)
    moved = values - center
    spread = jnp.mean(moved * moved, axis=-1, keepdims=True)
    return moved * lax.rsqrt(spread + 1e-06) * (1.0 + scaling) + offset_vec


def attend(q_t, k_t, v_t, mask=None):
    scores = mm(k_t, q_t, TN)
    if mask is not None:
        scores = jnp.where(mask, scores, F32(-1e30))
    highest = jnp.max(scores, axis=0, keepdims=True)
    expon = jnp.exp2((scores - highest) * F32(EXP2_SCALE))
    total = jnp.sum(expon, axis=0, keepdims=True)
    return mm(v_t, expon.astype(BF)) * (1.0 / total)


def turned(values_t):
    return values_t.astype(BF).T


def kernel_qkv(x_ref, mod_ref, w_ref, b_ref, out_ref):
    frames, patches, width = x_ref.shape
    x = x_ref[...].reshape(frames * patches, width).astype(F32)
    h = modulated(x, mod_ref[0:1, :], mod_ref[1:2, :]).astype(BF)
    for i in range(w_ref.shape[0]):
        qkv = mm(w_ref[i], h, NT) + b_ref[i]
        for c in range(3):
            out_ref[i, c] = qkv[c * HD : (c + 1) * HD].astype(BF)


def kernel_spatial(ids_ref, x_ref, own_ref, mod_ref, w_ref, b_ref, out_ref, part_ref, *, chunked):
    others, frames, patches, width = x_ref.shape
    heads = w_ref.shape[0]
    spaces = others + 1
    for j in range(others):
        x = x_ref[j].reshape(frames * patches, width).astype(F32)
        h = modulated(x, mod_ref[0:1, :], mod_ref[1:2, :]).astype(BF)
        for i in range(heads):
            qkv = mm(w_ref[i], h, NT) + b_ref[i]
            for c in range(3):
                part_ref[j, i, c] = qkv[c * HD : (c + 1) * HD].astype(BF)
    for f in range(frames):
        cols = slice(f * patches, (f + 1) * patches)
        done = []
        for i in range(heads):
            q_t, k_t, v_t = (
                jnp.concatenate(
                    [own_ref[i, c, :, cols]] + [part_ref[j, i, c, :, cols] for j in range(others)],
                    axis=1,
                )
                for c in range(3)
            )
            done.append(attend(q_t, k_t, v_t))
        rows = jnp.concatenate(done, axis=0).T
        for j in range(spaces):
            place = lax.rem(ids_ref[0] - j + spaces, spaces)
            mine = rows[j * patches : (j + 1) * patches]
            if chunked:
                pieces, _, size, columns = out_ref.shape[1:]
                out_ref[place, :, f] = mine.reshape(pieces, size, columns).astype(BF)
            else:
                out_ref[place, f] = mine.astype(BF)


def middle(tokens, parts, outbias, gate):
    summed = parts[0].astype(BF).astype(F32)
    for part in parts[1:]:
        summed = summed + part.astype(BF).astype(F32)
    return (tokens.astype(F32) + gate * (summed + outbias)).astype(BF)


def kernel_temporal(ids_ref, o_ref, x_ref, out_w_ref, other_w_ref, outbias_ref, mod_ref, b_ref, *refs, size):
    w_refs, out_ref = refs[:-1], refs[-1]
    spaces, rows, _ = o_ref.shape
    space, core = ids_ref[0], ids_ref[1]
    parts = [mm(o_ref[space], out_w_ref[...])]
    for k in range(1, spaces):
        parts.append(mm(o_ref[lax.rem(space - k + spaces, spaces)], other_w_ref[k - 1]))
    y = middle(x_ref[...], parts, outbias_ref[...], mod_ref[2:3, :])
    h = modulated(y.astype(F32), mod_ref[3:4, :], mod_ref[4:5, :]).astype(BF)

    def place(axis):
        row = lax.broadcasted_iota(jnp.int32, (rows, rows), axis)
        frame = row // (2 * size) * 2 + row % (2 * size) // size
        return frame, row % size

    key_frame, key_patch = place(0)
    query_frame, query_patch = place(1)
    back = query_frame - key_frame
    mask = (key_patch == query_patch) & (back >= 0) & (back < WIN)

    heads = w_refs[0].shape[0]
    half = heads // 2
    done, order = [], []
    for n, w_ref in enumerate(w_refs):
        if n == 0:
            first = space * heads
        else:
            first = lax.rem(space - (n + 1) // 2 + spaces, spaces) * heads
            first = first + half * (core if n % 2 else 1 - core)
        for i in range(w_ref.shape[0]):
            qkv = (mm(w_ref[i], h, NT) + b_ref[first + i]).astype(BF)
            o_t = attend(qkv[0:HD], qkv[HD : 2 * HD], qkv[2 * HD : 3 * HD], mask)
            out_ref[first + i] = o_t.astype(BF)


def kernel_home(o_ref, x_ref, out_w_ref, other_w_ref, outbias_ref, mod_ref, out_ref):
    parts = [mm(o_ref[0], out_w_ref[...])]
    for k in range(1, o_ref.shape[0]):
        parts.append(mm(o_ref[k], other_w_ref[k - 1]))
    out_ref[...] = middle(x_ref[...], parts, outbias_ref[...], mod_ref[2:3, :])


def kernel_final(o_ref, y_ref, w_ref, outbias_ref, mod_ref, out_ref):
    final = mm(o_ref[...], w_ref[...]) + outbias_ref[...]
    out_ref[...] = (y_ref[...].astype(F32) + mod_ref[5:6, :] * final).astype(BF)


def call(kernel, out_shape, count, flops, nbytes, first_smem=False, scratch=()):
    return pl.pallas_call(
        kernel,
        out_shape=jax.ShapeDtypeStruct(out_shape, BF),
        in_specs=[SMEM if first_smem and i == 0 else VMEM for i in range(count)],
        out_specs=VMEM,
        scratch_shapes=list(scratch),
        compiler_params=PARAMS,
        cost_estimate=pl.CostEstimate(flops=int(flops), bytes_accessed=int(nbytes), transcendentals=0),
    )


def local(
    tokens,
    modulation,
    qkv_spatial,
    bias_spatial,
    out_spatial,
    outbias_spatial,
    qkv_temporal,
    bias_temporal,
    out_temporal,
    outbias_temporal,
):
    patches, frames, width = tokens.shape
    spaces, times = lax.axis_size("space"), lax.axis_size("tm")
    space, time = lax.axis_index("space"), lax.axis_index("tm")
    core = lax.rem(time, 2)
    heads = qkv_spatial.shape[1] // (3 * HD)
    cols = heads * HD
    half = heads // 2
    size = patches // times
    rows = patches * frames
    ids = jnp.stack([space, core]).astype(jnp.int32)

    def across(array, k):
        return lax.ppermute(array, "space", [(i, (i + k) % spaces) for i in range(spaces)])

    def beside(array):
        return lax.ppermute(array, "tm", [(i, i ^ 1) for i in range(times)])

    def frame_major(array):
        return jnp.swapaxes(array, -3, -2)

    arrived = [across(tokens, k) for k in range(1, spaces)]
    spread = lax.all_to_all(tokens.reshape(times, size, frames, width), "tm", 0, 0, tiled=True)

    w_spatial = qkv_spatial.T.reshape(heads, 3 * HD, width)
    b_spatial = bias_spatial.reshape(heads, 3 * HD, 1)
    own_tokens = frame_major(tokens)
    own = call(kernel_qkv, (heads, 3, HD, rows), 4, 2 * rows * width * cols * 3, 3e6)(
        own_tokens, modulation, w_spatial, b_spatial
    )

    w_temporal = qkv_temporal.T.reshape(heads, 3 * HD, width)
    my_heads = lax.dynamic_slice_in_dim(w_temporal, core * half, half, 0)
    my_out = lax.dynamic_slice_in_dim(out_spatial, core * half * HD, half * HD, 0)
    my_heads, my_out, *arrived = lax.optimization_barrier((my_heads, my_out, *arrived))
    other_out, other_heads = [], []
    for k in range(1, spaces):
        direct = across(my_out, k)
        passed = beside(direct)
        other_out.append(
            jnp.where(core == 0, jnp.concatenate([direct, passed]), jnp.concatenate([passed, direct]))
        )
    for k in range(1, spaces):
        direct = across(my_heads, k)
        other_heads += [direct, beside(direct)]
    other_out = jnp.stack(other_out)
    b_temporal = lax.all_gather(bias_temporal, "space", axis=0, tiled=True)
    b_temporal = b_temporal.reshape(spaces * heads, 3 * HD, 1)

    chunked = size % 8 == 0
    o_shape = (spaces, times, frames, size, cols) if chunked else (spaces, frames, patches, cols)
    o_all = call(
        functools.partial(kernel_spatial, chunked=chunked),
        o_shape,
        6,
        2 * rows * width * cols * 3 * (spaces - 1) + 4 * rows * cols * patches * spaces * spaces,
        4e6,
        True,
        [pltpu.VMEM((spaces - 1, heads, 3, HD, rows), BF)],
    )(ids, jnp.stack([frame_major(a) for a in arrived]), own, modulation, w_spatial, b_spatial)
    if not chunked:
        o_all = jnp.transpose(o_all.reshape(spaces, frames, times, size, cols), (0, 2, 1, 3, 4))

    o_here = lax.all_to_all(
        o_all.reshape(spaces * times, frames * size, cols), ("space", "tm"), 0, 0, tiled=True
    ).reshape(spaces, rows, cols)
    o_home = [lax.dynamic_index_in_dim(o_all, space, 0, keepdims=False)]
    for k in range(1, spaces):
        o_home.append(across(lax.dynamic_index_in_dim(o_all, (space + k) % spaces, 0, keepdims=False), k))
    o_home = jnp.stack(o_home).reshape(spaces, rows, cols)

    outbias_s = outbias_spatial.reshape(1, width)
    outbias_t = outbias_temporal.reshape(1, width)
    x_here = frame_major(spread).reshape(rows, width)
    o_t = call(
        functools.partial(kernel_temporal, size=size),
        (spaces * heads, HD, rows),
        8 + 1 + len(other_heads),
        2 * rows * width * cols * 4 * spaces + 4 * rows * rows * cols * spaces,
        8e6,
        True,
    )(ids, o_here, x_here, out_spatial, other_out, outbias_s, modulation, b_temporal, w_temporal, *other_heads)
    o_t = jnp.transpose(o_t, (2, 0, 1)).reshape(times, frames * size, spaces * cols)
    o_final = lax.all_to_all(o_t, "tm", 0, 0, tiled=True).reshape(rows, spaces * cols)

    x_home = jnp.swapaxes(tokens.reshape(times, size, frames, width), 1, 2).reshape(rows, width)
    y_home = call(kernel_home, (rows, width), 6, 2 * rows * width * cols * spaces, 3e6)(
        o_home, x_home, out_spatial, other_out, outbias_s, modulation
    )
    result = call(kernel_final, (rows, width), 5, 2 * rows * width * cols * spaces, 3e6)(
        o_final, y_home, out_temporal, outbias_t, modulation
    )
    return jnp.swapaxes(result.reshape(times, frames, size, width), 1, 2).reshape(patches, frames, width)


def solution(mesh):
    return jax.shard_map(
        local,
        mesh=mesh,
        in_specs=(
            P("space", ("grp", "tm"), None),
            P("grp", None),
            P(None, "space"),
            P("space"),
            P("space", None),
            P(),
            P(None, "space"),
            P("space"),
            P(),
            P(),
        ),
        out_specs=P("space", ("grp", "tm"), None),
        check_vma=False,
    )
```

time: 283 us -> 106 us (0.37)
  the two profiles are of different devices: /device:TPU:8 before, /device:TPU:0 now
where the time goes in v1:
time: 106 us; the launch traced here: 105 us
  waiting for transfers between devices  43.3 us (41%)
  starting transfers between devices  22.6 us (21%)
  Pallas kernels  18.6 us (18%)
  local copies, waits for them, and re-layouts  13.3 us (13%)
  blocking collectives  5.12 us (5%)
  other arithmetic  1.41 us (1%)
    ppermute x4, waiting for transfers between devices, across(): lax.ppermute(array, 'space', [(i, (i + k) % spaces) for i in range(spaces)])  38.1 us
    pallas_call x1, Pallas kernels, local(): call(functools.partial(kernel_temporal, size=size), (spaces * heads, HD,...  9.9 us
    ppermute x4, starting transfers between devices, across(): lax.ppermute(array, 'space', [(i, (i + k) % spaces) for i in range(spaces)])  7.24 us
    all_to_all x1, starting transfers between devices, local(): lax.all_to_all(tokens.reshape(times, size, frames, width), 'tm', 0, 0, ti...  5.98 us
    all_to_all x1, starting transfers between devices, local(): lax.all_to_all(o_all.reshape(spaces * times, frames * size, cols), ('spac...  5.87 us
    unnamed x32, local copies, waits for them, and re-layouts  5.34 us
    unnamed x1, blocking collectives  5.12 us
    pallas_call x1, Pallas kernels, local(): call(functools.partial(kernel_spatial, chunked=chunked), o_shape, 6, 2 *...  4.85 us
  transfers between devices with their start and end apart: 9, of which 6 were waited for; matrix products, arithmetic and copies ran while one was open for 7% of the time, Pallas kernels for 8%

profile of v1, /device:TPU:0, one launch (start us, length us, event | category | flops | bytes accessed | tf_op | source)
XLA Modules:
  0.0 105.3 jit_solution(11959818781229168713)
XLA Ops:
  0.0 1.2 %copy.28 = bf16[128,2,1152]{2,0,1:T(8,128)(2,1)S(1)} copy(bf16[128,2,1152]{2,1,0:T(2,128)(2,1)} %param.10) | data formatting | bytes 1179648 | tf_op args[0]
  1.2 3.0 %collective-permute-start = (bf16[128,2,1152]{2,0,1:T(8,128)(2,1)S(1)}, bf16[128,2,1152]{2,0,1:T(8,128)(2,1)S(1)}, u32[]{:S(2)}, u32[]{:S(2)}) collective-permute-start(bf16[128,2,1152]{2,0,1:T(8,128)(2,1)S(1)} %copy.28), channel_id=1, source_target_pairs={{0,1},{1,0},{2,3},{3,2},{4,5},{5,4},{6,7},{7,6},{8,9},{9,8},{10,11... | collective-permute-start | bytes 1769480 | tf_op jit(solution)/shard_map/ppermute | solution.py:184
  4.2 2.3 %constant_dynamic-slice_fusion.2 = bf16[2,216,1152]{2,1,0:T(8,128)(2,1)} fusion(bf16[4,216,1152]{2,1,0:T(8,128)(2,1)} %bitcast.44, s32[]{:T(128)S(6)} %select_n.35), kind=kLoop, calls=%fused_computation.5 | loop fusion | bytes 1990660 | tf_op jit(solution)/shard_map/dynamic_slice | solution.py:203
  6.6 11.0 %collective-permute-done = bf16[128,2,1152]{2,0,1:T(8,128)(2,1)S(1)} collective-permute-done((bf16[128,2,1152]{2,0,1:T(8,128)(2,1)S(1)}, bf16[128,2,1152]{2,0,1:T(8,128)(2,1)S(1)}, u32[]{:S(2)}, u32[]{:S(2)}) %collective-permute-start) | collective-permute-done | bytes 589856 | tf_op jit(solution)/shard_map/ppermute | solution.py:184
  17.5 0.8 copy-done.6
  18.4 1.7 %collective-permute-start.3 = (bf16[2,216,1152]{2,1,0:T(8,128)(2,1)}, bf16[2,216,1152]{2,1,0:T(8,128)(2,1)}, u32[]{:S(2)}, u32[]{:S(2)}) collective-permute-start(bf16[2,216,1152]{2,1,0:T(8,128)(2,1)} %constant_dynamic-slice_fusion.2), channel_id=1, source_target_pairs={{0,1},{1,0},{2,3},{3,2},{4,5},{5,4},{6,7},{7,6},{8,9},{9,8},{10,11... | collective-permute-start | bytes 2985992 | tf_op jit(solution)/shard_map/ppermute | solution.py:184
  20.1 0.9 copy.21
  21.0 6.0 %all-to-all-start.1 = ((bf16[16,8,2,1152]{3,1,2,0:T(8,128)(2,1)}), bf16[16,8,2,1152]{3,1,2,0:T(8,128)(2,1)}, u32[]{:S(2)}, u32[]{:S(2)}) async-start(bf16[16,8,2,1152]{3,1,2,0:T(8,128)(2,1)} %copy.21), calls=%async_computation.1 | async-start | bytes 1179648 | tf_op jit(solution)/shard_map/all_to_all | solution.py:193
  27.0 14.9 %collective-permute-done.3.refs_1_ = bf16[2,216,1152]{2,1,0:T(8,128)(2,1)} collective-permute-done((bf16[2,216,1152]{2,1,0:T(8,128)(2,1)}, bf16[2,216,1152]{2,1,0:T(8,128)(2,1)}, u32[]{:S(2)}, u32[]{:S(2)}) %collective-permute-start.3) | collective-permute-done | bytes 995360 | tf_op jit(solution)/shard_map/ppermute | solution.py:184
  41.9 1.4 %collective-permute-start.1 = (bf16[144,1152]{1,0:T(8,128)(2,1)S(1)}, bf16[144,1152]{1,0:T(8,128)(2,1)}, u32[]{:S(2)}, u32[]{:S(2)}) collective-permute-start(bf16[144,1152]{1,0:T(8,128)(2,1)S(1)} %constant_dynamic-slice_fusion.1), channel_id=1, source_target_pairs={{0,1},{1,0},{2,3},{3,2},{4,5},{5,4},{6,7},{7,6},{8,9},{9,8},{10,11... | collective-permute-start | bytes 995336 | tf_op jit(solution)/shard_map/ppermute | solution.py:184
  43.6 1.1 %copy-done.3 = bf16[128,2,1152]{2,0,1:T(8,128)(2,1)S(1)} copy-done((bf16[128,2,1152]{2,0,1:T(8,128)(2,1)S(1)}, bf16[128,2,1152]{2,0,1:T(8,128)(2,1)}, u32[]{:S(2)}) %copy-start.3) | copy-done | bytes 589848
  44.7 1.2 %shard_map.100.own_ref = bf16[4,3,72,256]{3,2,1,0:T(8,128)(2,1)S(1)} custom-call(bf16[2,128,1152]{2,1,0:T(8,128)(2,1)S(1)} %bitcast.38, f32[6,1152]{1,0:T(8,128)S(1)} %copy-done.5, bf16[4,216,1152]{2,1,0:T(8,128)(2,1)S(1)} %bitcast.36, f32[4,216,1]{2,1,0:T(8,128)S(1)} %reshape.125.b_ref), custom_call_target="tpu_custom_call" | custom-call | flops 509607936 | bytes 3000000 | tf_op jit(solution)/shard_map/pallas_call | solution.py:198
  46.0 6.2 %collective-permute-done.1 = bf16[144,1152]{1,0:T(8,128)(2,1)} collective-permute-done((bf16[144,1152]{1,0:T(8,128)(2,1)S(1)}, bf16[144,1152]{1,0:T(8,128)(2,1)}, u32[]{:S(2)}, u32[]{:S(2)}) %collective-permute-start.1) | collective-permute-done | bytes 331808 | tf_op jit(solution)/shard_map/ppermute | solution.py:184
  52.2 4.8 %shard_map.101 = bf16[2,16,2,8,288]{4,3,2,1,0:T(8,128)(2,1)} custom-call(s32[2]{0:T(128)S(1)} %pad_add_fusion.ids_ref, bf16[1,2,128,1152]{3,2,1,0:T(8,128)(2,1)S(1)} %bitcast.43, bf16[4,3,72,256]{3,2,1,0:T(8,128)(2,1)S(1)} %shard_map.100.own_ref, f32[6,1152]{1,0:T(8,128)S(1)} %copy-done.5, bf16[4,216,1152]{2,1,0:T(8,128)(2,1)S(1)} %bitcast.37, ...), custom_call_target="tpu_custom_call" | custom-call | flops 660602880 | bytes 4000000 | tf_op jit(solution)/shard_map/pallas_call | solution.py:222
  57.1 5.9 %all-to-all-start = ((bf16[32,16,288]{2,1,0:T(8,128)(2,1)}), bf16[32,16,288]{2,1,0:T(8,128)(2,1)S(1)}, u32[]{:S(2)}, u32[]{:S(2)}) async-start(bf16[32,16,288]{2,1,0:T(8,128)(2,1)} %bitcast.9), calls=%async_computation | async-start | bytes 786432 | tf_op jit(solution)/shard_map/all_to_all | solution.py:234
  63.0 0.6 dynamic-slice
  64.6 5.1 %all-reduce = f32[1728]{0:T(1024)S(1)} all-reduce(f32[1728]{0:T(1024)S(1)} %dynamic-update-slice), channel_id=1, replica_groups=mesh['grp'=1,'tm'=16,'space'=2] {'space'}, use_global_device_ids=true, to_apply=%add | all-reduce | flops 1728 | bytes 13824
  69.7 0.7 reshape.126.b_ref
  70.4 1.3 %maximum_select_fusion.other_w_ref = bf16[1,288,1152]{2,1,0:T(8,128)(2,1)S(1)} fusion(bf16[1,144,1152]{2,1,0:T(8,128)(2,1)S(1)} %bitcast.48, bf16[1,144,1152]{2,1,0:T(8,128)(2,1)} %bitcast.14, pred[]{:T(512)S(6)} %eq.5), kind=kLoop, calls=%fused_computation | loop fusion | flops 2985984 | bytes 1327105 | tf_op jit(solution)/shard_map/jit(_where)/select_n | solution.py:211
  71.7 4.4 %all-to-all-done = bf16[32,16,288]{2,1,0:T(8,128)(2,1)S(1)} async-done(((bf16[32,16,288]{2,1,0:T(8,128)(2,1)}), bf16[32,16,288]{2,1,0:T(8,128)(2,1)S(1)}, u32[]{:S(2)}, u32[]{:S(2)}) %all-to-all-start) | async-done | bytes 294944 | tf_op jit(solution)/shard_map/all_to_all | solution.py:234
  76.1 9.9 %shard_map.102 = bf16[8,72,256]{2,1,0:T(8,128)(2,1)S(1)} custom-call(s32[2]{0:T(128)S(1)} %pad_add_fusion.ids_ref, bf16[2,256,288]{2,1,0:T(8,128)(2,1)S(1)} %bitcast.40, bf16[256,1152]{1,0:T(8,128)(2,1)} %bitcast.13.x_ref, bf16[288,1152]{1,0:T(8,128)(2,1)S(1)} %copy-done.1, bf16[1,288,1152]{2,1,0:T(8,128)(2,1)S(1)} %maximum_select_fusion.other_w_ref, ...), custom_call_target="tpu_custom_call" | custom-call | flops 1509949440 | bytes 8000000 | tf_op jit(solution)/shard_map/pallas_call | solution.py:245
  86.0 0.3 copy.23
  86.3 1.1 %reshape.114 = bf16[16,16,576]{2,1,0:T(8,128)(2,1)} reshape(bf16[256,8,72]{2,1,0:T(8,128)(2,1)S(1)} %copy.23) | data formatting | bytes 589824 | tf_op jit(solution)/shard_map/reshape | solution.py:253
  87.4 3.5 %all-to-all-start.2 = ((bf16[16,16,576]{2,1,0:T(8,128)(2,1)}), bf16[16,16,576]{2,1,0:T(8,128)(2,1)S(1)}, u32[]{:S(2)}, u32[]{:S(2)}) async-start(bf16[16,16,576]{2,1,0:T(8,128)(2,1)} %reshape.114), calls=%async_computation.2 | async-start | bytes 655360 | tf_op jit(solution)/shard_map/all_to_all | solution.py:254
  91.0 1.1 %constant_dynamic-slice_fusion = (bf16[1,16,2,8,288]{4,3,2,1,0:T(8,128)(2,1)S(1)}, bf16[16,2,8,288]{3,2,1,0:T(8,128)(2,1)S(1)}) fusion(bf16[2,16,2,8,288]{4,3,2,1,0:T(8,128)(2,1)} %shard_map.101, s32[]{:T(128)S(6)} %select_n.39, s32[]{:T(128)S(6)} %select_n.41), kind=kLoop, calls=%fused_computation.3 | loop fusion | bytes 589832 | tf_op jit(solution)/shard_map/jit(dynamic_index_in_dim)/dynamic_slice | solution.py:237
  92.0 1.1 %collective-permute-start.5 = (bf16[16,2,8,288]{3,2,1,0:T(8,128)(2,1)S(1)}, bf16[16,2,8,288]{3,2,1,0:T(8,128)(2,1)S(1)}, u32[]{:S(2)}, u32[]{:S(2)}) collective-permute-start(bf16[16,2,8,288]{3,2,1,0:T(8,128)(2,1)S(1)} %get-tuple-element.14), channel_id=1, source_target_pairs={{0,1},{1,0},{2,3},{3,2},{4,5},{5,4},{6,7},{7,6},{8,9},{9,8},{10,11... | collective-permute-start | bytes 442376 | tf_op jit(solution)/shard_map/ppermute | solution.py:184
  93.1 6.1 %collective-permute-done.5 = bf16[16,2,8,288]{3,2,1,0:T(8,128)(2,1)S(1)} collective-permute-done((bf16[16,2,8,288]{3,2,1,0:T(8,128)(2,1)S(1)}, bf16[16,2,8,288]{3,2,1,0:T(8,128)(2,1)S(1)}, u32[]{:S(2)}, u32[]{:S(2)}) %collective-permute-start.5) | collective-permute-done | bytes 147488 | tf_op jit(solution)/shard_map/ppermute | solution.py:184
  99.3 2.0 %shard_map.103.y_ref = bf16[256,1152]{1,0:T(8,128)(2,1)S(1)} custom-call(bf16[2,256,288]{2,1,0:T(8,128)(2,1)S(1)} %pad_maximum_fusion.o_ref, bf16[256,1152]{1,0:T(8,128)(2,1)} %bitcast.23.x_ref, bf16[288,1152]{1,0:T(8,128)(2,1)S(1)} %copy-done.1, bf16[1,288,1152]{2,1,0:T(8,128)(2,1)S(1)} %maximum_select_fusion.other_w_ref, ...), custom_call_target="tpu_custom_call" | custom-call | flops 339738624 | bytes 3000000 | tf_op jit(solution)/shard_map/pallas_call | solution.py:257
  101.2 0.8 all-to-all-done.2
  102.0 1.3 %copy-done.4 = bf16[576,1152]{1,0:T(8,128)(2,1)S(1)} copy-done((bf16[576,1152]{1,0:T(8,128)(2,1)S(1)}, bf16[576,1152]{1,0:T(8,128)(2,1)}, u32[]{:S(2)}) %copy-start.4) | copy-done | bytes 1327128
  103.3 0.7 shard_map.104
  104.0 1.3 %copy.25 = bf16[16,8,2,1152]{3,2,1,0:T(2,128)(2,1)} copy(bf16[16,8,2,1152]{3,1,2,0:T(8,128)(2,1)S(1)} %bitcast.39) | data formatting | bytes 1179648 | tf_op jit(solution)/shard_map/transpose | solution.py:263
  (38 shorter events, 0.9 us)
Async XLA Ops:
  0.0 4.2 %copy-start.1 = (bf16[288,1152]{1,0:T(8,128)(2,1)S(1)}, bf16[288,1152]{1,0:T(8,128)(2,1)}, u32[]{:S(2)}) copy-start(bf16[288,1152]{1,0:T(8,128)(2,1)} %out_w_ref.3) | copy-start | bytes 1990660
  1.2 5.4 %copy-start.2 = (bf16[128,2,1152]{2,0,1:T(8,128)(2,1)}, bf16[128,2,1152]{2,0,1:T(8,128)(2,1)S(1)}, u32[]{:S(2)}) copy-start(bf16[128,2,1152]{2,0,1:T(8,128)(2,1)S(1)} %copy.28) | copy-start | bytes 1769476
  1.2 16.3 %collective-permute-start = (bf16[128,2,1152]{2,0,1:T(8,128)(2,1)S(1)}, bf16[128,2,1152]{2,0,1:T(8,128)(2,1)S(1)}, u32[]{:S(2)}, u32[]{:S(2)}) collective-permute-start(bf16[128,2,1152]{2,0,1:T(8,128)(2,1)S(1)} %copy.28), channel_id=1, source_target_pairs={{0,1},{1,0},{2,3},{3,2},{4,5},{5,4},{6,7},{7,6},{8,9},{9,8},{10,11... | collective-permute-start | bytes 1769480 | tf_op jit(solution)/shard_map/ppermute | solution.py:184
  4.2 15.9 %copy-start.8 = (bf16[128,2,1152]{2,1,0:T(2,128)(2,1)S(1)}, bf16[128,2,1152]{2,1,0:T(2,128)(2,1)}, u32[]{:S(2)}) copy-start(bf16[128,2,1152]{2,1,0:T(2,128)(2,1)} %param.10) | copy-start | bytes 1769476
  6.6 36.7 %copy-start.11 = (f32[864]{0:T(1024)S(1)}, f32[864]{0:T(1024)}, u32[]{:S(2)}) copy-start(f32[864]{0:T(1024)} %param.13) | copy-start | bytes 10372
  17.5 0.8 copy-start.6
  18.4 23.5 %collective-permute-start.3 = (bf16[2,216,1152]{2,1,0:T(8,128)(2,1)}, bf16[2,216,1152]{2,1,0:T(8,128)(2,1)}, u32[]{:S(2)}, u32[]{:S(2)}) collective-permute-start(bf16[2,216,1152]{2,1,0:T(8,128)(2,1)} %constant_dynamic-slice_fusion.2), channel_id=1, source_target_pairs={{0,1},{1,0},{2,3},{3,2},{4,5},{5,4},{6,7},{7,6},{8,9},{9,8},{10,11... | collective-permute-start | bytes 2985992 | tf_op jit(solution)/shard_map/ppermute | solution.py:184
  20.1 23.5 %copy-start = (bf16[1152,864]{0,1:T(8,128)(2,1)S(1)}, bf16[1152,864]{0,1:T(8,128)(2,1)}, u32[]{:S(2)}) copy-start(bf16[1152,864]{0,1:T(8,128)(2,1)} %param.12) | copy-start | bytes 5971972
  20.1 23.5 %copy-start.5 = (f32[6,1152]{1,0:T(8,128)S(1)}, f32[6,1152]{1,0:T(8,128)}, u32[]{:S(2)}) copy-start(f32[6,1152]{1,0:T(8,128)} %mod_ref.9) | copy-start | bytes 82948
  21.0 36.1 %all-to-all-start.1 = ((bf16[16,8,2,1152]{3,1,2,0:T(8,128)(2,1)}), bf16[16,8,2,1152]{3,1,2,0:T(8,128)(2,1)}, u32[]{:S(2)}, u32[]{:S(2)}) async-start(bf16[16,8,2,1152]{3,1,2,0:T(8,128)(2,1)} %copy.21), calls=%async_computation.1 | async-start | bytes 1179648 | tf_op jit(solution)/shard_map/all_to_all | solution.py:193
  41.9 34.2 %collective-permute-start.4 = (bf16[2,216,1152]{2,1,0:T(8,128)(2,1)}, bf16[2,216,1152]{2,1,0:T(8,128)(2,1)}, u32[]{:S(2)}, u32[]{:S(2)}) collective-permute-start(bf16[2,216,1152]{2,1,0:T(8,128)(2,1)} %collective-permute-done.3.refs_1_), channel_id=1, source_target_pairs={{0,2},{2,0},{4,6},{6,4},{8,10},{10,8},{12,14},{14,12},{16,18},{18,... | collective-permute-start | bytes 2985992 | tf_op jit(solution)/shard_map/ppermute | solution.py:187
  41.9 10.3 %collective-permute-start.1 = (bf16[144,1152]{1,0:T(8,128)(2,1)S(1)}, bf16[144,1152]{1,0:T(8,128)(2,1)}, u32[]{:S(2)}, u32[]{:S(2)}) collective-permute-start(bf16[144,1152]{1,0:T(8,128)(2,1)S(1)} %constant_dynamic-slice_fusion.1), channel_id=1, source_target_pairs={{0,1},{1,0},{2,3},{3,2},{4,5},{5,4},{6,7},{7,6},{8,9},{9,8},{10,11... | collective-permute-start | bytes 995336 | tf_op jit(solution)/shard_map/ppermute | solution.py:184
  43.6 1.1 %copy-start.3 = (bf16[128,2,1152]{2,0,1:T(8,128)(2,1)S(1)}, bf16[128,2,1152]{2,0,1:T(8,128)(2,1)}, u32[]{:S(2)}) copy-start(bf16[128,2,1152]{2,0,1:T(8,128)(2,1)} %copy-done.2) | copy-start | bytes 1769476
  44.7 7.5 %copy-start.7 = (bf16[128,2,1152]{2,0,1:T(8,128)(2,1)S(1)}, bf16[128,2,1152]{2,0,1:T(8,128)(2,1)}, u32[]{:S(2)}) copy-start(bf16[128,2,1152]{2,0,1:T(8,128)(2,1)} %copy-done.6) | copy-start | bytes 1769476
  52.2 18.2 %collective-permute-start.2 = (bf16[144,1152]{1,0:T(8,128)(2,1)}, bf16[144,1152]{1,0:T(8,128)(2,1)S(1)}, u32[]{:S(2)}, u32[]{:S(2)}) collective-permute-start(bf16[144,1152]{1,0:T(8,128)(2,1)} %collective-permute-done.1), channel_id=1, source_target_pairs={{0,2},{2,0},{4,6},{6,4},{8,10},{10,8},{12,14},{14,12},{16,18},{18,... | collective-permute-start | bytes 995336 | tf_op jit(solution)/shard_map/ppermute | solution.py:187
  52.2 10.8 %copy-start.9 = (f32[1152]{0:T(1024)S(1)}, f32[1152]{0:T(1024)}, u32[]{:S(2)}) copy-start(f32[1152]{0:T(1024)} %param.15) | copy-start | bytes 13828
  52.2 10.8 %copy-start.13 = (u32[32]{0:T(128)S(1)}, u32[32]{0:T(128)}, u32[]{:S(2)}) copy-start(u32[32]{0:T(128)} %constant.41) | copy-start | bytes 388
  52.2 12.0 %copy-start.12 = (f32[864]{0:T(1024)S(1)}, f32[864]{0:T(1024)}, u32[]{:S(2)}) copy-start(f32[864]{0:T(1024)} %param.17) | copy-start | bytes 10372
  57.1 19.0 %all-to-all-start = ((bf16[32,16,288]{2,1,0:T(8,128)(2,1)}), bf16[32,16,288]{2,1,0:T(8,128)(2,1)S(1)}, u32[]{:S(2)}, u32[]{:S(2)}) async-start(bf16[32,16,288]{2,1,0:T(8,128)(2,1)} %bitcast.9), calls=%async_computation | async-start | bytes 786432 | tf_op jit(solution)/shard_map/all_to_all | solution.py:234
  86.3 6.8 %copy-start.10 = (f32[1152]{0:T(1024)S(1)}, f32[1152]{0:T(1024)}, u32[]{:S(2)}) copy-start(f32[1152]{0:T(1024)} %param.19) | copy-start | bytes 13828
  87.4 14.6 %all-to-all-start.2 = ((bf16[16,16,576]{2,1,0:T(8,128)(2,1)}), bf16[16,16,576]{2,1,0:T(8,128)(2,1)S(1)}, u32[]{:S(2)}, u32[]{:S(2)}) async-start(bf16[16,16,576]{2,1,0:T(8,128)(2,1)} %reshape.114), calls=%async_computation.2 | async-start | bytes 655360 | tf_op jit(solution)/shard_map/all_to_all | solution.py:254
  92.0 7.1 %collective-permute-start.5 = (bf16[16,2,8,288]{3,2,1,0:T(8,128)(2,1)S(1)}, bf16[16,2,8,288]{3,2,1,0:T(8,128)(2,1)S(1)}, u32[]{:S(2)}, u32[]{:S(2)}) collective-permute-start(bf16[16,2,8,288]{3,2,1,0:T(8,128)(2,1)S(1)} %get-tuple-element.14), channel_id=1, source_target_pairs={{0,1},{1,0},{2,3},{3,2},{4,5},{5,4},{6,7},{7,6},{8,9},{9,8},{10,11... | collective-permute-start | bytes 442376 | tf_op jit(solution)/shard_map/ppermute | solution.py:184
  102.0 1.3 %copy-start.4 = (bf16[576,1152]{1,0:T(8,128)(2,1)S(1)}, bf16[576,1152]{1,0:T(8,128)(2,1)}, u32[]{:S(2)}) copy-start(bf16[576,1152]{1,0:T(8,128)(2,1)} %w_ref.1) | copy-start | bytes 3981316

commit v2 on v1

--- a/solution.py
+++ b/solution.py
@@ -43,8 +43,8 @@
     return mm(v_t, expon.astype(BF)) * (1.0 / total)
 
 
-def turned(values_t):
-    return values_t.astype(BF).T
+def after(arrays, *others):
+    return lax.optimization_barrier((*arrays, *others))[: len(arrays)]
 
 
 def kernel_qkv(x_ref, mod_ref, w_ref, b_ref, out_ref):
@@ -98,16 +98,7 @@
     return (tokens.astype(F32) + gate * (summed + outbias)).astype(BF)
 
 
-def kernel_temporal(ids_ref, o_ref, x_ref, out_w_ref, other_w_ref, outbias_ref, mod_ref, b_ref, *refs, size):
-    w_refs, out_ref = refs[:-1], refs[-1]
-    spaces, rows, _ = o_ref.shape
-    space, core = ids_ref[0], ids_ref[1]
-    parts = [mm(o_ref[space], out_w_ref[...])]
-    for k in range(1, spaces):
-        parts.append(mm(o_ref[lax.rem(space - k + spaces, spaces)], other_w_ref[k - 1]))
-    y = middle(x_ref[...], parts, outbias_ref[...], mod_ref[2:3, :])
-    h = modulated(y.astype(F32), mod_ref[3:4, :], mod_ref[4:5, :]).astype(BF)
-
+def temporal_mask(rows, size):
     def place(axis):
         row = lax.broadcasted_iota(jnp.int32, (rows, rows), axis)
         frame = row // (2 * size) * 2 + row % (2 * size) // size
@@ -116,27 +107,48 @@
     key_frame, key_patch = place(0)
     query_frame, query_patch = place(1)
     back = query_frame - key_frame
-    mask = (key_patch == query_patch) & (back >= 0) & (back < WIN)
-
-    heads = w_refs[0].shape[0]
+    return (key_patch == query_patch) & (back >= 0) & (back < WIN)
+
+
+def temporal_head(w, b, h, mask):
+    qkv = (mm(w, h, NT) + b).astype(BF)
+    return attend(qkv[0:HD], qkv[HD : 2 * HD], qkv[2 * HD : 3 * HD], mask)
+
+
+def kernel_temporal(o_ref, x_ref, out_w_ref, outbias_ref, mod_ref, b_ref, w_ref, h_ref, out_ref, *, size):
+    spaces, rows, _ = o_ref.shape
+    parts = [mm(o_ref[g], out_w_ref[g]) for g in range(spaces)]
+    y = middle(x_ref[...], parts, outbias_ref[...], mod_ref[2:3, :])
+    h = modulated(y.astype(F32), mod_ref[3:4, :], mod_ref[4:5, :]).astype(BF)
+    h_ref[...] = h
+    mask = temporal_mask(rows, size)
+    for i in range(w_ref.shape[0]):
+        out_ref[i] = temporal_head(w_ref[i], b_ref[i], h, mask)
+
+
+def kernel_rest(ids_ref, h_ref, own_ref, b_ref, *refs, size):
+    w_refs, (out_ref, turn_ref) = refs[:-2], refs[-2:]
+    h = h_ref[...]
+    rows = h.shape[0]
+    mask = temporal_mask(rows, size)
+    heads = own_ref.shape[0]
     half = heads // 2
-    done, order = [], []
+    spaces = turn_ref.shape[0] // heads
+    space, core = ids_ref[0], ids_ref[1]
+    for i in range(heads):
+        turn_ref[space * heads + i] = own_ref[i]
     for n, w_ref in enumerate(w_refs):
-        if n == 0:
-            first = space * heads
-        else:
-            first = lax.rem(space - (n + 1) // 2 + spaces, spaces) * heads
-            first = first + half * (core if n % 2 else 1 - core)
-        for i in range(w_ref.shape[0]):
-            qkv = (mm(w_ref[i], h, NT) + b_ref[first + i]).astype(BF)
-            o_t = attend(qkv[0:HD], qkv[HD : 2 * HD], qkv[2 * HD : 3 * HD], mask)
-            out_ref[first + i] = o_t.astype(BF)
-
-
-def kernel_home(o_ref, x_ref, out_w_ref, other_w_ref, outbias_ref, mod_ref, out_ref):
-    parts = [mm(o_ref[0], out_w_ref[...])]
-    for k in range(1, o_ref.shape[0]):
-        parts.append(mm(o_ref[k], other_w_ref[k - 1]))
+        shift = n // 2 + 1
+        within = half * (1 - core if n % 2 else core)
+        for i in range(half):
+            o_t = temporal_head(w_ref[i], b_ref[shift * heads + within + i], h, mask)
+            turn_ref[lax.rem(space - shift + spaces, spaces) * heads + within + i] = o_t
+    out_ref[...] = turn_ref[...].reshape(-1, rows).T.astype(BF)
+
+
+def kernel_home(ids_ref, o_ref, x_ref, out_w_ref, outbias_ref, mod_ref, out_ref):
+    spaces = o_ref.shape[0]
+    parts = [mm(o_ref[k], out_w_ref[lax.rem(ids_ref[0] - k + spaces, spaces)]) for k in range(spaces)]
     out_ref[...] = middle(x_ref[...], parts, outbias_ref[...], mod_ref[2:3, :])
 
 
@@ -189,8 +201,19 @@
     def frame_major(array):
         return jnp.swapaxes(array, -3, -2)
 
+    share = math.gcd(times, 4)
+    part = cols // share
+    gathered = lax.all_gather(
+        lax.dynamic_slice_in_dim(out_spatial, lax.rem(time, share) * part, part, 0),
+        ("space", "tm"),
+        axis=0,
+        tiled=True,
+        axis_index_groups=[
+            [s * times + g * share + i for s in range(spaces) for i in range(share)] for g in range(times // share)
+        ],
+    ).reshape(spaces, cols, width)
+
     arrived = [across(tokens, k) for k in range(1, spaces)]
-    spread = lax.all_to_all(tokens.reshape(times, size, frames, width), "tm", 0, 0, tiled=True)
 
     w_spatial = qkv_spatial.T.reshape(heads, 3 * HD, width)
     b_spatial = bias_spatial.reshape(heads, 3 * HD, 1)
@@ -199,22 +222,15 @@
         own_tokens, modulation, w_spatial, b_spatial
     )
 
+    (spread,) = after((tokens,), own)
+    spread = lax.all_to_all(spread.reshape(times, size, frames, width), "tm", 0, 0, tiled=True)
+
     w_temporal = qkv_temporal.T.reshape(heads, 3 * HD, width)
     my_heads = lax.dynamic_slice_in_dim(w_temporal, core * half, half, 0)
-    my_out = lax.dynamic_slice_in_dim(out_spatial, core * half * HD, half * HD, 0)
-    my_heads, my_out, *arrived = lax.optimization_barrier((my_heads, my_out, *arrived))
-    other_out, other_heads = [], []
-    for k in range(1, spaces):
-        direct = across(my_out, k)
-        passed = beside(direct)
-        other_out.append(
-            jnp.where(core == 0, jnp.concatenate([direct, passed]), jnp.concatenate([passed, direct]))
-        )
-    for k in range(1, spaces):
-        direct = across(my_heads, k)
-        other_heads += [direct, beside(direct)]
-    other_out = jnp.stack(other_out)
-    b_temporal = lax.all_gather(bias_temporal, "space", axis=0, tiled=True)
+    (my_heads,) = after((my_heads,), own, *arrived)
+    arrived = [after((a,), own)[0] for a in arrived]
+    direct_heads = [across(my_heads, k) for k in range(1, spaces)]
+    b_temporal = jnp.stack([bias_temporal] + [across(bias_temporal, k) for k in range(1, spaces)])
     b_temporal = b_temporal.reshape(spaces * heads, 3 * HD, 1)
 
     chunked = size % 8 == 0
@@ -223,7 +239,7 @@
         functools.partial(kernel_spatial, chunked=chunked),
         o_shape,
         6,
-        2 * rows * width * cols * 3 * (spaces - 1) + 4 * rows * cols * patches * spaces * spaces,
+        1e10,
         4e6,
         True,
         [pltpu.VMEM((spaces - 1, heads, 3, HD, rows), BF)],
@@ -232,8 +248,12 @@
         o_all = jnp.transpose(o_all.reshape(spaces, frames, times, size, cols), (0, 2, 1, 3, 4))
 
     o_here = lax.all_to_all(
-        o_all.reshape(spaces * times, frames * size, cols), ("space", "tm"), 0, 0, tiled=True
+        after((o_all,), spread, b_temporal)[0].reshape(spaces * times, frames * size, cols), ("space", "tm"), 0, 0, tiled=True
     ).reshape(spaces, rows, cols)
+    other_heads = []
+    for a in direct_heads:
+        other_heads += [a, beside(after((a,), o_here)[0])]
+
     o_home = [lax.dynamic_index_in_dim(o_all, space, 0, keepdims=False)]
     for k in range(1, spaces):
         o_home.append(across(lax.dynamic_index_in_dim(o_all, (space + k) % spaces, 0, keepdims=False), k))
@@ -242,20 +262,31 @@
     outbias_s = outbias_spatial.reshape(1, width)
     outbias_t = outbias_temporal.reshape(1, width)
     x_here = frame_major(spread).reshape(rows, width)
+    h_here, o_own = pl.pallas_call(
+        functools.partial(kernel_temporal, size=size),
+        out_shape=(jax.ShapeDtypeStruct((rows, width), BF), jax.ShapeDtypeStruct((heads, HD, rows), F32)),
+        in_specs=[VMEM] * 7,
+        out_specs=(VMEM, VMEM),
+        compiler_params=PARAMS,
+        cost_estimate=pl.CostEstimate(
+            flops=2 * rows * width * cols * (3 + spaces), bytes_accessed=5 * 10**6, transcendentals=0
+        ),
+    )(o_here, x_here, gathered, outbias_s, modulation, b_temporal, w_temporal)
     o_t = call(
-        functools.partial(kernel_temporal, size=size),
-        (spaces * heads, HD, rows),
-        8 + 1 + len(other_heads),
-        2 * rows * width * cols * 4 * spaces + 4 * rows * rows * cols * spaces,
-        8e6,
+        functools.partial(kernel_rest, size=size),
+        (rows, spaces * cols),
+        4 + len(other_heads),
+        2 * rows * width * cols * 3 * (spaces - 1),
+        5e6,
         True,
-    )(ids, o_here, x_here, out_spatial, other_out, outbias_s, modulation, b_temporal, w_temporal, *other_heads)
-    o_t = jnp.transpose(o_t, (2, 0, 1)).reshape(times, frames * size, spaces * cols)
+        [pltpu.VMEM((spaces * heads, HD, rows), F32)],
+    )(ids, h_here, o_own, b_temporal, *other_heads)
+    o_t = o_t.reshape(times, frames * size, spaces * cols)
     o_final = lax.all_to_all(o_t, "tm", 0, 0, tiled=True).reshape(rows, spaces * cols)
 
     x_home = jnp.swapaxes(tokens.reshape(times, size, frames, width), 1, 2).reshape(rows, width)
-    y_home = call(kernel_home, (rows, width), 6, 2 * rows * width * cols * spaces, 3e6)(
-        o_home, x_home, out_spatial, other_out, outbias_s, modulation
+    y_home = call(kernel_home, (rows, width), 6, 2 * rows * width * cols * spaces, 3e6, True)(
+        ids, o_home, x_home, gathered, outbias_s, modulation
     )
     result = call(kernel_final, (rows, width), 5, 2 * rows * width * cols * spaces, 3e6)(
         o_final, y_home, out_temporal, outbias_t, modulation

time: 106 us -> 102 us (0.962)
  waiting for transfers between devices: 43.3 us -> 26.2 us
  between operations: 0.87 us -> 13.6 us
  local copies, waits for them, and re-layouts: 13.3 us -> 20.2 us
  blocking collectives: 5.12 us -> 0 us
  starting transfers between devices: 22.6 us -> 21.1 us
  other arithmetic: 1.41 us -> 0.16 us
    ppermute x4, waiting for transfers between devices: 38.1 us -> 21.4 us  [across(): lax.ppermute(array, 'space', [(i, (i + k) % spaces) for i in range(spaces)])]
    unnamed x32 -> x45, local copies, waits for them, and re-layouts: 5.34 us -> 11.7 us
    unnamed x1 -> x0, blocking collectives: 5.12 us -> none
    ppermute x4, starting transfers between devices: 7.24 us -> 5.1 us  [across(): lax.ppermute(array, 'space', [(i, (i + k) % spaces) for i in range(spaces)])]
    all_to_all x1, starting transfers between devices: 3.54 us -> 5.18 us  [local(): lax.all_to_all(o_t, 'tm', 0, 0, tiled=True).reshape(rows, spaces * cols)]
    reshape x1, local copies, waits for them, and re-layouts: 0.29 us -> 1.75 us  [local(): b_spatial = bias_spatial.reshape(heads, 3 * HD, 1)]
    dynamic_slice x1, local copies, waits for them, and re-layouts: 2.31 us -> 1.03 us  [local(): my_heads = lax.dynamic_slice_in_dim(w_temporal, core * half, half, 0)]
    select_n x1 -> x0, other arithmetic: 1.25 us -> none  [local(): jnp.where(core == 0, jnp.concatenate([direct, passed]), jnp.concatenate([...]
  transfers between devices with their start and end apart: 9 -> 9, of which waited for: 6 -> 6; matrix products, arithmetic and copies ran while one was open for 7% -> 8% of each run, Pallas kernels for 8% -> 14%
where the time goes in v2:
time: 102 us; the launch traced here: 101 us
  waiting for transfers between devices  26.2 us (26%)
  starting transfers between devices  21.1 us (21%)
  local copies, waits for them, and re-layouts  20.2 us (20%)
  Pallas kernels  19.3 us (19%)
  between operations  13.6 us (13%)
    ppermute x4, waiting for transfers between devices, across(): lax.ppermute(array, 'space', [(i, (i + k) % spaces) for i in range(spaces)])  21.4 us
    unnamed x45, local copies, waits for them, and re-layouts  11.7 us
    all_to_all x1, starting transfers between devices, local(): lax.all_to_all(spread.reshape(times, size, frames, width), 'tm', 0, 0, ti...  6.55 us
    pallas_call x1, Pallas kernels, local(): call(functools.partial(kernel_spatial, chunked=chunked), o_shape, 6, 1000...  5.6 us
    pallas_call x1, Pallas kernels, local(): pl.pallas_call(functools.partial(kernel_temporal, size=size), out_shape=(...  5.53 us
    all_to_all x1, starting transfers between devices, local(): lax.all_to_all(o_t, 'tm', 0, 0, tiled=True).reshape(rows, spaces * cols)  5.18 us
    ppermute x4, starting transfers between devices, across(): lax.ppermute(array, 'space', [(i, (i + k) % spaces) for i in range(spaces)])  5.1 us
    pallas_call x1, Pallas kernels, local(): call(functools.partial(kernel_rest, size=size), (rows, spaces * cols), 4...  4.87 us
  transfers between devices with their start and end apart: 9, of which 6 were waited for; matrix products, arithmetic and copies ran while one was open for 8% of the time, Pallas kernels for 14%

profile of v2, /device:TPU:0, one launch (start us, length us, event | category | flops | bytes accessed | tf_op | source)
XLA Modules:
  0.0 100.6 jit_solution(17491306548751483349)
XLA Ops:
  6.5 3.0 %collective-permute-start.1 = (f32[864]{0:T(1024)}, f32[864]{0:T(1024)S(1)}, u32[]{:S(2)}, u32[]{:S(2)}) collective-permute-start(f32[864]{0:T(1024)} %param.17), channel_id=1, source_target_pairs={{0,1},{1,0},{2,3},{3,2},{4,5},{5,4},{6,7},{7,6},{8,9},{9,8},{10,11... | collective-permute-start | bytes 10376 | tf_op jit(solution)/shard_map/ppermute | solution.py:196
  9.6 1.1 %copy.27 = bf16[128,2,1152]{2,0,1:T(8,128)(2,1)S(1)} copy(bf16[128,2,1152]{2,1,0:T(2,128)(2,1)} %param.10) | data formatting | bytes 1179648 | tf_op args[0]
  11.6 1.8 %reshape.72.b_ref = f32[4,216,1]{2,1,0:T(8,128)} reshape(f32[864]{0:T(1024)} %param.13) | data formatting | bytes 6912 | tf_op jit(solution)/shard_map/reshape | solution.py:219
  13.4 1.0 %copy-done.6 = f32[4,216,1]{2,1,0:T(8,128)S(1)} copy-done((f32[4,216,1]{2,1,0:T(8,128)S(1)}, f32[4,216,1]{2,1,0:T(8,128)}, u32[]{:S(2)}) %copy-start.6) | copy-done | bytes 3480
  14.4 1.2 %shard_map.100.own_ref = bf16[4,3,72,256]{3,2,1,0:T(8,128)(2,1)S(1)} custom-call(bf16[2,128,1152]{2,1,0:T(8,128)(2,1)S(1)} %bitcast.39, f32[6,1152]{1,0:T(8,128)S(1)} %copy-done.11, bf16[4,216,1152]{2,1,0:T(8,128)(2,1)S(1)} %bitcast.42, f32[4,216,1]{2,1,0:T(8,128)S(1)} %copy-done.6), custom_call_target="tpu_custom_call" | custom-call | flops 509607936 | bytes 3000000 | tf_op jit(solution)/shard_map/pallas_call | solution.py:221
  15.7 0.8 copy-done.15
  16.5 0.9 copy.20
  17.3 6.5 %all-to-all-start = ((bf16[16,8,2,1152]{3,1,2,0:T(8,128)(2,1)}), bf16[16,8,2,1152]{3,1,2,0:T(8,128)(2,1)}, u32[]{:S(2)}, u32[]{:S(2)}) async-start(bf16[16,8,2,1152]{3,1,2,0:T(8,128)(2,1)} %copy.20), calls=%async_computation | async-start | bytes 1179648 | tf_op jit(solution)/shard_map/all_to_all | solution.py:226
  23.9 1.0 %constant_dynamic-slice_fusion.1 = bf16[2,216,1152]{2,1,0:T(8,128)(2,1)} fusion(bf16[4,216,1152]{2,1,0:T(8,128)(2,1)S(1)} %bitcast.37, s32[]{:T(128)S(6)} %select_n.21), kind=kLoop, calls=%fused_computation.4 | loop fusion | bytes 1990660 | tf_op jit(solution)/shard_map/dynamic_slice | solution.py:229
  25.8 1.7 %collective-permute-done = bf16[128,2,1152]{2,0,1:T(8,128)(2,1)} collective-permute-done((bf16[128,2,1152]{2,0,1:T(8,128)(2,1)S(1)}, bf16[128,2,1152]{2,0,1:T(8,128)(2,1)}, u32[]{:S(2)}, u32[]{:S(2)}) %collective-permute-start) | collective-permute-done | bytes 589856 | tf_op jit(solution)/shard_map/ppermute | solution.py:196
  27.9 1.6 %copy-done.5 = bf16[1152,864]{0,1:T(8,128)(2,1)S(1)} copy-done((bf16[1152,864]{0,1:T(8,128)(2,1)S(1)}, bf16[1152,864]{0,1:T(8,128)(2,1)}, u32[]{:S(2)}) %copy-start.5) | copy-done | bytes 1990680
  29.5 1.0 %copy-done.7 = f32[4,216,1]{2,1,0:T(8,128)S(1)} copy-done((f32[4,216,1]{2,1,0:T(8,128)S(1)}, f32[4,216,1]{2,1,0:T(8,128)}, u32[]{:S(2)}) %copy-start.7) | copy-done | bytes 3480
  30.5 1.0 %copy-done.16 = bf16[4,3,72,256]{3,2,1,0:T(8,128)(2,1)S(1)} copy-done((bf16[4,3,72,256]{3,2,1,0:T(8,128)(2,1)S(1)}, bf16[4,3,72,256]{3,2,1,0:T(8,128)(2,1)}, u32[]{:S(2)}) %copy-start.16) | copy-done | bytes 442392
  31.5 5.6 %shard_map.101 = bf16[2,16,2,8,288]{4,3,2,1,0:T(8,128)(2,1)} custom-call(s32[2]{0:T(128)S(1)} %pad_add_fusion.ids_ref, bf16[1,2,128,1152]{3,2,1,0:T(8,128)(2,1)} %bitcast.6.x_ref, bf16[4,3,72,256]{3,2,1,0:T(8,128)(2,1)S(1)} %copy-done.16, f32[6,1152]{1,0:T(8,128)S(1)} %copy-done.12, bf16[4,216,1152]{2,1,0:T(8,128)(2,1)S(1)} %bitcast.43, ...), custom_call_target="tpu_custom_call" | custom-call | flops 10000000000 | bytes 4000000 | tf_op jit(solution)/shard_map/pallas_call | solution.py:238
  37.1 2.5 %all-to-all-done = bf16[16,8,2,1152]{3,1,2,0:T(8,128)(2,1)} async-done(((bf16[16,8,2,1152]{3,1,2,0:T(8,128)(2,1)}), bf16[16,8,2,1152]{3,1,2,0:T(8,128)(2,1)}, u32[]{:S(2)}, u32[]{:S(2)}) %all-to-all-start) | async-done | bytes 589856 | tf_op jit(solution)/shard_map/all_to_all | solution.py:226
  39.6 4.1 %all-to-all-start.1 = ((bf16[32,16,288]{2,1,0:T(8,128)(2,1)}), bf16[32,16,288]{2,1,0:T(8,128)(2,1)S(1)}, u32[]{:S(2)}, u32[]{:S(2)}) async-start(bf16[32,16,288]{2,1,0:T(8,128)(2,1)} %bitcast.8), calls=%async_computation.1 | async-start | bytes 786432 | tf_op jit(solution)/shard_map/all_to_all | solution.py:250
  43.7 13.9 %collective-permute-done.2.refs_0_ = bf16[2,216,1152]{2,1,0:T(8,128)(2,1)} collective-permute-done((bf16[2,216,1152]{2,1,0:T(8,128)(2,1)}, bf16[2,216,1152]{2,1,0:T(8,128)(2,1)}, u32[]{:S(2)}, u32[]{:S(2)}) %collective-permute-start.2) | collective-permute-done | bytes 995360 | tf_op jit(solution)/shard_map/ppermute | solution.py:196
  57.6 1.1 %all-to-all-done.1 = bf16[32,16,288]{2,1,0:T(8,128)(2,1)S(1)} async-done(((bf16[32,16,288]{2,1,0:T(8,128)(2,1)}), bf16[32,16,288]{2,1,0:T(8,128)(2,1)S(1)}, u32[]{:S(2)}, u32[]{:S(2)}) %all-to-all-start.1) | async-done | bytes 294944 | tf_op jit(solution)/shard_map/all_to_all | solution.py:250
  59.6 1.0 %copy.21.b_ref = f32[8,216,1]{2,1,0:T(8,128)S(1)} copy(f32[8,216,1]{1,0,2:T(8,128)} %reshape.58) | data formatting | bytes 13824 | tf_op jit(solution)/shard_map/reshape | solution.py:234
  60.6 1.3 %copy-done.1 = bf16[576,1152]{1,0:T(8,128)(2,1)S(1)} copy-done((bf16[576,1152]{1,0:T(8,128)(2,1)S(1)}, bf16[576,1152]{1,0:T(8,128)(2,1)}, u32[]{:S(2)}) %copy-start.1) | copy-done | bytes 1327128
  62.0 1.0 copy-done.9
  63.0 0.8 copy-done.13
  63.7 5.5 %shard_map.102 = (bf16[256,1152]{1,0:T(8,128)(2,1)S(1)}, f32[4,72,256]{2,1,0:T(8,128)S(1)}) custom-call(bf16[2,256,288]{2,1,0:T(8,128)(2,1)S(1)} %bitcast.44, bf16[256,1152]{1,0:T(8,128)(2,1)} %bitcast.11.x_ref, bf16[2,288,1152]{2,1,0:T(8,128)(2,1)S(1)} %bitcast.35, f32[1,1152]{1,0:T(1,128)S(1)} %reshape.63.outbias_ref, f32[6,1152]{1,0:T(8,128)S(1)} %copy-done.13, ...), custom_call_target="tpu_custom_call" | custom-call | flops 849346560 | bytes 5000000 | tf_op jit(solution)/shard_map/pallas_call | solution.py:265
  69.3 4.9 %shard_map.103 = bf16[256,576]{1,0:T(8,128)(2,1)} custom-call(s32[2]{0:T(128)S(1)} %pad_add_fusion.ids_ref, bf16[256,1152]{1,0:T(8,128)(2,1)S(1)} %get-tuple-element.15.h_ref, f32[4,72,256]{2,1,0:T(8,128)S(1)} %get-tuple-element.16.own_ref, f32[8,216,1]{2,1,0:T(8,128)S(1)} %copy.21.b_ref, bf16[2,216,1152]{2,1,0:T(8,128)(2,1)} %collective-permute-done.2.refs_0_, ...), custom_call_target="tpu_custom_call" | custom-call | flops 509607936 | bytes 5000000 | tf_op jit(solution)/shard_map/pallas_call | solution.py:275
  74.2 5.2 %all-to-all-start.2 = ((bf16[16,16,576]{2,1,0:T(8,128)(2,1)}), bf16[16,16,576]{2,1,0:T(8,128)(2,1)S(1)}, u32[]{:S(2)}, u32[]{:S(2)}) async-start(bf16[16,16,576]{2,1,0:T(8,128)(2,1)} %bitcast.16), calls=%async_computation.2 | async-start | bytes 655360 | tf_op jit(solution)/shard_map/all_to_all | solution.py:285
  79.4 1.1 %constant_dynamic-slice_fusion = (bf16[1,16,2,8,288]{4,3,2,1,0:T(8,128)(2,1)S(1)}, bf16[16,2,8,288]{3,2,1,0:T(8,128)(2,1)S(1)}) fusion(bf16[2,16,2,8,288]{4,3,2,1,0:T(8,128)(2,1)} %shard_map.101, s32[]{:T(128)S(6)} %select_n.22, s32[]{:T(128)S(6)} %select_n.24), kind=kLoop, calls=%fused_computation.3 | loop fusion | bytes 589832 | tf_op jit(solution)/shard_map/jit(dynamic_index_in_dim)/dynamic_slice | solution.py:257
  80.4 1.4 %collective-permute-start.4 = (bf16[16,2,8,288]{3,2,1,0:T(8,128)(2,1)S(1)}, bf16[16,2,8,288]{3,2,1,0:T(8,128)(2,1)S(1)}, u32[]{:S(2)}, u32[]{:S(2)}) collective-permute-start(bf16[16,2,8,288]{3,2,1,0:T(8,128)(2,1)S(1)} %get-tuple-element.22), channel_id=1, source_target_pairs={{0,1},{1,0},{2,3},{3,2},{4,5},{5,4},{6,7},{7,6},{8,9},{9,8},{10,11... | collective-permute-start | bytes 442376 | tf_op jit(solution)/shard_map/ppermute | solution.py:196
  81.9 5.8 %collective-permute-done.4 = bf16[16,2,8,288]{3,2,1,0:T(8,128)(2,1)S(1)} collective-permute-done((bf16[16,2,8,288]{3,2,1,0:T(8,128)(2,1)S(1)}, bf16[16,2,8,288]{3,2,1,0:T(8,128)(2,1)S(1)}, u32[]{:S(2)}, u32[]{:S(2)}) %collective-permute-start.4) | collective-permute-done | bytes 147488 | tf_op jit(solution)/shard_map/ppermute | solution.py:196
  87.8 1.4 %shard_map.104.y_ref = bf16[256,1152]{1,0:T(8,128)(2,1)S(1)} custom-call(s32[2]{0:T(128)S(1)} %pad_add_fusion.ids_ref, bf16[2,256,288]{2,1,0:T(8,128)(2,1)S(1)} %pad_maximum_fusion.o_ref, bf16[256,1152]{1,0:T(8,128)(2,1)S(1)} %bitcast.40, bf16[2,288,1152]{2,1,0:T(8,128)(2,1)S(1)} %bitcast.36, f32[1,1152]{1,0:T(1,128)S(1)} %reshape.63.outbias_ref, ...), custom_call_target="tpu_custom_call" | custom-call | flops 339738624 | bytes 3000000 | tf_op jit(solution)/shard_map/pallas_call | solution.py:288
  89.2 1.2 %all-to-all-done.2 = bf16[16,16,576]{2,1,0:T(8,128)(2,1)S(1)} async-done(((bf16[16,16,576]{2,1,0:T(8,128)(2,1)}), bf16[16,16,576]{2,1,0:T(8,128)(2,1)S(1)}, u32[]{:S(2)}, u32[]{:S(2)}) %all-to-all-start.2) | async-done | bytes 294944 | tf_op jit(solution)/shard_map/all_to_all | solution.py:285
  90.5 1.3 %copy-done.10 = bf16[576,1152]{1,0:T(8,128)(2,1)S(1)} copy-done((bf16[576,1152]{1,0:T(8,128)(2,1)S(1)}, bf16[576,1152]{1,0:T(8,128)(2,1)}, u32[]{:S(2)}) %copy-start.10) | copy-done | bytes 1327128
  92.4 1.3 %copy.24 = bf16[16,8,2,1152]{3,2,1,0:T(2,128)(2,1)} copy(bf16[16,8,2,1152]{3,1,2,0:T(8,128)(2,1)S(1)} %bitcast.41) | data formatting | bytes 1179648 | tf_op jit(solution)/shard_map/transpose | solution.py:294
  (54 shorter events, 4.0 us)
Async XLA Ops:
  6.5 4.4 %copy-start = (bf16[288,1152]{1,0:T(8,128)(2,1)S(1)}, bf16[288,1152]{1,0:T(8,128)(2,1)}, u32[]{:S(2)}) copy-start(bf16[288,1152]{1,0:T(8,128)(2,1)} %param.14) | copy-start | bytes 1990660
  6.5 6.9 %copy-start.11 = (f32[6,1152]{1,0:T(8,128)S(1)}, f32[6,1152]{1,0:T(8,128)}, u32[]{:S(2)}) copy-start(f32[6,1152]{1,0:T(8,128)} %mod_ref.9) | copy-start | bytes 82948
  6.5 6.9 %copy-start.4 = (bf16[1152,864]{0,1:T(8,128)(2,1)S(1)}, bf16[1152,864]{0,1:T(8,128)(2,1)}, u32[]{:S(2)}) copy-start(bf16[1152,864]{0,1:T(8,128)(2,1)} %param.12) | copy-start | bytes 5971972
  6.5 54.1 %all-gather.2.cloned.1.call-start = ((), (), s32[]{:S(2)}) async-start(), calls=%async_computation.3 | async-start | bytes 1492992 | tf_op jit(solution)/shard_map/all_gather | solution.py:206
  6.5 18.5 %collective-permute-start.1 = (f32[864]{0:T(1024)}, f32[864]{0:T(1024)S(1)}, u32[]{:S(2)}, u32[]{:S(2)}) collective-permute-start(f32[864]{0:T(1024)} %param.17), channel_id=1, source_target_pairs={{0,1},{1,0},{2,3},{3,2},{4,5},{5,4},{6,7},{7,6},{8,9},{9,8},{10,11... | collective-permute-start | bytes 10376 | tf_op jit(solution)/shard_map/ppermute | solution.py:196
  10.7 16.7 %collective-permute-start = (bf16[128,2,1152]{2,0,1:T(8,128)(2,1)S(1)}, bf16[128,2,1152]{2,0,1:T(8,128)(2,1)}, u32[]{:S(2)}, u32[]{:S(2)}) collective-permute-start(bf16[128,2,1152]{2,0,1:T(8,128)(2,1)S(1)} %copy.27), channel_id=1, source_target_pairs={{0,1},{1,0},{2,3},{3,2},{4,5},{5,4},{6,7},{7,6},{8,9},{9,8},{10,11... | collective-permute-start | bytes 1769480 | tf_op jit(solution)/shard_map/ppermute | solution.py:196
  13.4 1.0 %copy-start.6 = (f32[4,216,1]{2,1,0:T(8,128)S(1)}, f32[4,216,1]{2,1,0:T(8,128)}, u32[]{:S(2)}) copy-start(f32[4,216,1]{2,1,0:T(8,128)} %reshape.72.b_ref) | copy-start | bytes 10372
  14.4 2.1 %copy-start.17 = (bf16[128,2,1152]{2,1,0:T(2,128)(2,1)S(1)}, bf16[128,2,1152]{2,1,0:T(2,128)(2,1)}, u32[]{:S(2)}) copy-start(bf16[128,2,1152]{2,1,0:T(2,128)(2,1)} %param.10) | copy-start | bytes 1769476
  15.7 0.8 copy-start.15
  16.5 7.5 %copy-start.3 = (bf16[1152,864]{0,1:T(8,128)(2,1)S(1)}, bf16[1152,864]{0,1:T(8,128)(2,1)}, u32[]{:S(2)}) copy-start(bf16[1152,864]{0,1:T(8,128)(2,1)} %param.16) | copy-start | bytes 5971972
  16.5 8.6 %copy-start.21 = (f32[864]{0:T(1024)S(1)}, f32[864]{0:T(1024)}, u32[]{:S(2)}) copy-start(f32[864]{0:T(1024)} %param.17) | copy-start | bytes 10372
  16.5 11.4 %copy-start.12 = (f32[6,1152]{1,0:T(8,128)S(1)}, f32[6,1152]{1,0:T(8,128)}, u32[]{:S(2)}) copy-start(f32[6,1152]{1,0:T(8,128)} %mod_ref.9) | copy-start | bytes 82948
  17.3 22.2 %all-to-all-start = ((bf16[16,8,2,1152]{3,1,2,0:T(8,128)(2,1)}), bf16[16,8,2,1152]{3,1,2,0:T(8,128)(2,1)}, u32[]{:S(2)}, u32[]{:S(2)}) async-start(bf16[16,8,2,1152]{3,1,2,0:T(8,128)(2,1)} %copy.20), calls=%async_computation | async-start | bytes 1179648 | tf_op jit(solution)/shard_map/all_to_all | solution.py:226
  27.4 30.2 %collective-permute-start.2 = (bf16[2,216,1152]{2,1,0:T(8,128)(2,1)}, bf16[2,216,1152]{2,1,0:T(8,128)(2,1)}, u32[]{:S(2)}, u32[]{:S(2)}) collective-permute-start(bf16[2,216,1152]{2,1,0:T(8,128)(2,1)} %constant_dynamic-slice_fusion.1), channel_id=1, source_target_pairs={{0,1},{1,0},{2,3},{3,2},{4,5},{5,4},{6,7},{7,6},{8,9},{9,8},{10,11... | collective-permute-start | bytes 2985992 | tf_op jit(solution)/shard_map/ppermute | solution.py:196
  27.9 1.6 %copy-start.5 = (bf16[1152,864]{0,1:T(8,128)(2,1)S(1)}, bf16[1152,864]{0,1:T(8,128)(2,1)}, u32[]{:S(2)}) copy-start(bf16[1152,864]{0,1:T(8,128)(2,1)} %param.12) | copy-start | bytes 5971972
  29.4 1.0 %copy-start.7 = (f32[4,216,1]{2,1,0:T(8,128)S(1)}, f32[4,216,1]{2,1,0:T(8,128)}, u32[]{:S(2)}) copy-start(f32[4,216,1]{2,1,0:T(8,128)} %reshape.72.b_ref) | copy-start | bytes 10372
  30.5 1.0 %copy-start.16 = (bf16[4,3,72,256]{3,2,1,0:T(8,128)(2,1)S(1)}, bf16[4,3,72,256]{3,2,1,0:T(8,128)(2,1)}, u32[]{:S(2)}) copy-start(bf16[4,3,72,256]{3,2,1,0:T(8,128)(2,1)} %copy-done.15) | copy-start | bytes 1327108
  31.5 28.1 %copy-start.19 = (f32[1152]{0:T(1024)S(1)}, f32[1152]{0:T(1024)}, u32[]{:S(2)}) copy-start(f32[1152]{0:T(1024)} %param.15) | copy-start | bytes 13828
  39.6 19.2 %all-to-all-start.1 = ((bf16[32,16,288]{2,1,0:T(8,128)(2,1)}), bf16[32,16,288]{2,1,0:T(8,128)(2,1)S(1)}, u32[]{:S(2)}, u32[]{:S(2)}) async-start(bf16[32,16,288]{2,1,0:T(8,128)(2,1)} %bitcast.8), calls=%async_computation.1 | async-start | bytes 786432 | tf_op jit(solution)/shard_map/all_to_all | solution.py:250
  58.7 0.7 copy-start.8
  59.5 9.8 %collective-permute-start.3 = (bf16[2,216,1152]{2,1,0:T(8,128)(2,1)}, bf16[2,216,1152]{2,1,0:T(8,128)(2,1)}, u32[]{:S(2)}, u32[]{:S(2)}) collective-permute-start(bf16[2,216,1152]{2,1,0:T(8,128)(2,1)} %collective-permute-done.2.refs_0_), channel_id=1, source_target_pairs={{0,2},{2,0},{4,6},{6,4},{8,10},{10,8},{12,14},{14,12},{16,18},{18,... | collective-permute-start | bytes 2985992 | tf_op jit(solution)/shard_map/ppermute | solution.py:199
  60.6 1.3 %copy-start.1 = (bf16[576,1152]{1,0:T(8,128)(2,1)S(1)}, bf16[576,1152]{1,0:T(8,128)(2,1)}, u32[]{:S(2)}) copy-start(bf16[576,1152]{1,0:T(8,128)(2,1)} %all-gather.2.cloned.1.call-done) | copy-start | bytes 3981316
  62.0 1.0 copy-start.9
  63.0 0.8 copy-start.13
  69.3 12.6 %copy-start.20 = (f32[1152]{0:T(1024)S(1)}, f32[1152]{0:T(1024)}, u32[]{:S(2)}) copy-start(f32[1152]{0:T(1024)} %param.19) | copy-start | bytes 13828
  69.3 12.5 %copy-start.18 = (bf16[128,2,1152]{2,1,0:T(2,128)(2,1)S(1)}, bf16[128,2,1152]{2,1,0:T(2,128)(2,1)}, u32[]{:S(2)}) copy-start(bf16[128,2,1152]{2,1,0:T(2,128)(2,1)} %param.10) | copy-start | bytes 1769476
  74.2 13.6 %copy-start.2 = (bf16[576,1152]{1,0:T(8,128)(2,1)S(1)}, bf16[576,1152]{1,0:T(8,128)(2,1)}, u32[]{:S(2)}) copy-start(bf16[576,1152]{1,0:T(8,128)(2,1)} %all-gather.2.cloned.1.call-done) | copy-start | bytes 3981316
  74.2 13.6 %copy-start.14 = (f32[6,1152]{1,0:T(8,128)S(1)}, f32[6,1152]{1,0:T(8,128)}, u32[]{:S(2)}) copy-start(f32[6,1152]{1,0:T(8,128)} %mod_ref.9) | copy-start | bytes 82948
  74.2 16.3 %all-to-all-start.2 = ((bf16[16,16,576]{2,1,0:T(8,128)(2,1)}), bf16[16,16,576]{2,1,0:T(8,128)(2,1)S(1)}, u32[]{:S(2)}, u32[]{:S(2)}) async-start(bf16[16,16,576]{2,1,0:T(8,128)(2,1)} %bitcast.16), calls=%async_computation.2 | async-start | bytes 655360 | tf_op jit(solution)/shard_map/all_to_all | solution.py:285
  80.4 7.3 %collective-permute-start.4 = (bf16[16,2,8,288]{3,2,1,0:T(8,128)(2,1)S(1)}, bf16[16,2,8,288]{3,2,1,0:T(8,128)(2,1)S(1)}, u32[]{:S(2)}, u32[]{:S(2)}) collective-permute-start(bf16[16,2,8,288]{3,2,1,0:T(8,128)(2,1)S(1)} %get-tuple-element.22), channel_id=1, source_target_pairs={{0,1},{1,0},{2,3},{3,2},{4,5},{5,4},{6,7},{7,6},{8,9},{9,8},{10,11... | collective-permute-start | bytes 442376 | tf_op jit(solution)/shard_map/ppermute | solution.py:196
  90.5 1.3 %copy-start.10 = (bf16[576,1152]{1,0:T(8,128)(2,1)S(1)}, bf16[576,1152]{1,0:T(8,128)(2,1)}, u32[]{:S(2)}) copy-start(bf16[576,1152]{1,0:T(8,128)(2,1)} %w_ref.1) | copy-start | bytes 3981316
Sparse Core Ops, SparseCore 0:
  11.8 31.3 all-gather.1

commit v3 on v2

v3 whole, which is shorter than its diff:
```python
import functools
import math

import jax
import jax.numpy as jnp
from jax import lax
from jax.experimental import pallas as pl
from jax.experimental.pallas import tpu as pltpu
from jax.sharding import PartitionSpec as P

HD = 72
WIN = 16
BF = jnp.bfloat16
F32 = jnp.float32
EXP2_SCALE = 1.0 / (math.sqrt(HD) * math.log(2.0))

VMEM = pl.BlockSpec(memory_space=pltpu.VMEM)
ANY = pl.BlockSpec(memory_space=pl.ANY)
SMEM = pl.BlockSpec(memory_space=pltpu.SMEM)
PARAMS = pltpu.CompilerParams(vmem_limit_bytes=63 * 1024 * 1024)

NT = (((1,), (1,)), ((), ()))
TN = (((0,), (0,)), ((), ()))


def mm(a, b, dims=(((1,), (0,)), ((), ()))):
    return lax.dot_general(a, b, dims, preferred_element_type=F32)


def modulated(values, offset_vec, scaling):
    center = jnp.mean(values, axis=-1, keepdims=True)
    moved = values - center
    spread = jnp.mean(moved * moved, axis=-1, keepdims=True)
    return moved * lax.rsqrt(spread + 1e-06) * (1.0 + scaling) + offset_vec


def attend(q_t, k_t, v_t, mask=None):
    scores = mm(k_t, q_t, TN)
    if mask is not None:
        scores = jnp.where(mask, scores, F32(-1e30))
    highest = jnp.max(scores, axis=0, keepdims=True)
    expon = jnp.exp2((scores - highest) * F32(EXP2_SCALE))
    total = jnp.sum(expon, axis=0, keepdims=True)
    return mm(v_t, expon.astype(BF)) * (1.0 / total)


def after(arrays, *others):
    return lax.optimization_barrier((*arrays, *others))[: len(arrays)]


def flat(ref, *index):
    block = ref[index] if index else ref[...]
    return block.reshape(-1, block.shape[-1])


def regroup(rows, frames):
    target = lax.broadcasted_iota(jnp.int32, (rows, rows), 0)
    source = lax.broadcasted_iota(jnp.int32, (rows, rows), 1)
    patches = rows // frames
    return (source == target % patches * frames + target // patches).astype(F32).astype(BF)


def spatial_rows(x, mod_ref, frames):
    h = modulated(x.astype(F32), mod_ref[0:1, :], mod_ref[1:2, :]).astype(BF)
    return mm(regroup(x.shape[0], frames), h).astype(BF)


def kernel_qkv(x_ref, mod_ref, w_ref, b_ref, out_ref):
    h = spatial_rows(flat(x_ref), mod_ref, x_ref.shape[1])
    bias = b_ref[...].T
    for i in range(w_ref.shape[0]):
        qkv = mm(w_ref[i], h, NT) + bias[:, i : i + 1]
        for c in range(3):
            out_ref[i, c] = qkv[c * HD : (c + 1) * HD].astype(BF)


def fetch(sources, targets, sems):
    copies = [pltpu.make_async_copy(a, b, sems.at[i]) for i, (a, b) in enumerate(zip(sources, targets))]
    for copy in copies:
        copy.start()
    return copies


def kernel_spatial(ids_ref, own_hbm, w_hbm, mod_ref, b_ref, *refs):
    x_refs, (out_ref, part_ref, own_ref, w_ref, sems) = refs[:-5], refs[-5:]
    copies = fetch((w_hbm, own_hbm), (w_ref, own_ref), sems)
    patches, frames, _ = x_refs[0].shape
    heads = w_ref.shape[0]
    spaces = len(x_refs) + 1
    bias = b_ref[...].T
    for j, x_ref in enumerate(x_refs):
        h = spatial_rows(flat(x_ref), mod_ref, frames)
        if j == 0:
            copies[0].wait()
        for i in range(heads):
            qkv = mm(w_ref[i], h, NT) + bias[:, i : i + 1]
            for c in range(3):
                part_ref[j, i, c] = qkv[c * HD : (c + 1) * HD].astype(BF)
    copies[1].wait()
    by_frame = []
    for f in range(frames):
        cols = slice(f * patches, (f + 1) * patches)
        done = []
        for i in range(heads):
            q_t, k_t, v_t = (
                jnp.concatenate(
                    [own_ref[i, c, :, cols]] + [part_ref[j, i, c, :, cols] for j in range(spaces - 1)],
                    axis=1,
                )
                for c in range(3)
            )
            done.append(attend(q_t, k_t, v_t))
        by_frame.append(jnp.concatenate(done, axis=0).astype(BF))
    back = regroup(patches * frames, frames)
    for j in range(spaces):
        mine = jnp.concatenate([o[:, j * patches : (j + 1) * patches] for o in by_frame], axis=1)
        out_ref[lax.rem(ids_ref[0] - j + spaces, spaces)] = lax.dot_general(
            back, mine, (((0,), (1,)), ((), ())), preferred_element_type=F32
        ).astype(BF)


def middle(tokens, parts, outbias, gate):
    summed = parts[0].astype(BF).astype(F32)
    for part in parts[1:]:
        summed = summed + part.astype(BF).astype(F32)
    return (tokens.astype(F32) + gate * (summed + outbias)).astype(BF)


def temporal_mask(rows, size, frames):
    def place(axis):
        row = lax.broadcasted_iota(jnp.int32, (rows, rows), axis)
        return row // (frames * size) * frames + row % frames, row // frames % size

    key_frame, key_patch = place(0)
    query_frame, query_patch = place(1)
    back = query_frame - key_frame
    return (key_patch == query_patch) & (back >= 0) & (back < WIN)


def temporal_head(w, b, h, mask):
    qkv = (mm(w, h, NT) + b).astype(BF)
    return attend(qkv[0:HD], qkv[HD : 2 * HD], qkv[2 * HD : 3 * HD], mask)


def out_places(pieces, out_w_ref, core):
    half = pieces[1].shape[0]
    places = [out_w_ref.at[0]]
    for n in range(1, len(pieces)):
        start = half * (core if n % 2 else 1 - core)
        places.append(out_w_ref.at[(n + 1) // 2, pl.ds(pl.multiple_of(start, half), half)])
    return places


def kernel_temporal(
    ids_ref, o_hbm, x_hbm, w_hbm, outbias_ref, mod_ref, b_ref, *refs, size, frames
):
    pieces, (h_ref, out_ref, o_ref, x_ref, out_w_ref, w_ref, sems) = refs[:-7], refs[-7:]
    copies = fetch(
        (*pieces, o_hbm, x_hbm, w_hbm),
        (*out_places(pieces, out_w_ref, ids_ref[1]), o_ref, x_ref, w_ref),
        sems,
    )
    spaces, rows, _ = o_ref.shape
    mask = temporal_mask(rows, size, frames)
    for copy in copies[:-1]:
        copy.wait()
    parts = [mm(o_ref[lax.rem(ids_ref[0] - k + spaces, spaces)], out_w_ref[k]) for k in range(spaces)]
    y = middle(flat(x_ref), parts, outbias_ref[...], mod_ref[2:3, :])
    h = modulated(y.astype(F32), mod_ref[3:4, :], mod_ref[4:5, :]).astype(BF)
    h_ref[...] = h
    bias = b_ref[...].T
    copies[-1].wait()
    for i in range(w_ref.shape[0]):
        out_ref[i] = temporal_head(w_ref[i], bias[:, i : i + 1], h, mask)


def kernel_rest(ids_ref, h_ref, own_ref, b_ref, *refs, size, frames):
    w_refs, (out_ref, turn_ref) = refs[:-2], refs[-2:]
    h = h_ref[...]
    rows = h.shape[0]
    mask = temporal_mask(rows, size, frames)
    heads = own_ref.shape[0]
    half = heads // 2
    spaces = turn_ref.shape[0] // heads
    space, core = ids_ref[0], ids_ref[1]
    bias = b_ref[...].T
    for i in range(heads):
        turn_ref[space * heads + i] = own_ref[i]
    for n, w_ref in enumerate(w_refs):
        shift = n // 2 + 1
        second = (core == 0) == (n % 2 == 1)
        within = jnp.where(second, half, 0)
        for i in range(half):
            first = shift * heads + i
            column = jnp.where(second, bias[:, first + half : first + half + 1], bias[:, first : first + 1])
            o_t = temporal_head(w_ref[i], column, h, mask)
            turn_ref[lax.rem(space - shift + spaces, spaces) * heads + within + i] = o_t
    out_ref[...] = turn_ref[...].reshape(-1, rows).T.astype(BF)


def kernel_home(ids_ref, o_own_ref, x_ref, outbias_ref, mod_ref, *refs):
    spaces = refs[-2].shape[0]
    o_refs, pieces, (out_ref, out_w_ref, sems) = refs[: spaces - 1], refs[spaces - 1 : -3], refs[-3:]
    copies = fetch(pieces, out_places(pieces, out_w_ref, ids_ref[1]), sems)
    for copy in copies:
        copy.wait()
    parts = [mm(o_own_ref[ids_ref[0]], out_w_ref[0])]
    for k in range(1, spaces):
        parts.append(mm(o_refs[k - 1][...], out_w_ref[k]))
    out_ref[...] = middle(flat(x_ref), parts, outbias_ref[...], mod_ref[2:3, :])


def kernel_final(o_ref, y_ref, w_ref, outbias_ref, mod_ref, out_ref):
    final = mm(o_ref[...], w_ref[...]) + outbias_ref[...]
    result = (y_ref[...].astype(F32) + mod_ref[5:6, :] * final).astype(BF)
    out_ref[...] = result.reshape(out_ref.shape)


def call(kernel, out_shape, count, flops, nbytes, first_smem=False, scratch=(), in_any=()):
    return pl.pallas_call(
        kernel,
        out_shape=jax.ShapeDtypeStruct(out_shape, BF),
        in_specs=[SMEM if first_smem and i == 0 else ANY if i in in_any else VMEM for i in range(count)],
        out_specs=VMEM,
        scratch_shapes=list(scratch),
        compiler_params=PARAMS,
        cost_estimate=pl.CostEstimate(flops=int(flops), bytes_accessed=int(nbytes), transcendentals=0),
    )


def local(
    tokens,
    modulation,
    qkv_spatial,
    bias_spatial,
    out_spatial,
    outbias_spatial,
    qkv_temporal,
    bias_temporal,
    out_temporal,
    outbias_temporal,
):
    patches, frames, width = tokens.shape
    spaces, times = lax.axis_size("space"), lax.axis_size("tm")
    space, time = lax.axis_index("space"), lax.axis_index("tm")
    core = lax.rem(time, 2)
    heads = qkv_spatial.shape[1] // (3 * HD)
    cols = heads * HD
    half = heads // 2
    size = patches // times
    rows = patches * frames
    ids = jnp.stack([space, core]).astype(jnp.int32)

    def across(array, k):
        return lax.ppermute(array, "space", [(i, (i + k) % spaces) for i in range(spaces)])

    def beside(array):
        return lax.ppermute(array, "tm", [(i, i ^ 1) for i in range(times)])

    arrived = [across(tokens, k) for k in range(1, spaces)]

    w_spatial = qkv_spatial.T.reshape(heads, 3 * HD, width)
    b_spatial = bias_spatial.reshape(heads, 3 * HD)
    own = call(kernel_qkv, (heads, 3, HD, rows), 4, 2 * rows * width * cols * 3, 3e6)(
        tokens, modulation, w_spatial, b_spatial
    )

    (spread,) = after((tokens,), own)
    spread = lax.all_to_all(spread.reshape(times, size, frames, width), "tm", 0, 0, tiled=True)

    w_temporal = qkv_temporal.T.reshape(heads, 3 * HD, width)
    my_heads = lax.dynamic_slice_in_dim(w_temporal, core * half, half, 0)
    b_temporal = jnp.stack([bias_temporal] + [across(bias_temporal, k) for k in range(1, spaces)])
    b_temporal = b_temporal.reshape(spaces * heads, 3 * HD)
    my_out = lax.dynamic_slice_in_dim(out_spatial, core * half * HD, half * HD, 0)
    (my_out,) = after((my_out,), own, b_temporal, *arrived)
    arrived = [after((a,), own)[0] for a in arrived]
    direct_out = [across(my_out, k) for k in range(1, spaces)]

    o_all = call(
        kernel_spatial,
        (spaces, rows, cols),
        5 + len(arrived),
        1e10,
        4e6,
        True,
        [
            pltpu.VMEM((spaces - 1, heads, 3, HD, rows), BF),
            pltpu.VMEM(own.shape, BF),
            pltpu.VMEM(w_spatial.shape, BF),
            pltpu.SemaphoreType.DMA((2,)),
        ],
        (1, 2),
    )(ids, own, w_spatial, modulation, b_spatial, *arrived)

    (my_heads,) = after((my_heads,), o_all, *direct_out)
    direct_heads = [across(my_heads, k) for k in range(1, spaces)]
    out_pieces = [out_spatial]
    for a in direct_out:
        out_pieces += [a, beside(after((a,), o_all)[0])]

    o_here = lax.all_to_all(
        after((o_all,), spread, *out_pieces)[0].reshape(spaces * times, frames * size, cols), ("space", "tm"), 0, 0, tiled=True
    ).reshape(spaces, rows, cols)
    other_heads = []
    for a in direct_heads:
        other_heads += [a, beside(after((a,), o_here)[0])]

    o_home = [
        across(lax.dynamic_index_in_dim(o_all, (space + k) % spaces, 0, keepdims=False), k)
        for k in range(1, spaces)
    ]

    outbias_s = outbias_spatial.reshape(1, width)
    outbias_t = outbias_temporal.reshape(1, width)
    x_here = spread.reshape(rows // frames, frames, width)
    h_here, o_own = pl.pallas_call(
        functools.partial(kernel_temporal, size=size, frames=frames),
        out_shape=(jax.ShapeDtypeStruct((rows, width), BF), jax.ShapeDtypeStruct((heads, HD, rows), F32)),
        in_specs=[SMEM] + [ANY] * 3 + [VMEM] * 3 + [ANY] * len(out_pieces),
        out_specs=(VMEM, VMEM),
        scratch_shapes=[
            pltpu.VMEM(o_here.shape, BF),
            pltpu.VMEM(x_here.shape, BF),
            pltpu.VMEM((spaces, cols, width), BF),
            pltpu.VMEM(w_temporal.shape, BF),
            pltpu.SemaphoreType.DMA((len(out_pieces) + 3,)),
        ],
        compiler_params=PARAMS,
        cost_estimate=pl.CostEstimate(
            flops=2 * rows * width * cols * (3 + spaces), bytes_accessed=5 * 10**6, transcendentals=0
        ),
    )(ids, o_here, x_here, w_temporal, outbias_s, modulation, b_temporal, *out_pieces)
    o_t = call(
        functools.partial(kernel_rest, size=size, frames=frames),
        (rows, spaces * cols),
        4 + len(other_heads),
        2 * rows * width * cols * 3 * (spaces - 1),
        5e6,
        True,
        [pltpu.VMEM((spaces * heads, HD, rows), F32)],
    )(ids, h_here, o_own, b_temporal, *other_heads)
    o_t = o_t.reshape(times, frames * size, spaces * cols)
    o_final = lax.all_to_all(o_t, "tm", 0, 0, tiled=True).reshape(rows, spaces * cols)

    y_home = call(
        kernel_home,
        (rows, width),
        5 + len(o_home) + len(out_pieces),
        2 * rows * width * cols * spaces,
        3e6,
        True,
        [pltpu.VMEM((spaces, cols, width), BF), pltpu.SemaphoreType.DMA((len(out_pieces),))],
        range(5 + len(o_home), 5 + len(o_home) + len(out_pieces)),
    )(ids, o_all, tokens, outbias_s, modulation, *o_home, *out_pieces)
    return call(kernel_final, (patches, frames, width), 5, 2 * rows * width * cols * spaces, 3e6)(
        o_final, y_home, out_temporal, outbias_t, modulation
    )


def solution(mesh):
    return jax.shard_map(
        local,
        mesh=mesh,
        in_specs=(
            P("space", ("grp", "tm"), None),
            P("grp", None),
            P(None, "space"),
            P("space"),
            P("space", None),
            P(),
            P(None, "space"),
            P("space"),
            P(),
            P(),
        ),
        out_specs=P("space", ("grp", "tm"), None),
        check_vma=False,
    )
```

time: 102 us -> 94.7 us (0.928)
  blocking collectives: 0 us -> 25.4 us
  waiting for transfers between devices: 26.2 us -> 8.69 us
  between operations: 13.6 us -> 0.17 us
  Pallas kernels: 19.3 us -> 32 us
  local copies, waits for them, and re-layouts: 20.2 us -> 7.69 us
  starting transfers between devices: 21.1 us -> 19.3 us
    all_to_all x0 -> x1, blocking collectives: none -> 25.4 us  [local(): lax.all_to_all(after((o_all,), spread, *out_pieces)[0].reshape(spaces * t...]
    ppermute x4 -> x5, waiting for transfers between devices: 21.4 us -> 7.06 us  [across(): lax.ppermute(array, 'space', [(i, (i + k) % spaces) for i in range(spaces)])]
    unnamed x45 -> x18, local copies, waits for them, and re-layouts: 11.7 us -> 1.44 us
    pallas_call x5, Pallas kernels: 18.1 us -> 27.6 us  [the longest x1 8.02 us: local(): pl.pallas_call(functools.partial(kernel_temporal, size=size, frames=frame...]
    all_to_all x1 -> x0, starting transfers between devices: 4.12 us -> none  [local(): lax.all_to_all(after((o_all,), spread, b_temporal)[0].reshape(spaces * ti...]
    pallas_call x1, Pallas kernels: 1.25 us -> 4.39 us  [local(): call(kernel_qkv, (heads, 3, HD, rows), 4, 2 * rows * width * cols * 3, 30...]
    all_to_all x1, waiting for transfers between devices: 2.48 us -> 0.01 us  [local(): lax.all_to_all(spread.reshape(times, size, frames, width), 'tm', 0, 0, ti...]
    ppermute x4 -> x5, starting transfers between devices: 5.1 us -> 7.55 us  [across(): lax.ppermute(array, 'space', [(i, (i + k) % spaces) for i in range(spaces)])]
  transfers between devices with their start and end apart: 9 -> 9, of which waited for: 6 -> 3; matrix products, arithmetic and copies ran while one was open for 8% -> 7% of each run, Pallas kernels for 14% -> 25%
where the time goes in v3:
time: 94.7 us; the launch traced here: 93.9 us
  Pallas kernels  32 us (34%)
  blocking collectives  25.4 us (27%)
  starting transfers between devices  19.3 us (20%)
  waiting for transfers between devices  8.69 us (9%)
  local copies, waits for them, and re-layouts  7.69 us (8%)
    all_to_all x1, blocking collectives, local(): lax.all_to_all(after((o_all,), spread, *out_pieces)[0].reshape(spaces * t...  25.4 us
    pallas_call x1, Pallas kernels, local(): pl.pallas_call(functools.partial(kernel_temporal, size=size, frames=frame...  8.02 us
    ppermute x5, starting transfers between devices, across(): lax.ppermute(array, 'space', [(i, (i + k) % spaces) for i in range(spaces)])  7.55 us
    ppermute x5, waiting for transfers between devices, across(): lax.ppermute(array, 'space', [(i, (i + k) % spaces) for i in range(spaces)])  7.06 us
    pallas_call x1, Pallas kernels, local(): call(kernel_spatial, (spaces, rows, cols), 5 + len(arrived), 10000000000....  6.78 us
    all_to_all x1, starting transfers between devices, local(): lax.all_to_all(spread.reshape(times, size, frames, width), 'tm', 0, 0, ti...  6.62 us
    pallas_call x1, Pallas kernels, local(): call(functools.partial(kernel_rest, size=size, frames=frames), (rows, spa...  5.09 us
    all_to_all x1, starting transfers between devices, local(): lax.all_to_all(o_t, 'tm', 0, 0, tiled=True).reshape(rows, spaces * cols)  5.04 us
  transfers between devices with their start and end apart: 9, of which 3 were waited for; matrix products, arithmetic and copies ran while one was open for 7% of the time, Pallas kernels for 25%

profile of v3, /device:TPU:0, one launch (start us, length us, event | category | flops | bytes accessed | tf_op | source)
XLA Modules:
  0.0 93.9 jit_solution(6285885720263512584)
XLA Ops:
  0.0 2.9 %collective-permute-start.1 = (f32[864]{0:T(1024)}, f32[864]{0:T(1024)S(1)}, u32[]{:S(2)}, u32[]{:S(2)}) collective-permute-start(f32[864]{0:T(1024)} %param.17), channel_id=1, source_target_pairs={{0,1},{1,0},{2,3},{3,2},{4,5},{5,4},{6,7},{7,6},{8,9},{9,8},{10,11... | collective-permute-start | bytes 10376 | tf_op jit(solution)/shard_map/ppermute | solution.py:255
  2.9 0.0 collective-permute-start
  3.0 1.4 %reshape.37.b_ref = f32[4,216]{1,0:T(4,128)} reshape(f32[864]{0:T(1024)} %param.13) | data formatting | bytes 6912 | tf_op jit(solution)/shard_map/reshape | solution.py:263
  4.3 4.4 %shard_map.100.own_hbm = bf16[4,3,72,256]{3,2,1,0:T(8,128)(2,1)} custom-call(bf16[128,2,1152]{2,1,0:T(2,128)(2,1)} %x_ref.3, f32[6,1152]{1,0:T(8,128)} %mod_ref.9, bf16[4,216,1152]{2,1,0:T(8,128)(2,1)} %bitcast.19, f32[4,216]{1,0:T(4,128)} %reshape.37.b_ref), custom_call_target="tpu_custom_call" | custom-call | flops 509607936 | bytes 3000000 | tf_op jit(solution)/shard_map/pallas_call | solution.py:264
  8.7 6.6 %all-to-all-start = ((bf16[16,8,2,1152]{3,2,1,0:T(2,128)(2,1)}), bf16[16,8,2,1152]{3,2,1,0:T(2,128)(2,1)}, u32[]{:S(2)}, u32[]{:S(2)}) async-start(bf16[16,8,2,1152]{3,2,1,0:T(2,128)(2,1)} %bitcast.4), calls=%async_computation | async-start | bytes 1179648 | tf_op jit(solution)/shard_map/all_to_all | solution.py:269
  15.4 0.8 constant_dynamic-slice_fusion.1
  16.1 2.3 %constant_dynamic-slice_fusion = bf16[2,216,1152]{2,1,0:T(8,128)(2,1)} fusion(bf16[4,216,1152]{2,1,0:T(8,128)(2,1)} %bitcast.16, s32[]{:T(128)S(6)} %select_n.18), kind=kLoop, calls=%fused_computation.2 | loop fusion | bytes 1990660 | tf_op jit(solution)/shard_map/dynamic_slice | solution.py:272
  18.4 0.7 pad_add_fusion.ids_ref
  19.0 0.0 collective-permute-done.1
  19.1 0.7 reshape.39.b_ref
  19.7 0.0 collective-permute-done.refs_0_
  19.8 1.5 %collective-permute-start.2 = (bf16[144,1152]{1,0:T(8,128)(2,1)}, bf16[144,1152]{1,0:T(8,128)(2,1)S(1)}, u32[]{:S(2)}, u32[]{:S(2)}) collective-permute-start(bf16[144,1152]{1,0:T(8,128)(2,1)} %constant_dynamic-slice_fusion.1), channel_id=1, source_target_pairs={{0,1},{1,0},{2,3},{3,2},{4,5},{5,4},{6,7},{7,6},{8,9},{9,8},{10,11... | collective-permute-start | bytes 995336 | tf_op jit(solution)/shard_map/ppermute | solution.py:255
  21.2 6.8 %shard_map.101.o_own_ref = bf16[2,256,288]{2,1,0:T(8,128)(2,1)} custom-call(s32[2]{0:T(128)} %pad_add_fusion.ids_ref, bf16[4,3,72,256]{3,2,1,0:T(8,128)(2,1)} %shard_map.100.own_hbm, bf16[4,216,1152]{2,1,0:T(8,128)(2,1)} %bitcast.20, f32[6,1152]{1,0:T(8,128)} %mod_ref.9, f32[4,216]{1,0:T(4,128)} %reshape.37.b_ref, ...), custom_call_target="tpu_custom_call" | custom-call | flops 10000000000 | bytes 4000000 | tf_op jit(solution)/shard_map/pallas_call | solution.py:280
  28.0 2.0 %collective-permute-done.2.refs_1_.refs_2_ = bf16[144,1152]{1,0:T(8,128)(2,1)S(1)} collective-permute-done((bf16[144,1152]{1,0:T(8,128)(2,1)}, bf16[144,1152]{1,0:T(8,128)(2,1)S(1)}, u32[]{:S(2)}, u32[]{:S(2)}) %collective-permute-start.2) | collective-permute-done | bytes 331808 | tf_op jit(solution)/shard_map/ppermute | solution.py:255
  30.0 1.5 %collective-permute-start.4 = (bf16[2,216,1152]{2,1,0:T(8,128)(2,1)}, bf16[2,216,1152]{2,1,0:T(8,128)(2,1)}, u32[]{:S(2)}, u32[]{:S(2)}) collective-permute-start(bf16[2,216,1152]{2,1,0:T(8,128)(2,1)} %constant_dynamic-slice_fusion), channel_id=1, source_target_pairs={{0,1},{1,0},{2,3},{3,2},{4,5},{5,4},{6,7},{7,6},{8,9},{9,8},{10,11... | collective-permute-start | bytes 2985992 | tf_op jit(solution)/shard_map/ppermute | solution.py:255
  31.5 0.0 collective-permute-start.3
  31.5 1.6 %collective-permute-done.3.refs_2_.refs_3_ = bf16[144,1152]{1,0:T(8,128)(2,1)S(1)} collective-permute-done((bf16[144,1152]{1,0:T(8,128)(2,1)S(1)}, bf16[144,1152]{1,0:T(8,128)(2,1)S(1)}, u32[]{:S(2)}, u32[]{:S(2)}) %collective-permute-start.3) | collective-permute-done | bytes 331808 | tf_op jit(solution)/shard_map/ppermute | solution.py:258
  33.2 25.4 %all_to_all.15 = bf16[32,16,288]{2,1,0:T(8,128)(2,1)} all-to-all(bf16[32,16,288]{2,1,0:T(8,128)(2,1)} %bitcast.18), channel_id=1, replica_groups=mesh['grp'=1,'tm'=16,'space'=2] {'space','tm'}, dimensions={0} | all-to-all | bytes 589824 | tf_op jit(solution)/shard_map/all_to_all | solution.py:302
  58.6 0.1 collective-permute-start.5
  58.7 0.6 reshape.44.outbias_ref
  59.3 8.0 %shard_map.102 = (bf16[256,1152]{1,0:T(8,128)(2,1)}, f32[4,72,256]{2,1,0:T(8,128)}) custom-call(s32[2]{0:T(128)} %pad_add_fusion.ids_ref, bf16[2,256,288]{2,1,0:T(8,128)(2,1)} %bitcast.21, bf16[128,2,1152]{2,1,0:T(2,128)(2,1)} %bitcast.7.x_hbm, bf16[4,216,1152]{2,1,0:T(8,128)(2,1)} %bitcast.17, f32[1,1152]{1,0:T(1,128)} %reshape.44.outbias_ref, ...), custom_call_target="tpu_custom_call" | custom-call | flops 849346560 | bytes 5000000 | tf_op jit(solution)/shard_map/pallas_call | solution.py:317
  67.4 0.0 copy-start.7
  67.4 5.1 %shard_map.103 = bf16[256,576]{1,0:T(8,128)(2,1)} custom-call(s32[2]{0:T(128)} %pad_add_fusion.ids_ref, bf16[256,1152]{1,0:T(8,128)(2,1)} %get-tuple-element.19.h_ref, f32[4,72,256]{2,1,0:T(8,128)} %get-tuple-element.20.own_ref, f32[8,216]{1,0:T(8,128)} %reshape.39.b_ref, bf16[2,216,1152]{2,1,0:T(8,128)(2,1)} %collective-permute-done.4.refs_0_, ...), custom_call_target="tpu_custom_call" | custom-call | flops 509607936 | bytes 5000000 | tf_op jit(solution)/shard_map/pallas_call | solution.py:334
  72.5 5.0 %all-to-all-start.2 = ((bf16[16,16,576]{2,1,0:T(8,128)(2,1)}), bf16[16,16,576]{2,1,0:T(8,128)(2,1)S(1)}, u32[]{:S(2)}, u32[]{:S(2)}) async-start(bf16[16,16,576]{2,1,0:T(8,128)(2,1)} %bitcast.23), calls=%async_computation.2 | async-start | bytes 655360 | tf_op jit(solution)/shard_map/all_to_all | solution.py:344
  77.6 1.6 %collective-permute-start.6 = (bf16[256,288]{1,0:T(8,128)(2,1)S(1)}, bf16[256,288]{1,0:T(8,128)(2,1)S(1)}, u32[]{:S(2)}, u32[]{:S(2)}) collective-permute-start(bf16[256,288]{1,0:T(8,128)(2,1)S(1)} %dynamic-slice_bitcast_fusion), channel_id=1, source_target_pairs={{0,1},{1,0},{2,3},{3,2},{4,5},{5,4},{6,7},{7,6},{8,9},{9,8},{10,11... | collective-permute-start | bytes 442376 | tf_op jit(solution)/shard_map/ppermute | solution.py:255
  79.2 0.6 reshape.47.outbias_ref
  79.8 5.1 %collective-permute-done.6.refs_0_ = bf16[256,288]{1,0:T(8,128)(2,1)S(1)} collective-permute-done((bf16[256,288]{1,0:T(8,128)(2,1)S(1)}, bf16[256,288]{1,0:T(8,128)(2,1)S(1)}, u32[]{:S(2)}, u32[]{:S(2)}) %collective-permute-start.6) | collective-permute-done | bytes 147488 | tf_op jit(solution)/shard_map/ppermute | solution.py:255
  84.8 0.7 copy-done.5
  85.5 4.5 %shard_map.104.y_ref = bf16[256,1152]{1,0:T(8,128)(2,1)} custom-call(s32[2]{0:T(128)} %pad_add_fusion.ids_ref, bf16[2,256,288]{2,1,0:T(8,128)(2,1)} %shard_map.101.o_own_ref, bf16[128,2,1152]{2,1,0:T(2,128)(2,1)} %x_ref.3, f32[1,1152]{1,0:T(1,128)} %reshape.44.outbias_ref, f32[6,1152]{1,0:T(8,128)} %mod_ref.9, bf16[256,288]{1,0:T(8,128)(2,1)} %copy-done.5, ...), custom_call_target="tpu_custom_call" | custom-call | flops 339738624 | bytes 3000000 | tf_op jit(solution)/shard_map/pallas_call | solution.py:346
  90.1 0.0 all-to-all-done.2
  90.1 0.7 copy-done.4
  90.8 3.1 %shard_map.105 = bf16[128,2,1152]{2,1,0:T(2,128)(2,1)} custom-call(bf16[256,576]{1,0:T(8,128)(2,1)} %bitcast.22, bf16[256,1152]{1,0:T(8,128)(2,1)} %shard_map.104.y_ref, bf16[576,1152]{1,0:T(8,128)(2,1)} %w_ref.1, f32[1,1152]{1,0:T(1,128)} %reshape.47.outbias_ref, f32[6,1152]{1,0:T(8,128)} %mod_ref.9), custom_call_target="tpu_custom_call" | custom-call | flops 339738624 | bytes 3000000 | tf_op jit(solution)/shard_map/pallas_call | solution.py:356
  (22 shorter events, 0.1 us)
Async XLA Ops:
  0.0 19.0 %collective-permute-start.1 = (f32[864]{0:T(1024)}, f32[864]{0:T(1024)S(1)}, u32[]{:S(2)}, u32[]{:S(2)}) collective-permute-start(f32[864]{0:T(1024)} %param.17), channel_id=1, source_target_pairs={{0,1},{1,0},{2,3},{3,2},{4,5},{5,4},{6,7},{7,6},{8,9},{9,8},{10,11... | collective-permute-start | bytes 10376 | tf_op jit(solution)/shard_map/ppermute | solution.py:255
  2.9 16.8 %collective-permute-start = (bf16[128,2,1152]{2,1,0:T(2,128)(2,1)}, bf16[128,2,1152]{2,1,0:T(2,128)(2,1)}, u32[]{:S(2)}, u32[]{:S(2)}) collective-permute-start(bf16[128,2,1152]{2,1,0:T(2,128)(2,1)} %x_ref.3), channel_id=1, source_target_pairs={{0,1},{1,0},{2,3},{3,2},{4,5},{5,4},{6,7},{7,6},{8,9},{9,8},{10,11... | collective-permute-start | bytes 1769480 | tf_op jit(solution)/shard_map/ppermute | solution.py:255
  4.3 11.0 %copy-start = (bf16[288,1152]{1,0:T(8,128)(2,1)S(1)}, bf16[288,1152]{1,0:T(8,128)(2,1)}, u32[]{:S(2)}) copy-start(bf16[288,1152]{1,0:T(8,128)(2,1)} %refs_1_.1) | copy-start | bytes 1990660
  8.7 10.3 %copy-start.8 = (f32[864]{0:T(1024)S(1)}, f32[864]{0:T(1024)}, u32[]{:S(2)}) copy-start(f32[864]{0:T(1024)} %param.17) | copy-start | bytes 10372
  8.7 22.8 %all-to-all-start = ((bf16[16,8,2,1152]{3,2,1,0:T(2,128)(2,1)}), bf16[16,8,2,1152]{3,2,1,0:T(2,128)(2,1)}, u32[]{:S(2)}, u32[]{:S(2)}) async-start(bf16[16,8,2,1152]{3,2,1,0:T(2,128)(2,1)} %bitcast.4), calls=%async_computation | async-start | bytes 1179648 | tf_op jit(solution)/shard_map/all_to_all | solution.py:269
  19.7 39.0 %copy-start.6 = (f32[1152]{0:T(1024)S(1)}, f32[1152]{0:T(1024)}, u32[]{:S(2)}) copy-start(f32[1152]{0:T(1024)} %param.15) | copy-start | bytes 13828
  19.8 10.3 %collective-permute-start.2 = (bf16[144,1152]{1,0:T(8,128)(2,1)}, bf16[144,1152]{1,0:T(8,128)(2,1)S(1)}, u32[]{:S(2)}, u32[]{:S(2)}) collective-permute-start(bf16[144,1152]{1,0:T(8,128)(2,1)} %constant_dynamic-slice_fusion.1), channel_id=1, source_target_pairs={{0,1},{1,0},{2,3},{3,2},{4,5},{5,4},{6,7},{7,6},{8,9},{9,8},{10,11... | collective-permute-start | bytes 995336 | tf_op jit(solution)/shard_map/ppermute | solution.py:255
  30.0 29.3 %copy-start.2 = (bf16[144,1152]{1,0:T(8,128)(2,1)}, bf16[144,1152]{1,0:T(8,128)(2,1)S(1)}, u32[]{:S(2)}) copy-start(bf16[144,1152]{1,0:T(8,128)(2,1)S(1)} %collective-permute-done.2.refs_1_.refs_2_) | copy-start | bytes 995332
  30.0 28.6 %collective-permute-start.4 = (bf16[2,216,1152]{2,1,0:T(8,128)(2,1)}, bf16[2,216,1152]{2,1,0:T(8,128)(2,1)}, u32[]{:S(2)}, u32[]{:S(2)}) collective-permute-start(bf16[2,216,1152]{2,1,0:T(8,128)(2,1)} %constant_dynamic-slice_fusion), channel_id=1, source_target_pairs={{0,1},{1,0},{2,3},{3,2},{4,5},{5,4},{6,7},{7,6},{8,9},{9,8},{10,11... | collective-permute-start | bytes 2985992 | tf_op jit(solution)/shard_map/ppermute | solution.py:255
  31.5 1.6 %collective-permute-start.3 = (bf16[144,1152]{1,0:T(8,128)(2,1)S(1)}, bf16[144,1152]{1,0:T(8,128)(2,1)S(1)}, u32[]{:S(2)}, u32[]{:S(2)}) collective-permute-start(bf16[144,1152]{1,0:T(8,128)(2,1)S(1)} %collective-permute-done.2.refs_1_.refs_2_), channel_id=1, source_target_pairs={{0,2},{2,0},{4,6},{6,4},{8,10},{10,8},{12,14},{14,12},{16,18},{18,... | collective-permute-start | bytes 995336 | tf_op jit(solution)/shard_map/ppermute | solution.py:258
  33.2 26.2 %copy-start.3 = (bf16[144,1152]{1,0:T(8,128)(2,1)}, bf16[144,1152]{1,0:T(8,128)(2,1)S(1)}, u32[]{:S(2)}) copy-start(bf16[144,1152]{1,0:T(8,128)(2,1)S(1)} %collective-permute-done.3.refs_2_.refs_3_) | copy-start | bytes 995332
  58.6 8.8 %collective-permute-start.5 = (bf16[2,216,1152]{2,1,0:T(8,128)(2,1)}, bf16[2,216,1152]{2,1,0:T(8,128)(2,1)}, u32[]{:S(2)}, u32[]{:S(2)}) collective-permute-start(bf16[2,216,1152]{2,1,0:T(8,128)(2,1)} %collective-permute-done.4.refs_0_), channel_id=1, source_target_pairs={{0,2},{2,0},{4,6},{6,4},{8,10},{10,8},{12,14},{14,12},{16,18},{18,... | collective-permute-start | bytes 2985992 | tf_op jit(solution)/shard_map/ppermute | solution.py:258
  67.4 10.2 %copy-start.1 = (bf16[2,256,288]{2,1,0:T(8,128)(2,1)S(1)}, bf16[2,256,288]{2,1,0:T(8,128)(2,1)}, u32[]{:S(2)}) copy-start(bf16[2,256,288]{2,1,0:T(8,128)(2,1)} %shard_map.101.o_own_ref) | copy-start | bytes 884740
  67.4 11.8 %copy-start.7 = (f32[1152]{0:T(1024)S(1)}, f32[1152]{0:T(1024)}, u32[]{:S(2)}) copy-start(f32[1152]{0:T(1024)} %param.19) | copy-start | bytes 13828
  72.5 17.6 %all-to-all-start.2 = ((bf16[16,16,576]{2,1,0:T(8,128)(2,1)}), bf16[16,16,576]{2,1,0:T(8,128)(2,1)S(1)}, u32[]{:S(2)}, u32[]{:S(2)}) async-start(bf16[16,16,576]{2,1,0:T(8,128)(2,1)} %bitcast.23), calls=%async_computation.2 | async-start | bytes 655360 | tf_op jit(solution)/shard_map/all_to_all | solution.py:344
  77.6 7.3 %collective-permute-start.6 = (bf16[256,288]{1,0:T(8,128)(2,1)S(1)}, bf16[256,288]{1,0:T(8,128)(2,1)S(1)}, u32[]{:S(2)}, u32[]{:S(2)}) collective-permute-start(bf16[256,288]{1,0:T(8,128)(2,1)S(1)} %dynamic-slice_bitcast_fusion), channel_id=1, source_target_pairs={{0,1},{1,0},{2,3},{3,2},{4,5},{5,4},{6,7},{7,6},{8,9},{9,8},{10,11... | collective-permute-start | bytes 442376 | tf_op jit(solution)/shard_map/ppermute | solution.py:255
  84.8 0.7 copy-start.5
  90.1 0.7 copy-start.4

commit v4 on v3

v4 whole, which is shorter than its diff:
```python
import functools
import math

import jax
import jax.numpy as jnp
from jax import lax
from jax.experimental import pallas as pl
from jax.experimental.pallas import tpu as pltpu
from jax.sharding import PartitionSpec as P

HD = 72
WIN = 16
BF = jnp.bfloat16
F32 = jnp.float32
EXP2_SCALE = 1.0 / (math.sqrt(HD) * math.log(2.0))

VMEM = pl.BlockSpec(memory_space=pltpu.VMEM)
ANY = pl.BlockSpec(memory_space=pl.ANY)
SMALL = pltpu.CompilerParams(vmem_limit_bytes=16 * 1024 * 1024)
PARAMS = pltpu.CompilerParams(vmem_limit_bytes=63 * 1024 * 1024)

NT = (((1,), (1,)), ((), ()))
TN = (((0,), (0,)), ((), ()))


def mm(a, b, dims=(((1,), (0,)), ((), ()))):
    return lax.dot_general(a, b, dims, preferred_element_type=F32)


def modulated(values, offset_vec, scaling):
    center = jnp.mean(values, axis=-1, keepdims=True)
    moved = values - center
    spread = jnp.mean(moved * moved, axis=-1, keepdims=True)
    return moved * lax.rsqrt(spread + 1e-06) * (1.0 + scaling) + offset_vec


def attend(q_t, k_t, v_t, mask=None):
    scores = mm(k_t, q_t, TN)
    if mask is not None:
        scores = jnp.where(mask, scores, F32(-1e30))
    highest = jnp.max(scores, axis=0, keepdims=True)
    expon = jnp.exp2((scores - highest) * F32(EXP2_SCALE))
    total = jnp.sum(expon, axis=0, keepdims=True)
    return mm(v_t, expon.astype(BF)) * (1.0 / total)


def after(arrays, *others):
    return lax.optimization_barrier((*arrays, *others))[: len(arrays)]


def flat(ref, *index):
    block = ref[index] if index else ref[...]
    return block.reshape(-1, block.shape[-1])


def column(rows):
    return lax.broadcasted_iota(jnp.int32, (rows, 1), 0)


def line(rows):
    return lax.broadcasted_iota(jnp.int32, (1, rows), 1)


def chosen(source, rows):
    return (source == line(rows)).astype(F32).astype(BF)


def by_frame_first(rows, frames):
    r = column(rows)
    return chosen(lax.rem(r, rows // frames) * frames + lax.div(r, rows // frames), rows)


def by_patch_first(rows, frames):
    r = column(rows)
    return chosen(lax.rem(r, frames) * (rows // frames) + lax.div(r, frames), rows)


def bias_column(b_ref):
    count = b_ref.shape[0]
    return jnp.broadcast_to(b_ref[...].reshape(1, count), (8, count)).T[:, 0:1]


def spatial_rows(x, mod_ref, frames):
    h = modulated(x.astype(F32), mod_ref[0:1, :], mod_ref[1:2, :]).astype(BF)
    return mm(by_frame_first(x.shape[0], frames), h).astype(BF)


def fetch(sources, targets, sems):
    copies = [pltpu.make_async_copy(a, b, sems.at[i]) for i, (a, b) in enumerate(zip(sources, targets))]
    for copy in copies:
        copy.start()
    return copies


def coordinates():
    return lax.axis_index("space"), lax.rem(lax.axis_index("tm"), 2)


def kernel_qkv(x_ref, w_hbm, w_other_hbm, out_w_hbm, mod_ref, b_ref, out_ref, heads_ref, half_ref, w_ref, sems):
    _, core = coordinates()
    half, rows = heads_ref.shape[0], half_ref.shape[0]
    copies = fetch(
        (
            w_hbm,
            out_w_hbm.at[pl.ds(pl.multiple_of(core * rows, rows), rows)],
            w_other_hbm.at[pl.ds(core * half, half)],
        ),
        (w_ref, half_ref, heads_ref),
        sems,
    )
    h = spatial_rows(flat(x_ref), mod_ref, x_ref.shape[1])
    bias = bias_column(b_ref)
    copies[0].wait()
    for i in range(w_ref.shape[0]):
        qkv = mm(w_ref[i], h, NT) + bias[i * 3 * HD : (i + 1) * 3 * HD]
        for c in range(3):
            out_ref[i, c] = qkv[c * HD : (c + 1) * HD].astype(BF)
    for copy in copies[1:]:
        copy.wait()


def kernel_spatial(own_hbm, w_hbm, mod_ref, b_ref, *refs):
    x_refs, (out_ref, part_ref, own_ref, w_ref, sems) = refs[:-5], refs[-5:]
    copies = fetch((w_hbm, own_hbm), (w_ref, own_ref), sems)
    space, _ = coordinates()
    patches, frames, _ = x_refs[0].shape
    heads = w_ref.shape[0]
    spaces = len(x_refs) + 1
    bias = bias_column(b_ref)
    for j, x_ref in enumerate(x_refs):
        h = spatial_rows(flat(x_ref), mod_ref, frames)
        if j == 0:
            copies[0].wait()
        for i in range(heads):
            qkv = mm(w_ref[i], h, NT) + bias[i * 3 * HD : (i + 1) * 3 * HD]
            for c in range(3):
                part_ref[j, i, c] = qkv[c * HD : (c + 1) * HD].astype(BF)
    copies[1].wait()
    by_frame = []
    for f in range(frames):
        cols = slice(f * patches, (f + 1) * patches)
        done = []
        for i in range(heads):
            q_t, k_t, v_t = (
                jnp.concatenate(
                    [own_ref[i, c, :, cols]] + [part_ref[j, i, c, :, cols] for j in range(spaces - 1)],
                    axis=1,
                )
                for c in range(3)
            )
            done.append(attend(q_t, k_t, v_t))
        by_frame.append(jnp.concatenate(done, axis=0).astype(BF))
    back = by_patch_first(patches * frames, frames)
    for j in range(spaces):
        mine = jnp.concatenate([o[:, j * patches : (j + 1) * patches] for o in by_frame], axis=1)
        out_ref[lax.rem(space - j + spaces, spaces)] = mm(back, mine, NT).astype(BF)


def middle(tokens, parts, outbias, gate):
    summed = parts[0].astype(BF).astype(F32)
    for part in parts[1:]:
        summed = summed + part.astype(BF).astype(F32)
    return (tokens.astype(F32) + gate * (summed + outbias)).astype(BF)


def temporal_mask(rows, size, frames):
    def place(row):
        device, within = lax.div(row, frames * size), lax.rem(row, frames * size)
        return device * frames + lax.rem(within, frames), lax.div(within, frames)

    key_frame, key_patch = place(column(rows))
    query_frame, query_patch = place(line(rows))
    code_key = key_patch * 4 * WIN * rows + key_frame
    code_query = query_patch * 4 * WIN * rows + query_frame
    back = code_query - code_key
    return (back >= 0) & (back < WIN)


def temporal_head(w, b, h, mask):
    qkv = (mm(w, h, NT) + b).astype(BF)
    return attend(qkv[0:HD], qkv[HD : 2 * HD], qkv[2 * HD : 3 * HD], mask)


def out_places(pieces, out_w_ref, core):
    half = pieces[1].shape[0]
    places = [out_w_ref.at[0]]
    for n in range(1, len(pieces)):
        start = half * (core if n % 2 else 1 - core)
        places.append(out_w_ref.at[(n + 1) // 2, pl.ds(pl.multiple_of(start, half), half)])
    return places


def kernel_temporal(
    o_hbm, x_hbm, w_hbm, outbias_ref, mod_ref, b_ref, *refs, size, frames
):
    space, core = coordinates()
    pieces, (h_ref, out_ref, o_ref, x_ref, out_w_ref, w_ref, sems) = refs[:-7], refs[-7:]
    copies = fetch(
        (*pieces, o_hbm, x_hbm, w_hbm),
        (*out_places(pieces, out_w_ref, core), o_ref, x_ref, w_ref),
        sems,
    )
    spaces, rows, _ = o_ref.shape
    mask = temporal_mask(rows, size, frames)
    for copy in copies[:-1]:
        copy.wait()
    parts = [mm(o_ref[lax.rem(space - k + spaces, spaces)], out_w_ref[k]) for k in range(spaces)]
    y = middle(flat(x_ref), parts, outbias_ref[...].reshape(1, -1), mod_ref[2:3, :])
    h = modulated(y.astype(F32), mod_ref[3:4, :], mod_ref[4:5, :]).astype(BF)
    h_ref[...] = h
    bias = bias_column(b_ref)
    copies[-1].wait()
    for i in range(w_ref.shape[0]):
        out_ref[i] = temporal_head(w_ref[i], bias[i * 3 * HD : (i + 1) * 3 * HD], h, mask)


def kernel_rest(h_ref, own_ref, *refs, size, frames, spaces):
    b_refs, w_hbms, (out_ref, turn_ref, w_ref, sems) = refs[: spaces - 1], refs[spaces - 1 : -4], refs[-4:]
    space, core = coordinates()
    copies = fetch(w_hbms, [w_ref.at[n] for n in range(len(w_hbms))], sems)
    h = h_ref[...]
    rows = h.shape[0]
    mask = temporal_mask(rows, size, frames)
    heads = own_ref.shape[0]
    half = heads // 2
    for i in range(heads):
        turn_ref[space * heads + i] = own_ref[i]
    for n in range(len(w_hbms)):
        shift = n // 2 + 1
        bias = bias_column(b_refs[shift - 1])
        second = (core == 0) == (n % 2 == 1)
        within = jnp.where(second, half, 0)
        group = lax.rem(space - shift + spaces, spaces)
        bias = jnp.where(second, bias[half * 3 * HD :], bias[: half * 3 * HD])
        copies[n].wait()
        for i in range(half):
            o_t = temporal_head(w_ref[n, i], bias[i * 3 * HD : (i + 1) * 3 * HD], h, mask)
            turn_ref[group * heads + within + i] = o_t
    out_ref[...] = turn_ref[...].reshape(-1, rows).T.astype(BF)


def kernel_home(o_own_ref, x_ref, outbias_ref, mod_ref, *refs):
    space, core = coordinates()
    spaces = refs[-2].shape[0]
    o_refs, pieces, (out_ref, out_w_ref, sems) = refs[: spaces - 1], refs[spaces - 1 : -3], refs[-3:]
    copies = fetch(pieces, out_places(pieces, out_w_ref, core), sems)
    for copy in copies:
        copy.wait()
    parts = [mm(o_own_ref[space], out_w_ref[0])]
    for k in range(1, spaces):
        parts.append(mm(o_refs[k - 1][...], out_w_ref[k]))
    out_ref[...] = middle(flat(x_ref), parts, outbias_ref[...].reshape(1, -1), mod_ref[2:3, :])


def kernel_final(o_ref, y_ref, w_ref, outbias_ref, mod_ref, out_ref):
    final = mm(o_ref[...], w_ref[...]) + outbias_ref[...].reshape(1, -1)
    result = (y_ref[...].astype(F32) + mod_ref[5:6, :] * final).astype(BF)
    out_ref[...] = result.reshape(out_ref.shape)


def call(kernel, out_shape, count, flops, nbytes, scratch=(), in_any=(), params=PARAMS):
    return pl.pallas_call(
        kernel,
        out_shape=jax.ShapeDtypeStruct(out_shape, BF),
        in_specs=[ANY if i in in_any else VMEM for i in range(count)],
        out_specs=VMEM,
        scratch_shapes=list(scratch),
        compiler_params=params,
        cost_estimate=pl.CostEstimate(flops=int(flops), bytes_accessed=int(nbytes), transcendentals=0),
    )


def local(
    tokens,
    modulation,
    qkv_spatial,
    bias_spatial,
    out_spatial,
    outbias_spatial,
    qkv_temporal,
    bias_temporal,
    out_temporal,
    outbias_temporal,
):
    patches, frames, width = tokens.shape
    spaces, times = lax.axis_size("space"), lax.axis_size("tm")
    space = lax.axis_index("space")
    heads = qkv_spatial.shape[1] // (3 * HD)
    cols = heads * HD
    half = heads // 2
    size = patches // times
    rows = patches * frames

    def across(array, k):
        return lax.ppermute(array, "space", [(i, (i + k) % spaces) for i in range(spaces)])

    def beside(array):
        return lax.ppermute(array, "tm", [(i, i ^ 1) for i in range(times)])

    arrived = [across(tokens, k) for k in range(1, spaces)]

    w_spatial = qkv_spatial.T.reshape(heads, 3 * HD, width)
    w_temporal = qkv_temporal.T.reshape(heads, 3 * HD, width)
    own, my_heads, my_out = pl.pallas_call(
        kernel_qkv,
        out_shape=tuple(
            jax.ShapeDtypeStruct(a, BF)
            for a in ((heads, 3, HD, rows), (half, 3 * HD, width), (half * HD, width))
        ),
        in_specs=[VMEM] + [ANY] * 3 + [VMEM] * 2,
        out_specs=(VMEM, ANY, ANY),
        scratch_shapes=[pltpu.VMEM(w_spatial.shape, BF), pltpu.SemaphoreType.DMA((3,))],
        compiler_params=PARAMS,
        cost_estimate=pl.CostEstimate(
            flops=2 * rows * width * cols * 3, bytes_accessed=3 * 10**6, transcendentals=0
        ),
    )(tokens, w_spatial, w_temporal, out_spatial, modulation, bias_spatial)

    (spread,) = after((tokens,), own)
    spread = lax.all_to_all(spread.reshape(times, size, frames, width), "tm", 0, 0, tiled=True)

    other_bias = [across(bias_temporal, k) for k in range(1, spaces)]
    (my_out,) = after((my_out,), *other_bias, *arrived)
    arrived = [after((a,), own)[0] for a in arrived]
    direct_out = [across(my_out, k) for k in range(1, spaces)]

    o_all = call(
        kernel_spatial,
        (spaces, rows, cols),
        4 + len(arrived),
        1e10,
        4e6,
        [
            pltpu.VMEM((spaces - 1, heads, 3, HD, rows), BF),
            pltpu.VMEM(own.shape, BF),
            pltpu.VMEM(w_spatial.shape, BF),
            pltpu.SemaphoreType.DMA((2,)),
        ],
        (0, 1),
    )(own, w_spatial, modulation, bias_spatial, *arrived)

    (my_heads,) = after((my_heads,), o_all, *direct_out)
    direct_heads = [across(my_heads, k) for k in range(1, spaces)]
    out_pieces = [out_spatial]
    for a in direct_out:
        out_pieces += [a, beside(after((a,), o_all)[0])]

    o_here = lax.all_to_all(
        after((o_all,), spread, *out_pieces)[0].reshape(spaces * times, frames * size, cols), ("space", "tm"), 0, 0, tiled=True
    ).reshape(spaces, rows, cols)
    other_heads = []
    for a in direct_heads:
        other_heads += [a, beside(after((a,), o_here)[0])]

    o_home = [
        across(lax.dynamic_index_in_dim(o_all, (space + k) % spaces, 0, keepdims=False), k)
        for k in range(1, spaces)
    ]

    y_home = call(
        kernel_home,
        (rows, width),
        4 + len(o_home) + len(out_pieces),
        2 * rows * width * cols * spaces,
        3e6,
        [pltpu.VMEM((spaces, cols, width), BF), pltpu.SemaphoreType.DMA((len(out_pieces),))],
        range(4 + len(o_home), 4 + len(o_home) + len(out_pieces)),
        SMALL,
    )(o_all, tokens, outbias_spatial, modulation, *o_home, *out_pieces)
    x_here = spread.reshape(rows // frames, frames, width)
    h_here, o_own = pl.pallas_call(
        functools.partial(kernel_temporal, size=size, frames=frames),
        out_shape=(jax.ShapeDtypeStruct((rows, width), BF), jax.ShapeDtypeStruct((heads, HD, rows), F32)),
        in_specs=[ANY] * 3 + [VMEM] * 3 + [ANY] * len(out_pieces),
        out_specs=(VMEM, VMEM),
        scratch_shapes=[
            pltpu.VMEM(o_here.shape, BF),
            pltpu.VMEM(x_here.shape, BF),
            pltpu.VMEM((spaces, cols, width), BF),
            pltpu.VMEM(w_temporal.shape, BF),
            pltpu.SemaphoreType.DMA((len(out_pieces) + 3,)),
        ],
        compiler_params=PARAMS,
        cost_estimate=pl.CostEstimate(
            flops=2 * rows * width * cols * (3 + spaces), bytes_accessed=5 * 10**6, transcendentals=0
        ),
    )(o_here, x_here, w_temporal, outbias_spatial, modulation, bias_temporal, *out_pieces)
    o_t = call(
        functools.partial(kernel_rest, size=size, frames=frames, spaces=spaces),
        (rows, spaces * cols),
        1 + spaces + len(other_heads),
        2 * rows * width * cols * 3 * (spaces - 1),
        5e6,
        [
            pltpu.VMEM((spaces * heads, HD, rows), F32),
            pltpu.VMEM((len(other_heads), half, 3 * HD, width), BF),
            pltpu.SemaphoreType.DMA((len(other_heads),)),
        ],
        range(1 + spaces, 1 + spaces + len(other_heads)),
    )(h_here, o_own, *other_bias, *other_heads)
    o_t = o_t.reshape(times, frames * size, spaces * cols)
    o_final = lax.all_to_all(o_t, "tm", 0, 0, tiled=True).reshape(rows, spaces * cols)

    return call(
        kernel_final, (patches, frames, width), 5, 2 * rows * width * cols * spaces, 3e6, params=SMALL
    )(o_final, y_home, out_temporal, outbias_temporal, modulation)


def solution(mesh):
    return jax.shard_map(
        local,
        mesh=mesh,
        in_specs=(
            P("space", ("grp", "tm"), None),
            P("grp", None),
            P(None, "space"),
            P("space"),
            P("space", None),
            P(),
            P(None, "space"),
            P("space"),
            P(),
            P(),
        ),
        out_specs=P("space", ("grp", "tm"), None),
        check_vma=False,
    )
```

time: 94.7 us -> 127 us (1.34)
  Pallas kernels: 32 us -> 68.6 us
  local copies, waits for them, and re-layouts: 7.69 us -> 3.93 us
  waiting for transfers between devices: 8.69 us -> 11.4 us
  blocking collectives: 25.4 us -> 23.4 us
    pallas_call x4, Pallas kernels: 20.8 us -> 59 us  [the longest x1 43.2 us: local(): pl.pallas_call(kernel_qkv, out_shape=tuple((jax.ShapeDtypeStruct(a, BF) f...]
    all_to_all x1, waiting for transfers between devices: 0.01 us -> 3.73 us  [local(): lax.all_to_all(spread.reshape(times, size, frames, width), 'tm', 0, 0, ti...]
    reshape x4 -> x0, local copies, waits for them, and re-layouts: 3.21 us -> none  [the longest x1 1.35 us: local(): b_spatial = bias_spatial.reshape(heads, 3 * HD)]
    dynamic_slice x2 -> x0, local copies, waits for them, and re-layouts: 3.01 us -> none  [the longest x1 2.25 us: local(): my_heads = lax.dynamic_slice_in_dim(w_temporal, core * half, half, 0)]
    all_to_all x1, blocking collectives: 25.4 us -> 23.4 us  [local(): lax.all_to_all(after((o_all,), spread, *out_pieces)[0].reshape(spaces * t...]
    ppermute x2, waiting for transfers between devices: 1.63 us -> 0.01 us  [beside(): return lax.ppermute(array, 'tm', [(i, i ^ 1) for i in range(times)])]
    pallas_call x1, Pallas kernels: 3.13 us -> 1.53 us  [local(): call(kernel_final, (patches, frames, width), 5, 2 * rows * width * cols *...]
    unnamed x18 -> x24, local copies, waits for them, and re-layouts: 1.44 us -> 2.98 us
  transfers between devices with their start and end apart: 9 -> 9, of which waited for: 3 -> 3; matrix products, arithmetic and copies ran while one was open for 7% -> 1% of each run, Pallas kernels for 25% -> 48%
where the time goes in v4:
time: 127 us
  Pallas kernels  68.6 us (54%)
  blocking collectives  23.4 us (18%)
  starting transfers between devices  19.3 us (15%)
  waiting for transfers between devices  11.4 us (9%)
  local copies, waits for them, and re-layouts  3.93 us (3%)
    pallas_call x1, Pallas kernels, local(): pl.pallas_call(kernel_qkv, out_shape=tuple((jax.ShapeDtypeStruct(a, BF) f...  43.2 us
    all_to_all x1, blocking collectives, local(): lax.all_to_all(after((o_all,), spread, *out_pieces)[0].reshape(spaces * t...  23.4 us
    pallas_call x1, Pallas kernels, local(): pl.pallas_call(functools.partial(kernel_temporal, size=size, frames=frame...  8.01 us
    ppermute x5, waiting for transfers between devices, across(): lax.ppermute(array, 'space', [(i, (i + k) % spaces) for i in range(spaces)])  7.63 us
    ppermute x5, starting transfers between devices, across(): lax.ppermute(array, 'space', [(i, (i + k) % spaces) for i in range(spaces)])  7.62 us
    pallas_call x1, Pallas kernels, local(): call(kernel_spatial, (spaces, rows, cols), 4 + len(arrived), 10000000000....  6.8 us
    all_to_all x1, starting transfers between devices, local(): lax.all_to_all(spread.reshape(times, size, frames, width), 'tm', 0, 0, ti...  6.48 us
    pallas_call x1, Pallas kernels, local(): call(functools.partial(kernel_rest, size=size, frames=frames, spaces=spac...  6.22 us
  transfers between devices with their start and end apart: 9, of which 3 were waited for; matrix products, arithmetic and copies ran while one was open for 1% of the time, Pallas kernels for 48%

profile of v4, /device:TPU:0, one launch (start us, length us, event | category | flops | bytes accessed | tf_op | source)
XLA Modules:
  0.0 126.7 jit_solution(13427614822677985211)
XLA Ops:
  0.0 2.9 %collective-permute-start = (bf16[128,2,1152]{2,1,0:T(2,128)(2,1)}, bf16[128,2,1152]{2,1,0:T(2,128)(2,1)S(1)}, u32[]{:S(2)}, u32[]{:S(2)}) collective-permute-start(bf16[128,2,1152]{2,1,0:T(2,128)(2,1)} %x_ref.3), channel_id=1, source_target_pairs={{0,1},{1,0},{2,3},{3,2},{4,5},{5,4},{6,7},{7,6},{8,9},{9,8},{10,11... | collective-permute-start | bytes 1769480 | tf_op jit(solution)/shard_map/ppermute | solution.py:295
  2.9 0.0 collective-permute-start.1
  3.0 43.2 %shard_map.100 = (bf16[4,3,72,256]{3,2,1,0:T(8,128)(2,1)}, bf16[2,216,1152]{2,1,0:T(8,128)(2,1)}, bf16[144,1152]{1,0:T(8,128)(2,1)}) custom-call(bf16[128,2,1152]{2,1,0:T(2,128)(2,1)} %x_ref.3, bf16[4,216,1152]{2,1,0:T(8,128)(2,1)} %bitcast.18, bf16[4,216,1152]{2,1,0:T(8,128)(2,1)} %bitcast.16, bf16[288,1152]{1,0:T(8,128)(2,1)} %refs_1_.1, ...), custom_call_target="tpu_custom_call" | custom-call | flops 509607936 | bytes 3000000 | tf_op jit(solution)/shard_map/pallas_call | solution.py:304
  46.2 6.5 %all-to-all-start = ((bf16[16,8,2,1152]{3,2,1,0:T(2,128)(2,1)}), bf16[16,8,2,1152]{3,2,1,0:T(2,128)(2,1)}, u32[]{:S(2)}, u32[]{:S(2)}) async-start(bf16[16,8,2,1152]{3,2,1,0:T(2,128)(2,1)} %bitcast.4), calls=%async_computation | async-start | bytes 1179648 | tf_op jit(solution)/shard_map/all_to_all | solution.py:320
  52.7 0.0 collective-permute-done.1.refs_0_
  52.7 0.0 collective-permute-done.refs_0_
  52.7 0.0 copy-start.11
  52.7 1.6 %collective-permute-start.2 = (bf16[144,1152]{1,0:T(8,128)(2,1)}, bf16[144,1152]{1,0:T(8,128)(2,1)S(1)}, u32[]{:S(2)}, u32[]{:S(2)}) collective-permute-start(bf16[144,1152]{1,0:T(8,128)(2,1)} %get-tuple-element.21), channel_id=1, source_target_pairs={{0,1},{1,0},{2,3},{3,2},{4,5},{5,4},{6,7},{7,6},{8,9},{9,8},{10,11... | collective-permute-start | bytes 995336 | tf_op jit(solution)/shard_map/ppermute | solution.py:295
  54.3 6.8 %shard_map.101.o_own_ref = bf16[2,256,288]{2,1,0:T(8,128)(2,1)} custom-call(bf16[4,3,72,256]{3,2,1,0:T(8,128)(2,1)} %get-tuple-element.17.own_hbm, bf16[4,216,1152]{2,1,0:T(8,128)(2,1)} %bitcast.19, f32[6,1152]{1,0:T(8,128)} %mod_ref.9, f32[864]{0:T(1024)} %b_ref.4, bf16[128,2,1152]{2,1,0:T(2,128)(2,1)} %copy-done.11), custom_call_target="tpu_custom_call" | custom-call | flops 10000000000 | bytes 4000000 | tf_op jit(solution)/shard_map/pallas_call | solution.py:327
  61.1 1.9 %collective-permute-done.2.refs_1_.refs_2_ = bf16[144,1152]{1,0:T(8,128)(2,1)S(1)} collective-permute-done((bf16[144,1152]{1,0:T(8,128)(2,1)}, bf16[144,1152]{1,0:T(8,128)(2,1)S(1)}, u32[]{:S(2)}, u32[]{:S(2)}) %collective-permute-start.2) | collective-permute-done | bytes 331808 | tf_op jit(solution)/shard_map/ppermute | solution.py:295
  63.1 1.5 %collective-permute-start.4 = (bf16[2,216,1152]{2,1,0:T(8,128)(2,1)}, bf16[2,216,1152]{2,1,0:T(8,128)(2,1)}, u32[]{:S(2)}, u32[]{:S(2)}) collective-permute-start(bf16[2,216,1152]{2,1,0:T(8,128)(2,1)} %get-tuple-element.27), channel_id=1, source_target_pairs={{0,1},{1,0},{2,3},{3,2},{4,5},{5,4},{6,7},{7,6},{8,9},{9,8},{10,11... | collective-permute-start | bytes 2985992 | tf_op jit(solution)/shard_map/ppermute | solution.py:295
  64.6 0.0 collective-permute-start.3
  64.6 3.7 %all-to-all-done = bf16[16,8,2,1152]{3,2,1,0:T(2,128)(2,1)} async-done(((bf16[16,8,2,1152]{3,2,1,0:T(2,128)(2,1)}), bf16[16,8,2,1152]{3,2,1,0:T(2,128)(2,1)}, u32[]{:S(2)}, u32[]{:S(2)}) %all-to-all-start) | async-done | bytes 589856 | tf_op jit(solution)/shard_map/all_to_all | solution.py:320
  68.3 0.0 collective-permute-done.3.refs_2_.refs_3_
  68.3 23.4 %all_to_all.15 = bf16[32,16,288]{2,1,0:T(8,128)(2,1)} all-to-all(bf16[32,16,288]{2,1,0:T(8,128)(2,1)} %bitcast.14), channel_id=1, replica_groups=mesh['grp'=1,'tm'=16,'space'=2] {'space','tm'}, dimensions={0} | all-to-all | bytes 589824 | tf_op jit(solution)/shard_map/all_to_all | solution.py:348
  91.7 0.1 collective-permute-start.5
  91.8 8.0 %shard_map.102 = (bf16[256,1152]{1,0:T(8,128)(2,1)}, f32[4,72,256]{2,1,0:T(8,128)}) custom-call(bf16[2,256,288]{2,1,0:T(8,128)(2,1)} %bitcast.20, bf16[128,2,1152]{2,1,0:T(2,128)(2,1)} %bitcast.7.x_hbm, bf16[4,216,1152]{2,1,0:T(8,128)(2,1)} %bitcast.17, f32[1152]{0:T(1024)} %outbias_ref.4, f32[6,1152]{1,0:T(8,128)} %mod_ref.9, f32[864]{0:T(1024)} %b_ref.5, ...), custom_call_target="tpu_custom_call" | custom-call | flops 849346560 | bytes 5000000 | tf_op jit(solution)/shard_map/pallas_call | solution.py:371
  99.8 0.0 copy-start
  99.8 0.0 copy-start.7
  99.8 0.0 copy-start.8
  99.8 6.2 %shard_map.103 = bf16[256,576]{1,0:T(8,128)(2,1)} custom-call(bf16[256,1152]{1,0:T(8,128)(2,1)} %get-tuple-element.24.h_ref, f32[4,72,256]{2,1,0:T(8,128)} %get-tuple-element.25.own_ref, f32[864]{0:T(1024)} %copy-done.10, bf16[2,216,1152]{2,1,0:T(8,128)(2,1)} %collective-permute-done.4.refs_1_, bf16[2,216,1152]{2,1,0:T(8,128)(2,1)} %collective-permute-done.5.refs_2_), custom_call_target="tpu_custom_call" | custom-call | flops 509607936 | bytes 5000000 | tf_op jit(solution)/shard_map/pallas_call | solution.py:388
  106.1 0.0 copy-start.9
  106.1 5.1 %all-to-all-start.2 = ((bf16[16,16,576]{2,1,0:T(8,128)(2,1)}), bf16[16,16,576]{2,1,0:T(8,128)(2,1)S(1)}, u32[]{:S(2)}, u32[]{:S(2)}) async-start(bf16[16,16,576]{2,1,0:T(8,128)(2,1)} %bitcast.21), calls=%async_computation.2 | async-start | bytes 655360 | tf_op jit(solution)/shard_map/all_to_all | solution.py:402
  111.2 1.0 dynamic-slice_bitcast_fusion
  112.1 1.6 %collective-permute-start.6 = (bf16[256,288]{1,0:T(8,128)(2,1)S(1)}, bf16[256,288]{1,0:T(8,128)(2,1)S(1)}, u32[]{:S(2)}, u32[]{:S(2)}) collective-permute-start(bf16[256,288]{1,0:T(8,128)(2,1)S(1)} %dynamic-slice_bitcast_fusion), channel_id=1, source_target_pairs={{0,1},{1,0},{2,3},{3,2},{4,5},{5,4},{6,7},{7,6},{8,9},{9,8},{10,11... | collective-permute-start | bytes 442376 | tf_op jit(solution)/shard_map/ppermute | solution.py:295
  113.7 5.7 %collective-permute-done.6.refs_0_ = bf16[256,288]{1,0:T(8,128)(2,1)S(1)} collective-permute-done((bf16[256,288]{1,0:T(8,128)(2,1)S(1)}, bf16[256,288]{1,0:T(8,128)(2,1)S(1)}, u32[]{:S(2)}, u32[]{:S(2)}) %collective-permute-start.6) | collective-permute-done | bytes 147488 | tf_op jit(solution)/shard_map/ppermute | solution.py:295
  119.4 1.0 copy-done.1
  120.4 1.0 copy-done.4
  121.4 1.0 copy-done.6
  122.3 2.8 %shard_map.104.y_ref = bf16[256,1152]{1,0:T(8,128)(2,1)S(1)} custom-call(bf16[2,256,288]{2,1,0:T(8,128)(2,1)S(1)} %copy-done.1, bf16[128,2,1152]{2,1,0:T(2,128)(2,1)} %x_ref.3, f32[1152]{0:T(1024)S(1)} %copy-done.8, f32[6,1152]{1,0:T(8,128)S(1)} %copy-done.7, bf16[256,288]{1,0:T(8,128)(2,1)S(1)} %collective-permute-done.6.refs_0_, ...), custom_call_target="tpu_custom_call" | custom-call | flops 339738624 | bytes 3000000 | tf_op jit(solution)/shard_map/pallas_call | solution.py:360
  125.1 0.0 all-to-all-done.2
  125.2 1.5 %shard_map.105 = bf16[128,2,1152]{2,1,0:T(2,128)(2,1)} custom-call(bf16[256,576]{1,0:T(8,128)(2,1)S(1)} %bitcast.15, bf16[256,1152]{1,0:T(8,128)(2,1)S(1)} %shard_map.104.y_ref, bf16[576,1152]{1,0:T(8,128)(2,1)S(1)} %copy-done.2, f32[1152]{0:T(1024)S(1)} %copy-done.9, f32[6,1152]{1,0:T(8,128)S(1)} %copy-done.7), custom_call_target="tpu_custom_call" | custom-call | flops 339738624 | bytes 3000000 | tf_op jit(solution)/shard_map/pallas_call | solution.py:404
  (18 shorter events, 0.0 us)
Async XLA Ops:
  0.0 52.7 %collective-permute-start = (bf16[128,2,1152]{2,1,0:T(2,128)(2,1)}, bf16[128,2,1152]{2,1,0:T(2,128)(2,1)S(1)}, u32[]{:S(2)}, u32[]{:S(2)}) collective-permute-start(bf16[128,2,1152]{2,1,0:T(2,128)(2,1)} %x_ref.3), channel_id=1, source_target_pairs={{0,1},{1,0},{2,3},{3,2},{4,5},{5,4},{6,7},{7,6},{8,9},{9,8},{10,11... | collective-permute-start | bytes 1769480 | tf_op jit(solution)/shard_map/ppermute | solution.py:295
  2.9 49.7 %collective-permute-start.1 = (f32[864]{0:T(1024)}, f32[864]{0:T(1024)S(1)}, u32[]{:S(2)}, u32[]{:S(2)}) collective-permute-start(f32[864]{0:T(1024)} %b_ref.5), channel_id=1, source_target_pairs={{0,1},{1,0},{2,3},{3,2},{4,5},{5,4},{6,7},{7,6},{8,9},{9,8},{10,11... | collective-permute-start | bytes 10376 | tf_op jit(solution)/shard_map/ppermute | solution.py:295
  46.2 22.1 %all-to-all-start = ((bf16[16,8,2,1152]{3,2,1,0:T(2,128)(2,1)}), bf16[16,8,2,1152]{3,2,1,0:T(2,128)(2,1)}, u32[]{:S(2)}, u32[]{:S(2)}) async-start(bf16[16,8,2,1152]{3,2,1,0:T(2,128)(2,1)} %bitcast.4), calls=%async_computation | async-start | bytes 1179648 | tf_op jit(solution)/shard_map/all_to_all | solution.py:320
  52.7 8.4 %copy-start.10 = (f32[864]{0:T(1024)}, f32[864]{0:T(1024)S(1)}, u32[]{:S(2)}) copy-start(f32[864]{0:T(1024)S(1)} %collective-permute-done.1.refs_0_) | copy-start | bytes 10372
  52.7 1.6 %copy-start.11 = (bf16[128,2,1152]{2,1,0:T(2,128)(2,1)}, bf16[128,2,1152]{2,1,0:T(2,128)(2,1)S(1)}, u32[]{:S(2)}) copy-start(bf16[128,2,1152]{2,1,0:T(2,128)(2,1)S(1)} %collective-permute-done.refs_0_) | copy-start | bytes 1769476
  52.7 10.3 %collective-permute-start.2 = (bf16[144,1152]{1,0:T(8,128)(2,1)}, bf16[144,1152]{1,0:T(8,128)(2,1)S(1)}, u32[]{:S(2)}, u32[]{:S(2)}) collective-permute-start(bf16[144,1152]{1,0:T(8,128)(2,1)} %get-tuple-element.21), channel_id=1, source_target_pairs={{0,1},{1,0},{2,3},{3,2},{4,5},{5,4},{6,7},{7,6},{8,9},{9,8},{10,11... | collective-permute-start | bytes 995336 | tf_op jit(solution)/shard_map/ppermute | solution.py:295
  63.1 28.7 %copy-start.3 = (bf16[144,1152]{1,0:T(8,128)(2,1)}, bf16[144,1152]{1,0:T(8,128)(2,1)S(1)}, u32[]{:S(2)}) copy-start(bf16[144,1152]{1,0:T(8,128)(2,1)S(1)} %collective-permute-done.2.refs_1_.refs_2_) | copy-start | bytes 995332
  63.1 28.6 %collective-permute-start.4 = (bf16[2,216,1152]{2,1,0:T(8,128)(2,1)}, bf16[2,216,1152]{2,1,0:T(8,128)(2,1)}, u32[]{:S(2)}, u32[]{:S(2)}) collective-permute-start(bf16[2,216,1152]{2,1,0:T(8,128)(2,1)} %get-tuple-element.27), channel_id=1, source_target_pairs={{0,1},{1,0},{2,3},{3,2},{4,5},{5,4},{6,7},{7,6},{8,9},{9,8},{10,11... | collective-permute-start | bytes 2985992 | tf_op jit(solution)/shard_map/ppermute | solution.py:295
  64.6 3.7 %collective-permute-start.3 = (bf16[144,1152]{1,0:T(8,128)(2,1)S(1)}, bf16[144,1152]{1,0:T(8,128)(2,1)S(1)}, u32[]{:S(2)}, u32[]{:S(2)}) collective-permute-start(bf16[144,1152]{1,0:T(8,128)(2,1)S(1)} %collective-permute-done.2.refs_1_.refs_2_), channel_id=1, source_target_pairs={{0,2},{2,0},{4,6},{6,4},{8,10},{10,8},{12,14},{14,12},{16,18},{18,... | collective-permute-start | bytes 995336 | tf_op jit(solution)/shard_map/ppermute | solution.py:298
  68.3 23.5 %copy-start.5 = (bf16[144,1152]{1,0:T(8,128)(2,1)}, bf16[144,1152]{1,0:T(8,128)(2,1)S(1)}, u32[]{:S(2)}) copy-start(bf16[144,1152]{1,0:T(8,128)(2,1)S(1)} %collective-permute-done.3.refs_2_.refs_3_) | copy-start | bytes 995332
  91.7 8.1 %collective-permute-start.5 = (bf16[2,216,1152]{2,1,0:T(8,128)(2,1)}, bf16[2,216,1152]{2,1,0:T(8,128)(2,1)}, u32[]{:S(2)}, u32[]{:S(2)}) collective-permute-start(bf16[2,216,1152]{2,1,0:T(8,128)(2,1)} %collective-permute-done.4.refs_1_), channel_id=1, source_target_pairs={{0,2},{2,0},{4,6},{6,4},{8,10},{10,8},{12,14},{14,12},{16,18},{18,... | collective-permute-start | bytes 2985992 | tf_op jit(solution)/shard_map/ppermute | solution.py:298
  99.8 19.6 %copy-start = (bf16[288,1152]{1,0:T(8,128)(2,1)S(1)}, bf16[288,1152]{1,0:T(8,128)(2,1)}, u32[]{:S(2)}) copy-start(bf16[288,1152]{1,0:T(8,128)(2,1)} %refs_1_.1) | copy-start | bytes 1990660
  99.8 19.6 %copy-start.7 = (f32[6,1152]{1,0:T(8,128)S(1)}, f32[6,1152]{1,0:T(8,128)}, u32[]{:S(2)}) copy-start(f32[6,1152]{1,0:T(8,128)} %mod_ref.9) | copy-start | bytes 82948
  99.8 19.6 %copy-start.8 = (f32[1152]{0:T(1024)S(1)}, f32[1152]{0:T(1024)}, u32[]{:S(2)}) copy-start(f32[1152]{0:T(1024)} %outbias_ref.4) | copy-start | bytes 13828
  106.1 19.1 %copy-start.9 = (f32[1152]{0:T(1024)S(1)}, f32[1152]{0:T(1024)}, u32[]{:S(2)}) copy-start(f32[1152]{0:T(1024)} %outbias_ref.5) | copy-start | bytes 13828
  106.1 19.0 %all-to-all-start.2 = ((bf16[16,16,576]{2,1,0:T(8,128)(2,1)}), bf16[16,16,576]{2,1,0:T(8,128)(2,1)S(1)}, u32[]{:S(2)}, u32[]{:S(2)}) async-start(bf16[16,16,576]{2,1,0:T(8,128)(2,1)} %bitcast.21), calls=%async_computation.2 | async-start | bytes 655360 | tf_op jit(solution)/shard_map/all_to_all | solution.py:402
  112.1 7.3 %collective-permute-start.6 = (bf16[256,288]{1,0:T(8,128)(2,1)S(1)}, bf16[256,288]{1,0:T(8,128)(2,1)S(1)}, u32[]{:S(2)}, u32[]{:S(2)}) collective-permute-start(bf16[256,288]{1,0:T(8,128)(2,1)S(1)} %dynamic-slice_bitcast_fusion), channel_id=1, source_target_pairs={{0,1},{1,0},{2,3},{3,2},{4,5},{5,4},{6,7},{7,6},{8,9},{9,8},{10,11... | collective-permute-start | bytes 442376 | tf_op jit(solution)/shard_map/ppermute | solution.py:295
  119.4 1.0 copy-start.1
  120.4 1.0 copy-start.4
  121.4 1.0 copy-start.6
  122.3 2.8 %copy-start.2 = (bf16[576,1152]{1,0:T(8,128)(2,1)S(1)}, bf16[576,1152]{1,0:T(8,128)(2,1)}, u32[]{:S(2)}) copy-start(bf16[576,1152]{1,0:T(8,128)(2,1)} %w_ref.1) | copy-start | bytes 3981316

commit v5 on v4

--- a/solution.py
+++ b/solution.py
@@ -121,21 +121,24 @@
 
 def kernel_spatial(own_hbm, w_hbm, mod_ref, b_ref, *refs):
     x_refs, (out_ref, part_ref, own_ref, w_ref, sems) = refs[:-5], refs[-5:]
-    copies = fetch((w_hbm, own_hbm), (w_ref, own_ref), sems)
+    heads = w_ref.shape[0]
+    copies = fetch(
+        (*[w_hbm.at[i] for i in range(heads)], own_hbm),
+        (*[w_ref.at[i] for i in range(heads)], own_ref),
+        sems,
+    )
     space, _ = coordinates()
     patches, frames, _ = x_refs[0].shape
-    heads = w_ref.shape[0]
     spaces = len(x_refs) + 1
     bias = bias_column(b_ref)
-    for j, x_ref in enumerate(x_refs):
-        h = spatial_rows(flat(x_ref), mod_ref, frames)
-        if j == 0:
-            copies[0].wait()
-        for i in range(heads):
-            qkv = mm(w_ref[i], h, NT) + bias[i * 3 * HD : (i + 1) * 3 * HD]
+    rows = [spatial_rows(flat(x_ref), mod_ref, frames) for x_ref in x_refs]
+    for i in range(heads):
+        copies[i].wait()
+        for j in range(spaces - 1):
+            qkv = mm(w_ref[i], rows[j], NT) + bias[i * 3 * HD : (i + 1) * 3 * HD]
             for c in range(3):
                 part_ref[j, i, c] = qkv[c * HD : (c + 1) * HD].astype(BF)
-    copies[1].wait()
+    copies[heads].wait()
     by_frame = []
     for f in range(frames):
         cols = slice(f * patches, (f + 1) * patches)
@@ -181,43 +184,33 @@
     return attend(qkv[0:HD], qkv[HD : 2 * HD], qkv[2 * HD : 3 * HD], mask)
 
 
-def out_places(pieces, out_w_ref, core):
+def parts_of(o, pieces, core):
     half = pieces[1].shape[0]
-    places = [out_w_ref.at[0]]
-    for n in range(1, len(pieces)):
-        start = half * (core if n % 2 else 1 - core)
-        places.append(out_w_ref.at[(n + 1) // 2, pl.ds(pl.multiple_of(start, half), half)])
-    return places
-
-
-def kernel_temporal(
-    o_hbm, x_hbm, w_hbm, outbias_ref, mod_ref, b_ref, *refs, size, frames
-):
+    parts = [mm(o(0), pieces[0][...])]
+    for k in range(1, (len(pieces) + 1) // 2):
+        first, second = pieces[2 * k - 1][...], pieces[2 * k][...]
+        rows = jnp.concatenate([jnp.where(core == 0, first, second), jnp.where(core == 0, second, first)])
+        parts.append(mm(o(k), rows))
+    return parts
+
+
+def kernel_temporal(o_ref, x_ref, w_ref, outbias_ref, mod_ref, b_ref, *refs, size, frames):
     space, core = coordinates()
-    pieces, (h_ref, out_ref, o_ref, x_ref, out_w_ref, w_ref, sems) = refs[:-7], refs[-7:]
-    copies = fetch(
-        (*pieces, o_hbm, x_hbm, w_hbm),
-        (*out_places(pieces, out_w_ref, core), o_ref, x_ref, w_ref),
-        sems,
-    )
+    pieces, (h_ref, out_ref) = refs[:-2], refs[-2:]
     spaces, rows, _ = o_ref.shape
     mask = temporal_mask(rows, size, frames)
-    for copy in copies[:-1]:
-        copy.wait()
-    parts = [mm(o_ref[lax.rem(space - k + spaces, spaces)], out_w_ref[k]) for k in range(spaces)]
+    parts = parts_of(lambda k: o_ref[lax.rem(space - k + spaces, spaces)], pieces, core)
     y = middle(flat(x_ref), parts, outbias_ref[...].reshape(1, -1), mod_ref[2:3, :])
     h = modulated(y.astype(F32), mod_ref[3:4, :], mod_ref[4:5, :]).astype(BF)
     h_ref[...] = h
     bias = bias_column(b_ref)
-    copies[-1].wait()
     for i in range(w_ref.shape[0]):
         out_ref[i] = temporal_head(w_ref[i], bias[i * 3 * HD : (i + 1) * 3 * HD], h, mask)
 
 
 def kernel_rest(h_ref, own_ref, *refs, size, frames, spaces):
-    b_refs, w_hbms, (out_ref, turn_ref, w_ref, sems) = refs[: spaces - 1], refs[spaces - 1 : -4], refs[-4:]
+    b_refs, w_refs, (out_ref, turn_ref) = refs[: spaces - 1], refs[spaces - 1 : -2], refs[-2:]
     space, core = coordinates()
-    copies = fetch(w_hbms, [w_ref.at[n] for n in range(len(w_hbms))], sems)
     h = h_ref[...]
     rows = h.shape[0]
     mask = temporal_mask(rows, size, frames)
@@ -225,30 +218,24 @@
     half = heads // 2
     for i in range(heads):
         turn_ref[space * heads + i] = own_ref[i]
-    for n in range(len(w_hbms)):
+    for n, w_ref in enumerate(w_refs):
         shift = n // 2 + 1
         bias = bias_column(b_refs[shift - 1])
         second = (core == 0) == (n % 2 == 1)
         within = jnp.where(second, half, 0)
         group = lax.rem(space - shift + spaces, spaces)
         bias = jnp.where(second, bias[half * 3 * HD :], bias[: half * 3 * HD])
-        copies[n].wait()
         for i in range(half):
-            o_t = temporal_head(w_ref[n, i], bias[i * 3 * HD : (i + 1) * 3 * HD], h, mask)
+            o_t = temporal_head(w_ref[i], bias[i * 3 * HD : (i + 1) * 3 * HD], h, mask)
             turn_ref[group * heads + within + i] = o_t
     out_ref[...] = turn_ref[...].reshape(-1, rows).T.astype(BF)
 
 
 def kernel_home(o_own_ref, x_ref, outbias_ref, mod_ref, *refs):
     space, core = coordinates()
-    spaces = refs[-2].shape[0]
-    o_refs, pieces, (out_ref, out_w_ref, sems) = refs[: spaces - 1], refs[spaces - 1 : -3], refs[-3:]
-    copies = fetch(pieces, out_places(pieces, out_w_ref, core), sems)
-    for copy in copies:
-        copy.wait()
-    parts = [mm(o_own_ref[space], out_w_ref[0])]
-    for k in range(1, spaces):
-        parts.append(mm(o_refs[k - 1][...], out_w_ref[k]))
+    spaces = o_own_ref.shape[0]
+    o_refs, pieces, out_ref = refs[: spaces - 1], refs[spaces - 1 : -1], refs[-1]
+    parts = parts_of(lambda k: o_refs[k - 1][...] if k else o_own_ref[space], pieces, core)
     out_ref[...] = middle(flat(x_ref), parts, outbias_ref[...].reshape(1, -1), mod_ref[2:3, :])
 
 
@@ -308,7 +295,7 @@
             for a in ((heads, 3, HD, rows), (half, 3 * HD, width), (half * HD, width))
         ),
         in_specs=[VMEM] + [ANY] * 3 + [VMEM] * 2,
-        out_specs=(VMEM, ANY, ANY),
+        out_specs=(VMEM, VMEM, VMEM),
         scratch_shapes=[pltpu.VMEM(w_spatial.shape, BF), pltpu.SemaphoreType.DMA((3,))],
         compiler_params=PARAMS,
         cost_estimate=pl.CostEstimate(
@@ -334,7 +321,7 @@
             pltpu.VMEM((spaces - 1, heads, 3, HD, rows), BF),
             pltpu.VMEM(own.shape, BF),
             pltpu.VMEM(w_spatial.shape, BF),
-            pltpu.SemaphoreType.DMA((2,)),
+            pltpu.SemaphoreType.DMA((heads + 1,)),
         ],
         (0, 1),
     )(own, w_spatial, modulation, bias_spatial, *arrived)
@@ -363,24 +350,15 @@
         4 + len(o_home) + len(out_pieces),
         2 * rows * width * cols * spaces,
         3e6,
-        [pltpu.VMEM((spaces, cols, width), BF), pltpu.SemaphoreType.DMA((len(out_pieces),))],
-        range(4 + len(o_home), 4 + len(o_home) + len(out_pieces)),
-        SMALL,
+        params=SMALL,
     )(o_all, tokens, outbias_spatial, modulation, *o_home, *out_pieces)
     x_here = spread.reshape(rows // frames, frames, width)
     h_here, o_own = pl.pallas_call(
         functools.partial(kernel_temporal, size=size, frames=frames),
         out_shape=(jax.ShapeDtypeStruct((rows, width), BF), jax.ShapeDtypeStruct((heads, HD, rows), F32)),
-        in_specs=[ANY] * 3 + [VMEM] * 3 + [ANY] * len(out_pieces),
+        in_specs=[VMEM] * (6 + len(out_pieces)),
         out_specs=(VMEM, VMEM),
-        scratch_shapes=[
-            pltpu.VMEM(o_here.shape, BF),
-            pltpu.VMEM(x_here.shape, BF),
-            pltpu.VMEM((spaces, cols, width), BF),
-            pltpu.VMEM(w_temporal.shape, BF),
-            pltpu.SemaphoreType.DMA((len(out_pieces) + 3,)),
-        ],
-        compiler_params=PARAMS,
+        compiler_params=SMALL,
         cost_estimate=pl.CostEstimate(
             flops=2 * rows * width * cols * (3 + spaces), bytes_accessed=5 * 10**6, transcendentals=0
         ),
@@ -393,10 +371,8 @@
         5e6,
         [
             pltpu.VMEM((spaces * heads, HD, rows), F32),
-            pltpu.VMEM((len(other_heads), half, 3 * HD, width), BF),
-            pltpu.SemaphoreType.DMA((len(other_heads),)),
         ],
-        range(1 + spaces, 1 + spaces + len(other_heads)),
+        params=SMALL,
     )(h_here, o_own, *other_bias, *other_heads)
     o_t = o_t.reshape(times, frames * size, spaces * cols)
     o_final = lax.all_to_all(o_t, "tm", 0, 0, tiled=True).reshape(rows, spaces * cols)

time: 127 us -> 85.1 us (0.67)
  Pallas kernels: 68.6 us -> 26.4 us
  local copies, waits for them, and re-layouts: 3.93 us -> 2.42 us
    pallas_call x1, Pallas kernels: 43.2 us -> 4.8 us  [local(): pl.pallas_call(kernel_qkv, out_shape=tuple((jax.ShapeDtypeStruct(a, BF) f...]
    pallas_call x1, Pallas kernels: 6.22 us -> 3.26 us  [local(): call(functools.partial(kernel_rest, size=size, frames=frames, spaces=spac...]
    all_to_all x1, waiting for transfers between devices: 3.73 us -> 1.68 us  [local(): lax.all_to_all(spread.reshape(times, size, frames, width), 'tm', 0, 0, ti...]
    pallas_call x1, Pallas kernels: 8.01 us -> 5.98 us  [local(): pl.pallas_call(functools.partial(kernel_temporal, size=size, frames=frame...]
    all_to_all x1, waiting for transfers between devices: 0.01 us -> 1.54 us  [local(): lax.all_to_all(o_t, 'tm', 0, 0, tiled=True).reshape(rows, spaces * cols)]
    unnamed x24 -> x18, local copies, waits for them, and re-layouts: 2.98 us -> 2.39 us
  transfers between devices with their start and end apart: 9 -> 9, of which waited for: 3 -> 5; matrix products, arithmetic and copies ran while one was open for 1% -> 0% of each run, Pallas kernels for 48% -> 24%
where the time goes in v5:
time: 85.1 us; the launch traced here: 84.5 us
  Pallas kernels  26.4 us (31%)
  blocking collectives  24.4 us (29%)
  starting transfers between devices  19.2 us (23%)
  waiting for transfers between devices  12.1 us (14%)
  local copies, waits for them, and re-layouts  2.42 us (3%)
    all_to_all x1, blocking collectives, local(): lax.all_to_all(after((o_all,), spread, *out_pieces)[0].reshape(spaces * t...  24.4 us
    ppermute x5, waiting for transfers between devices, across(): lax.ppermute(array, 'space', [(i, (i + k) % spaces) for i in range(spaces)])  8.74 us
    pallas_call x1, Pallas kernels, local(): call(kernel_spatial, (spaces, rows, cols), 4 + len(arrived), 10000000000....  7.5 us
    ppermute x5, starting transfers between devices, across(): lax.ppermute(array, 'space', [(i, (i + k) % spaces) for i in range(spaces)])  7.04 us
    all_to_all x1, starting transfers between devices, local(): lax.all_to_all(spread.reshape(times, size, frames, width), 'tm', 0, 0, ti...  6.48 us
    pallas_call x1, Pallas kernels, local(): pl.pallas_call(functools.partial(kernel_temporal, size=size, frames=frame...  5.98 us
    all_to_all x1, starting transfers between devices, local(): lax.all_to_all(o_t, 'tm', 0, 0, tiled=True).reshape(rows, spaces * cols)  5.54 us
    pallas_call x1, Pallas kernels, local(): pl.pallas_call(kernel_qkv, out_shape=tuple((jax.ShapeDtypeStruct(a, BF) f...  4.8 us
  transfers between devices with their start and end apart: 9, of which 5 were waited for; matrix products, arithmetic and copies ran while one was open for 0% of the time, Pallas kernels for 24%

profile of v5, /device:TPU:0, one launch (start us, length us, event | category | flops | bytes accessed | tf_op | source)
XLA Modules:
  0.0 84.5 jit_solution(16153803096878288966)
XLA Ops:
  0.0 2.9 %collective-permute-start = (bf16[128,2,1152]{2,1,0:T(2,128)(2,1)}, bf16[128,2,1152]{2,1,0:T(2,128)(2,1)S(1)}, u32[]{:S(2)}, u32[]{:S(2)}) collective-permute-start(bf16[128,2,1152]{2,1,0:T(2,128)(2,1)} %x_ref.3), channel_id=1, source_target_pairs={{0,1},{1,0},{2,3},{3,2},{4,5},{5,4},{6,7},{7,6},{8,9},{9,8},{10,11... | collective-permute-start | bytes 1769480 | tf_op jit(solution)/shard_map/ppermute | solution.py:282
  2.9 0.0 collective-permute-start.1
  3.0 4.8 %shard_map.100 = (bf16[4,3,72,256]{3,2,1,0:T(8,128)(2,1)}, bf16[2,216,1152]{2,1,0:T(8,128)(2,1)}, bf16[144,1152]{1,0:T(8,128)(2,1)}) custom-call(bf16[128,2,1152]{2,1,0:T(2,128)(2,1)} %x_ref.3, bf16[4,216,1152]{2,1,0:T(8,128)(2,1)} %bitcast.18, bf16[4,216,1152]{2,1,0:T(8,128)(2,1)} %bitcast.14, bf16[288,1152]{1,0:T(8,128)(2,1)} %refs_1_.1, ...), custom_call_target="tpu_custom_call" | custom-call | flops 509607936 | bytes 3000000 | tf_op jit(solution)/shard_map/pallas_call | solution.py:291
  7.8 6.5 %all-to-all-start = ((bf16[16,8,2,1152]{3,2,1,0:T(2,128)(2,1)}), bf16[16,8,2,1152]{3,2,1,0:T(2,128)(2,1)}, u32[]{:S(2)}, u32[]{:S(2)}) async-start(bf16[16,8,2,1152]{3,2,1,0:T(2,128)(2,1)} %bitcast.4), calls=%async_computation | async-start | bytes 1179648 | tf_op jit(solution)/shard_map/all_to_all | solution.py:307
  14.3 2.3 %collective-permute-done.1.refs_0_ = f32[864]{0:T(1024)S(1)} collective-permute-done((f32[864]{0:T(1024)}, f32[864]{0:T(1024)S(1)}, u32[]{:S(2)}, u32[]{:S(2)}) %collective-permute-start.1) | collective-permute-done | bytes 3488 | tf_op jit(solution)/shard_map/ppermute | solution.py:282
  16.6 0.0 collective-permute-done.refs_0_
  16.6 0.8 copy-done.8
  17.4 1.8 %collective-permute-start.2 = (bf16[144,1152]{1,0:T(8,128)(2,1)}, bf16[144,1152]{1,0:T(8,128)(2,1)}, u32[]{:S(2)}, u32[]{:S(2)}) collective-permute-start(bf16[144,1152]{1,0:T(8,128)(2,1)} %get-tuple-element.21), channel_id=1, source_target_pairs={{0,1},{1,0},{2,3},{3,2},{4,5},{5,4},{6,7},{7,6},{8,9},{9,8},{10,11... | collective-permute-start | bytes 995336 | tf_op jit(solution)/shard_map/ppermute | solution.py:282
  19.2 7.5 %shard_map.101.o_own_ref = bf16[2,256,288]{2,1,0:T(8,128)(2,1)} custom-call(bf16[4,3,72,256]{3,2,1,0:T(8,128)(2,1)} %get-tuple-element.17.own_hbm, bf16[4,216,1152]{2,1,0:T(8,128)(2,1)} %bitcast.19, f32[6,1152]{1,0:T(8,128)} %mod_ref.9, f32[864]{0:T(1024)} %b_ref.4, bf16[128,2,1152]{2,1,0:T(2,128)(2,1)} %copy-done.8), custom_call_target="tpu_custom_call" | custom-call | flops 10000000000 | bytes 4000000 | tf_op jit(solution)/shard_map/pallas_call | solution.py:314
  26.7 0.0 collective-permute-done.2.refs_1_.refs_2_
  26.8 1.4 %collective-permute-start.4 = (bf16[2,216,1152]{2,1,0:T(8,128)(2,1)}, bf16[2,216,1152]{2,1,0:T(8,128)(2,1)S(1)}, u32[]{:S(2)}, u32[]{:S(2)}) collective-permute-start(bf16[2,216,1152]{2,1,0:T(8,128)(2,1)} %get-tuple-element.27), channel_id=1, source_target_pairs={{0,1},{1,0},{2,3},{3,2},{4,5},{5,4},{6,7},{7,6},{8,9},{9,8},{10,11... | collective-permute-start | bytes 2985992 | tf_op jit(solution)/shard_map/ppermute | solution.py:282
  28.2 0.0 collective-permute-start.3
  28.2 1.7 %all-to-all-done = bf16[16,8,2,1152]{3,2,1,0:T(2,128)(2,1)} async-done(((bf16[16,8,2,1152]{3,2,1,0:T(2,128)(2,1)}), bf16[16,8,2,1152]{3,2,1,0:T(2,128)(2,1)}, u32[]{:S(2)}, u32[]{:S(2)}) %all-to-all-start) | async-done | bytes 589856 | tf_op jit(solution)/shard_map/all_to_all | solution.py:307
  29.9 0.2 collective-permute-done.3.refs_2_.refs_3_
  30.0 24.4 %all_to_all.15 = bf16[32,16,288]{2,1,0:T(8,128)(2,1)S(1)} all-to-all(bf16[32,16,288]{2,1,0:T(8,128)(2,1)} %bitcast.16), channel_id=1, replica_groups=mesh['grp'=1,'tm'=16,'space'=2] {'space','tm'}, dimensions={0} | all-to-all | bytes 589824 | tf_op jit(solution)/shard_map/all_to_all | solution.py:335
  54.4 0.0 collective-permute-done.4.refs_1_
  54.4 0.1 collective-permute-start.5
  54.5 0.0 copy-done.1
  54.5 0.0 copy-done.4
  54.5 0.0 copy-done.7
  54.5 0.0 copy-start
  54.5 1.5 %copy-done = bf16[1152,864]{0,1:T(8,128)(2,1)S(1)} copy-done((bf16[1152,864]{0,1:T(8,128)(2,1)S(1)}, bf16[1152,864]{0,1:T(8,128)(2,1)}, u32[]{:S(2)}) %copy-start) | copy-done | bytes 1990680
  56.1 6.0 %shard_map.102 = (bf16[256,1152]{1,0:T(8,128)(2,1)S(1)}, f32[4,72,256]{2,1,0:T(8,128)S(1)}) custom-call(bf16[2,256,288]{2,1,0:T(8,128)(2,1)S(1)} %bitcast.17, bf16[128,2,1152]{2,1,0:T(2,128)(2,1)} %bitcast.7.x_ref, bf16[4,216,1152]{2,1,0:T(8,128)(2,1)S(1)} %bitcast.15, f32[1152]{0:T(1024)S(1)} %copy-done.5, f32[6,1152]{1,0:T(8,128)S(1)} %copy-done.4, ...), custom_call_target="tpu_custom_call" | custom-call | flops 849346560 | bytes 5000000 | tf_op jit(solution)/shard_map/pallas_call | solution.py:356
  62.1 0.0 collective-permute-done.5.refs_2_
  62.1 3.3 %shard_map.103 = bf16[256,576]{1,0:T(8,128)(2,1)} custom-call(bf16[256,1152]{1,0:T(8,128)(2,1)S(1)} %get-tuple-element.24.h_ref, f32[4,72,256]{2,1,0:T(8,128)S(1)} %get-tuple-element.25.own_ref, f32[864]{0:T(1024)S(1)} %collective-permute-done.1.refs_0_, bf16[2,216,1152]{2,1,0:T(8,128)(2,1)S(1)} %collective-permute-done.4.refs_1_, ...), custom_call_target="tpu_custom_call" | custom-call | flops 509607936 | bytes 5000000 | tf_op jit(solution)/shard_map/pallas_call | solution.py:366
  65.3 5.5 %all-to-all-start.2 = ((bf16[16,16,576]{2,1,0:T(8,128)(2,1)}), bf16[16,16,576]{2,1,0:T(8,128)(2,1)}, u32[]{:S(2)}, u32[]{:S(2)}) async-start(bf16[16,16,576]{2,1,0:T(8,128)(2,1)} %bitcast.8), calls=%async_computation.2 | async-start | bytes 655360 | tf_op jit(solution)/shard_map/all_to_all | solution.py:378
  70.9 0.0 copy-done.2
  71.0 0.8 collective-permute-start.6
  71.8 6.4 %collective-permute-done.6.refs_0_ = bf16[256,288]{1,0:T(8,128)(2,1)S(1)} collective-permute-done((bf16[256,288]{1,0:T(8,128)(2,1)S(1)}, bf16[256,288]{1,0:T(8,128)(2,1)S(1)}, u32[]{:S(2)}, u32[]{:S(2)}) %collective-permute-start.6) | collective-permute-done | bytes 147488 | tf_op jit(solution)/shard_map/ppermute | solution.py:282
  78.2 2.3 %shard_map.104.y_ref = bf16[256,1152]{1,0:T(8,128)(2,1)S(1)} custom-call(bf16[2,256,288]{2,1,0:T(8,128)(2,1)S(1)} %copy-done.2, bf16[128,2,1152]{2,1,0:T(2,128)(2,1)} %x_ref.3, f32[1152]{0:T(1024)S(1)} %copy-done.5, f32[6,1152]{1,0:T(8,128)S(1)} %copy-done.4, bf16[256,288]{1,0:T(8,128)(2,1)S(1)} %collective-permute-done.6.refs_0_, ...), custom_call_target="tpu_custom_call" | custom-call | flops 339738624 | bytes 3000000 | tf_op jit(solution)/shard_map/pallas_call | solution.py:347
  80.5 1.5 %all-to-all-done.2 = bf16[16,16,576]{2,1,0:T(8,128)(2,1)} async-done(((bf16[16,16,576]{2,1,0:T(8,128)(2,1)}), bf16[16,16,576]{2,1,0:T(8,128)(2,1)}, u32[]{:S(2)}, u32[]{:S(2)}) %all-to-all-start.2) | async-done | bytes 294944 | tf_op jit(solution)/shard_map/all_to_all | solution.py:378
  82.1 2.5 %shard_map.105 = bf16[128,2,1152]{2,1,0:T(2,128)(2,1)} custom-call(bf16[256,576]{1,0:T(8,128)(2,1)} %bitcast.9.o_ref, bf16[256,1152]{1,0:T(8,128)(2,1)S(1)} %shard_map.104.y_ref, bf16[576,1152]{1,0:T(8,128)(2,1)S(1)} %copy-done.3, f32[1152]{0:T(1024)S(1)} %copy-done.6, f32[6,1152]{1,0:T(8,128)S(1)} %copy-done.4), custom_call_target="tpu_custom_call" | custom-call | flops 339738624 | bytes 3000000 | tf_op jit(solution)/shard_map/pallas_call | solution.py:380
  (12 shorter events, 0.0 us)
Async XLA Ops:
  0.0 16.6 %collective-permute-start = (bf16[128,2,1152]{2,1,0:T(2,128)(2,1)}, bf16[128,2,1152]{2,1,0:T(2,128)(2,1)S(1)}, u32[]{:S(2)}, u32[]{:S(2)}) collective-permute-start(bf16[128,2,1152]{2,1,0:T(2,128)(2,1)} %x_ref.3), channel_id=1, source_target_pairs={{0,1},{1,0},{2,3},{3,2},{4,5},{5,4},{6,7},{7,6},{8,9},{9,8},{10,11... | collective-permute-start | bytes 1769480 | tf_op jit(solution)/shard_map/ppermute | solution.py:282
  2.9 13.6 %collective-permute-start.1 = (f32[864]{0:T(1024)}, f32[864]{0:T(1024)S(1)}, u32[]{:S(2)}, u32[]{:S(2)}) collective-permute-start(f32[864]{0:T(1024)} %b_ref.5), channel_id=1, source_target_pairs={{0,1},{1,0},{2,3},{3,2},{4,5},{5,4},{6,7},{7,6},{8,9},{9,8},{10,11... | collective-permute-start | bytes 10376 | tf_op jit(solution)/shard_map/ppermute | solution.py:282
  7.8 22.1 %all-to-all-start = ((bf16[16,8,2,1152]{3,2,1,0:T(2,128)(2,1)}), bf16[16,8,2,1152]{3,2,1,0:T(2,128)(2,1)}, u32[]{:S(2)}, u32[]{:S(2)}) async-start(bf16[16,8,2,1152]{3,2,1,0:T(2,128)(2,1)} %bitcast.4), calls=%async_computation | async-start | bytes 1179648 | tf_op jit(solution)/shard_map/all_to_all | solution.py:307
  16.6 0.8 copy-start.8
  17.4 37.1 %copy-start.1 = (bf16[288,1152]{1,0:T(8,128)(2,1)S(1)}, bf16[288,1152]{1,0:T(8,128)(2,1)}, u32[]{:S(2)}) copy-start(bf16[288,1152]{1,0:T(8,128)(2,1)} %refs_1_.1) | copy-start | bytes 1990660
  17.4 37.1 %copy-start.4 = (f32[6,1152]{1,0:T(8,128)S(1)}, f32[6,1152]{1,0:T(8,128)}, u32[]{:S(2)}) copy-start(f32[6,1152]{1,0:T(8,128)} %mod_ref.9) | copy-start | bytes 82948
  17.4 37.1 %copy-start.5 = (f32[1152]{0:T(1024)S(1)}, f32[1152]{0:T(1024)}, u32[]{:S(2)}) copy-start(f32[1152]{0:T(1024)} %outbias_ref.4) | copy-start | bytes 13828
  17.4 37.1 %copy-start.7 = (f32[864]{0:T(1024)S(1)}, f32[864]{0:T(1024)}, u32[]{:S(2)}) copy-start(f32[864]{0:T(1024)} %b_ref.5) | copy-start | bytes 10372
  17.4 9.4 %collective-permute-start.2 = (bf16[144,1152]{1,0:T(8,128)(2,1)}, bf16[144,1152]{1,0:T(8,128)(2,1)}, u32[]{:S(2)}, u32[]{:S(2)}) collective-permute-start(bf16[144,1152]{1,0:T(8,128)(2,1)} %get-tuple-element.21), channel_id=1, source_target_pairs={{0,1},{1,0},{2,3},{3,2},{4,5},{5,4},{6,7},{7,6},{8,9},{9,8},{10,11... | collective-permute-start | bytes 995336 | tf_op jit(solution)/shard_map/ppermute | solution.py:282
  26.8 27.6 %collective-permute-start.4 = (bf16[2,216,1152]{2,1,0:T(8,128)(2,1)}, bf16[2,216,1152]{2,1,0:T(8,128)(2,1)S(1)}, u32[]{:S(2)}, u32[]{:S(2)}) collective-permute-start(bf16[2,216,1152]{2,1,0:T(8,128)(2,1)} %get-tuple-element.27), channel_id=1, source_target_pairs={{0,1},{1,0},{2,3},{3,2},{4,5},{5,4},{6,7},{7,6},{8,9},{9,8},{10,11... | collective-permute-start | bytes 2985992 | tf_op jit(solution)/shard_map/ppermute | solution.py:282
  28.2 1.8 %collective-permute-start.3 = (bf16[144,1152]{1,0:T(8,128)(2,1)}, bf16[144,1152]{1,0:T(8,128)(2,1)S(1)}, u32[]{:S(2)}, u32[]{:S(2)}) collective-permute-start(bf16[144,1152]{1,0:T(8,128)(2,1)} %collective-permute-done.2.refs_1_.refs_2_), channel_id=1, source_target_pairs={{0,2},{2,0},{4,6},{6,4},{8,10},{10,8},{12,14},{14,12},{16,18},{18,... | collective-permute-start | bytes 995336 | tf_op jit(solution)/shard_map/ppermute | solution.py:285
  54.4 7.7 %collective-permute-start.5 = (bf16[2,216,1152]{2,1,0:T(8,128)(2,1)S(1)}, bf16[2,216,1152]{2,1,0:T(8,128)(2,1)S(1)}, u32[]{:S(2)}, u32[]{:S(2)}) collective-permute-start(bf16[2,216,1152]{2,1,0:T(8,128)(2,1)S(1)} %collective-permute-done.4.refs_1_), channel_id=1, source_target_pairs={{0,2},{2,0},{4,6},{6,4},{8,10},{10,8},{12,14},{14,12},{16,18},{18,... | collective-permute-start | bytes 2985992 | tf_op jit(solution)/shard_map/ppermute | solution.py:285
  54.5 1.6 %copy-start = (bf16[1152,864]{0,1:T(8,128)(2,1)S(1)}, bf16[1152,864]{0,1:T(8,128)(2,1)}, u32[]{:S(2)}) copy-start(bf16[1152,864]{0,1:T(8,128)(2,1)} %param.16) | copy-start | bytes 5971972
  62.1 8.8 %copy-start.2 = (bf16[2,256,288]{2,1,0:T(8,128)(2,1)S(1)}, bf16[2,256,288]{2,1,0:T(8,128)(2,1)}, u32[]{:S(2)}) copy-start(bf16[2,256,288]{2,1,0:T(8,128)(2,1)} %shard_map.101.o_own_ref) | copy-start | bytes 884740
  65.3 16.7 %copy-start.3 = (bf16[576,1152]{1,0:T(8,128)(2,1)S(1)}, bf16[576,1152]{1,0:T(8,128)(2,1)}, u32[]{:S(2)}) copy-start(bf16[576,1152]{1,0:T(8,128)(2,1)} %w_ref.1) | copy-start | bytes 3981316
  65.3 16.7 %copy-start.6 = (f32[1152]{0:T(1024)S(1)}, f32[1152]{0:T(1024)}, u32[]{:S(2)}) copy-start(f32[1152]{0:T(1024)} %outbias_ref.5) | copy-start | bytes 13828
  65.3 16.7 %all-to-all-start.2 = ((bf16[16,16,576]{2,1,0:T(8,128)(2,1)}), bf16[16,16,576]{2,1,0:T(8,128)(2,1)}, u32[]{:S(2)}, u32[]{:S(2)}) async-start(bf16[16,16,576]{2,1,0:T(8,128)(2,1)} %bitcast.8), calls=%async_computation.2 | async-start | bytes 655360 | tf_op jit(solution)/shard_map/all_to_all | solution.py:378
  71.0 7.2 %collective-permute-start.6 = (bf16[256,288]{1,0:T(8,128)(2,1)S(1)}, bf16[256,288]{1,0:T(8,128)(2,1)S(1)}, u32[]{:S(2)}, u32[]{:S(2)}) collective-permute-start(bf16[256,288]{1,0:T(8,128)(2,1)S(1)} %dynamic-slice_bitcast_fusion), channel_id=1, source_target_pairs={{0,1},{1,0},{2,3},{3,2},{4,5},{5,4},{6,7},{7,6},{8,9},{9,8},{10,11... | collective-permute-start | bytes 442376 | tf_op jit(solution)/shard_map/ppermute | solution.py:282

commit v6 on v5

--- a/solution.py
+++ b/solution.py
@@ -96,49 +96,40 @@
     return lax.axis_index("space"), lax.rem(lax.axis_index("tm"), 2)
 
 
-def kernel_qkv(x_ref, w_hbm, w_other_hbm, out_w_hbm, mod_ref, b_ref, out_ref, heads_ref, half_ref, w_ref, sems):
+def kernel_qkv(x_ref, w_ref, w_other_hbm, out_w_hbm, mod_ref, b_ref, out_ref, heads_ref, half_ref, sems):
     _, core = coordinates()
     half, rows = heads_ref.shape[0], half_ref.shape[0]
     copies = fetch(
         (
-            w_hbm,
             out_w_hbm.at[pl.ds(pl.multiple_of(core * rows, rows), rows)],
             w_other_hbm.at[pl.ds(core * half, half)],
         ),
-        (w_ref, half_ref, heads_ref),
+        (half_ref, heads_ref),
         sems,
     )
     h = spatial_rows(flat(x_ref), mod_ref, x_ref.shape[1])
     bias = bias_column(b_ref)
-    copies[0].wait()
     for i in range(w_ref.shape[0]):
         qkv = mm(w_ref[i], h, NT) + bias[i * 3 * HD : (i + 1) * 3 * HD]
         for c in range(3):
             out_ref[i, c] = qkv[c * HD : (c + 1) * HD].astype(BF)
-    for copy in copies[1:]:
+    for copy in copies:
         copy.wait()
 
 
-def kernel_spatial(own_hbm, w_hbm, mod_ref, b_ref, *refs):
-    x_refs, (out_ref, part_ref, own_ref, w_ref, sems) = refs[:-5], refs[-5:]
+def kernel_spatial(own_ref, w_ref, mod_ref, b_ref, *refs):
+    x_refs, (out_ref, part_ref) = refs[:-2], refs[-2:]
     heads = w_ref.shape[0]
-    copies = fetch(
-        (*[w_hbm.at[i] for i in range(heads)], own_hbm),
-        (*[w_ref.at[i] for i in range(heads)], own_ref),
-        sems,
-    )
     space, _ = coordinates()
     patches, frames, _ = x_refs[0].shape
     spaces = len(x_refs) + 1
     bias = bias_column(b_ref)
     rows = [spatial_rows(flat(x_ref), mod_ref, frames) for x_ref in x_refs]
     for i in range(heads):
-        copies[i].wait()
         for j in range(spaces - 1):
             qkv = mm(w_ref[i], rows[j], NT) + bias[i * 3 * HD : (i + 1) * 3 * HD]
             for c in range(3):
                 part_ref[j, i, c] = qkv[c * HD : (c + 1) * HD].astype(BF)
-    copies[heads].wait()
     by_frame = []
     for f in range(frames):
         cols = slice(f * patches, (f + 1) * patches)
@@ -294,17 +285,16 @@
             jax.ShapeDtypeStruct(a, BF)
             for a in ((heads, 3, HD, rows), (half, 3 * HD, width), (half * HD, width))
         ),
-        in_specs=[VMEM] + [ANY] * 3 + [VMEM] * 2,
+        in_specs=[VMEM] * 2 + [ANY] * 2 + [VMEM] * 2,
         out_specs=(VMEM, VMEM, VMEM),
-        scratch_shapes=[pltpu.VMEM(w_spatial.shape, BF), pltpu.SemaphoreType.DMA((3,))],
-        compiler_params=PARAMS,
+        scratch_shapes=[pltpu.SemaphoreType.DMA((2,))],
+        compiler_params=SMALL,
         cost_estimate=pl.CostEstimate(
             flops=2 * rows * width * cols * 3, bytes_accessed=3 * 10**6, transcendentals=0
         ),
     )(tokens, w_spatial, w_temporal, out_spatial, modulation, bias_spatial)
 
-    (spread,) = after((tokens,), own)
-    spread = lax.all_to_all(spread.reshape(times, size, frames, width), "tm", 0, 0, tiled=True)
+    spread = lax.all_to_all(tokens.reshape(times, size, frames, width), "tm", 0, 0, tiled=True)
 
     other_bias = [across(bias_temporal, k) for k in range(1, spaces)]
     (my_out,) = after((my_out,), *other_bias, *arrived)
@@ -319,11 +309,8 @@
         4e6,
         [
             pltpu.VMEM((spaces - 1, heads, 3, HD, rows), BF),
-            pltpu.VMEM(own.shape, BF),
-            pltpu.VMEM(w_spatial.shape, BF),
-            pltpu.SemaphoreType.DMA((heads + 1,)),
         ],
-        (0, 1),
+        params=SMALL,
     )(own, w_spatial, modulation, bias_spatial, *arrived)
 
     (my_heads,) = after((my_heads,), o_all, *direct_out)

time: 85.1 us -> 88.8 us (1.043)
  local copies, waits for them, and re-layouts: 2.42 us -> 9.96 us
  Pallas kernels: 26.4 us -> 21.6 us
    unnamed x18 -> x32, local copies, waits for them, and re-layouts: 2.39 us -> 9.94 us
    pallas_call x1, Pallas kernels: 7.5 us -> 4.12 us  [local(): call(kernel_spatial, (spaces, rows, cols), 4 + len(arrived), 10000000000....]
    all_to_all x1, waiting for transfers between devices: 1.68 us -> 0.01 us  [local(): lax.all_to_all(tokens.reshape(times, size, frames, width), 'tm', 0, 0, ti...]
    ppermute x2, waiting for transfers between devices: 0.16 us -> 1.76 us  [beside(): return lax.ppermute(array, 'tm', [(i, i ^ 1) for i in range(times)])]
    pallas_call x1, Pallas kernels: 4.8 us -> 3.31 us  [local(): pl.pallas_call(kernel_qkv, out_shape=tuple((jax.ShapeDtypeStruct(a, BF) f...]
    pallas_call x1, Pallas kernels: 3.26 us -> 4.5 us  [local(): call(functools.partial(kernel_rest, size=size, frames=frames, spaces=spac...]
    ppermute x5, starting transfers between devices: 7.04 us -> 8.13 us  [across(): lax.ppermute(array, 'space', [(i, (i + k) % spaces) for i in range(spaces)])]
    pallas_call x1, Pallas kernels: 2.48 us -> 1.53 us  [local(): call(kernel_final, (patches, frames, width), 5, 2 * rows * width * cols *...]
  transfers between devices with their start and end apart: 9 -> 9, of which waited for: 5 -> 4; matrix products, arithmetic and copies ran while one was open for 0% -> 0% of each run, Pallas kernels for 24% -> 18%
where the time goes in v6:
time: 88.8 us; the launch traced here: 88.1 us
  blocking collectives  24.8 us (28%)
  Pallas kernels  21.6 us (24%)
  starting transfers between devices  19.4 us (22%)
  waiting for transfers between devices  12.1 us (14%)
  local copies, waits for them, and re-layouts  9.96 us (11%)
    all_to_all x1, blocking collectives, local(): lax.all_to_all(after((o_all,), spread, *out_pieces)[0].reshape(spaces * t...  24.8 us
    unnamed x32, local copies, waits for them, and re-layouts  9.94 us
    ppermute x5, waiting for transfers between devices, across(): lax.ppermute(array, 'space', [(i, (i + k) % spaces) for i in range(spaces)])  8.76 us
    ppermute x5, starting transfers between devices, across(): lax.ppermute(array, 'space', [(i, (i + k) % spaces) for i in range(spaces)])  8.13 us
    all_to_all x1, starting transfers between devices, local(): lax.all_to_all(tokens.reshape(times, size, frames, width), 'tm', 0, 0, ti...  5.98 us
    pallas_call x1, Pallas kernels, local(): pl.pallas_call(functools.partial(kernel_temporal, size=size, frames=frame...  5.98 us
    all_to_all x1, starting transfers between devices, local(): lax.all_to_all(o_t, 'tm', 0, 0, tiled=True).reshape(rows, spaces * cols)  5.17 us
    pallas_call x1, Pallas kernels, local(): call(functools.partial(kernel_rest, size=size, frames=frames, spaces=spac...  4.5 us
  transfers between devices with their start and end apart: 9, of which 4 were waited for; matrix products, arithmetic and copies ran while one was open for 0% of the time, Pallas kernels for 18%

profile of v6, /device:TPU:0, one launch (start us, length us, event | category | flops | bytes accessed | tf_op | source)
XLA Modules:
  0.0 88.1 jit_solution(12996002200311207809)
XLA Ops:
  0.0 2.9 %collective-permute-start = (bf16[128,2,1152]{2,1,0:T(2,128)(2,1)}, bf16[128,2,1152]{2,1,0:T(2,128)(2,1)S(1)}, u32[]{:S(2)}, u32[]{:S(2)}) collective-permute-start(bf16[128,2,1152]{2,1,0:T(2,128)(2,1)} %x_ref.3), channel_id=1, source_target_pairs={{0,1},{1,0},{2,3},{3,2},{4,5},{5,4},{6,7},{7,6},{8,9},{9,8},{10,11... | collective-permute-start | bytes 1769480 | tf_op jit(solution)/shard_map/ppermute | solution.py:273
  2.9 6.0 %all-to-all-start = ((bf16[16,8,2,1152]{3,2,1,0:T(2,128)(2,1)}), bf16[16,8,2,1152]{3,2,1,0:T(2,128)(2,1)}, u32[]{:S(2)}, u32[]{:S(2)}) async-start(bf16[16,8,2,1152]{3,2,1,0:T(2,128)(2,1)} %bitcast.16), calls=%async_computation | async-start | bytes 1179648 | tf_op jit(solution)/shard_map/all_to_all | solution.py:297
  8.9 0.6 collective-permute-start.1
  9.5 1.6 %copy-done = bf16[1152,864]{0,1:T(8,128)(2,1)S(1)} copy-done((bf16[1152,864]{0,1:T(8,128)(2,1)S(1)}, bf16[1152,864]{0,1:T(8,128)(2,1)}, u32[]{:S(2)}) %copy-start) | copy-done | bytes 1990680
  11.1 1.1 %copy-done.2 = bf16[288,1152]{1,0:T(8,128)(2,1)S(1)} copy-done((bf16[288,1152]{1,0:T(8,128)(2,1)S(1)}, bf16[288,1152]{1,0:T(8,128)(2,1)}, u32[]{:S(2)}) %copy-start.2) | copy-done | bytes 663576
  12.2 1.1 %copy-done.4 = bf16[128,2,1152]{2,1,0:T(2,128)(2,1)S(1)} copy-done((bf16[128,2,1152]{2,1,0:T(2,128)(2,1)S(1)}, bf16[128,2,1152]{2,1,0:T(2,128)(2,1)}, u32[]{:S(2)}) %copy-start.4) | copy-done | bytes 589848
  13.2 1.6 %copy-done.6 = bf16[1152,864]{0,1:T(8,128)(2,1)S(1)} copy-done((bf16[1152,864]{0,1:T(8,128)(2,1)S(1)}, bf16[1152,864]{0,1:T(8,128)(2,1)}, u32[]{:S(2)}) %copy-start.6) | copy-done | bytes 1990680
  14.8 0.8 copy-done.8
  15.6 0.7 copy-done.12
  16.2 3.3 %shard_map.100 = (bf16[4,3,72,256]{3,2,1,0:T(8,128)(2,1)S(1)}, bf16[2,216,1152]{2,1,0:T(8,128)(2,1)}, bf16[144,1152]{1,0:T(8,128)(2,1)S(1)}) custom-call(bf16[128,2,1152]{2,1,0:T(2,128)(2,1)S(1)} %copy-done.4, bf16[4,216,1152]{2,1,0:T(8,128)(2,1)S(1)} %bitcast.18, bf16[4,216,1152]{2,1,0:T(8,128)(2,1)S(1)} %bitcast.14, bf16[288,1152]{1,0:T(8,128)(2,1)S(1)} %copy-done.2, ...), custom_call_target="tpu_custom_call" | custom-call | flops 509607936 | bytes 3000000 | tf_op jit(solution)/shard_map/pallas_call | solution.py:282
  19.6 0.0 collective-permute-done.1.refs_0_
  19.6 0.0 copy-start.14
  19.6 0.8 copy-done.14
  20.4 1.6 %collective-permute-start.2 = (bf16[144,1152]{1,0:T(8,128)(2,1)S(1)}, bf16[144,1152]{1,0:T(8,128)(2,1)S(1)}, u32[]{:S(2)}, u32[]{:S(2)}) collective-permute-start(bf16[144,1152]{1,0:T(8,128)(2,1)S(1)} %get-tuple-element.19), channel_id=1, source_target_pairs={{0,1},{1,0},{2,3},{3,2},{4,5},{5,4},{6,7},{7,6},{8,9},{9,8},{10,11... | collective-permute-start | bytes 995336 | tf_op jit(solution)/shard_map/ppermute | solution.py:273
  22.0 1.1 %copy-done.15 = bf16[128,2,1152]{2,1,0:T(2,128)(2,1)S(1)} copy-done((bf16[128,2,1152]{2,1,0:T(2,128)(2,1)S(1)}, bf16[128,2,1152]{2,1,0:T(2,128)(2,1)}, u32[]{:S(2)}) %copy-start.15) | copy-done | bytes 589848
  23.0 4.1 %shard_map.101.o_own_ref = bf16[2,256,288]{2,1,0:T(8,128)(2,1)S(1)} custom-call(bf16[4,3,72,256]{3,2,1,0:T(8,128)(2,1)S(1)} %get-tuple-element.16.own_ref, bf16[4,216,1152]{2,1,0:T(8,128)(2,1)S(1)} %bitcast.19, f32[6,1152]{1,0:T(8,128)S(1)} %copy-done.8, f32[864]{0:T(1024)S(1)} %copy-done.12, bf16[128,2,1152]{2,1,0:T(2,128)(2,1)S(1)} %copy-done.15), custom_call_target="tpu_custom_call" | custom-call | flops 10000000000 | bytes 4000000 | tf_op jit(solution)/shard_map/pallas_call | solution.py:304
  27.2 3.1 %collective-permute-done.2.refs_1_.refs_2_ = bf16[144,1152]{1,0:T(8,128)(2,1)S(1)} collective-permute-done((bf16[144,1152]{1,0:T(8,128)(2,1)S(1)}, bf16[144,1152]{1,0:T(8,128)(2,1)S(1)}, u32[]{:S(2)}, u32[]{:S(2)}) %collective-permute-start.2) | collective-permute-done | bytes 331808 | tf_op jit(solution)/shard_map/ppermute | solution.py:273
  30.2 1.5 %collective-permute-start.4 = (bf16[2,216,1152]{2,1,0:T(8,128)(2,1)}, bf16[2,216,1152]{2,1,0:T(8,128)(2,1)}, u32[]{:S(2)}, u32[]{:S(2)}) collective-permute-start(bf16[2,216,1152]{2,1,0:T(8,128)(2,1)} %get-tuple-element.25), channel_id=1, source_target_pairs={{0,1},{1,0},{2,3},{3,2},{4,5},{5,4},{6,7},{7,6},{8,9},{9,8},{10,11... | collective-permute-start | bytes 2985992 | tf_op jit(solution)/shard_map/ppermute | solution.py:273
  31.7 0.0 collective-permute-start.3
  31.7 1.8 %collective-permute-done.3.refs_2_.refs_3_ = bf16[144,1152]{1,0:T(8,128)(2,1)} collective-permute-done((bf16[144,1152]{1,0:T(8,128)(2,1)S(1)}, bf16[144,1152]{1,0:T(8,128)(2,1)}, u32[]{:S(2)}, u32[]{:S(2)}) %collective-permute-start.3) | collective-permute-done | bytes 331808 | tf_op jit(solution)/shard_map/ppermute | solution.py:276
  33.5 24.8 %all_to_all.15 = bf16[32,16,288]{2,1,0:T(8,128)(2,1)S(1)} all-to-all(bf16[32,16,288]{2,1,0:T(8,128)(2,1)S(1)} %bitcast.17), channel_id=1, replica_groups=mesh['grp'=1,'tm'=16,'space'=2] {'space','tm'}, dimensions={0} | all-to-all | bytes 589824 | tf_op jit(solution)/shard_map/all_to_all | solution.py:322
  58.3 0.1 collective-permute-start.5
  58.4 6.0 %shard_map.102 = (bf16[256,1152]{1,0:T(8,128)(2,1)S(1)}, f32[4,72,256]{2,1,0:T(8,128)S(1)}) custom-call(bf16[2,256,288]{2,1,0:T(8,128)(2,1)S(1)} %bitcast.20, bf16[128,2,1152]{2,1,0:T(2,128)(2,1)} %bitcast.7.x_ref, bf16[4,216,1152]{2,1,0:T(8,128)(2,1)S(1)} %bitcast.15, f32[1152]{0:T(1024)S(1)} %copy-done.10, f32[6,1152]{1,0:T(8,128)S(1)} %copy-done.9, ...), custom_call_target="tpu_custom_call" | custom-call | flops 849346560 | bytes 5000000 | tf_op jit(solution)/shard_map/pallas_call | solution.py:343
  64.4 0.0 copy-start.5
  64.4 4.5 %shard_map.103 = bf16[256,576]{1,0:T(8,128)(2,1)} custom-call(bf16[256,1152]{1,0:T(8,128)(2,1)S(1)} %get-tuple-element.22.h_ref, f32[4,72,256]{2,1,0:T(8,128)S(1)} %get-tuple-element.23.own_ref, f32[864]{0:T(1024)S(1)} %collective-permute-done.1.refs_0_, bf16[2,216,1152]{2,1,0:T(8,128)(2,1)} %collective-permute-done.4.refs_1_, ...), custom_call_target="tpu_custom_call" | custom-call | flops 509607936 | bytes 5000000 | tf_op jit(solution)/shard_map/pallas_call | solution.py:353
  68.9 5.2 %all-to-all-start.2 = ((bf16[16,16,576]{2,1,0:T(8,128)(2,1)}), bf16[16,16,576]{2,1,0:T(8,128)(2,1)S(1)}, u32[]{:S(2)}, u32[]{:S(2)}) async-start(bf16[16,16,576]{2,1,0:T(8,128)(2,1)} %bitcast.8), calls=%async_computation.2 | async-start | bytes 655360 | tf_op jit(solution)/shard_map/all_to_all | solution.py:365
  74.2 1.6 %collective-permute-start.6 = (bf16[256,288]{1,0:T(8,128)(2,1)S(1)}, bf16[256,288]{1,0:T(8,128)(2,1)S(1)}, u32[]{:S(2)}, u32[]{:S(2)}) collective-permute-start(bf16[256,288]{1,0:T(8,128)(2,1)S(1)} %dynamic-slice_bitcast_fusion), channel_id=1, source_target_pairs={{0,1},{1,0},{2,3},{3,2},{4,5},{5,4},{6,7},{7,6},{8,9},{9,8},{10,11... | collective-permute-start | bytes 442376 | tf_op jit(solution)/shard_map/ppermute | solution.py:273
  75.7 5.7 %collective-permute-done.6.refs_0_ = bf16[256,288]{1,0:T(8,128)(2,1)S(1)} collective-permute-done((bf16[256,288]{1,0:T(8,128)(2,1)S(1)}, bf16[256,288]{1,0:T(8,128)(2,1)S(1)}, u32[]{:S(2)}, u32[]{:S(2)}) %collective-permute-start.6) | collective-permute-done | bytes 147488 | tf_op jit(solution)/shard_map/ppermute | solution.py:273
  81.4 2.2 %shard_map.104.y_ref = bf16[256,1152]{1,0:T(8,128)(2,1)S(1)} custom-call(bf16[2,256,288]{2,1,0:T(8,128)(2,1)S(1)} %shard_map.101.o_own_ref, bf16[128,2,1152]{2,1,0:T(2,128)(2,1)S(1)} %copy-done.5, f32[1152]{0:T(1024)S(1)} %copy-done.10, f32[6,1152]{1,0:T(8,128)S(1)} %copy-done.9, bf16[256,288]{1,0:T(8,128)(2,1)S(1)} %collective-permute-done.6.refs_0_, ...), custom_call_target="tpu_custom_call" | custom-call | flops 339738624 | bytes 3000000 | tf_op jit(solution)/shard_map/pallas_call | solution.py:334
  83.6 1.6 %all-to-all-done.2 = bf16[16,16,576]{2,1,0:T(8,128)(2,1)S(1)} async-done(((bf16[16,16,576]{2,1,0:T(8,128)(2,1)}), bf16[16,16,576]{2,1,0:T(8,128)(2,1)S(1)}, u32[]{:S(2)}, u32[]{:S(2)}) %all-to-all-start.2) | async-done | bytes 294944 | tf_op jit(solution)/shard_map/all_to_all | solution.py:365
  85.2 1.3 %copy-done.7 = bf16[576,1152]{1,0:T(8,128)(2,1)S(1)} copy-done((bf16[576,1152]{1,0:T(8,128)(2,1)S(1)}, bf16[576,1152]{1,0:T(8,128)(2,1)}, u32[]{:S(2)}) %copy-start.7) | copy-done | bytes 1327128
  86.5 1.5 %shard_map.105 = bf16[128,2,1152]{2,1,0:T(2,128)(2,1)} custom-call(bf16[256,576]{1,0:T(8,128)(2,1)S(1)} %bitcast.21, bf16[256,1152]{1,0:T(8,128)(2,1)S(1)} %shard_map.104.y_ref, bf16[576,1152]{1,0:T(8,128)(2,1)S(1)} %copy-done.7, f32[1152]{0:T(1024)S(1)} %copy-done.11, f32[6,1152]{1,0:T(8,128)S(1)} %copy-done.9), custom_call_target="tpu_custom_call" | custom-call | flops 339738624 | bytes 3000000 | tf_op jit(solution)/shard_map/pallas_call | solution.py:367
  (26 shorter events, 0.1 us)
Async XLA Ops:
  0.0 19.6 %collective-permute-start = (bf16[128,2,1152]{2,1,0:T(2,128)(2,1)}, bf16[128,2,1152]{2,1,0:T(2,128)(2,1)S(1)}, u32[]{:S(2)}, u32[]{:S(2)}) collective-permute-start(bf16[128,2,1152]{2,1,0:T(2,128)(2,1)} %x_ref.3), channel_id=1, source_target_pairs={{0,1},{1,0},{2,3},{3,2},{4,5},{5,4},{6,7},{7,6},{8,9},{9,8},{10,11... | collective-permute-start | bytes 1769480 | tf_op jit(solution)/shard_map/ppermute | solution.py:273
  2.9 28.8 %all-to-all-start = ((bf16[16,8,2,1152]{3,2,1,0:T(2,128)(2,1)}), bf16[16,8,2,1152]{3,2,1,0:T(2,128)(2,1)}, u32[]{:S(2)}, u32[]{:S(2)}) async-start(bf16[16,8,2,1152]{3,2,1,0:T(2,128)(2,1)} %bitcast.16), calls=%async_computation | async-start | bytes 1179648 | tf_op jit(solution)/shard_map/all_to_all | solution.py:297
  8.9 10.6 %collective-permute-start.1 = (f32[864]{0:T(1024)}, f32[864]{0:T(1024)S(1)}, u32[]{:S(2)}, u32[]{:S(2)}) collective-permute-start(f32[864]{0:T(1024)} %b_ref.5), channel_id=1, source_target_pairs={{0,1},{1,0},{2,3},{3,2},{4,5},{5,4},{6,7},{7,6},{8,9},{9,8},{10,11... | collective-permute-start | bytes 10376 | tf_op jit(solution)/shard_map/ppermute | solution.py:273
  9.5 1.6 %copy-start = (bf16[1152,864]{0,1:T(8,128)(2,1)S(1)}, bf16[1152,864]{0,1:T(8,128)(2,1)}, u32[]{:S(2)}) copy-start(bf16[1152,864]{0,1:T(8,128)(2,1)} %param.16) | copy-start | bytes 5971972
  11.1 1.1 %copy-start.2 = (bf16[288,1152]{1,0:T(8,128)(2,1)S(1)}, bf16[288,1152]{1,0:T(8,128)(2,1)}, u32[]{:S(2)}) copy-start(bf16[288,1152]{1,0:T(8,128)(2,1)} %refs_1_.1) | copy-start | bytes 1990660
  12.2 1.1 %copy-start.4 = (bf16[128,2,1152]{2,1,0:T(2,128)(2,1)S(1)}, bf16[128,2,1152]{2,1,0:T(2,128)(2,1)}, u32[]{:S(2)}) copy-start(bf16[128,2,1152]{2,1,0:T(2,128)(2,1)} %x_ref.3) | copy-start | bytes 1769476
  13.2 1.6 %copy-start.6 = (bf16[1152,864]{0,1:T(8,128)(2,1)S(1)}, bf16[1152,864]{0,1:T(8,128)(2,1)}, u32[]{:S(2)}) copy-start(bf16[1152,864]{0,1:T(8,128)(2,1)} %param.12) | copy-start | bytes 5971972
  14.8 0.8 copy-start.8
  15.6 0.7 copy-start.12
  19.6 0.8 copy-start.14
  20.4 38.0 %copy-start.3 = (bf16[288,1152]{1,0:T(8,128)(2,1)S(1)}, bf16[288,1152]{1,0:T(8,128)(2,1)}, u32[]{:S(2)}) copy-start(bf16[288,1152]{1,0:T(8,128)(2,1)} %refs_1_.1) | copy-start | bytes 1990660
  20.4 38.0 %copy-start.9 = (f32[6,1152]{1,0:T(8,128)S(1)}, f32[6,1152]{1,0:T(8,128)}, u32[]{:S(2)}) copy-start(f32[6,1152]{1,0:T(8,128)} %mod_ref.9) | copy-start | bytes 82948
  20.4 38.0 %copy-start.10 = (f32[1152]{0:T(1024)S(1)}, f32[1152]{0:T(1024)}, u32[]{:S(2)}) copy-start(f32[1152]{0:T(1024)} %outbias_ref.4) | copy-start | bytes 13828
  20.4 38.0 %copy-start.13 = (f32[864]{0:T(1024)S(1)}, f32[864]{0:T(1024)}, u32[]{:S(2)}) copy-start(f32[864]{0:T(1024)} %b_ref.5) | copy-start | bytes 10372
  20.4 9.8 %collective-permute-start.2 = (bf16[144,1152]{1,0:T(8,128)(2,1)S(1)}, bf16[144,1152]{1,0:T(8,128)(2,1)S(1)}, u32[]{:S(2)}, u32[]{:S(2)}) collective-permute-start(bf16[144,1152]{1,0:T(8,128)(2,1)S(1)} %get-tuple-element.19), channel_id=1, source_target_pairs={{0,1},{1,0},{2,3},{3,2},{4,5},{5,4},{6,7},{7,6},{8,9},{9,8},{10,11... | collective-permute-start | bytes 995336 | tf_op jit(solution)/shard_map/ppermute | solution.py:273
  22.0 1.1 %copy-start.15 = (bf16[128,2,1152]{2,1,0:T(2,128)(2,1)S(1)}, bf16[128,2,1152]{2,1,0:T(2,128)(2,1)}, u32[]{:S(2)}) copy-start(bf16[128,2,1152]{2,1,0:T(2,128)(2,1)} %copy-done.14) | copy-start | bytes 1769476
  23.0 35.4 %copy-start.1 = (bf16[1152,864]{0,1:T(8,128)(2,1)S(1)}, bf16[1152,864]{0,1:T(8,128)(2,1)}, u32[]{:S(2)}) copy-start(bf16[1152,864]{0,1:T(8,128)(2,1)} %param.16) | copy-start | bytes 5971972
  30.2 28.1 %collective-permute-start.4 = (bf16[2,216,1152]{2,1,0:T(8,128)(2,1)}, bf16[2,216,1152]{2,1,0:T(8,128)(2,1)}, u32[]{:S(2)}, u32[]{:S(2)}) collective-permute-start(bf16[2,216,1152]{2,1,0:T(8,128)(2,1)} %get-tuple-element.25), channel_id=1, source_target_pairs={{0,1},{1,0},{2,3},{3,2},{4,5},{5,4},{6,7},{7,6},{8,9},{9,8},{10,11... | collective-permute-start | bytes 2985992 | tf_op jit(solution)/shard_map/ppermute | solution.py:273
  31.7 1.8 %collective-permute-start.3 = (bf16[144,1152]{1,0:T(8,128)(2,1)S(1)}, bf16[144,1152]{1,0:T(8,128)(2,1)}, u32[]{:S(2)}, u32[]{:S(2)}) collective-permute-start(bf16[144,1152]{1,0:T(8,128)(2,1)S(1)} %collective-permute-done.2.refs_1_.refs_2_), channel_id=1, source_target_pairs={{0,2},{2,0},{4,6},{6,4},{8,10},{10,8},{12,14},{14,12},{16,18},{18,... | collective-permute-start | bytes 995336 | tf_op jit(solution)/shard_map/ppermute | solution.py:276
  58.3 6.1 %collective-permute-start.5 = (bf16[2,216,1152]{2,1,0:T(8,128)(2,1)}, bf16[2,216,1152]{2,1,0:T(8,128)(2,1)S(1)}, u32[]{:S(2)}, u32[]{:S(2)}) collective-permute-start(bf16[2,216,1152]{2,1,0:T(8,128)(2,1)} %collective-permute-done.4.refs_1_), channel_id=1, source_target_pairs={{0,2},{2,0},{4,6},{6,4},{8,10},{10,8},{12,14},{14,12},{16,18},{18,... | collective-permute-start | bytes 2985992 | tf_op jit(solution)/shard_map/ppermute | solution.py:276
  64.4 17.0 %copy-start.5 = (bf16[128,2,1152]{2,1,0:T(2,128)(2,1)S(1)}, bf16[128,2,1152]{2,1,0:T(2,128)(2,1)}, u32[]{:S(2)}) copy-start(bf16[128,2,1152]{2,1,0:T(2,128)(2,1)} %x_ref.3) | copy-start | bytes 1769476
  68.9 16.3 %copy-start.11 = (f32[1152]{0:T(1024)S(1)}, f32[1152]{0:T(1024)}, u32[]{:S(2)}) copy-start(f32[1152]{0:T(1024)} %outbias_ref.5) | copy-start | bytes 13828
  68.9 16.3 %all-to-all-start.2 = ((bf16[16,16,576]{2,1,0:T(8,128)(2,1)}), bf16[16,16,576]{2,1,0:T(8,128)(2,1)S(1)}, u32[]{:S(2)}, u32[]{:S(2)}) async-start(bf16[16,16,576]{2,1,0:T(8,128)(2,1)} %bitcast.8), calls=%async_computation.2 | async-start | bytes 655360 | tf_op jit(solution)/shard_map/all_to_all | solution.py:365
  74.2 7.3 %collective-permute-start.6 = (bf16[256,288]{1,0:T(8,128)(2,1)S(1)}, bf16[256,288]{1,0:T(8,128)(2,1)S(1)}, u32[]{:S(2)}, u32[]{:S(2)}) collective-permute-start(bf16[256,288]{1,0:T(8,128)(2,1)S(1)} %dynamic-slice_bitcast_fusion), channel_id=1, source_target_pairs={{0,1},{1,0},{2,3},{3,2},{4,5},{5,4},{6,7},{7,6},{8,9},{9,8},{10,11... | collective-permute-start | bytes 442376 | tf_op jit(solution)/shard_map/ppermute | solution.py:273
  85.2 1.3 %copy-start.7 = (bf16[576,1152]{1,0:T(8,128)(2,1)S(1)}, bf16[576,1152]{1,0:T(8,128)(2,1)}, u32[]{:S(2)}) copy-start(bf16[576,1152]{1,0:T(8,128)(2,1)} %w_ref.1) | copy-start | bytes 3981316

commit v7 on v6

--- a/solution.py
+++ b/solution.py
@@ -96,25 +96,18 @@
     return lax.axis_index("space"), lax.rem(lax.axis_index("tm"), 2)
 
 
-def kernel_qkv(x_ref, w_ref, w_other_hbm, out_w_hbm, mod_ref, b_ref, out_ref, heads_ref, half_ref, sems):
+def kernel_qkv(x_ref, w_hbm, w_other_hbm, mod_ref, b_ref, out_ref, heads_ref, w_ref, sems):
     _, core = coordinates()
-    half, rows = heads_ref.shape[0], half_ref.shape[0]
-    copies = fetch(
-        (
-            out_w_hbm.at[pl.ds(pl.multiple_of(core * rows, rows), rows)],
-            w_other_hbm.at[pl.ds(core * half, half)],
-        ),
-        (half_ref, heads_ref),
-        sems,
-    )
+    half = heads_ref.shape[0]
+    copies = fetch((w_hbm, w_other_hbm.at[pl.ds(core * half, half)]), (w_ref, heads_ref), sems)
     h = spatial_rows(flat(x_ref), mod_ref, x_ref.shape[1])
     bias = bias_column(b_ref)
+    copies[0].wait()
     for i in range(w_ref.shape[0]):
         qkv = mm(w_ref[i], h, NT) + bias[i * 3 * HD : (i + 1) * 3 * HD]
         for c in range(3):
             out_ref[i, c] = qkv[c * HD : (c + 1) * HD].astype(BF)
-    for copy in copies:
-        copy.wait()
+    copies[1].wait()
 
 
 def kernel_spatial(own_ref, w_ref, mod_ref, b_ref, *refs):
@@ -279,26 +272,25 @@
 
     w_spatial = qkv_spatial.T.reshape(heads, 3 * HD, width)
     w_temporal = qkv_temporal.T.reshape(heads, 3 * HD, width)
-    own, my_heads, my_out = pl.pallas_call(
+    own, my_heads = pl.pallas_call(
         kernel_qkv,
         out_shape=tuple(
-            jax.ShapeDtypeStruct(a, BF)
-            for a in ((heads, 3, HD, rows), (half, 3 * HD, width), (half * HD, width))
+            jax.ShapeDtypeStruct(a, BF) for a in ((heads, 3, HD, rows), (half, 3 * HD, width))
         ),
-        in_specs=[VMEM] * 2 + [ANY] * 2 + [VMEM] * 2,
-        out_specs=(VMEM, VMEM, VMEM),
-        scratch_shapes=[pltpu.SemaphoreType.DMA((2,))],
-        compiler_params=SMALL,
+        in_specs=[VMEM] + [ANY] * 2 + [VMEM] * 2,
+        out_specs=(VMEM, VMEM),
+        scratch_shapes=[pltpu.VMEM(w_spatial.shape, BF), pltpu.SemaphoreType.DMA((2,))],
+        compiler_params=PARAMS,
         cost_estimate=pl.CostEstimate(
             flops=2 * rows * width * cols * 3, bytes_accessed=3 * 10**6, transcendentals=0
         ),
-    )(tokens, w_spatial, w_temporal, out_spatial, modulation, bias_spatial)
+    )(tokens, w_spatial, w_temporal, modulation, bias_spatial)
 
     spread = lax.all_to_all(tokens.reshape(times, size, frames, width), "tm", 0, 0, tiled=True)
 
     other_bias = [across(bias_temporal, k) for k in range(1, spaces)]
-    (my_out,) = after((my_out,), *other_bias, *arrived)
-    arrived = [after((a,), own)[0] for a in arrived]
+    my_out = lax.dynamic_slice_in_dim(out_spatial, lax.rem(lax.axis_index("tm"), 2) * half * HD, half * HD, 0)
+    arrived = [after((a,), own, *other_bias)[0] for a in arrived]
     direct_out = [across(my_out, k) for k in range(1, spaces)]
 
     o_all = call(
@@ -313,11 +305,11 @@
         params=SMALL,
     )(own, w_spatial, modulation, bias_spatial, *arrived)
 
-    (my_heads,) = after((my_heads,), o_all, *direct_out)
+    (my_heads,) = after((my_heads,), *arrived)
     direct_heads = [across(my_heads, k) for k in range(1, spaces)]
     out_pieces = [out_spatial]
     for a in direct_out:
-        out_pieces += [a, beside(after((a,), o_all)[0])]
+        out_pieces += [a, beside(a)]
 
     o_here = lax.all_to_all(
         after((o_all,), spread, *out_pieces)[0].reshape(spaces * times, frames * size, cols), ("space", "tm"), 0, 0, tiled=True

time: 88.8 us -> 85.4 us (0.962)
  blocking collectives: 24.8 us -> 0 us
  waiting for transfers between devices: 12.1 us -> 26 us
  starting transfers between devices: 19.4 us -> 25.2 us
  Pallas kernels: 21.6 us -> 25 us
  local copies, waits for them, and re-layouts: 9.96 us -> 8.32 us
    all_to_all x1 -> x0, blocking collectives: 24.8 us -> none  [local(): lax.all_to_all(after((o_all,), spread, *out_pieces)[0].reshape(spaces * t...]
    ppermute x5, waiting for transfers between devices: 8.76 us -> 23.7 us  [across(): lax.ppermute(array, 'space', [(i, (i + k) % spaces) for i in range(spaces)])]
    all_to_all x0 -> x1, starting transfers between devices: none -> 5.04 us  [local(): lax.all_to_all(after((o_all,), spread, *out_pieces)[0].reshape(spaces * t...]
    unnamed x32 -> x28, local copies, waits for them, and re-layouts: 9.94 us -> 5.63 us
    pallas_call x1, Pallas kernels: 4.12 us -> 6.06 us  [local(): call(kernel_spatial, (spaces, rows, cols), 4 + len(arrived), 10000000000....]
    ppermute x2, waiting for transfers between devices: 1.76 us -> 0.01 us  [beside(): return lax.ppermute(array, 'tm', [(i, i ^ 1) for i in range(times)])]
    all_to_all x0 -> x1, waiting for transfers between devices: none -> 1.74 us  [local(): lax.all_to_all(after((o_all,), spread, *out_pieces)[0].reshape(spaces * t...]
    dynamic_slice x0 -> x1, local copies, waits for them, and re-layouts: none -> 1.73 us  [local(): lax.dynamic_slice_in_dim(out_spatial, lax.rem(lax.axis_index('tm'), 2) *...]
  transfers between devices with their start and end apart: 9 -> 10, of which waited for: 4 -> 5; matrix products, arithmetic and copies ran while one was open for 0% -> 3% of each run, Pallas kernels for 18% -> 22%
where the time goes in v7:
time: 85.4 us; the launch traced here: 84.6 us
  waiting for transfers between devices  26 us (30%)
  starting transfers between devices  25.2 us (30%)
  Pallas kernels  25 us (29%)
  local copies, waits for them, and re-layouts  8.32 us (10%)
    ppermute x5, waiting for transfers between devices, across(): lax.ppermute(array, 'space', [(i, (i + k) % spaces) for i in range(spaces)])  23.7 us
    ppermute x5, starting transfers between devices, across(): lax.ppermute(array, 'space', [(i, (i + k) % spaces) for i in range(spaces)])  7.9 us
    all_to_all x1, starting transfers between devices, local(): lax.all_to_all(tokens.reshape(times, size, frames, width), 'tm', 0, 0, ti...  6.47 us
    pallas_call x1, Pallas kernels, local(): call(kernel_spatial, (spaces, rows, cols), 4 + len(arrived), 10000000000....  6.06 us
    pallas_call x1, Pallas kernels, local(): pl.pallas_call(functools.partial(kernel_temporal, size=size, frames=frame...  5.9 us
    all_to_all x1, starting transfers between devices, local(): lax.all_to_all(o_t, 'tm', 0, 0, tiled=True).reshape(rows, spaces * cols)  5.64 us
    unnamed x28, local copies, waits for them, and re-layouts  5.63 us
    all_to_all x1, starting transfers between devices, local(): lax.all_to_all(after((o_all,), spread, *out_pieces)[0].reshape(spaces * t...  5.04 us
  transfers between devices with their start and end apart: 10, of which 5 were waited for; matrix products, arithmetic and copies ran while one was open for 3% of the time, Pallas kernels for 22%

profile of v7, /device:TPU:0, one launch (start us, length us, event | category | flops | bytes accessed | tf_op | source)
XLA Modules:
  0.0 84.6 jit_solution(18383975982262748558)
XLA Ops:
  0.0 2.9 %collective-permute-start = (bf16[128,2,1152]{2,1,0:T(2,128)(2,1)}, bf16[128,2,1152]{2,1,0:T(2,128)(2,1)}, u32[]{:S(2)}, u32[]{:S(2)}) collective-permute-start(bf16[128,2,1152]{2,1,0:T(2,128)(2,1)} %x_ref.3), channel_id=1, source_target_pairs={{0,1},{1,0},{2,3},{3,2},{4,5},{5,4},{6,7},{7,6},{8,9},{9,8},{10,11... | collective-permute-start | bytes 1769480 | tf_op jit(solution)/shard_map/ppermute | solution.py:266
  2.9 1.7 %constant_dynamic-slice_fusion = bf16[144,1152]{1,0:T(8,128)(2,1)} fusion(bf16[288,1152]{1,0:T(8,128)(2,1)} %refs_1_.1, s32[]{:T(128)S(6)} %select_n.14), kind=kLoop, calls=%fused_computation.1 | loop fusion | bytes 663556 | tf_op jit(solution)/shard_map/dynamic_slice | solution.py:292
  4.7 0.0 collective-permute-start.2
  4.7 6.5 %all-to-all-start = ((bf16[16,8,2,1152]{3,2,1,0:T(2,128)(2,1)}), bf16[16,8,2,1152]{3,2,1,0:T(2,128)(2,1)S(1)}, u32[]{:S(2)}, u32[]{:S(2)}) async-start(bf16[16,8,2,1152]{3,2,1,0:T(2,128)(2,1)} %bitcast.16), calls=%async_computation | async-start | bytes 1179648 | tf_op jit(solution)/shard_map/all_to_all | solution.py:289
  11.2 1.6 %collective-permute-start.1 = (f32[864]{0:T(1024)}, f32[864]{0:T(1024)S(1)}, u32[]{:S(2)}, u32[]{:S(2)}) collective-permute-start(f32[864]{0:T(1024)} %b_ref.5), channel_id=1, source_target_pairs={{0,1},{1,0},{2,3},{3,2},{4,5},{5,4},{6,7},{7,6},{8,9},{9,8},{10,11... | collective-permute-start | bytes 10376 | tf_op jit(solution)/shard_map/ppermute | solution.py:266
  12.7 4.7 %shard_map.100 = (bf16[4,3,72,256]{3,2,1,0:T(8,128)(2,1)}, bf16[2,216,1152]{2,1,0:T(8,128)(2,1)}) custom-call(bf16[128,2,1152]{2,1,0:T(2,128)(2,1)} %x_ref.3, bf16[4,216,1152]{2,1,0:T(8,128)(2,1)} %bitcast.18, bf16[4,216,1152]{2,1,0:T(8,128)(2,1)} %bitcast.14, f32[6,1152]{1,0:T(8,128)} %mod_ref.9, f32[864]{0:T(1024)} %b_ref.4), custom_call_target="tpu_custom_call" | custom-call | flops 509607936 | bytes 3000000 | tf_op jit(solution)/shard_map/pallas_call | solution.py:275
  17.4 6.3 %collective-permute-done.2.refs_1_.refs_2_ = bf16[144,1152]{1,0:T(8,128)(2,1)} collective-permute-done((bf16[144,1152]{1,0:T(8,128)(2,1)}, bf16[144,1152]{1,0:T(8,128)(2,1)}, u32[]{:S(2)}, u32[]{:S(2)}) %collective-permute-start.2) | collective-permute-done | bytes 331808 | tf_op jit(solution)/shard_map/ppermute | solution.py:266
  23.7 0.0 collective-permute-start.3
  23.7 0.0 collective-permute-done.1.refs_0_
  23.7 0.0 collective-permute-done.refs_0_
  23.7 0.0 copy-start.2
  23.8 1.8 %collective-permute-start.4 = (bf16[2,216,1152]{2,1,0:T(8,128)(2,1)}, bf16[2,216,1152]{2,1,0:T(8,128)(2,1)}, u32[]{:S(2)}, u32[]{:S(2)}) collective-permute-start(bf16[2,216,1152]{2,1,0:T(8,128)(2,1)} %get-tuple-element.19), channel_id=1, source_target_pairs={{0,1},{1,0},{2,3},{3,2},{4,5},{5,4},{6,7},{7,6},{8,9},{9,8},{10,11... | collective-permute-start | bytes 2985992 | tf_op jit(solution)/shard_map/ppermute | solution.py:266
  25.6 1.6 %copy-done.3 = bf16[1152,864]{0,1:T(8,128)(2,1)S(1)} copy-done((bf16[1152,864]{0,1:T(8,128)(2,1)S(1)}, bf16[1152,864]{0,1:T(8,128)(2,1)}, u32[]{:S(2)}) %copy-start.3) | copy-done | bytes 1990680
  27.1 1.0 %copy-done.13 = bf16[4,3,72,256]{3,2,1,0:T(8,128)(2,1)S(1)} copy-done((bf16[4,3,72,256]{3,2,1,0:T(8,128)(2,1)S(1)}, bf16[4,3,72,256]{3,2,1,0:T(8,128)(2,1)}, u32[]{:S(2)}) %copy-start.13) | copy-done | bytes 442392
  28.1 6.1 %shard_map.101.o_own_ref = bf16[2,256,288]{2,1,0:T(8,128)(2,1)} custom-call(bf16[4,3,72,256]{3,2,1,0:T(8,128)(2,1)S(1)} %copy-done.13, bf16[4,216,1152]{2,1,0:T(8,128)(2,1)S(1)} %bitcast.19, f32[6,1152]{1,0:T(8,128)S(1)} %copy-done.8, f32[864]{0:T(1024)S(1)} %copy-done.11, bf16[128,2,1152]{2,1,0:T(2,128)(2,1)} %collective-permute-done.refs_0_), custom_call_target="tpu_custom_call" | custom-call | flops 10000000000 | bytes 4000000 | tf_op jit(solution)/shard_map/pallas_call | solution.py:296
  34.2 0.7 copy-done.5
  35.0 5.0 %all-to-all-start.1 = ((bf16[32,16,288]{2,1,0:T(8,128)(2,1)}), bf16[32,16,288]{2,1,0:T(8,128)(2,1)}, u32[]{:S(2)}, u32[]{:S(2)}) async-start(bf16[32,16,288]{2,1,0:T(8,128)(2,1)} %bitcast.5), calls=%async_computation.1 | async-start | bytes 786432 | tf_op jit(solution)/shard_map/all_to_all | solution.py:314
  40.0 11.7 %collective-permute-done.4.refs_1_ = bf16[2,216,1152]{2,1,0:T(8,128)(2,1)} collective-permute-done((bf16[2,216,1152]{2,1,0:T(8,128)(2,1)}, bf16[2,216,1152]{2,1,0:T(8,128)(2,1)}, u32[]{:S(2)}, u32[]{:S(2)}) %collective-permute-start.4) | collective-permute-done | bytes 995360 | tf_op jit(solution)/shard_map/ppermute | solution.py:266
  51.7 1.7 %all-to-all-done.1 = bf16[32,16,288]{2,1,0:T(8,128)(2,1)} async-done(((bf16[32,16,288]{2,1,0:T(8,128)(2,1)}), bf16[32,16,288]{2,1,0:T(8,128)(2,1)}, u32[]{:S(2)}, u32[]{:S(2)}) %all-to-all-start.1) | async-done | bytes 294944 | tf_op jit(solution)/shard_map/all_to_all | solution.py:314
  53.5 0.1 collective-permute-start.5
  53.6 1.0 %copy-done.6 = bf16[144,1152]{1,0:T(8,128)(2,1)S(1)} copy-done((bf16[144,1152]{1,0:T(8,128)(2,1)S(1)}, bf16[144,1152]{1,0:T(8,128)(2,1)}, u32[]{:S(2)}) %copy-start.6) | copy-done | bytes 331800
  54.6 5.9 %shard_map.102 = (bf16[256,1152]{1,0:T(8,128)(2,1)S(1)}, f32[4,72,256]{2,1,0:T(8,128)S(1)}) custom-call(bf16[2,256,288]{2,1,0:T(8,128)(2,1)} %bitcast.6.o_ref, bf16[128,2,1152]{2,1,0:T(2,128)(2,1)S(1)} %bitcast.17, bf16[4,216,1152]{2,1,0:T(8,128)(2,1)S(1)} %bitcast.15, f32[1152]{0:T(1024)S(1)} %copy-done.9, f32[6,1152]{1,0:T(8,128)S(1)} %copy-done.8, ...), custom_call_target="tpu_custom_call" | custom-call | flops 849346560 | bytes 5000000 | tf_op jit(solution)/shard_map/pallas_call | solution.py:335
  60.5 0.0 copy-start.1
  60.5 4.5 %shard_map.103 = bf16[256,576]{1,0:T(8,128)(2,1)} custom-call(bf16[256,1152]{1,0:T(8,128)(2,1)S(1)} %get-tuple-element.16.h_ref, f32[4,72,256]{2,1,0:T(8,128)S(1)} %get-tuple-element.17.own_ref, f32[864]{0:T(1024)S(1)} %collective-permute-done.1.refs_0_, bf16[2,216,1152]{2,1,0:T(8,128)(2,1)} %collective-permute-done.4.refs_1_, ...), custom_call_target="tpu_custom_call" | custom-call | flops 509607936 | bytes 5000000 | tf_op jit(solution)/shard_map/pallas_call | solution.py:345
  65.0 5.6 %all-to-all-start.2 = ((bf16[16,16,576]{2,1,0:T(8,128)(2,1)}), bf16[16,16,576]{2,1,0:T(8,128)(2,1)S(1)}, u32[]{:S(2)}, u32[]{:S(2)}) async-start(bf16[16,16,576]{2,1,0:T(8,128)(2,1)} %bitcast.8), calls=%async_computation.2 | async-start | bytes 655360 | tf_op jit(solution)/shard_map/all_to_all | solution.py:357
  70.7 1.0 %dynamic-slice_bitcast_fusion = bf16[256,288]{1,0:T(8,128)(2,1)S(1)} fusion(bf16[2,256,288]{2,1,0:T(8,128)(2,1)} %shard_map.101.o_own_ref, s32[]{:T(128)S(6)} %select_n.16), kind=kLoop, calls=%fused_computation | loop fusion | bytes 294916 | tf_op jit(solution)/shard_map/jit(dynamic_index_in_dim)/squeeze | solution.py:322
  71.6 1.6 %collective-permute-start.6 = (bf16[256,288]{1,0:T(8,128)(2,1)S(1)}, bf16[256,288]{1,0:T(8,128)(2,1)S(1)}, u32[]{:S(2)}, u32[]{:S(2)}) collective-permute-start(bf16[256,288]{1,0:T(8,128)(2,1)S(1)} %dynamic-slice_bitcast_fusion), channel_id=1, source_target_pairs={{0,1},{1,0},{2,3},{3,2},{4,5},{5,4},{6,7},{7,6},{8,9},{9,8},{10,11... | collective-permute-start | bytes 442376 | tf_op jit(solution)/shard_map/ppermute | solution.py:266
  73.2 5.7 %collective-permute-done.6.refs_0_ = bf16[256,288]{1,0:T(8,128)(2,1)S(1)} collective-permute-done((bf16[256,288]{1,0:T(8,128)(2,1)S(1)}, bf16[256,288]{1,0:T(8,128)(2,1)S(1)}, u32[]{:S(2)}, u32[]{:S(2)}) %collective-permute-start.6) | collective-permute-done | bytes 147488 | tf_op jit(solution)/shard_map/ppermute | solution.py:266
  78.9 2.3 %shard_map.104.y_ref = bf16[256,1152]{1,0:T(8,128)(2,1)S(1)} custom-call(bf16[2,256,288]{2,1,0:T(8,128)(2,1)} %shard_map.101.o_own_ref, bf16[128,2,1152]{2,1,0:T(2,128)(2,1)S(1)} %copy-done.1, f32[1152]{0:T(1024)S(1)} %copy-done.9, f32[6,1152]{1,0:T(8,128)S(1)} %copy-done.8, bf16[256,288]{1,0:T(8,128)(2,1)S(1)} %collective-permute-done.6.refs_0_, ...), custom_call_target="tpu_custom_call" | custom-call | flops 339738624 | bytes 3000000 | tf_op jit(solution)/shard_map/pallas_call | solution.py:326
  81.2 0.6 all-to-all-done.2
  81.8 1.3 %copy-done.4 = bf16[576,1152]{1,0:T(8,128)(2,1)S(1)} copy-done((bf16[576,1152]{1,0:T(8,128)(2,1)S(1)}, bf16[576,1152]{1,0:T(8,128)(2,1)}, u32[]{:S(2)}) %copy-start.4) | copy-done | bytes 1327128
  83.1 1.5 %shard_map.105 = bf16[128,2,1152]{2,1,0:T(2,128)(2,1)} custom-call(bf16[256,576]{1,0:T(8,128)(2,1)S(1)} %bitcast.20, bf16[256,1152]{1,0:T(8,128)(2,1)S(1)} %shard_map.104.y_ref, bf16[576,1152]{1,0:T(8,128)(2,1)S(1)} %copy-done.4, f32[1152]{0:T(1024)S(1)} %copy-done.10, f32[6,1152]{1,0:T(8,128)S(1)} %copy-done.8), custom_call_target="tpu_custom_call" | custom-call | flops 339738624 | bytes 3000000 | tf_op jit(solution)/shard_map/pallas_call | solution.py:359
  (24 shorter events, 0.0 us)
Async XLA Ops:
  0.0 23.7 %collective-permute-start = (bf16[128,2,1152]{2,1,0:T(2,128)(2,1)}, bf16[128,2,1152]{2,1,0:T(2,128)(2,1)}, u32[]{:S(2)}, u32[]{:S(2)}) collective-permute-start(bf16[128,2,1152]{2,1,0:T(2,128)(2,1)} %x_ref.3), channel_id=1, source_target_pairs={{0,1},{1,0},{2,3},{3,2},{4,5},{5,4},{6,7},{7,6},{8,9},{9,8},{10,11... | collective-permute-start | bytes 1769480 | tf_op jit(solution)/shard_map/ppermute | solution.py:266
  4.7 19.1 %collective-permute-start.2 = (bf16[144,1152]{1,0:T(8,128)(2,1)}, bf16[144,1152]{1,0:T(8,128)(2,1)}, u32[]{:S(2)}, u32[]{:S(2)}) collective-permute-start(bf16[144,1152]{1,0:T(8,128)(2,1)} %constant_dynamic-slice_fusion), channel_id=1, source_target_pairs={{0,1},{1,0},{2,3},{3,2},{4,5},{5,4},{6,7},{7,6},{8,9},{9,8},{10,11... | collective-permute-start | bytes 995336 | tf_op jit(solution)/shard_map/ppermute | solution.py:266
  4.7 30.3 %all-to-all-start = ((bf16[16,8,2,1152]{3,2,1,0:T(2,128)(2,1)}), bf16[16,8,2,1152]{3,2,1,0:T(2,128)(2,1)S(1)}, u32[]{:S(2)}, u32[]{:S(2)}) async-start(bf16[16,8,2,1152]{3,2,1,0:T(2,128)(2,1)} %bitcast.16), calls=%async_computation | async-start | bytes 1179648 | tf_op jit(solution)/shard_map/all_to_all | solution.py:289
  11.2 12.6 %collective-permute-start.1 = (f32[864]{0:T(1024)}, f32[864]{0:T(1024)S(1)}, u32[]{:S(2)}, u32[]{:S(2)}) collective-permute-start(f32[864]{0:T(1024)} %b_ref.5), channel_id=1, source_target_pairs={{0,1},{1,0},{2,3},{3,2},{4,5},{5,4},{6,7},{7,6},{8,9},{9,8},{10,11... | collective-permute-start | bytes 10376 | tf_op jit(solution)/shard_map/ppermute | solution.py:266
  12.7 12.9 %copy-start.8 = (f32[6,1152]{1,0:T(8,128)S(1)}, f32[6,1152]{1,0:T(8,128)}, u32[]{:S(2)}) copy-start(f32[6,1152]{1,0:T(8,128)} %mod_ref.9) | copy-start | bytes 82948
  12.7 12.9 %copy-start.11 = (f32[864]{0:T(1024)S(1)}, f32[864]{0:T(1024)}, u32[]{:S(2)}) copy-start(f32[864]{0:T(1024)} %b_ref.4) | copy-start | bytes 10372
  23.7 10.5 %collective-permute-start.3 = (bf16[144,1152]{1,0:T(8,128)(2,1)}, bf16[144,1152]{1,0:T(8,128)(2,1)S(1)}, u32[]{:S(2)}, u32[]{:S(2)}) collective-permute-start(bf16[144,1152]{1,0:T(8,128)(2,1)} %collective-permute-done.2.refs_1_.refs_2_), channel_id=1, source_target_pairs={{0,2},{2,0},{4,6},{6,4},{8,10},{10,8},{12,14},{14,12},{16,18},{18,... | collective-permute-start | bytes 995336 | tf_op jit(solution)/shard_map/ppermute | solution.py:269
  23.7 29.8 %copy-start.2 = (bf16[288,1152]{1,0:T(8,128)(2,1)S(1)}, bf16[288,1152]{1,0:T(8,128)(2,1)}, u32[]{:S(2)}) copy-start(bf16[288,1152]{1,0:T(8,128)(2,1)} %refs_1_.1) | copy-start | bytes 1990660
  23.8 28.0 %collective-permute-start.4 = (bf16[2,216,1152]{2,1,0:T(8,128)(2,1)}, bf16[2,216,1152]{2,1,0:T(8,128)(2,1)}, u32[]{:S(2)}, u32[]{:S(2)}) collective-permute-start(bf16[2,216,1152]{2,1,0:T(8,128)(2,1)} %get-tuple-element.19), channel_id=1, source_target_pairs={{0,1},{1,0},{2,3},{3,2},{4,5},{5,4},{6,7},{7,6},{8,9},{9,8},{10,11... | collective-permute-start | bytes 2985992 | tf_op jit(solution)/shard_map/ppermute | solution.py:266
  25.6 1.6 %copy-start.3 = (bf16[1152,864]{0,1:T(8,128)(2,1)S(1)}, bf16[1152,864]{0,1:T(8,128)(2,1)}, u32[]{:S(2)}) copy-start(bf16[1152,864]{0,1:T(8,128)(2,1)} %param.12) | copy-start | bytes 5971972
  27.1 1.0 %copy-start.13 = (bf16[4,3,72,256]{3,2,1,0:T(8,128)(2,1)S(1)}, bf16[4,3,72,256]{3,2,1,0:T(8,128)(2,1)}, u32[]{:S(2)}) copy-start(bf16[4,3,72,256]{3,2,1,0:T(8,128)(2,1)} %get-tuple-element.13.own_ref) | copy-start | bytes 1327108
  28.1 25.4 %copy-start = (bf16[1152,864]{0,1:T(8,128)(2,1)S(1)}, bf16[1152,864]{0,1:T(8,128)(2,1)}, u32[]{:S(2)}) copy-start(bf16[1152,864]{0,1:T(8,128)(2,1)} %param.16) | copy-start | bytes 5971972
  28.1 25.4 %copy-start.9 = (f32[1152]{0:T(1024)S(1)}, f32[1152]{0:T(1024)}, u32[]{:S(2)}) copy-start(f32[1152]{0:T(1024)} %outbias_ref.4) | copy-start | bytes 13828
  28.1 25.4 %copy-start.12 = (f32[864]{0:T(1024)S(1)}, f32[864]{0:T(1024)}, u32[]{:S(2)}) copy-start(f32[864]{0:T(1024)} %b_ref.5) | copy-start | bytes 10372
  34.2 0.7 copy-start.5
  35.0 18.5 %all-to-all-start.1 = ((bf16[32,16,288]{2,1,0:T(8,128)(2,1)}), bf16[32,16,288]{2,1,0:T(8,128)(2,1)}, u32[]{:S(2)}, u32[]{:S(2)}) async-start(bf16[32,16,288]{2,1,0:T(8,128)(2,1)} %bitcast.5), calls=%async_computation.1 | async-start | bytes 786432 | tf_op jit(solution)/shard_map/all_to_all | solution.py:314
  53.5 7.0 %collective-permute-start.5 = (bf16[2,216,1152]{2,1,0:T(8,128)(2,1)}, bf16[2,216,1152]{2,1,0:T(8,128)(2,1)S(1)}, u32[]{:S(2)}, u32[]{:S(2)}) collective-permute-start(bf16[2,216,1152]{2,1,0:T(8,128)(2,1)} %collective-permute-done.4.refs_1_), channel_id=1, source_target_pairs={{0,2},{2,0},{4,6},{6,4},{8,10},{10,8},{12,14},{14,12},{16,18},{18,... | collective-permute-start | bytes 2985992 | tf_op jit(solution)/shard_map/ppermute | solution.py:269
  53.6 1.0 %copy-start.6 = (bf16[144,1152]{1,0:T(8,128)(2,1)S(1)}, bf16[144,1152]{1,0:T(8,128)(2,1)}, u32[]{:S(2)}) copy-start(bf16[144,1152]{1,0:T(8,128)(2,1)} %copy-done.5) | copy-start | bytes 995332
  60.5 18.4 %copy-start.1 = (bf16[128,2,1152]{2,1,0:T(2,128)(2,1)S(1)}, bf16[128,2,1152]{2,1,0:T(2,128)(2,1)}, u32[]{:S(2)}) copy-start(bf16[128,2,1152]{2,1,0:T(2,128)(2,1)} %x_ref.3) | copy-start | bytes 1769476
  60.5 18.4 %copy-start.7 = (bf16[144,1152]{1,0:T(8,128)(2,1)S(1)}, bf16[144,1152]{1,0:T(8,128)(2,1)}, u32[]{:S(2)}) copy-start(bf16[144,1152]{1,0:T(8,128)(2,1)} %copy-done.5) | copy-start | bytes 995332
  65.0 16.8 %copy-start.10 = (f32[1152]{0:T(1024)S(1)}, f32[1152]{0:T(1024)}, u32[]{:S(2)}) copy-start(f32[1152]{0:T(1024)} %outbias_ref.5) | copy-start | bytes 13828
  65.0 16.7 %all-to-all-start.2 = ((bf16[16,16,576]{2,1,0:T(8,128)(2,1)}), bf16[16,16,576]{2,1,0:T(8,128)(2,1)S(1)}, u32[]{:S(2)}, u32[]{:S(2)}) async-start(bf16[16,16,576]{2,1,0:T(8,128)(2,1)} %bitcast.8), calls=%async_computation.2 | async-start | bytes 655360 | tf_op jit(solution)/shard_map/all_to_all | solution.py:357
  71.6 7.3 %collective-permute-start.6 = (bf16[256,288]{1,0:T(8,128)(2,1)S(1)}, bf16[256,288]{1,0:T(8,128)(2,1)S(1)}, u32[]{:S(2)}, u32[]{:S(2)}) collective-permute-start(bf16[256,288]{1,0:T(8,128)(2,1)S(1)} %dynamic-slice_bitcast_fusion), channel_id=1, source_target_pairs={{0,1},{1,0},{2,3},{3,2},{4,5},{5,4},{6,7},{7,6},{8,9},{9,8},{10,11... | collective-permute-start | bytes 442376 | tf_op jit(solution)/shard_map/ppermute | solution.py:266
  81.8 1.3 %copy-start.4 = (bf16[576,1152]{1,0:T(8,128)(2,1)S(1)}, bf16[576,1152]{1,0:T(8,128)(2,1)}, u32[]{:S(2)}) copy-start(bf16[576,1152]{1,0:T(8,128)(2,1)} %w_ref.1) | copy-start | bytes 3981316

commit v8 on v7

--- a/solution.py
+++ b/solution.py
@@ -96,18 +96,17 @@
     return lax.axis_index("space"), lax.rem(lax.axis_index("tm"), 2)
 
 
-def kernel_qkv(x_ref, w_hbm, w_other_hbm, mod_ref, b_ref, out_ref, heads_ref, w_ref, sems):
+def kernel_qkv(x_ref, w_ref, w_other_hbm, mod_ref, b_ref, out_ref, heads_ref, sems):
     _, core = coordinates()
     half = heads_ref.shape[0]
-    copies = fetch((w_hbm, w_other_hbm.at[pl.ds(core * half, half)]), (w_ref, heads_ref), sems)
+    copies = fetch((w_other_hbm.at[pl.ds(core * half, half)],), (heads_ref,), sems)
     h = spatial_rows(flat(x_ref), mod_ref, x_ref.shape[1])
     bias = bias_column(b_ref)
-    copies[0].wait()
     for i in range(w_ref.shape[0]):
         qkv = mm(w_ref[i], h, NT) + bias[i * 3 * HD : (i + 1) * 3 * HD]
         for c in range(3):
             out_ref[i, c] = qkv[c * HD : (c + 1) * HD].astype(BF)
-    copies[1].wait()
+    copies[0].wait()
 
 
 def kernel_spatial(own_ref, w_ref, mod_ref, b_ref, *refs):
@@ -277,10 +276,10 @@
         out_shape=tuple(
             jax.ShapeDtypeStruct(a, BF) for a in ((heads, 3, HD, rows), (half, 3 * HD, width))
         ),
-        in_specs=[VMEM] + [ANY] * 2 + [VMEM] * 2,
+        in_specs=[VMEM] * 2 + [ANY] + [VMEM] * 2,
         out_specs=(VMEM, VMEM),
-        scratch_shapes=[pltpu.VMEM(w_spatial.shape, BF), pltpu.SemaphoreType.DMA((2,))],
-        compiler_params=PARAMS,
+        scratch_shapes=[pltpu.SemaphoreType.DMA((1,))],
+        compiler_params=SMALL,
         cost_estimate=pl.CostEstimate(
             flops=2 * rows * width * cols * 3, bytes_accessed=3 * 10**6, transcendentals=0
         ),

time: 85.4 us -> 86.4 us (1.012)
  Pallas kernels: 25 us -> 21.6 us
  local copies, waits for them, and re-layouts: 8.32 us -> 11.3 us
  waiting for transfers between devices: 26 us -> 27.6 us
    unnamed x28 -> x38, local copies, waits for them, and re-layouts: 5.63 us -> 10.2 us
    pallas_call x1, Pallas kernels: 6.06 us -> 4.11 us  [local(): call(kernel_spatial, (spaces, rows, cols), 4 + len(arrived), 10000000000....]
    pallas_call x1, Pallas kernels: 4.7 us -> 3.17 us  [local(): pl.pallas_call(kernel_qkv, out_shape=tuple((jax.ShapeDtypeStruct(a, BF) f...]
    all_to_all x1, waiting for transfers between devices: 0.59 us -> 1.61 us  [local(): lax.all_to_all(o_t, 'tm', 0, 0, tiled=True).reshape(rows, spaces * cols)]
    squeeze x1, local copies, waits for them, and re-layouts: 0.95 us -> 0.03 us  [local(): lax.dynamic_index_in_dim(o_all, (space + k) % spaces, 0, keepdims=False)]
  transfers between devices with their start and end apart: 10 -> 10, of which waited for: 5 -> 5; matrix products, arithmetic and copies ran while one was open for 3% -> 1% of each run, Pallas kernels for 22% -> 18%
where the time goes in v8:
time: 86.4 us; the launch traced here: 85.6 us
  waiting for transfers between devices  27.6 us (32%)
  starting transfers between devices  25.1 us (29%)
  Pallas kernels  21.6 us (25%)
  local copies, waits for them, and re-layouts  11.3 us (13%)
    ppermute x5, waiting for transfers between devices, across(): lax.ppermute(array, 'space', [(i, (i + k) % spaces) for i in range(spaces)])  24.5 us
    unnamed x38, local copies, waits for them, and re-layouts  10.2 us
    ppermute x5, starting transfers between devices, across(): lax.ppermute(array, 'space', [(i, (i + k) % spaces) for i in range(spaces)])  7.95 us
    all_to_all x1, starting transfers between devices, local(): lax.all_to_all(tokens.reshape(times, size, frames, width), 'tm', 0, 0, ti...  6.45 us
    pallas_call x1, Pallas kernels, local(): pl.pallas_call(functools.partial(kernel_temporal, size=size, frames=frame...  6.09 us
    all_to_all x1, starting transfers between devices, local(): lax.all_to_all(o_t, 'tm', 0, 0, tiled=True).reshape(rows, spaces * cols)  5.51 us
    all_to_all x1, starting transfers between devices, local(): lax.all_to_all(after((o_all,), spread, *out_pieces)[0].reshape(spaces * t...  5.04 us
    pallas_call x1, Pallas kernels, local(): call(functools.partial(kernel_rest, size=size, frames=frames, spaces=spac...  4.51 us
  transfers between devices with their start and end apart: 10, of which 5 were waited for; matrix products, arithmetic and copies ran while one was open for 1% of the time, Pallas kernels for 18%

profile of v8, /device:TPU:0, one launch (start us, length us, event | category | flops | bytes accessed | tf_op | source)
XLA Modules:
  0.0 85.6 jit_solution(579764534806595492)
XLA Ops:
  0.0 2.9 %collective-permute-start = (bf16[128,2,1152]{2,1,0:T(2,128)(2,1)}, bf16[128,2,1152]{2,1,0:T(2,128)(2,1)S(1)}, u32[]{:S(2)}, u32[]{:S(2)}) collective-permute-start(bf16[128,2,1152]{2,1,0:T(2,128)(2,1)} %x_ref.3), channel_id=1, source_target_pairs={{0,1},{1,0},{2,3},{3,2},{4,5},{5,4},{6,7},{7,6},{8,9},{9,8},{10,11... | collective-permute-start | bytes 1769480 | tf_op jit(solution)/shard_map/ppermute | solution.py:265
  2.9 1.0 %constant_dynamic-slice_fusion = bf16[144,1152]{1,0:T(8,128)(2,1)S(1)} fusion(bf16[288,1152]{1,0:T(8,128)(2,1)} %refs_1_.1, s32[]{:T(128)S(6)} %select_n.14), kind=kLoop, calls=%fused_computation.1 | loop fusion | bytes 663556 | tf_op jit(solution)/shard_map/dynamic_slice | solution.py:291
  3.9 0.1 collective-permute-start.2
  4.1 6.5 %all-to-all-start = ((bf16[16,8,2,1152]{3,2,1,0:T(2,128)(2,1)}), bf16[16,8,2,1152]{3,2,1,0:T(2,128)(2,1)}, u32[]{:S(2)}, u32[]{:S(2)}) async-start(bf16[16,8,2,1152]{3,2,1,0:T(2,128)(2,1)} %bitcast.16), calls=%async_computation | async-start | bytes 1179648 | tf_op jit(solution)/shard_map/all_to_all | solution.py:288
  10.5 1.6 %collective-permute-start.1 = (f32[864]{0:T(1024)}, f32[864]{0:T(1024)S(1)}, u32[]{:S(2)}, u32[]{:S(2)}) collective-permute-start(f32[864]{0:T(1024)} %b_ref.5), channel_id=1, source_target_pairs={{0,1},{1,0},{2,3},{3,2},{4,5},{5,4},{6,7},{7,6},{8,9},{9,8},{10,11... | collective-permute-start | bytes 10376 | tf_op jit(solution)/shard_map/ppermute | solution.py:265
  12.1 1.6 %copy-done = bf16[1152,864]{0,1:T(8,128)(2,1)S(1)} copy-done((bf16[1152,864]{0,1:T(8,128)(2,1)S(1)}, bf16[1152,864]{0,1:T(8,128)(2,1)}, u32[]{:S(2)}) %copy-start) | copy-done | bytes 1990680
  13.7 1.6 %copy-done.6 = bf16[1152,864]{0,1:T(8,128)(2,1)S(1)} copy-done((bf16[1152,864]{0,1:T(8,128)(2,1)S(1)}, bf16[1152,864]{0,1:T(8,128)(2,1)}, u32[]{:S(2)}) %copy-start.6) | copy-done | bytes 1990680
  15.2 0.8 copy-done.11
  16.0 0.7 copy-done.15
  16.7 3.2 %shard_map.100 = (bf16[4,3,72,256]{3,2,1,0:T(8,128)(2,1)S(1)}, bf16[2,216,1152]{2,1,0:T(8,128)(2,1)}) custom-call(bf16[128,2,1152]{2,1,0:T(2,128)(2,1)S(1)} %copy-done.2, bf16[4,216,1152]{2,1,0:T(8,128)(2,1)S(1)} %bitcast.18, bf16[4,216,1152]{2,1,0:T(8,128)(2,1)S(1)} %bitcast.14, f32[6,1152]{1,0:T(8,128)S(1)} %copy-done.11, f32[864]{0:T(1024)S(1)} %copy-done.15), custom_call_target="tpu_custom_call" | custom-call | flops 509607936 | bytes 3000000 | tf_op jit(solution)/shard_map/pallas_call | solution.py:274
  19.8 4.0 %collective-permute-done.2.refs_1_.refs_2_ = bf16[144,1152]{1,0:T(8,128)(2,1)} collective-permute-done((bf16[144,1152]{1,0:T(8,128)(2,1)S(1)}, bf16[144,1152]{1,0:T(8,128)(2,1)}, u32[]{:S(2)}, u32[]{:S(2)}) %collective-permute-start.2) | collective-permute-done | bytes 331808 | tf_op jit(solution)/shard_map/ppermute | solution.py:265
  23.8 0.0 copy-start.17
  23.8 0.8 copy-done.17
  24.6 1.7 %collective-permute-start.4 = (bf16[2,216,1152]{2,1,0:T(8,128)(2,1)}, bf16[2,216,1152]{2,1,0:T(8,128)(2,1)}, u32[]{:S(2)}, u32[]{:S(2)}) collective-permute-start(bf16[2,216,1152]{2,1,0:T(8,128)(2,1)} %get-tuple-element.19), channel_id=1, source_target_pairs={{0,1},{1,0},{2,3},{3,2},{4,5},{5,4},{6,7},{7,6},{8,9},{9,8},{10,11... | collective-permute-start | bytes 2985992 | tf_op jit(solution)/shard_map/ppermute | solution.py:265
  26.4 1.1 %copy-done.18 = bf16[128,2,1152]{2,1,0:T(2,128)(2,1)S(1)} copy-done((bf16[128,2,1152]{2,1,0:T(2,128)(2,1)S(1)}, bf16[128,2,1152]{2,1,0:T(2,128)(2,1)}, u32[]{:S(2)}) %copy-start.18) | copy-done | bytes 589848
  27.5 4.1 %shard_map.101.o_own_ref = bf16[2,256,288]{2,1,0:T(8,128)(2,1)S(1)} custom-call(bf16[4,3,72,256]{3,2,1,0:T(8,128)(2,1)S(1)} %get-tuple-element.13.own_ref, bf16[4,216,1152]{2,1,0:T(8,128)(2,1)S(1)} %bitcast.19, f32[6,1152]{1,0:T(8,128)S(1)} %copy-done.11, f32[864]{0:T(1024)S(1)} %copy-done.15, bf16[128,2,1152]{2,1,0:T(2,128)(2,1)S(1)} %copy-done.18), custom_call_target="tpu_custom_call" | custom-call | flops 10000000000 | bytes 4000000 | tf_op jit(solution)/shard_map/pallas_call | solution.py:295
  31.6 0.7 copy-done.4
  32.3 0.7 copy-done.8
  33.1 5.0 %all-to-all-start.1 = ((bf16[32,16,288]{2,1,0:T(8,128)(2,1)}), bf16[32,16,288]{2,1,0:T(8,128)(2,1)}, u32[]{:S(2)}, u32[]{:S(2)}) async-start(bf16[32,16,288]{2,1,0:T(8,128)(2,1)} %bitcast.17), calls=%async_computation.1 | async-start | bytes 786432 | tf_op jit(solution)/shard_map/all_to_all | solution.py:313
  38.1 14.9 %collective-permute-done.4.refs_1_ = bf16[2,216,1152]{2,1,0:T(8,128)(2,1)} collective-permute-done((bf16[2,216,1152]{2,1,0:T(8,128)(2,1)}, bf16[2,216,1152]{2,1,0:T(8,128)(2,1)}, u32[]{:S(2)}, u32[]{:S(2)}) %collective-permute-start.4) | collective-permute-done | bytes 995360 | tf_op jit(solution)/shard_map/ppermute | solution.py:265
  53.0 1.4 %all-to-all-done.1 = bf16[32,16,288]{2,1,0:T(8,128)(2,1)} async-done(((bf16[32,16,288]{2,1,0:T(8,128)(2,1)}), bf16[32,16,288]{2,1,0:T(8,128)(2,1)}, u32[]{:S(2)}, u32[]{:S(2)}) %all-to-all-start.1) | async-done | bytes 294944 | tf_op jit(solution)/shard_map/all_to_all | solution.py:313
  54.4 0.1 collective-permute-start.5
  54.6 1.0 %copy-done.9 = bf16[144,1152]{1,0:T(8,128)(2,1)S(1)} copy-done((bf16[144,1152]{1,0:T(8,128)(2,1)S(1)}, bf16[144,1152]{1,0:T(8,128)(2,1)}, u32[]{:S(2)}) %copy-start.9) | copy-done | bytes 331800
  55.5 6.1 %shard_map.102 = (bf16[256,1152]{1,0:T(8,128)(2,1)S(1)}, f32[4,72,256]{2,1,0:T(8,128)S(1)}) custom-call(bf16[2,256,288]{2,1,0:T(8,128)(2,1)} %bitcast.6.o_ref, bf16[128,2,1152]{2,1,0:T(2,128)(2,1)} %bitcast.7.x_ref, bf16[4,216,1152]{2,1,0:T(8,128)(2,1)S(1)} %bitcast.15, f32[1152]{0:T(1024)S(1)} %copy-done.13, f32[6,1152]{1,0:T(8,128)S(1)} %copy-done.12, ...), custom_call_target="tpu_custom_call" | custom-call | flops 849346560 | bytes 5000000 | tf_op jit(solution)/shard_map/pallas_call | solution.py:334
  61.7 4.5 %shard_map.103 = bf16[256,576]{1,0:T(8,128)(2,1)} custom-call(bf16[256,1152]{1,0:T(8,128)(2,1)S(1)} %get-tuple-element.16.h_ref, f32[4,72,256]{2,1,0:T(8,128)S(1)} %get-tuple-element.17.own_ref, f32[864]{0:T(1024)S(1)} %collective-permute-done.1.refs_0_, bf16[2,216,1152]{2,1,0:T(8,128)(2,1)} %collective-permute-done.4.refs_1_, ...), custom_call_target="tpu_custom_call" | custom-call | flops 509607936 | bytes 5000000 | tf_op jit(solution)/shard_map/pallas_call | solution.py:344
  66.2 5.5 %all-to-all-start.2 = ((bf16[16,16,576]{2,1,0:T(8,128)(2,1)}), bf16[16,16,576]{2,1,0:T(8,128)(2,1)S(1)}, u32[]{:S(2)}, u32[]{:S(2)}) async-start(bf16[16,16,576]{2,1,0:T(8,128)(2,1)} %bitcast.8), calls=%async_computation.2 | async-start | bytes 655360 | tf_op jit(solution)/shard_map/all_to_all | solution.py:356
  71.7 1.6 %collective-permute-start.6 = (bf16[256,288]{1,0:T(8,128)(2,1)S(1)}, bf16[256,288]{1,0:T(8,128)(2,1)S(1)}, u32[]{:S(2)}, u32[]{:S(2)}) collective-permute-start(bf16[256,288]{1,0:T(8,128)(2,1)S(1)} %dynamic-slice_bitcast_fusion), channel_id=1, source_target_pairs={{0,1},{1,0},{2,3},{3,2},{4,5},{5,4},{6,7},{7,6},{8,9},{9,8},{10,11... | collective-permute-start | bytes 442376 | tf_op jit(solution)/shard_map/ppermute | solution.py:265
  73.3 5.7 %collective-permute-done.6.refs_0_ = bf16[256,288]{1,0:T(8,128)(2,1)S(1)} collective-permute-done((bf16[256,288]{1,0:T(8,128)(2,1)S(1)}, bf16[256,288]{1,0:T(8,128)(2,1)S(1)}, u32[]{:S(2)}, u32[]{:S(2)}) %collective-permute-start.6) | collective-permute-done | bytes 147488 | tf_op jit(solution)/shard_map/ppermute | solution.py:265
  79.0 2.2 %shard_map.104.y_ref = bf16[256,1152]{1,0:T(8,128)(2,1)S(1)} custom-call(bf16[2,256,288]{2,1,0:T(8,128)(2,1)S(1)} %copy-done.5, bf16[128,2,1152]{2,1,0:T(2,128)(2,1)S(1)} %copy-done.2, f32[1152]{0:T(1024)S(1)} %copy-done.13, f32[6,1152]{1,0:T(8,128)S(1)} %copy-done.12, bf16[256,288]{1,0:T(8,128)(2,1)S(1)} %collective-permute-done.6.refs_0_, ...), custom_call_target="tpu_custom_call" | custom-call | flops 339738624 | bytes 3000000 | tf_op jit(solution)/shard_map/pallas_call | solution.py:325
  81.2 1.6 %all-to-all-done.2 = bf16[16,16,576]{2,1,0:T(8,128)(2,1)S(1)} async-done(((bf16[16,16,576]{2,1,0:T(8,128)(2,1)}), bf16[16,16,576]{2,1,0:T(8,128)(2,1)S(1)}, u32[]{:S(2)}, u32[]{:S(2)}) %all-to-all-start.2) | async-done | bytes 294944 | tf_op jit(solution)/shard_map/all_to_all | solution.py:356
  82.8 1.3 %copy-done.7 = bf16[576,1152]{1,0:T(8,128)(2,1)S(1)} copy-done((bf16[576,1152]{1,0:T(8,128)(2,1)S(1)}, bf16[576,1152]{1,0:T(8,128)(2,1)}, u32[]{:S(2)}) %copy-start.7) | copy-done | bytes 1327128
  84.1 1.5 %shard_map.105 = bf16[128,2,1152]{2,1,0:T(2,128)(2,1)} custom-call(bf16[256,576]{1,0:T(8,128)(2,1)S(1)} %bitcast.20, bf16[256,1152]{1,0:T(8,128)(2,1)S(1)} %shard_map.104.y_ref, bf16[576,1152]{1,0:T(8,128)(2,1)S(1)} %copy-done.7, f32[1152]{0:T(1024)S(1)} %copy-done.14, f32[6,1152]{1,0:T(8,128)S(1)} %copy-done.12), custom_call_target="tpu_custom_call" | custom-call | flops 339738624 | bytes 3000000 | tf_op jit(solution)/shard_map/pallas_call | solution.py:358
  (34 shorter events, 0.1 us)
Async XLA Ops:
  0.0 12.1 %copy-start.2 = (bf16[128,2,1152]{2,1,0:T(2,128)(2,1)S(1)}, bf16[128,2,1152]{2,1,0:T(2,128)(2,1)}, u32[]{:S(2)}) copy-start(bf16[128,2,1152]{2,1,0:T(2,128)(2,1)} %x_ref.3) | copy-start | bytes 1769476
  0.0 23.8 %collective-permute-start = (bf16[128,2,1152]{2,1,0:T(2,128)(2,1)}, bf16[128,2,1152]{2,1,0:T(2,128)(2,1)S(1)}, u32[]{:S(2)}, u32[]{:S(2)}) collective-permute-start(bf16[128,2,1152]{2,1,0:T(2,128)(2,1)} %x_ref.3), channel_id=1, source_target_pairs={{0,1},{1,0},{2,3},{3,2},{4,5},{5,4},{6,7},{7,6},{8,9},{9,8},{10,11... | collective-permute-start | bytes 1769480 | tf_op jit(solution)/shard_map/ppermute | solution.py:265
  3.9 19.9 %collective-permute-start.2 = (bf16[144,1152]{1,0:T(8,128)(2,1)S(1)}, bf16[144,1152]{1,0:T(8,128)(2,1)}, u32[]{:S(2)}, u32[]{:S(2)}) collective-permute-start(bf16[144,1152]{1,0:T(8,128)(2,1)S(1)} %constant_dynamic-slice_fusion), channel_id=1, source_target_pairs={{0,1},{1,0},{2,3},{3,2},{4,5},{5,4},{6,7},{7,6},{8,9},{9,8},{10,11... | collective-permute-start | bytes 995336 | tf_op jit(solution)/shard_map/ppermute | solution.py:265
  4.1 29.0 %all-to-all-start = ((bf16[16,8,2,1152]{3,2,1,0:T(2,128)(2,1)}), bf16[16,8,2,1152]{3,2,1,0:T(2,128)(2,1)}, u32[]{:S(2)}, u32[]{:S(2)}) async-start(bf16[16,8,2,1152]{3,2,1,0:T(2,128)(2,1)} %bitcast.16), calls=%async_computation | async-start | bytes 1179648 | tf_op jit(solution)/shard_map/all_to_all | solution.py:288
  10.5 13.3 %collective-permute-start.1 = (f32[864]{0:T(1024)}, f32[864]{0:T(1024)S(1)}, u32[]{:S(2)}, u32[]{:S(2)}) collective-permute-start(f32[864]{0:T(1024)} %b_ref.5), channel_id=1, source_target_pairs={{0,1},{1,0},{2,3},{3,2},{4,5},{5,4},{6,7},{7,6},{8,9},{9,8},{10,11... | collective-permute-start | bytes 10376 | tf_op jit(solution)/shard_map/ppermute | solution.py:265
  12.1 1.6 %copy-start = (bf16[1152,864]{0,1:T(8,128)(2,1)S(1)}, bf16[1152,864]{0,1:T(8,128)(2,1)}, u32[]{:S(2)}) copy-start(bf16[1152,864]{0,1:T(8,128)(2,1)} %param.16) | copy-start | bytes 5971972
  13.6 1.6 %copy-start.6 = (bf16[1152,864]{0,1:T(8,128)(2,1)S(1)}, bf16[1152,864]{0,1:T(8,128)(2,1)}, u32[]{:S(2)}) copy-start(bf16[1152,864]{0,1:T(8,128)(2,1)} %param.12) | copy-start | bytes 5971972
  15.2 0.8 copy-start.11
  16.0 0.7 copy-start.15
  23.8 8.5 %collective-permute-start.3 = (bf16[144,1152]{1,0:T(8,128)(2,1)}, bf16[144,1152]{1,0:T(8,128)(2,1)S(1)}, u32[]{:S(2)}, u32[]{:S(2)}) collective-permute-start(bf16[144,1152]{1,0:T(8,128)(2,1)} %collective-permute-done.2.refs_1_.refs_2_), channel_id=1, source_target_pairs={{0,2},{2,0},{4,6},{6,4},{8,10},{10,8},{12,14},{14,12},{16,18},{18,... | collective-permute-start | bytes 995336 | tf_op jit(solution)/shard_map/ppermute | solution.py:268
  23.8 0.8 copy-start.17
  24.6 29.9 %copy-start.3 = (bf16[288,1152]{1,0:T(8,128)(2,1)S(1)}, bf16[288,1152]{1,0:T(8,128)(2,1)}, u32[]{:S(2)}) copy-start(bf16[288,1152]{1,0:T(8,128)(2,1)} %refs_1_.1) | copy-start | bytes 1990660
  24.6 29.9 %copy-start.12 = (f32[6,1152]{1,0:T(8,128)S(1)}, f32[6,1152]{1,0:T(8,128)}, u32[]{:S(2)}) copy-start(f32[6,1152]{1,0:T(8,128)} %mod_ref.9) | copy-start | bytes 82948
  24.6 29.9 %copy-start.13 = (f32[1152]{0:T(1024)S(1)}, f32[1152]{0:T(1024)}, u32[]{:S(2)}) copy-start(f32[1152]{0:T(1024)} %outbias_ref.4) | copy-start | bytes 13828
  24.6 29.9 %copy-start.16 = (f32[864]{0:T(1024)S(1)}, f32[864]{0:T(1024)}, u32[]{:S(2)}) copy-start(f32[864]{0:T(1024)} %b_ref.5) | copy-start | bytes 10372
  24.6 28.4 %collective-permute-start.4 = (bf16[2,216,1152]{2,1,0:T(8,128)(2,1)}, bf16[2,216,1152]{2,1,0:T(8,128)(2,1)}, u32[]{:S(2)}, u32[]{:S(2)}) collective-permute-start(bf16[2,216,1152]{2,1,0:T(8,128)(2,1)} %get-tuple-element.19), channel_id=1, source_target_pairs={{0,1},{1,0},{2,3},{3,2},{4,5},{5,4},{6,7},{7,6},{8,9},{9,8},{10,11... | collective-permute-start | bytes 2985992 | tf_op jit(solution)/shard_map/ppermute | solution.py:265
  26.4 1.1 %copy-start.18 = (bf16[128,2,1152]{2,1,0:T(2,128)(2,1)S(1)}, bf16[128,2,1152]{2,1,0:T(2,128)(2,1)}, u32[]{:S(2)}) copy-start(bf16[128,2,1152]{2,1,0:T(2,128)(2,1)} %copy-done.17) | copy-start | bytes 1769476
  27.5 27.1 %copy-start.1 = (bf16[1152,864]{0,1:T(8,128)(2,1)S(1)}, bf16[1152,864]{0,1:T(8,128)(2,1)}, u32[]{:S(2)}) copy-start(bf16[1152,864]{0,1:T(8,128)(2,1)} %param.16) | copy-start | bytes 5971972
  31.6 0.7 copy-start.4
  32.3 0.7 copy-start.8
  33.1 21.3 %all-to-all-start.1 = ((bf16[32,16,288]{2,1,0:T(8,128)(2,1)}), bf16[32,16,288]{2,1,0:T(8,128)(2,1)}, u32[]{:S(2)}, u32[]{:S(2)}) async-start(bf16[32,16,288]{2,1,0:T(8,128)(2,1)} %bitcast.17), calls=%async_computation.1 | async-start | bytes 786432 | tf_op jit(solution)/shard_map/all_to_all | solution.py:313
  54.4 7.2 %collective-permute-start.5 = (bf16[2,216,1152]{2,1,0:T(8,128)(2,1)}, bf16[2,216,1152]{2,1,0:T(8,128)(2,1)S(1)}, u32[]{:S(2)}, u32[]{:S(2)}) collective-permute-start(bf16[2,216,1152]{2,1,0:T(8,128)(2,1)} %collective-permute-done.4.refs_1_), channel_id=1, source_target_pairs={{0,2},{2,0},{4,6},{6,4},{8,10},{10,8},{12,14},{14,12},{16,18},{18,... | collective-permute-start | bytes 2985992 | tf_op jit(solution)/shard_map/ppermute | solution.py:268
  54.5 1.0 %copy-start.9 = (bf16[144,1152]{1,0:T(8,128)(2,1)S(1)}, bf16[144,1152]{1,0:T(8,128)(2,1)}, u32[]{:S(2)}) copy-start(bf16[144,1152]{1,0:T(8,128)(2,1)} %copy-done.8) | copy-start | bytes 995332
  61.6 10.1 %copy-start.5 = (bf16[2,256,288]{2,1,0:T(8,128)(2,1)S(1)}, bf16[2,256,288]{2,1,0:T(8,128)(2,1)}, u32[]{:S(2)}) copy-start(bf16[2,256,288]{2,1,0:T(8,128)(2,1)} %copy-done.4) | copy-start | bytes 884740
  61.6 17.4 %copy-start.10 = (bf16[144,1152]{1,0:T(8,128)(2,1)S(1)}, bf16[144,1152]{1,0:T(8,128)(2,1)}, u32[]{:S(2)}) copy-start(bf16[144,1152]{1,0:T(8,128)(2,1)} %copy-done.8) | copy-start | bytes 995332
  66.2 16.6 %copy-start.14 = (f32[1152]{0:T(1024)S(1)}, f32[1152]{0:T(1024)}, u32[]{:S(2)}) copy-start(f32[1152]{0:T(1024)} %outbias_ref.5) | copy-start | bytes 13828
  66.2 16.6 %all-to-all-start.2 = ((bf16[16,16,576]{2,1,0:T(8,128)(2,1)}), bf16[16,16,576]{2,1,0:T(8,128)(2,1)S(1)}, u32[]{:S(2)}, u32[]{:S(2)}) async-start(bf16[16,16,576]{2,1,0:T(8,128)(2,1)} %bitcast.8), calls=%async_computation.2 | async-start | bytes 655360 | tf_op jit(solution)/shard_map/all_to_all | solution.py:356
  71.7 7.3 %collective-permute-start.6 = (bf16[256,288]{1,0:T(8,128)(2,1)S(1)}, bf16[256,288]{1,0:T(8,128)(2,1)S(1)}, u32[]{:S(2)}, u32[]{:S(2)}) collective-permute-start(bf16[256,288]{1,0:T(8,128)(2,1)S(1)} %dynamic-slice_bitcast_fusion), channel_id=1, source_target_pairs={{0,1},{1,0},{2,3},{3,2},{4,5},{5,4},{6,7},{7,6},{8,9},{9,8},{10,11... | collective-permute-start | bytes 442376 | tf_op jit(solution)/shard_map/ppermute | solution.py:265
  82.8 1.3 %copy-start.7 = (bf16[576,1152]{1,0:T(8,128)(2,1)S(1)}, bf16[576,1152]{1,0:T(8,128)(2,1)}, u32[]{:S(2)}) copy-start(bf16[576,1152]{1,0:T(8,128)(2,1)} %w_ref.1) | copy-start | bytes 3981316

commit v9 on v7

--- a/solution.py
+++ b/solution.py
@@ -92,14 +92,25 @@
     return copies
 
 
-def coordinates():
-    return lax.axis_index("space"), lax.rem(lax.axis_index("tm"), 2)
+def hops_of(heads, times):
+    return [hop for hop in (2, 1) if heads % (2 * hop) == 0 and times % (2 * hop) == 0]
+
+
+def masks_of(hops):
+    masks = [0]
+    for hop in hops:
+        masks += [mask ^ hop for mask in masks]
+    return masks
+
+
+def coordinates(share):
+    return lax.axis_index("space"), lax.rem(lax.axis_index("tm"), share)
 
 
 def kernel_qkv(x_ref, w_hbm, w_other_hbm, mod_ref, b_ref, out_ref, heads_ref, w_ref, sems):
-    _, core = coordinates()
-    half = heads_ref.shape[0]
-    copies = fetch((w_hbm, w_other_hbm.at[pl.ds(core * half, half)]), (w_ref, heads_ref), sems)
+    part = heads_ref.shape[0]
+    _, turn = coordinates(w_ref.shape[0] // part)
+    copies = fetch((w_hbm, w_other_hbm.at[pl.ds(turn * part, part)]), (w_ref, heads_ref), sems)
     h = spatial_rows(flat(x_ref), mod_ref, x_ref.shape[1])
     bias = bias_column(b_ref)
     copies[0].wait()
@@ -113,7 +124,7 @@
 def kernel_spatial(own_ref, w_ref, mod_ref, b_ref, *refs):
     x_refs, (out_ref, part_ref) = refs[:-2], refs[-2:]
     heads = w_ref.shape[0]
-    space, _ = coordinates()
+    space = lax.axis_index("space")
     patches, frames, _ = x_refs[0].shape
     spaces = len(x_refs) + 1
     bias = bias_column(b_ref)
@@ -168,22 +179,25 @@
     return attend(qkv[0:HD], qkv[HD : 2 * HD], qkv[2 * HD : 3 * HD], mask)
 
 
-def parts_of(o, pieces, core):
-    half = pieces[1].shape[0]
-    parts = [mm(o(0), pieces[0][...])]
-    for k in range(1, (len(pieces) + 1) // 2):
-        first, second = pieces[2 * k - 1][...], pieces[2 * k][...]
-        rows = jnp.concatenate([jnp.where(core == 0, first, second), jnp.where(core == 0, second, first)])
-        parts.append(mm(o(k), rows))
+def parts_of(o, own_w_ref, pieces, w_ref, masks):
+    share = len(masks)
+    _, turn = coordinates(share)
+    rows = pieces[0].shape[0]
+    parts = [mm(o(0), own_w_ref[...])]
+    for k in range(len(pieces) // share):
+        for mask, piece in zip(masks, pieces[k * share : (k + 1) * share]):
+            w_ref[turn ^ mask] = piece[...]
+        columns = o(k + 1)
+        parts.append(sum(mm(columns[:, q * rows : (q + 1) * rows], w_ref[q]) for q in range(share)))
     return parts
 
 
-def kernel_temporal(o_ref, x_ref, w_ref, outbias_ref, mod_ref, b_ref, *refs, size, frames):
-    space, core = coordinates()
-    pieces, (h_ref, out_ref) = refs[:-2], refs[-2:]
+def kernel_temporal(o_ref, x_ref, w_ref, outbias_ref, mod_ref, b_ref, own_w_ref, *refs, size, frames, masks):
+    space = lax.axis_index("space")
+    pieces, (h_ref, out_ref, piece_ref) = refs[:-3], refs[-3:]
     spaces, rows, _ = o_ref.shape
     mask = temporal_mask(rows, size, frames)
-    parts = parts_of(lambda k: o_ref[lax.rem(space - k + spaces, spaces)], pieces, core)
+    parts = parts_of(lambda k: o_ref[lax.rem(space - k + spaces, spaces)], own_w_ref, pieces, piece_ref, masks)
     y = middle(flat(x_ref), parts, outbias_ref[...].reshape(1, -1), mod_ref[2:3, :])
     h = modulated(y.astype(F32), mod_ref[3:4, :], mod_ref[4:5, :]).astype(BF)
     h_ref[...] = h
@@ -192,34 +206,36 @@
         out_ref[i] = temporal_head(w_ref[i], bias[i * 3 * HD : (i + 1) * 3 * HD], h, mask)
 
 
-def kernel_rest(h_ref, own_ref, *refs, size, frames, spaces):
-    b_refs, w_refs, (out_ref, turn_ref) = refs[: spaces - 1], refs[spaces - 1 : -2], refs[-2:]
-    space, core = coordinates()
+def kernel_rest(h_ref, own_ref, *refs, size, frames, spaces, masks):
+    b_refs, w_refs, (out_ref, turn_ref, bias_ref) = refs[: spaces - 1], refs[spaces - 1 : -3], refs[-3:]
+    share = len(masks)
+    space, turn = coordinates(share)
     h = h_ref[...]
     rows = h.shape[0]
     mask = temporal_mask(rows, size, frames)
     heads = own_ref.shape[0]
-    half = heads // 2
+    part = heads // share
     for i in range(heads):
         turn_ref[space * heads + i] = own_ref[i]
-    for n, w_ref in enumerate(w_refs):
-        shift = n // 2 + 1
-        bias = bias_column(b_refs[shift - 1])
-        second = (core == 0) == (n % 2 == 1)
-        within = jnp.where(second, half, 0)
-        group = lax.rem(space - shift + spaces, spaces)
-        bias = jnp.where(second, bias[half * 3 * HD :], bias[: half * 3 * HD])
-        for i in range(half):
-            o_t = temporal_head(w_ref[i], bias[i * 3 * HD : (i + 1) * 3 * HD], h, mask)
-            turn_ref[group * heads + within + i] = o_t
+    for k in range(spaces - 1):
+        bias = bias_column(b_refs[k])
+        for i in range(heads):
+            bias_ref[i] = bias[i * 3 * HD : (i + 1) * 3 * HD]
+        group = lax.rem(space - k - 1 + spaces, spaces)
+        for n, w_ref in zip(masks, w_refs[k * share : (k + 1) * share]):
+            for i in range(part):
+                head = (turn ^ n) * part + i
+                turn_ref[group * heads + head] = temporal_head(w_ref[i], bias_ref[head], h, mask)
     out_ref[...] = turn_ref[...].reshape(-1, rows).T.astype(BF)
 
 
-def kernel_home(o_own_ref, x_ref, outbias_ref, mod_ref, *refs):
-    space, core = coordinates()
+def kernel_home(o_own_ref, x_ref, outbias_ref, mod_ref, own_w_ref, *refs, masks):
+    space = lax.axis_index("space")
     spaces = o_own_ref.shape[0]
-    o_refs, pieces, out_ref = refs[: spaces - 1], refs[spaces - 1 : -1], refs[-1]
-    parts = parts_of(lambda k: o_refs[k - 1][...] if k else o_own_ref[space], pieces, core)
+    o_refs, pieces, (out_ref, piece_ref) = refs[: spaces - 1], refs[spaces - 1 : -2], refs[-2:]
+    parts = parts_of(
+        lambda k: o_refs[k - 1][...] if k else o_own_ref[space], own_w_ref, pieces, piece_ref, masks
+    )
     out_ref[...] = middle(flat(x_ref), parts, outbias_ref[...].reshape(1, -1), mod_ref[2:3, :])
 
 
@@ -258,15 +274,23 @@
     space = lax.axis_index("space")
     heads = qkv_spatial.shape[1] // (3 * HD)
     cols = heads * HD
-    half = heads // 2
+    out_hops = hops_of(heads, times)
+    out_masks = masks_of(out_hops)
+    out_part = heads // len(out_masks) * HD
+    hops = out_hops[-1:]
+    masks = masks_of(hops)
+    part = heads // len(masks)
     size = patches // times
     rows = patches * frames
 
     def across(array, k):
         return lax.ppermute(array, "space", [(i, (i + k) % spaces) for i in range(spaces)])
 
-    def beside(array):
-        return lax.ppermute(array, "tm", [(i, i ^ 1) for i in range(times)])
+    def handed_on(array, hops):
+        pieces = [array]
+        for hop in hops:
+            pieces += [lax.ppermute(a, "tm", [(i, i ^ hop) for i in range(times)]) for a in pieces]
+        return pieces
 
     arrived = [across(tokens, k) for k in range(1, spaces)]
 
@@ -275,7 +299,7 @@
     own, my_heads = pl.pallas_call(
         kernel_qkv,
         out_shape=tuple(
-            jax.ShapeDtypeStruct(a, BF) for a in ((heads, 3, HD, rows), (half, 3 * HD, width))
+            jax.ShapeDtypeStruct(a, BF) for a in ((heads, 3, HD, rows), (part, 3 * HD, width))
         ),
         in_specs=[VMEM] + [ANY] * 2 + [VMEM] * 2,
         out_specs=(VMEM, VMEM),
@@ -289,9 +313,13 @@
     spread = lax.all_to_all(tokens.reshape(times, size, frames, width), "tm", 0, 0, tiled=True)
 
     other_bias = [across(bias_temporal, k) for k in range(1, spaces)]
-    my_out = lax.dynamic_slice_in_dim(out_spatial, lax.rem(lax.axis_index("tm"), 2) * half * HD, half * HD, 0)
+    my_out = lax.dynamic_slice_in_dim(
+        out_spatial, lax.rem(lax.axis_index("tm"), len(out_masks)) * out_part, out_part, 0
+    )
+    out_pieces = []
+    for k in range(1, spaces):
+        out_pieces += handed_on(after((across(my_out, k),), own)[0], out_hops)
     arrived = [after((a,), own, *other_bias)[0] for a in arrived]
-    direct_out = [across(my_out, k) for k in range(1, spaces)]
 
     o_all = call(
         kernel_spatial,
@@ -307,16 +335,12 @@
 
     (my_heads,) = after((my_heads,), *arrived)
     direct_heads = [across(my_heads, k) for k in range(1, spaces)]
-    out_pieces = [out_spatial]
-    for a in direct_out:
-        out_pieces += [a, beside(a)]
-
     o_here = lax.all_to_all(
         after((o_all,), spread, *out_pieces)[0].reshape(spaces * times, frames * size, cols), ("space", "tm"), 0, 0, tiled=True
     ).reshape(spaces, rows, cols)
     other_heads = []
     for a in direct_heads:
-        other_heads += [a, beside(after((a,), o_here)[0])]
+        other_heads += handed_on(after((a,), o_here)[0], hops)
 
     o_home = [
         across(lax.dynamic_index_in_dim(o_all, (space + k) % spaces, 0, keepdims=False), k)
@@ -324,32 +348,35 @@
     ]
 
     y_home = call(
-        kernel_home,
+        functools.partial(kernel_home, masks=out_masks),
         (rows, width),
-        4 + len(o_home) + len(out_pieces),
+        5 + len(o_home) + len(out_pieces),
         2 * rows * width * cols * spaces,
         3e6,
+        [pltpu.VMEM((len(out_masks), out_part, width), BF)],
         params=SMALL,
-    )(o_all, tokens, outbias_spatial, modulation, *o_home, *out_pieces)
+    )(o_all, tokens, outbias_spatial, modulation, out_spatial, *o_home, *out_pieces)
     x_here = spread.reshape(rows // frames, frames, width)
     h_here, o_own = pl.pallas_call(
-        functools.partial(kernel_temporal, size=size, frames=frames),
+        functools.partial(kernel_temporal, size=size, frames=frames, masks=out_masks),
         out_shape=(jax.ShapeDtypeStruct((rows, width), BF), jax.ShapeDtypeStruct((heads, HD, rows), F32)),
-        in_specs=[VMEM] * (6 + len(out_pieces)),
+        in_specs=[VMEM] * (7 + len(out_pieces)),
         out_specs=(VMEM, VMEM),
+        scratch_shapes=[pltpu.VMEM((len(out_masks), out_part, width), BF)],
         compiler_params=SMALL,
         cost_estimate=pl.CostEstimate(
             flops=2 * rows * width * cols * (3 + spaces), bytes_accessed=5 * 10**6, transcendentals=0
         ),
-    )(o_here, x_here, w_temporal, outbias_spatial, modulation, bias_temporal, *out_pieces)
+    )(o_here, x_here, w_temporal, outbias_spatial, modulation, bias_temporal, out_spatial, *out_pieces)
     o_t = call(
-        functools.partial(kernel_rest, size=size, frames=frames, spaces=spaces),
+        functools.partial(kernel_rest, size=size, frames=frames, spaces=spaces, masks=masks),
         (rows, spaces * cols),
         1 + spaces + len(other_heads),
         2 * rows * width * cols * 3 * (spaces - 1),
         5e6,
         [
             pltpu.VMEM((spaces * heads, HD, rows), F32),
+            pltpu.VMEM((heads, 3 * HD, 1), F32),
         ],
         params=SMALL,
     )(h_here, o_own, *other_bias, *other_heads)
@@ -357,7 +384,7 @@
     o_final = lax.all_to_all(o_t, "tm", 0, 0, tiled=True).reshape(rows, spaces * cols)
 
     return call(
-        kernel_final, (patches, frames, width), 5, 2 * rows * width * cols * spaces, 3e6, params=SMALL
+        kernel_final, (patches, frames, width), 5, 2 * rows * width * cols * spaces, 3e6
     )(o_final, y_home, out_temporal, outbias_temporal, modulation)
 
 

time: 85.4 us -> 91.1 us (1.067)
  Pallas kernels: 25 us -> 27.2 us
  local copies, waits for them, and re-layouts: 8.32 us -> 10.1 us
    ppermute x2 -> x4, waiting for transfers between devices: 0.01 us -> 3.92 us  [handed_on(): lax.ppermute(a, 'tm', [(i, i ^ hop) for i in range(times)])]
    ppermute x5, waiting for transfers between devices: 23.7 us -> 21.6 us  [across(): lax.ppermute(array, 'space', [(i, (i + k) % spaces) for i in range(spaces)])]
    unnamed x28 -> x38, local copies, waits for them, and re-layouts: 5.63 us -> 7.51 us
    ppermute x2 -> x4, starting transfers between devices: 0.12 us -> 1.78 us  [handed_on(): lax.ppermute(a, 'tm', [(i, i ^ hop) for i in range(times)])]
    pallas_call x1, Pallas kernels: 1.52 us -> 3.13 us  [local(): call(kernel_final, (patches, frames, width), 5, 2 * rows * width * cols *...]
  transfers between devices with their start and end apart: 10 -> 12, of which waited for: 5 -> 5; matrix products, arithmetic and copies ran while one was open for 3% -> 3% of each run, Pallas kernels for 22% -> 22%
where the time goes in v9:
time: 91.1 us; the launch traced here: 90.3 us
  Pallas kernels  27.2 us (30%)
  waiting for transfers between devices  26.9 us (30%)
  starting transfers between devices  25.9 us (28%)
  local copies, waits for them, and re-layouts  10.1 us (11%)
    ppermute x5, waiting for transfers between devices, across(): lax.ppermute(array, 'space', [(i, (i + k) % spaces) for i in range(spaces)])  21.6 us
    ppermute x5, starting transfers between devices, across(): lax.ppermute(array, 'space', [(i, (i + k) % spaces) for i in range(spaces)])  7.54 us
    unnamed x38, local copies, waits for them, and re-layouts  7.51 us
    all_to_all x1, starting transfers between devices, local(): lax.all_to_all(tokens.reshape(times, size, frames, width), 'tm', 0, 0, ti...  6.47 us
    pallas_call x1, Pallas kernels, local(): pl.pallas_call(functools.partial(kernel_temporal, size=size, frames=frame...  6.17 us
    pallas_call x1, Pallas kernels, local(): call(kernel_spatial, (spaces, rows, cols), 4 + len(arrived), 10000000000....  6.06 us
    all_to_all x1, starting transfers between devices, local(): lax.all_to_all(o_t, 'tm', 0, 0, tiled=True).reshape(rows, spaces * cols)  5.41 us
    all_to_all x1, starting transfers between devices, local(): lax.all_to_all(after((o_all,), spread, *out_pieces)[0].reshape(spaces * t...  4.72 us
  transfers between devices with their start and end apart: 12, of which 5 were waited for; matrix products, arithmetic and copies ran while one was open for 3% of the time, Pallas kernels for 22%

profile of v9, /device:TPU:0, one launch (start us, length us, event | category | flops | bytes accessed | tf_op | source)
XLA Modules:
  0.0 90.3 jit_solution(909777100302073840)
XLA Ops:
  0.0 2.9 %collective-permute-start = (bf16[128,2,1152]{2,1,0:T(2,128)(2,1)}, bf16[128,2,1152]{2,1,0:T(2,128)(2,1)}, u32[]{:S(2)}, u32[]{:S(2)}) collective-permute-start(bf16[128,2,1152]{2,1,0:T(2,128)(2,1)} %x_ref.3), channel_id=1, source_target_pairs={{0,1},{1,0},{2,3},{3,2},{4,5},{5,4},{6,7},{7,6},{8,9},{9,8},{10,11... | collective-permute-start | bytes 1769480 | tf_op jit(solution)/shard_map/ppermute | solution.py:287
  2.9 1.6 %constant_dynamic-slice_fusion = bf16[72,1152]{1,0:T(8,128)(2,1)} fusion(bf16[288,1152]{1,0:T(8,128)(2,1)} %own_w_ref.3, s32[]{:T(128)S(6)} %select_n.14), kind=kLoop, calls=%fused_computation.1 | loop fusion | bytes 331780 | tf_op jit(solution)/shard_map/dynamic_slice | solution.py:316
  4.5 6.5 %all-to-all-start = ((bf16[16,8,2,1152]{3,2,1,0:T(2,128)(2,1)}), bf16[16,8,2,1152]{3,2,1,0:T(2,128)(2,1)S(1)}, u32[]{:S(2)}, u32[]{:S(2)}) async-start(bf16[16,8,2,1152]{3,2,1,0:T(2,128)(2,1)} %bitcast.16), calls=%async_computation | async-start | bytes 1179648 | tf_op jit(solution)/shard_map/all_to_all | solution.py:313
  11.0 0.0 copy-start.17
  11.0 0.0 copy-start.14
  11.0 4.7 %shard_map.100 = (bf16[4,3,72,256]{3,2,1,0:T(8,128)(2,1)}, bf16[2,216,1152]{2,1,0:T(8,128)(2,1)}) custom-call(bf16[128,2,1152]{2,1,0:T(2,128)(2,1)} %x_ref.3, bf16[4,216,1152]{2,1,0:T(8,128)(2,1)} %bitcast.18, bf16[4,216,1152]{2,1,0:T(8,128)(2,1)} %bitcast.14, f32[6,1152]{1,0:T(8,128)} %mod_ref.9, f32[864]{0:T(1024)} %b_ref.4), custom_call_target="tpu_custom_call" | custom-call | flops 509607936 | bytes 3000000 | tf_op jit(solution)/shard_map/pallas_call | solution.py:299
  15.8 4.3 %collective-permute-done.2.refs_0_.refs_1_ = bf16[72,1152]{1,0:T(8,128)(2,1)S(1)} collective-permute-done((bf16[72,1152]{1,0:T(8,128)(2,1)}, bf16[72,1152]{1,0:T(8,128)(2,1)S(1)}, u32[]{:S(2)}, u32[]{:S(2)}) %collective-permute-start.2) | collective-permute-done | bytes 165920 | tf_op jit(solution)/shard_map/ppermute | solution.py:287
  20.0 1.8 %collective-permute-start.3 = (bf16[72,1152]{1,0:T(8,128)(2,1)S(1)}, bf16[72,1152]{1,0:T(8,128)(2,1)S(1)}, u32[]{:S(2)}, u32[]{:S(2)}) collective-permute-start(bf16[72,1152]{1,0:T(8,128)(2,1)S(1)} %collective-permute-done.2.refs_0_.refs_1_), channel_id=1, source_target_pairs={{0,4},{2,6},{4,0},{6,2},{8,12},{10,14},{12,8},{14,10},{16,20},{18,... | collective-permute-start | bytes 497672 | tf_op jit(solution)/shard_map/ppermute | solution.py:292
  21.8 1.5 %collective-permute-start.1 = (f32[864]{0:T(1024)S(1)}, f32[864]{0:T(1024)S(1)}, u32[]{:S(2)}, u32[]{:S(2)}) collective-permute-start(f32[864]{0:T(1024)S(1)} %copy-done.17), channel_id=1, source_target_pairs={{0,1},{1,0},{2,3},{3,2},{4,5},{5,4},{6,7},{7,6},{8,9},{9,8},{10,11... | collective-permute-start | bytes 10376 | tf_op jit(solution)/shard_map/ppermute | solution.py:287
  23.3 3.9 %collective-permute-done.3.refs_1_.refs_2_ = bf16[72,1152]{1,0:T(8,128)(2,1)S(1)} collective-permute-done((bf16[72,1152]{1,0:T(8,128)(2,1)S(1)}, bf16[72,1152]{1,0:T(8,128)(2,1)S(1)}, u32[]{:S(2)}, u32[]{:S(2)}) %collective-permute-start.3) | collective-permute-done | bytes 165920 | tf_op jit(solution)/shard_map/ppermute | solution.py:292
  27.2 0.0 copy-start.2
  27.2 1.5 %collective-permute-start.6 = (bf16[2,216,1152]{2,1,0:T(8,128)(2,1)}, bf16[2,216,1152]{2,1,0:T(8,128)(2,1)}, u32[]{:S(2)}, u32[]{:S(2)}) collective-permute-start(bf16[2,216,1152]{2,1,0:T(8,128)(2,1)} %get-tuple-element.21), channel_id=1, source_target_pairs={{0,1},{1,0},{2,3},{3,2},{4,5},{5,4},{6,7},{7,6},{8,9},{9,8},{10,11... | collective-permute-start | bytes 2985992 | tf_op jit(solution)/shard_map/ppermute | solution.py:287
  28.8 1.6 %copy-done.4 = bf16[1152,864]{0,1:T(8,128)(2,1)S(1)} copy-done((bf16[1152,864]{0,1:T(8,128)(2,1)S(1)}, bf16[1152,864]{0,1:T(8,128)(2,1)}, u32[]{:S(2)}) %copy-start.4) | copy-done | bytes 1990680
  30.4 1.0 %copy-done.18 = bf16[4,3,72,256]{3,2,1,0:T(8,128)(2,1)S(1)} copy-done((bf16[4,3,72,256]{3,2,1,0:T(8,128)(2,1)S(1)}, bf16[4,3,72,256]{3,2,1,0:T(8,128)(2,1)}, u32[]{:S(2)}) %copy-start.18) | copy-done | bytes 442392
  31.4 6.1 %shard_map.101.o_own_ref = bf16[2,256,288]{2,1,0:T(8,128)(2,1)} custom-call(bf16[4,3,72,256]{3,2,1,0:T(8,128)(2,1)S(1)} %copy-done.18, bf16[4,216,1152]{2,1,0:T(8,128)(2,1)S(1)} %bitcast.19, f32[6,1152]{1,0:T(8,128)S(1)} %copy-done.14, f32[864]{0:T(1024)S(1)} %copy-done.16, bf16[128,2,1152]{2,1,0:T(2,128)(2,1)} %collective-permute-done.refs_0_), custom_call_target="tpu_custom_call" | custom-call | flops 10000000000 | bytes 4000000 | tf_op jit(solution)/shard_map/pallas_call | solution.py:324
  37.4 0.7 copy-done.8
  38.1 0.7 copy-done.11
  38.8 4.7 %all-to-all-start.1 = ((bf16[32,16,288]{2,1,0:T(8,128)(2,1)}), bf16[32,16,288]{2,1,0:T(8,128)(2,1)}, u32[]{:S(2)}, u32[]{:S(2)}) async-start(bf16[32,16,288]{2,1,0:T(8,128)(2,1)} %bitcast.5), calls=%async_computation.1 | async-start | bytes 786432 | tf_op jit(solution)/shard_map/all_to_all | solution.py:338
  43.5 11.7 %collective-permute-done.6.refs_1_ = bf16[2,216,1152]{2,1,0:T(8,128)(2,1)} collective-permute-done((bf16[2,216,1152]{2,1,0:T(8,128)(2,1)}, bf16[2,216,1152]{2,1,0:T(8,128)(2,1)}, u32[]{:S(2)}, u32[]{:S(2)}) %collective-permute-start.6) | collective-permute-done | bytes 995360 | tf_op jit(solution)/shard_map/ppermute | solution.py:287
  55.2 1.4 %all-to-all-done.1 = bf16[32,16,288]{2,1,0:T(8,128)(2,1)} async-done(((bf16[32,16,288]{2,1,0:T(8,128)(2,1)}), bf16[32,16,288]{2,1,0:T(8,128)(2,1)}, u32[]{:S(2)}, u32[]{:S(2)}) %all-to-all-start.1) | async-done | bytes 294944 | tf_op jit(solution)/shard_map/all_to_all | solution.py:338
  56.6 0.9 %copy-done.6 = bf16[72,1152]{1,0:T(8,128)(2,1)S(1)} copy-done((bf16[72,1152]{1,0:T(8,128)(2,1)S(1)}, bf16[72,1152]{1,0:T(8,128)(2,1)}, u32[]{:S(2)}) %copy-start.6) | copy-done | bytes 165912
  57.6 0.9 %copy-done.9 = bf16[72,1152]{1,0:T(8,128)(2,1)S(1)} copy-done((bf16[72,1152]{1,0:T(8,128)(2,1)S(1)}, bf16[72,1152]{1,0:T(8,128)(2,1)}, u32[]{:S(2)}) %copy-start.9) | copy-done | bytes 165912
  58.5 0.9 %copy-done.12 = bf16[72,1152]{1,0:T(8,128)(2,1)S(1)} copy-done((bf16[72,1152]{1,0:T(8,128)(2,1)S(1)}, bf16[72,1152]{1,0:T(8,128)(2,1)}, u32[]{:S(2)}) %copy-start.12) | copy-done | bytes 165912
  59.4 6.2 %shard_map.102 = (bf16[256,1152]{1,0:T(8,128)(2,1)S(1)}, f32[4,72,256]{2,1,0:T(8,128)S(1)}) custom-call(bf16[2,256,288]{2,1,0:T(8,128)(2,1)} %bitcast.6.o_ref, bf16[128,2,1152]{2,1,0:T(2,128)(2,1)S(1)} %bitcast.17, bf16[4,216,1152]{2,1,0:T(8,128)(2,1)S(1)} %bitcast.15, f32[1152]{0:T(1024)S(1)} %copy-done.15, f32[6,1152]{1,0:T(8,128)S(1)} %copy-done.14, ...), custom_call_target="tpu_custom_call" | custom-call | flops 849346560 | bytes 5000000 | tf_op jit(solution)/shard_map/pallas_call | solution.py:360
  65.6 4.6 %shard_map.103 = bf16[256,576]{1,0:T(8,128)(2,1)} custom-call(bf16[256,1152]{1,0:T(8,128)(2,1)S(1)} %get-tuple-element.18.h_ref, f32[4,72,256]{2,1,0:T(8,128)S(1)} %get-tuple-element.19.own_ref, f32[864]{0:T(1024)S(1)} %collective-permute-done.1.refs_0_, bf16[2,216,1152]{2,1,0:T(8,128)(2,1)} %collective-permute-done.6.refs_1_, ...), custom_call_target="tpu_custom_call" | custom-call | flops 509607936 | bytes 5000000 | tf_op jit(solution)/shard_map/pallas_call | solution.py:371
  70.2 5.4 %all-to-all-start.2 = ((bf16[16,16,576]{2,1,0:T(8,128)(2,1)}), bf16[16,16,576]{2,1,0:T(8,128)(2,1)}, u32[]{:S(2)}, u32[]{:S(2)}) async-start(bf16[16,16,576]{2,1,0:T(8,128)(2,1)} %bitcast.8), calls=%async_computation.2 | async-start | bytes 655360 | tf_op jit(solution)/shard_map/all_to_all | solution.py:384
  75.6 1.0 %dynamic-slice_bitcast_fusion = bf16[256,288]{1,0:T(8,128)(2,1)S(1)} fusion(bf16[2,256,288]{2,1,0:T(8,128)(2,1)} %shard_map.101.o_own_ref, s32[]{:T(128)S(6)} %select_n.16), kind=kLoop, calls=%fused_computation | loop fusion | bytes 294916 | tf_op jit(solution)/shard_map/jit(dynamic_index_in_dim)/squeeze | solution.py:346
  76.6 1.6 %collective-permute-start.8 = (bf16[256,288]{1,0:T(8,128)(2,1)S(1)}, bf16[256,288]{1,0:T(8,128)(2,1)S(1)}, u32[]{:S(2)}, u32[]{:S(2)}) collective-permute-start(bf16[256,288]{1,0:T(8,128)(2,1)S(1)} %dynamic-slice_bitcast_fusion), channel_id=1, source_target_pairs={{0,1},{1,0},{2,3},{3,2},{4,5},{5,4},{6,7},{7,6},{8,9},{9,8},{10,11... | collective-permute-start | bytes 442376 | tf_op jit(solution)/shard_map/ppermute | solution.py:287
  78.2 5.7 %collective-permute-done.8.refs_0_ = bf16[256,288]{1,0:T(8,128)(2,1)S(1)} collective-permute-done((bf16[256,288]{1,0:T(8,128)(2,1)S(1)}, bf16[256,288]{1,0:T(8,128)(2,1)S(1)}, u32[]{:S(2)}, u32[]{:S(2)}) %collective-permute-start.8) | collective-permute-done | bytes 147488 | tf_op jit(solution)/shard_map/ppermute | solution.py:287
  83.8 2.5 %shard_map.104.y_ref = bf16[256,1152]{1,0:T(8,128)(2,1)S(1)} custom-call(bf16[2,256,288]{2,1,0:T(8,128)(2,1)} %shard_map.101.o_own_ref, bf16[128,2,1152]{2,1,0:T(2,128)(2,1)S(1)} %copy-done.1, f32[1152]{0:T(1024)S(1)} %copy-done.15, f32[6,1152]{1,0:T(8,128)S(1)} %copy-done.14, bf16[288,1152]{1,0:T(8,128)(2,1)S(1)} %copy-done.2, ...), custom_call_target="tpu_custom_call" | custom-call | flops 339738624 | bytes 3000000 | tf_op jit(solution)/shard_map/pallas_call | solution.py:350
  86.4 0.8 copy-done.3
  87.2 3.1 %shard_map.105 = bf16[128,2,1152]{2,1,0:T(2,128)(2,1)} custom-call(bf16[256,576]{1,0:T(8,128)(2,1)} %bitcast.9.o_ref, bf16[256,1152]{1,0:T(8,128)(2,1)} %copy-done.3, bf16[576,1152]{1,0:T(8,128)(2,1)} %w_ref.1, f32[1152]{0:T(1024)} %outbias_ref.5, f32[6,1152]{1,0:T(8,128)} %mod_ref.9), custom_call_target="tpu_custom_call" | custom-call | flops 339738624 | bytes 3000000 | tf_op jit(solution)/shard_map/pallas_call | solution.py:386
  (38 shorter events, 0.1 us)
Async XLA Ops:
  0.0 27.2 %collective-permute-start = (bf16[128,2,1152]{2,1,0:T(2,128)(2,1)}, bf16[128,2,1152]{2,1,0:T(2,128)(2,1)}, u32[]{:S(2)}, u32[]{:S(2)}) collective-permute-start(bf16[128,2,1152]{2,1,0:T(2,128)(2,1)} %x_ref.3), channel_id=1, source_target_pairs={{0,1},{1,0},{2,3},{3,2},{4,5},{5,4},{6,7},{7,6},{8,9},{9,8},{10,11... | collective-permute-start | bytes 1769480 | tf_op jit(solution)/shard_map/ppermute | solution.py:287
  4.5 15.5 %collective-permute-start.2 = (bf16[72,1152]{1,0:T(8,128)(2,1)}, bf16[72,1152]{1,0:T(8,128)(2,1)S(1)}, u32[]{:S(2)}, u32[]{:S(2)}) collective-permute-start(bf16[72,1152]{1,0:T(8,128)(2,1)} %constant_dynamic-slice_fusion), channel_id=1, source_target_pairs={{0,1},{1,0},{2,3},{3,2},{4,5},{5,4},{6,7},{7,6},{8,9},{9,8},{10,11... | collective-permute-start | bytes 497672 | tf_op jit(solution)/shard_map/ppermute | solution.py:287
  4.5 34.3 %all-to-all-start = ((bf16[16,8,2,1152]{3,2,1,0:T(2,128)(2,1)}), bf16[16,8,2,1152]{3,2,1,0:T(2,128)(2,1)S(1)}, u32[]{:S(2)}, u32[]{:S(2)}) async-start(bf16[16,8,2,1152]{3,2,1,0:T(2,128)(2,1)} %bitcast.16), calls=%async_computation | async-start | bytes 1179648 | tf_op jit(solution)/shard_map/all_to_all | solution.py:313
  11.0 10.8 %copy-start.17 = (f32[864]{0:T(1024)S(1)}, f32[864]{0:T(1024)}, u32[]{:S(2)}) copy-start(f32[864]{0:T(1024)} %b_ref.5) | copy-start | bytes 10372
  11.0 17.8 %copy-start.14 = (f32[6,1152]{1,0:T(8,128)S(1)}, f32[6,1152]{1,0:T(8,128)}, u32[]{:S(2)}) copy-start(f32[6,1152]{1,0:T(8,128)} %mod_ref.9) | copy-start | bytes 82948
  11.0 17.8 %copy-start.16 = (f32[864]{0:T(1024)S(1)}, f32[864]{0:T(1024)}, u32[]{:S(2)}) copy-start(f32[864]{0:T(1024)} %b_ref.4) | copy-start | bytes 10372
  20.0 7.2 %collective-permute-start.3 = (bf16[72,1152]{1,0:T(8,128)(2,1)S(1)}, bf16[72,1152]{1,0:T(8,128)(2,1)S(1)}, u32[]{:S(2)}, u32[]{:S(2)}) collective-permute-start(bf16[72,1152]{1,0:T(8,128)(2,1)S(1)} %collective-permute-done.2.refs_0_.refs_1_), channel_id=1, source_target_pairs={{0,4},{2,6},{4,0},{6,2},{8,12},{10,14},{12,8},{14,10},{16,20},{18,... | collective-permute-start | bytes 497672 | tf_op jit(solution)/shard_map/ppermute | solution.py:292
  21.8 5.4 %collective-permute-start.1 = (f32[864]{0:T(1024)S(1)}, f32[864]{0:T(1024)S(1)}, u32[]{:S(2)}, u32[]{:S(2)}) collective-permute-start(f32[864]{0:T(1024)S(1)} %copy-done.17), channel_id=1, source_target_pairs={{0,1},{1,0},{2,3},{3,2},{4,5},{5,4},{6,7},{7,6},{8,9},{9,8},{10,11... | collective-permute-start | bytes 10376 | tf_op jit(solution)/shard_map/ppermute | solution.py:287
  23.3 14.1 %collective-permute-start.4 = (bf16[72,1152]{1,0:T(8,128)(2,1)S(1)}, bf16[72,1152]{1,0:T(8,128)(2,1)S(1)}, u32[]{:S(2)}, u32[]{:S(2)}) collective-permute-start(bf16[72,1152]{1,0:T(8,128)(2,1)S(1)} %collective-permute-done.2.refs_0_.refs_1_), channel_id=1, source_target_pairs={{0,2},{2,0},{4,6},{6,4},{8,10},{10,8},{12,14},{14,12},{16,18},{18,... | collective-permute-start | bytes 497672 | tf_op jit(solution)/shard_map/ppermute | solution.py:292
  27.2 10.2 %copy-start.5 = (bf16[72,1152]{1,0:T(8,128)(2,1)}, bf16[72,1152]{1,0:T(8,128)(2,1)S(1)}, u32[]{:S(2)}) copy-start(bf16[72,1152]{1,0:T(8,128)(2,1)S(1)} %collective-permute-done.3.refs_1_.refs_2_) | copy-start | bytes 497668
  27.2 10.9 %collective-permute-start.5 = (bf16[72,1152]{1,0:T(8,128)(2,1)S(1)}, bf16[72,1152]{1,0:T(8,128)(2,1)S(1)}, u32[]{:S(2)}, u32[]{:S(2)}) collective-permute-start(bf16[72,1152]{1,0:T(8,128)(2,1)S(1)} %collective-permute-done.3.refs_1_.refs_2_), channel_id=1, source_target_pairs={{0,2},{2,0},{4,6},{6,4},{8,10},{10,8},{12,14},{14,12},{16,18},{18,... | collective-permute-start | bytes 497672 | tf_op jit(solution)/shard_map/ppermute | solution.py:292
  27.2 29.4 %copy-start.2 = (bf16[288,1152]{1,0:T(8,128)(2,1)S(1)}, bf16[288,1152]{1,0:T(8,128)(2,1)}, u32[]{:S(2)}) copy-start(bf16[288,1152]{1,0:T(8,128)(2,1)} %own_w_ref.3) | copy-start | bytes 1990660
  27.2 28.0 %collective-permute-start.6 = (bf16[2,216,1152]{2,1,0:T(8,128)(2,1)}, bf16[2,216,1152]{2,1,0:T(8,128)(2,1)}, u32[]{:S(2)}, u32[]{:S(2)}) collective-permute-start(bf16[2,216,1152]{2,1,0:T(8,128)(2,1)} %get-tuple-element.21), channel_id=1, source_target_pairs={{0,1},{1,0},{2,3},{3,2},{4,5},{5,4},{6,7},{7,6},{8,9},{9,8},{10,11... | collective-permute-start | bytes 2985992 | tf_op jit(solution)/shard_map/ppermute | solution.py:287
  28.8 1.6 %copy-start.4 = (bf16[1152,864]{0,1:T(8,128)(2,1)S(1)}, bf16[1152,864]{0,1:T(8,128)(2,1)}, u32[]{:S(2)}) copy-start(bf16[1152,864]{0,1:T(8,128)(2,1)} %param.12) | copy-start | bytes 5971972
  30.4 1.0 %copy-start.18 = (bf16[4,3,72,256]{3,2,1,0:T(8,128)(2,1)S(1)}, bf16[4,3,72,256]{3,2,1,0:T(8,128)(2,1)}, u32[]{:S(2)}) copy-start(bf16[4,3,72,256]{3,2,1,0:T(8,128)(2,1)} %get-tuple-element.14.own_ref) | copy-start | bytes 1327108
  31.4 25.2 %copy-start = (bf16[1152,864]{0,1:T(8,128)(2,1)S(1)}, bf16[1152,864]{0,1:T(8,128)(2,1)}, u32[]{:S(2)}) copy-start(bf16[1152,864]{0,1:T(8,128)(2,1)} %param.16) | copy-start | bytes 5971972
  31.4 25.3 %copy-start.15 = (f32[1152]{0:T(1024)S(1)}, f32[1152]{0:T(1024)}, u32[]{:S(2)}) copy-start(f32[1152]{0:T(1024)} %outbias_ref.4) | copy-start | bytes 13828
  37.4 0.7 copy-start.8
  38.1 0.7 copy-start.11
  38.8 17.8 %all-to-all-start.1 = ((bf16[32,16,288]{2,1,0:T(8,128)(2,1)}), bf16[32,16,288]{2,1,0:T(8,128)(2,1)}, u32[]{:S(2)}, u32[]{:S(2)}) async-start(bf16[32,16,288]{2,1,0:T(8,128)(2,1)} %bitcast.5), calls=%async_computation.1 | async-start | bytes 786432 | tf_op jit(solution)/shard_map/all_to_all | solution.py:338
  56.6 9.0 %collective-permute-start.7 = (bf16[2,216,1152]{2,1,0:T(8,128)(2,1)}, bf16[2,216,1152]{2,1,0:T(8,128)(2,1)S(1)}, u32[]{:S(2)}, u32[]{:S(2)}) collective-permute-start(bf16[2,216,1152]{2,1,0:T(8,128)(2,1)} %collective-permute-done.6.refs_1_), channel_id=1, source_target_pairs={{0,2},{2,0},{4,6},{6,4},{8,10},{10,8},{12,14},{14,12},{16,18},{18,... | collective-permute-start | bytes 2985992 | tf_op jit(solution)/shard_map/ppermute | solution.py:292
  56.6 0.9 %copy-start.6 = (bf16[72,1152]{1,0:T(8,128)(2,1)S(1)}, bf16[72,1152]{1,0:T(8,128)(2,1)}, u32[]{:S(2)}) copy-start(bf16[72,1152]{1,0:T(8,128)(2,1)} %copy-done.5) | copy-start | bytes 497668
  57.5 0.9 %copy-start.9 = (bf16[72,1152]{1,0:T(8,128)(2,1)S(1)}, bf16[72,1152]{1,0:T(8,128)(2,1)}, u32[]{:S(2)}) copy-start(bf16[72,1152]{1,0:T(8,128)(2,1)} %copy-done.8) | copy-start | bytes 497668
  58.5 0.9 %copy-start.12 = (bf16[72,1152]{1,0:T(8,128)(2,1)S(1)}, bf16[72,1152]{1,0:T(8,128)(2,1)}, u32[]{:S(2)}) copy-start(bf16[72,1152]{1,0:T(8,128)(2,1)} %copy-done.11) | copy-start | bytes 497668
  65.6 18.3 %copy-start.1 = (bf16[128,2,1152]{2,1,0:T(2,128)(2,1)S(1)}, bf16[128,2,1152]{2,1,0:T(2,128)(2,1)}, u32[]{:S(2)}) copy-start(bf16[128,2,1152]{2,1,0:T(2,128)(2,1)} %x_ref.3) | copy-start | bytes 1769476
  65.6 18.2 %copy-start.7 = (bf16[72,1152]{1,0:T(8,128)(2,1)S(1)}, bf16[72,1152]{1,0:T(8,128)(2,1)}, u32[]{:S(2)}) copy-start(bf16[72,1152]{1,0:T(8,128)(2,1)} %copy-done.5) | copy-start | bytes 497668
  65.6 18.2 %copy-start.10 = (bf16[72,1152]{1,0:T(8,128)(2,1)S(1)}, bf16[72,1152]{1,0:T(8,128)(2,1)}, u32[]{:S(2)}) copy-start(bf16[72,1152]{1,0:T(8,128)(2,1)} %copy-done.8) | copy-start | bytes 497668
  65.6 18.2 %copy-start.13 = (bf16[72,1152]{1,0:T(8,128)(2,1)S(1)}, bf16[72,1152]{1,0:T(8,128)(2,1)}, u32[]{:S(2)}) copy-start(bf16[72,1152]{1,0:T(8,128)(2,1)} %copy-done.11) | copy-start | bytes 497668
  70.2 17.0 %all-to-all-start.2 = ((bf16[16,16,576]{2,1,0:T(8,128)(2,1)}), bf16[16,16,576]{2,1,0:T(8,128)(2,1)}, u32[]{:S(2)}, u32[]{:S(2)}) async-start(bf16[16,16,576]{2,1,0:T(8,128)(2,1)} %bitcast.8), calls=%async_computation.2 | async-start | bytes 655360 | tf_op jit(solution)/shard_map/all_to_all | solution.py:384
  76.6 7.2 %collective-permute-start.8 = (bf16[256,288]{1,0:T(8,128)(2,1)S(1)}, bf16[256,288]{1,0:T(8,128)(2,1)S(1)}, u32[]{:S(2)}, u32[]{:S(2)}) collective-permute-start(bf16[256,288]{1,0:T(8,128)(2,1)S(1)} %dynamic-slice_bitcast_fusion), channel_id=1, source_target_pairs={{0,1},{1,0},{2,3},{3,2},{4,5},{5,4},{6,7},{7,6},{8,9},{9,8},{10,11... | collective-permute-start | bytes 442376 | tf_op jit(solution)/shard_map/ppermute | solution.py:287
  86.4 0.8 copy-start.3

commit v10 on v5

--- a/solution.py
+++ b/solution.py
@@ -194,15 +194,18 @@
     return parts
 
 
-def kernel_temporal(o_ref, x_ref, w_ref, outbias_ref, mod_ref, b_ref, *refs, size, frames):
+def kernel_between(o_ref, x_ref, outbias_ref, mod_ref, *refs):
     space, core = coordinates()
-    pieces, (h_ref, out_ref) = refs[:-2], refs[-2:]
-    spaces, rows, _ = o_ref.shape
-    mask = temporal_mask(rows, size, frames)
+    pieces, h_ref = refs[:-1], refs[-1]
+    spaces = o_ref.shape[0]
     parts = parts_of(lambda k: o_ref[lax.rem(space - k + spaces, spaces)], pieces, core)
     y = middle(flat(x_ref), parts, outbias_ref[...].reshape(1, -1), mod_ref[2:3, :])
-    h = modulated(y.astype(F32), mod_ref[3:4, :], mod_ref[4:5, :]).astype(BF)
-    h_ref[...] = h
+    h_ref[...] = modulated(y.astype(F32), mod_ref[3:4, :], mod_ref[4:5, :]).astype(BF)
+
+
+def kernel_own(h_ref, w_ref, b_ref, out_ref, *, size, frames):
+    h = h_ref[...]
+    mask = temporal_mask(h.shape[0], size, frames)
     bias = bias_column(b_ref)
     for i in range(w_ref.shape[0]):
         out_ref[i] = temporal_head(w_ref[i], bias[i * 3 * HD : (i + 1) * 3 * HD], h, mask)
@@ -353,16 +356,19 @@
         params=SMALL,
     )(o_all, tokens, outbias_spatial, modulation, *o_home, *out_pieces)
     x_here = spread.reshape(rows // frames, frames, width)
-    h_here, o_own = pl.pallas_call(
-        functools.partial(kernel_temporal, size=size, frames=frames),
-        out_shape=(jax.ShapeDtypeStruct((rows, width), BF), jax.ShapeDtypeStruct((heads, HD, rows), F32)),
-        in_specs=[VMEM] * (6 + len(out_pieces)),
-        out_specs=(VMEM, VMEM),
+    h_here = call(
+        kernel_between, (rows, width), 4 + len(out_pieces), 2 * rows * width * cols * spaces, 3e6, params=SMALL
+    )(o_here, x_here, outbias_spatial, modulation, *out_pieces)
+    o_own = pl.pallas_call(
+        functools.partial(kernel_own, size=size, frames=frames),
+        out_shape=jax.ShapeDtypeStruct((heads, HD, rows), F32),
+        in_specs=[VMEM] * 3,
+        out_specs=VMEM,
         compiler_params=SMALL,
         cost_estimate=pl.CostEstimate(
-            flops=2 * rows * width * cols * (3 + spaces), bytes_accessed=5 * 10**6, transcendentals=0
+            flops=2 * rows * width * cols * 3, bytes_accessed=3 * 10**6, transcendentals=0
         ),
-    )(o_here, x_here, w_temporal, outbias_spatial, modulation, bias_temporal, *out_pieces)
+    )(h_here, w_temporal, bias_temporal)
     o_t = call(
         functools.partial(kernel_rest, size=size, frames=frames, spaces=spaces),
         (rows, spaces * cols),

time: 85.1 us -> 83.9 us (0.986)
  local copies, waits for them, and re-layouts: 2.42 us -> 0.88 us
    unnamed x18, local copies, waits for them, and re-layouts: 2.39 us -> 0.85 us
    pallas_call x1, Pallas kernels: 3.26 us -> 4.52 us  [local(): call(functools.partial(kernel_rest, size=size, frames=frames, spaces=spac...]
    pallas_call x1 -> x2, Pallas kernels: 5.98 us -> 5.12 us  [the longest x1 2.76 us: local(): call(kernel_between, (rows, width), 4 + len(out_pieces), 2 * rows * width...]
  transfers between devices with their start and end apart: 9 -> 9, of which waited for: 5 -> 4; matrix products, arithmetic and copies ran while one was open for 0% -> 0% of each run, Pallas kernels for 24% -> 24%
where the time goes in v10:
time: 83.9 us; the launch traced here: 83.4 us
  Pallas kernels  26.9 us (32%)
  blocking collectives  24.4 us (29%)
  starting transfers between devices  19.1 us (23%)
  waiting for transfers between devices  12.1 us (14%)
  local copies, waits for them, and re-layouts  0.88 us (1%)
    all_to_all x1, blocking collectives, local(): lax.all_to_all(after((o_all,), spread, *out_pieces)[0].reshape(spaces * t...  24.4 us
    ppermute x5, waiting for transfers between devices, across(): lax.ppermute(array, 'space', [(i, (i + k) % spaces) for i in range(spaces)])  8.69 us
    pallas_call x1, Pallas kernels, local(): call(kernel_spatial, (spaces, rows, cols), 4 + len(arrived), 10000000000....  7.52 us
    ppermute x5, starting transfers between devices, across(): lax.ppermute(array, 'space', [(i, (i + k) % spaces) for i in range(spaces)])  6.9 us
    all_to_all x1, starting transfers between devices, local(): lax.all_to_all(spread.reshape(times, size, frames, width), 'tm', 0, 0, ti...  6.48 us
    all_to_all x1, starting transfers between devices, local(): lax.all_to_all(o_t, 'tm', 0, 0, tiled=True).reshape(rows, spaces * cols)  5.56 us
    pallas_call x1, Pallas kernels, local(): pl.pallas_call(kernel_qkv, out_shape=tuple((jax.ShapeDtypeStruct(a, BF) f...  4.86 us
    pallas_call x1, Pallas kernels, local(): call(functools.partial(kernel_rest, size=size, frames=frames, spaces=spac...  4.52 us
  transfers between devices with their start and end apart: 9, of which 4 were waited for; matrix products, arithmetic and copies ran while one was open for 0% of the time, Pallas kernels for 24%

profile of v10, /device:TPU:0, one launch (start us, length us, event | category | flops | bytes accessed | tf_op | source)
XLA Modules:
  0.0 83.4 jit_solution(17020822027933478059)
XLA Ops:
  0.0 2.9 %collective-permute-start = (bf16[128,2,1152]{2,1,0:T(2,128)(2,1)}, bf16[128,2,1152]{2,1,0:T(2,128)(2,1)S(1)}, u32[]{:S(2)}, u32[]{:S(2)}) collective-permute-start(bf16[128,2,1152]{2,1,0:T(2,128)(2,1)} %x_ref.3), channel_id=1, source_target_pairs={{0,1},{1,0},{2,3},{3,2},{4,5},{5,4},{6,7},{7,6},{8,9},{9,8},{10,11... | collective-permute-start | bytes 1769480 | tf_op jit(solution)/shard_map/ppermute | solution.py:285
  2.9 0.0 collective-permute-start.1
  3.0 4.9 %shard_map.100 = (bf16[4,3,72,256]{3,2,1,0:T(8,128)(2,1)}, bf16[2,216,1152]{2,1,0:T(8,128)(2,1)}, bf16[144,1152]{1,0:T(8,128)(2,1)}) custom-call(bf16[128,2,1152]{2,1,0:T(2,128)(2,1)} %x_ref.3, bf16[4,216,1152]{2,1,0:T(8,128)(2,1)} %bitcast.18, bf16[4,216,1152]{2,1,0:T(8,128)(2,1)} %bitcast.14, bf16[288,1152]{1,0:T(8,128)(2,1)} %refs_1_.1, ...), custom_call_target="tpu_custom_call" | custom-call | flops 509607936 | bytes 3000000 | tf_op jit(solution)/shard_map/pallas_call | solution.py:294
  7.8 6.5 %all-to-all-start = ((bf16[16,8,2,1152]{3,2,1,0:T(2,128)(2,1)}), bf16[16,8,2,1152]{3,2,1,0:T(2,128)(2,1)}, u32[]{:S(2)}, u32[]{:S(2)}) async-start(bf16[16,8,2,1152]{3,2,1,0:T(2,128)(2,1)} %bitcast.4), calls=%async_computation | async-start | bytes 1179648 | tf_op jit(solution)/shard_map/all_to_all | solution.py:310
  14.3 2.2 %collective-permute-done.1.refs_0_ = f32[864]{0:T(1024)S(1)} collective-permute-done((f32[864]{0:T(1024)}, f32[864]{0:T(1024)S(1)}, u32[]{:S(2)}, u32[]{:S(2)}) %collective-permute-start.1) | collective-permute-done | bytes 3488 | tf_op jit(solution)/shard_map/ppermute | solution.py:285
  16.6 0.0 collective-permute-done.refs_0_
  16.6 0.8 copy-done.8
  17.4 1.7 %collective-permute-start.2 = (bf16[144,1152]{1,0:T(8,128)(2,1)}, bf16[144,1152]{1,0:T(8,128)(2,1)}, u32[]{:S(2)}, u32[]{:S(2)}) collective-permute-start(bf16[144,1152]{1,0:T(8,128)(2,1)} %get-tuple-element.19), channel_id=1, source_target_pairs={{0,1},{1,0},{2,3},{3,2},{4,5},{5,4},{6,7},{7,6},{8,9},{9,8},{10,11... | collective-permute-start | bytes 995336 | tf_op jit(solution)/shard_map/ppermute | solution.py:285
  19.1 7.5 %shard_map.101.o_own_ref = bf16[2,256,288]{2,1,0:T(8,128)(2,1)} custom-call(bf16[4,3,72,256]{3,2,1,0:T(8,128)(2,1)} %get-tuple-element.15.own_hbm, bf16[4,216,1152]{2,1,0:T(8,128)(2,1)} %bitcast.19, f32[6,1152]{1,0:T(8,128)} %mod_ref.9, f32[864]{0:T(1024)} %b_ref.4, bf16[128,2,1152]{2,1,0:T(2,128)(2,1)} %copy-done.8), custom_call_target="tpu_custom_call" | custom-call | flops 10000000000 | bytes 4000000 | tf_op jit(solution)/shard_map/pallas_call | solution.py:317
  26.7 0.0 copy-start
  26.7 0.0 copy-start.7
  26.7 0.0 collective-permute-done.2.refs_1_.refs_2_
  26.7 1.4 %collective-permute-start.4 = (bf16[2,216,1152]{2,1,0:T(8,128)(2,1)}, bf16[2,216,1152]{2,1,0:T(8,128)(2,1)}, u32[]{:S(2)}, u32[]{:S(2)}) collective-permute-start(bf16[2,216,1152]{2,1,0:T(8,128)(2,1)} %get-tuple-element.23), channel_id=1, source_target_pairs={{0,1},{1,0},{2,3},{3,2},{4,5},{5,4},{6,7},{7,6},{8,9},{9,8},{10,11... | collective-permute-start | bytes 2985992 | tf_op jit(solution)/shard_map/ppermute | solution.py:285
  28.1 0.0 collective-permute-start.3
  28.1 1.8 %all-to-all-done = bf16[16,8,2,1152]{3,2,1,0:T(2,128)(2,1)} async-done(((bf16[16,8,2,1152]{3,2,1,0:T(2,128)(2,1)}), bf16[16,8,2,1152]{3,2,1,0:T(2,128)(2,1)}, u32[]{:S(2)}, u32[]{:S(2)}) %all-to-all-start) | async-done | bytes 589856 | tf_op jit(solution)/shard_map/all_to_all | solution.py:310
  29.9 0.0 collective-permute-done.3.refs_2_.refs_3_
  30.0 24.4 %all_to_all.15 = bf16[32,16,288]{2,1,0:T(8,128)(2,1)S(1)} all-to-all(bf16[32,16,288]{2,1,0:T(8,128)(2,1)} %bitcast.16), channel_id=1, replica_groups=mesh['grp'=1,'tm'=16,'space'=2] {'space','tm'}, dimensions={0} | all-to-all | bytes 589824 | tf_op jit(solution)/shard_map/all_to_all | solution.py:338
  54.3 0.0 collective-permute-done.4.refs_1_
  54.3 0.1 collective-permute-start.5
  54.5 0.0 copy-done.1
  54.5 0.0 copy-done.5
  54.5 2.8 %shard_map.102.h_ref = bf16[256,1152]{1,0:T(8,128)(2,1)S(1)} custom-call(bf16[2,256,288]{2,1,0:T(8,128)(2,1)S(1)} %bitcast.17, bf16[128,2,1152]{2,1,0:T(2,128)(2,1)} %bitcast.7.x_ref, f32[1152]{0:T(1024)S(1)} %copy-done.5, f32[6,1152]{1,0:T(8,128)S(1)} %copy-done.4, bf16[288,1152]{1,0:T(8,128)(2,1)S(1)} %copy-done.1, ...), custom_call_target="tpu_custom_call" | custom-call | flops 339738624 | bytes 3000000 | tf_op jit(solution)/shard_map/pallas_call | solution.py:359
  57.3 2.4 %shard_map.103.own_ref = f32[4,72,256]{2,1,0:T(8,128)S(1)} custom-call(bf16[256,1152]{1,0:T(8,128)(2,1)S(1)} %shard_map.102.h_ref, bf16[4,216,1152]{2,1,0:T(8,128)(2,1)S(1)} %bitcast.15, f32[864]{0:T(1024)S(1)} %copy-done.7), custom_call_target="tpu_custom_call" | custom-call | flops 509607936 | bytes 3000000 | tf_op jit(solution)/shard_map/pallas_call | solution.py:362
  59.6 0.0 collective-permute-done.5.refs_2_
  59.7 4.5 %shard_map.104 = bf16[256,576]{1,0:T(8,128)(2,1)} custom-call(bf16[256,1152]{1,0:T(8,128)(2,1)S(1)} %shard_map.102.h_ref, f32[4,72,256]{2,1,0:T(8,128)S(1)} %shard_map.103.own_ref, f32[864]{0:T(1024)S(1)} %collective-permute-done.1.refs_0_, bf16[2,216,1152]{2,1,0:T(8,128)(2,1)} %collective-permute-done.4.refs_1_, ...), custom_call_target="tpu_custom_call" | custom-call | flops 509607936 | bytes 5000000 | tf_op jit(solution)/shard_map/pallas_call | solution.py:372
  64.2 5.6 %all-to-all-start.2 = ((bf16[16,16,576]{2,1,0:T(8,128)(2,1)}), bf16[16,16,576]{2,1,0:T(8,128)(2,1)}, u32[]{:S(2)}, u32[]{:S(2)}) async-start(bf16[16,16,576]{2,1,0:T(8,128)(2,1)} %bitcast.9), calls=%async_computation.2 | async-start | bytes 655360 | tf_op jit(solution)/shard_map/all_to_all | solution.py:384
  69.8 0.8 collective-permute-start.6
  70.6 6.4 %collective-permute-done.6.refs_0_ = bf16[256,288]{1,0:T(8,128)(2,1)S(1)} collective-permute-done((bf16[256,288]{1,0:T(8,128)(2,1)S(1)}, bf16[256,288]{1,0:T(8,128)(2,1)S(1)}, u32[]{:S(2)}, u32[]{:S(2)}) %collective-permute-start.6) | collective-permute-done | bytes 147488 | tf_op jit(solution)/shard_map/ppermute | solution.py:285
  77.0 2.3 %shard_map.105.y_ref = bf16[256,1152]{1,0:T(8,128)(2,1)S(1)} custom-call(bf16[2,256,288]{2,1,0:T(8,128)(2,1)S(1)} %copy-done.2, bf16[128,2,1152]{2,1,0:T(2,128)(2,1)} %x_ref.3, f32[1152]{0:T(1024)S(1)} %copy-done.5, f32[6,1152]{1,0:T(8,128)S(1)} %copy-done.4, bf16[256,288]{1,0:T(8,128)(2,1)S(1)} %collective-permute-done.6.refs_0_, ...), custom_call_target="tpu_custom_call" | custom-call | flops 339738624 | bytes 3000000 | tf_op jit(solution)/shard_map/pallas_call | solution.py:350
  79.4 1.5 %all-to-all-done.2 = bf16[16,16,576]{2,1,0:T(8,128)(2,1)} async-done(((bf16[16,16,576]{2,1,0:T(8,128)(2,1)}), bf16[16,16,576]{2,1,0:T(8,128)(2,1)}, u32[]{:S(2)}, u32[]{:S(2)}) %all-to-all-start.2) | async-done | bytes 294944 | tf_op jit(solution)/shard_map/all_to_all | solution.py:384
  80.9 0.0 copy-done.6
  80.9 2.5 %shard_map.106 = bf16[128,2,1152]{2,1,0:T(2,128)(2,1)} custom-call(bf16[256,576]{1,0:T(8,128)(2,1)} %bitcast.10.o_ref, bf16[256,1152]{1,0:T(8,128)(2,1)S(1)} %shard_map.105.y_ref, bf16[576,1152]{1,0:T(8,128)(2,1)S(1)} %copy-done.3, f32[1152]{0:T(1024)S(1)} %copy-done.6, f32[6,1152]{1,0:T(8,128)S(1)} %copy-done.4), custom_call_target="tpu_custom_call" | custom-call | flops 339738624 | bytes 3000000 | tf_op jit(solution)/shard_map/pallas_call | solution.py:386
  (13 shorter events, 0.0 us)
Async XLA Ops:
  0.0 16.6 %collective-permute-start = (bf16[128,2,1152]{2,1,0:T(2,128)(2,1)}, bf16[128,2,1152]{2,1,0:T(2,128)(2,1)S(1)}, u32[]{:S(2)}, u32[]{:S(2)}) collective-permute-start(bf16[128,2,1152]{2,1,0:T(2,128)(2,1)} %x_ref.3), channel_id=1, source_target_pairs={{0,1},{1,0},{2,3},{3,2},{4,5},{5,4},{6,7},{7,6},{8,9},{9,8},{10,11... | collective-permute-start | bytes 1769480 | tf_op jit(solution)/shard_map/ppermute | solution.py:285
  2.9 13.6 %collective-permute-start.1 = (f32[864]{0:T(1024)}, f32[864]{0:T(1024)S(1)}, u32[]{:S(2)}, u32[]{:S(2)}) collective-permute-start(f32[864]{0:T(1024)} %b_ref.5), channel_id=1, source_target_pairs={{0,1},{1,0},{2,3},{3,2},{4,5},{5,4},{6,7},{7,6},{8,9},{9,8},{10,11... | collective-permute-start | bytes 10376 | tf_op jit(solution)/shard_map/ppermute | solution.py:285
  7.8 22.1 %all-to-all-start = ((bf16[16,8,2,1152]{3,2,1,0:T(2,128)(2,1)}), bf16[16,8,2,1152]{3,2,1,0:T(2,128)(2,1)}, u32[]{:S(2)}, u32[]{:S(2)}) async-start(bf16[16,8,2,1152]{3,2,1,0:T(2,128)(2,1)} %bitcast.4), calls=%async_computation | async-start | bytes 1179648 | tf_op jit(solution)/shard_map/all_to_all | solution.py:310
  16.6 0.8 copy-start.8
  17.4 37.1 %copy-start.1 = (bf16[288,1152]{1,0:T(8,128)(2,1)S(1)}, bf16[288,1152]{1,0:T(8,128)(2,1)}, u32[]{:S(2)}) copy-start(bf16[288,1152]{1,0:T(8,128)(2,1)} %refs_1_.1) | copy-start | bytes 1990660
  17.4 37.1 %copy-start.4 = (f32[6,1152]{1,0:T(8,128)S(1)}, f32[6,1152]{1,0:T(8,128)}, u32[]{:S(2)}) copy-start(f32[6,1152]{1,0:T(8,128)} %mod_ref.9) | copy-start | bytes 82948
  17.4 37.1 %copy-start.5 = (f32[1152]{0:T(1024)S(1)}, f32[1152]{0:T(1024)}, u32[]{:S(2)}) copy-start(f32[1152]{0:T(1024)} %outbias_ref.4) | copy-start | bytes 13828
  17.4 9.3 %collective-permute-start.2 = (bf16[144,1152]{1,0:T(8,128)(2,1)}, bf16[144,1152]{1,0:T(8,128)(2,1)}, u32[]{:S(2)}, u32[]{:S(2)}) collective-permute-start(bf16[144,1152]{1,0:T(8,128)(2,1)} %get-tuple-element.19), channel_id=1, source_target_pairs={{0,1},{1,0},{2,3},{3,2},{4,5},{5,4},{6,7},{7,6},{8,9},{9,8},{10,11... | collective-permute-start | bytes 995336 | tf_op jit(solution)/shard_map/ppermute | solution.py:285
  26.7 30.6 %copy-start = (bf16[1152,864]{0,1:T(8,128)(2,1)S(1)}, bf16[1152,864]{0,1:T(8,128)(2,1)}, u32[]{:S(2)}) copy-start(bf16[1152,864]{0,1:T(8,128)(2,1)} %param.16) | copy-start | bytes 5971972
  26.7 30.6 %copy-start.7 = (f32[864]{0:T(1024)S(1)}, f32[864]{0:T(1024)}, u32[]{:S(2)}) copy-start(f32[864]{0:T(1024)} %b_ref.5) | copy-start | bytes 10372
  26.7 27.6 %collective-permute-start.4 = (bf16[2,216,1152]{2,1,0:T(8,128)(2,1)}, bf16[2,216,1152]{2,1,0:T(8,128)(2,1)}, u32[]{:S(2)}, u32[]{:S(2)}) collective-permute-start(bf16[2,216,1152]{2,1,0:T(8,128)(2,1)} %get-tuple-element.23), channel_id=1, source_target_pairs={{0,1},{1,0},{2,3},{3,2},{4,5},{5,4},{6,7},{7,6},{8,9},{9,8},{10,11... | collective-permute-start | bytes 2985992 | tf_op jit(solution)/shard_map/ppermute | solution.py:285
  28.1 1.8 %collective-permute-start.3 = (bf16[144,1152]{1,0:T(8,128)(2,1)}, bf16[144,1152]{1,0:T(8,128)(2,1)S(1)}, u32[]{:S(2)}, u32[]{:S(2)}) collective-permute-start(bf16[144,1152]{1,0:T(8,128)(2,1)} %collective-permute-done.2.refs_1_.refs_2_), channel_id=1, source_target_pairs={{0,2},{2,0},{4,6},{6,4},{8,10},{10,8},{12,14},{14,12},{16,18},{18,... | collective-permute-start | bytes 995336 | tf_op jit(solution)/shard_map/ppermute | solution.py:288
  54.3 5.3 %collective-permute-start.5 = (bf16[2,216,1152]{2,1,0:T(8,128)(2,1)}, bf16[2,216,1152]{2,1,0:T(8,128)(2,1)S(1)}, u32[]{:S(2)}, u32[]{:S(2)}) collective-permute-start(bf16[2,216,1152]{2,1,0:T(8,128)(2,1)} %collective-permute-done.4.refs_1_), channel_id=1, source_target_pairs={{0,2},{2,0},{4,6},{6,4},{8,10},{10,8},{12,14},{14,12},{16,18},{18,... | collective-permute-start | bytes 2985992 | tf_op jit(solution)/shard_map/ppermute | solution.py:288
  59.6 10.1 %copy-start.2 = (bf16[2,256,288]{2,1,0:T(8,128)(2,1)S(1)}, bf16[2,256,288]{2,1,0:T(8,128)(2,1)}, u32[]{:S(2)}) copy-start(bf16[2,256,288]{2,1,0:T(8,128)(2,1)} %shard_map.101.o_own_ref) | copy-start | bytes 884740
  64.2 16.7 %copy-start.3 = (bf16[576,1152]{1,0:T(8,128)(2,1)S(1)}, bf16[576,1152]{1,0:T(8,128)(2,1)}, u32[]{:S(2)}) copy-start(bf16[576,1152]{1,0:T(8,128)(2,1)} %w_ref.1) | copy-start | bytes 3981316
  64.2 16.7 %copy-start.6 = (f32[1152]{0:T(1024)S(1)}, f32[1152]{0:T(1024)}, u32[]{:S(2)}) copy-start(f32[1152]{0:T(1024)} %outbias_ref.5) | copy-start | bytes 13828
  64.2 16.7 %all-to-all-start.2 = ((bf16[16,16,576]{2,1,0:T(8,128)(2,1)}), bf16[16,16,576]{2,1,0:T(8,128)(2,1)}, u32[]{:S(2)}, u32[]{:S(2)}) async-start(bf16[16,16,576]{2,1,0:T(8,128)(2,1)} %bitcast.9), calls=%async_computation.2 | async-start | bytes 655360 | tf_op jit(solution)/shard_map/all_to_all | solution.py:384
  69.8 7.2 %collective-permute-start.6 = (bf16[256,288]{1,0:T(8,128)(2,1)S(1)}, bf16[256,288]{1,0:T(8,128)(2,1)S(1)}, u32[]{:S(2)}, u32[]{:S(2)}) collective-permute-start(bf16[256,288]{1,0:T(8,128)(2,1)S(1)} %dynamic-slice_bitcast_fusion), channel_id=1, source_target_pairs={{0,1},{1,0},{2,3},{3,2},{4,5},{5,4},{6,7},{7,6},{8,9},{9,8},{10,11... | collective-permute-start | bytes 442376 | tf_op jit(solution)/shard_map/ppermute | solution.py:285

commit v11 on v10

--- a/solution.py
+++ b/solution.py
@@ -16,6 +16,7 @@
 
 VMEM = pl.BlockSpec(memory_space=pltpu.VMEM)
 ANY = pl.BlockSpec(memory_space=pl.ANY)
+LARGE = pltpu.CompilerParams(vmem_limit_bytes=62 * 1024 * 1024)
 SMALL = pltpu.CompilerParams(vmem_limit_bytes=16 * 1024 * 1024)
 PARAMS = pltpu.CompilerParams(vmem_limit_bytes=63 * 1024 * 1024)
 
@@ -212,7 +213,8 @@
 
 
 def kernel_rest(h_ref, own_ref, *refs, size, frames, spaces):
-    b_refs, w_refs, (out_ref, turn_ref) = refs[: spaces - 1], refs[spaces - 1 : -2], refs[-2:]
+    b_refs, w_hbms, (out_ref, turn_ref, w_ref, sems) = refs[: spaces - 1], refs[spaces - 1 : -4], refs[-4:]
+    copies = fetch(w_hbms, [w_ref.at[n] for n in range(len(w_hbms))], sems)
     space, core = coordinates()
     h = h_ref[...]
     rows = h.shape[0]
@@ -221,15 +223,16 @@
     half = heads // 2
     for i in range(heads):
         turn_ref[space * heads + i] = own_ref[i]
-    for n, w_ref in enumerate(w_refs):
+    for n in range(len(w_hbms)):
         shift = n // 2 + 1
         bias = bias_column(b_refs[shift - 1])
         second = (core == 0) == (n % 2 == 1)
         within = jnp.where(second, half, 0)
         group = lax.rem(space - shift + spaces, spaces)
         bias = jnp.where(second, bias[half * 3 * HD :], bias[: half * 3 * HD])
+        copies[n].wait()
         for i in range(half):
-            o_t = temporal_head(w_ref[i], bias[i * 3 * HD : (i + 1) * 3 * HD], h, mask)
+            o_t = temporal_head(w_ref[n, i], bias[i * 3 * HD : (i + 1) * 3 * HD], h, mask)
             turn_ref[group * heads + within + i] = o_t
     out_ref[...] = turn_ref[...].reshape(-1, rows).T.astype(BF)
 
@@ -327,6 +330,7 @@
             pltpu.SemaphoreType.DMA((heads + 1,)),
         ],
         (0, 1),
+        params=LARGE,
     )(own, w_spatial, modulation, bias_spatial, *arrived)
 
     (my_heads,) = after((my_heads,), o_all, *direct_out)
@@ -377,7 +381,10 @@
         5e6,
         [
             pltpu.VMEM((spaces * heads, HD, rows), F32),
+            pltpu.VMEM((len(other_heads), half, 3 * HD, width), BF),
+            pltpu.SemaphoreType.DMA((len(other_heads),)),
         ],
+        range(1 + spaces, 1 + spaces + len(other_heads)),
         params=SMALL,
     )(h_here, o_own, *other_bias, *other_heads)
     o_t = o_t.reshape(times, frames * size, spaces * cols)

time: 83.9 us -> 83.9 us (level)
    pallas_call x1, Pallas kernels: 2.49 us -> 1.52 us  [local(): call(kernel_final, (patches, frames, width), 5, 2 * rows * width * cols *...]
  transfers between devices with their start and end apart: 9 -> 9, of which waited for: 4 -> 5; matrix products, arithmetic and copies ran while one was open for 0% -> 0% of each run, Pallas kernels for 24% -> 24%
where the time goes in v11:
time: 83.9 us; the launch traced here: 83.3 us
  Pallas kernels  26.3 us (31%)
  blocking collectives  23.9 us (28%)
  starting transfers between devices  19 us (23%)
  waiting for transfers between devices  12.5 us (15%)
  local copies, waits for them, and re-layouts  1.38 us (2%)
    all_to_all x1, blocking collectives, local(): lax.all_to_all(after((o_all,), spread, *out_pieces)[0].reshape(spaces * t...  23.9 us
    ppermute x5, waiting for transfers between devices, across(): lax.ppermute(array, 'space', [(i, (i + k) % spaces) for i in range(spaces)])  8.85 us
    pallas_call x1, Pallas kernels, local(): call(kernel_spatial, (spaces, rows, cols), 4 + len(arrived), 10000000000....  7.51 us
    ppermute x5, starting transfers between devices, across(): lax.ppermute(array, 'space', [(i, (i + k) % spaces) for i in range(spaces)])  7.07 us
    all_to_all x1, starting transfers between devices, local(): lax.all_to_all(spread.reshape(times, size, frames, width), 'tm', 0, 0, ti...  6.43 us
    all_to_all x1, starting transfers between devices, local(): lax.all_to_all(o_t, 'tm', 0, 0, tiled=True).reshape(rows, spaces * cols)  5.39 us
    pallas_call x1, Pallas kernels, local(): call(functools.partial(kernel_rest, size=size, frames=frames, spaces=spac...  5.04 us
    pallas_call x1, Pallas kernels, local(): pl.pallas_call(kernel_qkv, out_shape=tuple((jax.ShapeDtypeStruct(a, BF) f...  4.82 us
  transfers between devices with their start and end apart: 9, of which 5 were waited for; matrix products, arithmetic and copies ran while one was open for 0% of the time, Pallas kernels for 24%

profile of v11, /device:TPU:0, one launch (start us, length us, event | category | flops | bytes accessed | tf_op | source)
XLA Modules:
  0.0 83.3 jit_solution(577485726877040575)
XLA Ops:
  0.0 2.9 %collective-permute-start = (bf16[128,2,1152]{2,1,0:T(2,128)(2,1)}, bf16[128,2,1152]{2,1,0:T(2,128)(2,1)}, u32[]{:S(2)}, u32[]{:S(2)}) collective-permute-start(bf16[128,2,1152]{2,1,0:T(2,128)(2,1)} %x_ref.3), channel_id=1, source_target_pairs={{0,1},{1,0},{2,3},{3,2},{4,5},{5,4},{6,7},{7,6},{8,9},{9,8},{10,11... | collective-permute-start | bytes 1769480 | tf_op jit(solution)/shard_map/ppermute | solution.py:288
  2.9 0.0 collective-permute-start.1
  3.0 4.8 %shard_map.100 = (bf16[4,3,72,256]{3,2,1,0:T(8,128)(2,1)}, bf16[2,216,1152]{2,1,0:T(8,128)(2,1)}, bf16[144,1152]{1,0:T(8,128)(2,1)}) custom-call(bf16[128,2,1152]{2,1,0:T(2,128)(2,1)} %x_ref.3, bf16[4,216,1152]{2,1,0:T(8,128)(2,1)} %bitcast.20, bf16[4,216,1152]{2,1,0:T(8,128)(2,1)} %bitcast.14, bf16[288,1152]{1,0:T(8,128)(2,1)} %refs_1_.1, ...), custom_call_target="tpu_custom_call" | custom-call | flops 509607936 | bytes 3000000 | tf_op jit(solution)/shard_map/pallas_call | solution.py:297
  7.8 6.4 %all-to-all-start = ((bf16[16,8,2,1152]{3,2,1,0:T(2,128)(2,1)}), bf16[16,8,2,1152]{3,2,1,0:T(2,128)(2,1)S(1)}, u32[]{:S(2)}, u32[]{:S(2)}) async-start(bf16[16,8,2,1152]{3,2,1,0:T(2,128)(2,1)} %bitcast.4), calls=%async_computation | async-start | bytes 1179648 | tf_op jit(solution)/shard_map/all_to_all | solution.py:313
  14.2 2.4 %collective-permute-done.1.refs_0_ = f32[864]{0:T(1024)S(1)} collective-permute-done((f32[864]{0:T(1024)}, f32[864]{0:T(1024)S(1)}, u32[]{:S(2)}, u32[]{:S(2)}) %collective-permute-start.1) | collective-permute-done | bytes 3488 | tf_op jit(solution)/shard_map/ppermute | solution.py:288
  16.6 0.0 collective-permute-done.refs_0_
  16.6 1.8 %collective-permute-start.2 = (bf16[144,1152]{1,0:T(8,128)(2,1)}, bf16[144,1152]{1,0:T(8,128)(2,1)}, u32[]{:S(2)}, u32[]{:S(2)}) collective-permute-start(bf16[144,1152]{1,0:T(8,128)(2,1)} %get-tuple-element.19), channel_id=1, source_target_pairs={{0,1},{1,0},{2,3},{3,2},{4,5},{5,4},{6,7},{7,6},{8,9},{9,8},{10,11... | collective-permute-start | bytes 995336 | tf_op jit(solution)/shard_map/ppermute | solution.py:288
  18.4 7.5 %shard_map.101.o_own_ref = bf16[2,256,288]{2,1,0:T(8,128)(2,1)} custom-call(bf16[4,3,72,256]{3,2,1,0:T(8,128)(2,1)} %get-tuple-element.15.own_hbm, bf16[4,216,1152]{2,1,0:T(8,128)(2,1)} %bitcast.21, f32[6,1152]{1,0:T(8,128)} %mod_ref.9, f32[864]{0:T(1024)} %b_ref.4, bf16[128,2,1152]{2,1,0:T(2,128)(2,1)} %collective-permute-done.refs_0_), custom_call_target="tpu_custom_call" | custom-call | flops 10000000000 | bytes 4000000 | tf_op jit(solution)/shard_map/pallas_call | solution.py:320
  26.0 0.0 copy-start
  26.0 0.0 copy-start.7
  26.0 0.1 collective-permute-done.2.refs_1_.refs_2_
  26.0 1.4 %collective-permute-start.4 = (bf16[2,216,1152]{2,1,0:T(8,128)(2,1)}, bf16[2,216,1152]{2,1,0:T(8,128)(2,1)}, u32[]{:S(2)}, u32[]{:S(2)}) collective-permute-start(bf16[2,216,1152]{2,1,0:T(8,128)(2,1)} %get-tuple-element.23), channel_id=1, source_target_pairs={{0,1},{1,0},{2,3},{3,2},{4,5},{5,4},{6,7},{7,6},{8,9},{9,8},{10,11... | collective-permute-start | bytes 2985992 | tf_op jit(solution)/shard_map/ppermute | solution.py:288
  27.5 0.0 collective-permute-start.3
  27.5 2.3 %all-to-all-done = bf16[16,8,2,1152]{3,2,1,0:T(2,128)(2,1)S(1)} async-done(((bf16[16,8,2,1152]{3,2,1,0:T(2,128)(2,1)}), bf16[16,8,2,1152]{3,2,1,0:T(2,128)(2,1)S(1)}, u32[]{:S(2)}, u32[]{:S(2)}) %all-to-all-start) | async-done | bytes 589856 | tf_op jit(solution)/shard_map/all_to_all | solution.py:313
  29.8 0.0 collective-permute-done.3.refs_2_.refs_3_
  29.8 23.9 %all_to_all.15 = bf16[32,16,288]{2,1,0:T(8,128)(2,1)S(1)} all-to-all(bf16[32,16,288]{2,1,0:T(8,128)(2,1)} %bitcast.16), channel_id=1, replica_groups=mesh['grp'=1,'tm'=16,'space'=2] {'space','tm'}, dimensions={0} | all-to-all | bytes 589824 | tf_op jit(solution)/shard_map/all_to_all | solution.py:342
  53.7 0.0 collective-permute-done.4.refs_1_
  53.7 0.1 collective-permute-start.5
  53.8 2.7 %shard_map.102.h_ref = bf16[256,1152]{1,0:T(8,128)(2,1)S(1)} custom-call(bf16[2,256,288]{2,1,0:T(8,128)(2,1)S(1)} %bitcast.18, bf16[128,2,1152]{2,1,0:T(2,128)(2,1)S(1)} %bitcast.17, f32[1152]{0:T(1024)S(1)} %copy-done.5, f32[6,1152]{1,0:T(8,128)S(1)} %copy-done.4, bf16[288,1152]{1,0:T(8,128)(2,1)S(1)} %copy-done.1, ...), custom_call_target="tpu_custom_call" | custom-call | flops 339738624 | bytes 3000000 | tf_op jit(solution)/shard_map/pallas_call | solution.py:363
  56.5 2.4 %shard_map.103.own_ref = f32[4,72,256]{2,1,0:T(8,128)S(1)} custom-call(bf16[256,1152]{1,0:T(8,128)(2,1)S(1)} %shard_map.102.h_ref, bf16[4,216,1152]{2,1,0:T(8,128)(2,1)S(1)} %bitcast.15, f32[864]{0:T(1024)S(1)} %copy-done.7), custom_call_target="tpu_custom_call" | custom-call | flops 509607936 | bytes 3000000 | tf_op jit(solution)/shard_map/pallas_call | solution.py:366
  58.9 0.0 copy-start.2
  58.9 0.0 collective-permute-done.5.refs_2_
  58.9 5.0 %shard_map.104 = bf16[256,576]{1,0:T(8,128)(2,1)} custom-call(bf16[256,1152]{1,0:T(8,128)(2,1)S(1)} %shard_map.102.h_ref, f32[4,72,256]{2,1,0:T(8,128)S(1)} %shard_map.103.own_ref, f32[864]{0:T(1024)S(1)} %collective-permute-done.1.refs_0_, bf16[2,216,1152]{2,1,0:T(8,128)(2,1)} %collective-permute-done.4.refs_1_, ...), custom_call_target="tpu_custom_call" | custom-call | flops 509607936 | bytes 5000000 | tf_op jit(solution)/shard_map/pallas_call | solution.py:376
  63.9 0.0 copy-start.6
  64.0 5.4 %all-to-all-start.2 = ((bf16[16,16,576]{2,1,0:T(8,128)(2,1)}), bf16[16,16,576]{2,1,0:T(8,128)(2,1)S(1)}, u32[]{:S(2)}, u32[]{:S(2)}) async-start(bf16[16,16,576]{2,1,0:T(8,128)(2,1)} %bitcast.9), calls=%async_computation.2 | async-start | bytes 655360 | tf_op jit(solution)/shard_map/all_to_all | solution.py:391
  69.4 0.9 %collective-permute-start.6 = (bf16[256,288]{1,0:T(8,128)(2,1)S(1)}, bf16[256,288]{1,0:T(8,128)(2,1)S(1)}, u32[]{:S(2)}, u32[]{:S(2)}) collective-permute-start(bf16[256,288]{1,0:T(8,128)(2,1)S(1)} %dynamic-slice_bitcast_fusion), channel_id=1, source_target_pairs={{0,1},{1,0},{2,3},{3,2},{4,5},{5,4},{6,7},{7,6},{8,9},{9,8},{10,11... | collective-permute-start | bytes 442376 | tf_op jit(solution)/shard_map/ppermute | solution.py:288
  70.3 6.4 %collective-permute-done.6.refs_0_ = bf16[256,288]{1,0:T(8,128)(2,1)S(1)} collective-permute-done((bf16[256,288]{1,0:T(8,128)(2,1)S(1)}, bf16[256,288]{1,0:T(8,128)(2,1)S(1)}, u32[]{:S(2)}, u32[]{:S(2)}) %collective-permute-start.6) | collective-permute-done | bytes 147488 | tf_op jit(solution)/shard_map/ppermute | solution.py:288
  76.7 2.4 %shard_map.105.y_ref = bf16[256,1152]{1,0:T(8,128)(2,1)S(1)} custom-call(bf16[2,256,288]{2,1,0:T(8,128)(2,1)S(1)} %copy-done.2, bf16[128,2,1152]{2,1,0:T(2,128)(2,1)} %x_ref.3, f32[1152]{0:T(1024)S(1)} %copy-done.5, f32[6,1152]{1,0:T(8,128)S(1)} %copy-done.4, bf16[256,288]{1,0:T(8,128)(2,1)S(1)} %collective-permute-done.6.refs_0_, ...), custom_call_target="tpu_custom_call" | custom-call | flops 339738624 | bytes 3000000 | tf_op jit(solution)/shard_map/pallas_call | solution.py:354
  79.1 1.4 %all-to-all-done.2 = bf16[16,16,576]{2,1,0:T(8,128)(2,1)S(1)} async-done(((bf16[16,16,576]{2,1,0:T(8,128)(2,1)}), bf16[16,16,576]{2,1,0:T(8,128)(2,1)S(1)}, u32[]{:S(2)}, u32[]{:S(2)}) %all-to-all-start.2) | async-done | bytes 294944 | tf_op jit(solution)/shard_map/all_to_all | solution.py:391
  80.5 0.0 copy-done.6
  80.5 1.3 %copy-done.3 = bf16[576,1152]{1,0:T(8,128)(2,1)S(1)} copy-done((bf16[576,1152]{1,0:T(8,128)(2,1)S(1)}, bf16[576,1152]{1,0:T(8,128)(2,1)}, u32[]{:S(2)}) %copy-start.3) | copy-done | bytes 1327128
  81.8 1.5 %shard_map.106 = bf16[128,2,1152]{2,1,0:T(2,128)(2,1)} custom-call(bf16[256,576]{1,0:T(8,128)(2,1)S(1)} %bitcast.19, bf16[256,1152]{1,0:T(8,128)(2,1)S(1)} %shard_map.105.y_ref, bf16[576,1152]{1,0:T(8,128)(2,1)S(1)} %copy-done.3, f32[1152]{0:T(1024)S(1)} %copy-done.6, f32[6,1152]{1,0:T(8,128)S(1)} %copy-done.4), custom_call_target="tpu_custom_call" | custom-call | flops 339738624 | bytes 3000000 | tf_op jit(solution)/shard_map/pallas_call | solution.py:393
  (11 shorter events, 0.0 us)
Async XLA Ops:
  0.0 16.6 %collective-permute-start = (bf16[128,2,1152]{2,1,0:T(2,128)(2,1)}, bf16[128,2,1152]{2,1,0:T(2,128)(2,1)}, u32[]{:S(2)}, u32[]{:S(2)}) collective-permute-start(bf16[128,2,1152]{2,1,0:T(2,128)(2,1)} %x_ref.3), channel_id=1, source_target_pairs={{0,1},{1,0},{2,3},{3,2},{4,5},{5,4},{6,7},{7,6},{8,9},{9,8},{10,11... | collective-permute-start | bytes 1769480 | tf_op jit(solution)/shard_map/ppermute | solution.py:288
  2.9 13.7 %collective-permute-start.1 = (f32[864]{0:T(1024)}, f32[864]{0:T(1024)S(1)}, u32[]{:S(2)}, u32[]{:S(2)}) collective-permute-start(f32[864]{0:T(1024)} %b_ref.5), channel_id=1, source_target_pairs={{0,1},{1,0},{2,3},{3,2},{4,5},{5,4},{6,7},{7,6},{8,9},{9,8},{10,11... | collective-permute-start | bytes 10376 | tf_op jit(solution)/shard_map/ppermute | solution.py:288
  7.8 22.0 %all-to-all-start = ((bf16[16,8,2,1152]{3,2,1,0:T(2,128)(2,1)}), bf16[16,8,2,1152]{3,2,1,0:T(2,128)(2,1)S(1)}, u32[]{:S(2)}, u32[]{:S(2)}) async-start(bf16[16,8,2,1152]{3,2,1,0:T(2,128)(2,1)} %bitcast.4), calls=%async_computation | async-start | bytes 1179648 | tf_op jit(solution)/shard_map/all_to_all | solution.py:313
  16.6 37.2 %copy-start.1 = (bf16[288,1152]{1,0:T(8,128)(2,1)S(1)}, bf16[288,1152]{1,0:T(8,128)(2,1)}, u32[]{:S(2)}) copy-start(bf16[288,1152]{1,0:T(8,128)(2,1)} %refs_1_.1) | copy-start | bytes 1990660
  16.6 37.2 %copy-start.4 = (f32[6,1152]{1,0:T(8,128)S(1)}, f32[6,1152]{1,0:T(8,128)}, u32[]{:S(2)}) copy-start(f32[6,1152]{1,0:T(8,128)} %mod_ref.9) | copy-start | bytes 82948
  16.6 37.2 %copy-start.5 = (f32[1152]{0:T(1024)S(1)}, f32[1152]{0:T(1024)}, u32[]{:S(2)}) copy-start(f32[1152]{0:T(1024)} %outbias_ref.4) | copy-start | bytes 13828
  16.6 9.4 %collective-permute-start.2 = (bf16[144,1152]{1,0:T(8,128)(2,1)}, bf16[144,1152]{1,0:T(8,128)(2,1)}, u32[]{:S(2)}, u32[]{:S(2)}) collective-permute-start(bf16[144,1152]{1,0:T(8,128)(2,1)} %get-tuple-element.19), channel_id=1, source_target_pairs={{0,1},{1,0},{2,3},{3,2},{4,5},{5,4},{6,7},{7,6},{8,9},{9,8},{10,11... | collective-permute-start | bytes 995336 | tf_op jit(solution)/shard_map/ppermute | solution.py:288
  26.0 30.5 %copy-start = (bf16[1152,864]{0,1:T(8,128)(2,1)S(1)}, bf16[1152,864]{0,1:T(8,128)(2,1)}, u32[]{:S(2)}) copy-start(bf16[1152,864]{0,1:T(8,128)(2,1)} %param.16) | copy-start | bytes 5971972
  26.0 30.5 %copy-start.7 = (f32[864]{0:T(1024)S(1)}, f32[864]{0:T(1024)}, u32[]{:S(2)}) copy-start(f32[864]{0:T(1024)} %b_ref.5) | copy-start | bytes 10372
  26.0 27.6 %collective-permute-start.4 = (bf16[2,216,1152]{2,1,0:T(8,128)(2,1)}, bf16[2,216,1152]{2,1,0:T(8,128)(2,1)}, u32[]{:S(2)}, u32[]{:S(2)}) collective-permute-start(bf16[2,216,1152]{2,1,0:T(8,128)(2,1)} %get-tuple-element.23), channel_id=1, source_target_pairs={{0,1},{1,0},{2,3},{3,2},{4,5},{5,4},{6,7},{7,6},{8,9},{9,8},{10,11... | collective-permute-start | bytes 2985992 | tf_op jit(solution)/shard_map/ppermute | solution.py:288
  27.5 2.3 %collective-permute-start.3 = (bf16[144,1152]{1,0:T(8,128)(2,1)}, bf16[144,1152]{1,0:T(8,128)(2,1)}, u32[]{:S(2)}, u32[]{:S(2)}) collective-permute-start(bf16[144,1152]{1,0:T(8,128)(2,1)} %collective-permute-done.2.refs_1_.refs_2_), channel_id=1, source_target_pairs={{0,2},{2,0},{4,6},{6,4},{8,10},{10,8},{12,14},{14,12},{16,18},{18,... | collective-permute-start | bytes 995336 | tf_op jit(solution)/shard_map/ppermute | solution.py:291
  53.7 5.2 %collective-permute-start.5 = (bf16[2,216,1152]{2,1,0:T(8,128)(2,1)}, bf16[2,216,1152]{2,1,0:T(8,128)(2,1)S(1)}, u32[]{:S(2)}, u32[]{:S(2)}) collective-permute-start(bf16[2,216,1152]{2,1,0:T(8,128)(2,1)} %collective-permute-done.4.refs_1_), channel_id=1, source_target_pairs={{0,2},{2,0},{4,6},{6,4},{8,10},{10,8},{12,14},{14,12},{16,18},{18,... | collective-permute-start | bytes 2985992 | tf_op jit(solution)/shard_map/ppermute | solution.py:291
  58.9 10.5 %copy-start.2 = (bf16[2,256,288]{2,1,0:T(8,128)(2,1)S(1)}, bf16[2,256,288]{2,1,0:T(8,128)(2,1)}, u32[]{:S(2)}) copy-start(bf16[2,256,288]{2,1,0:T(8,128)(2,1)} %shard_map.101.o_own_ref) | copy-start | bytes 884740
  63.9 16.5 %copy-start.6 = (f32[1152]{0:T(1024)S(1)}, f32[1152]{0:T(1024)}, u32[]{:S(2)}) copy-start(f32[1152]{0:T(1024)} %outbias_ref.5) | copy-start | bytes 13828
  64.0 16.5 %all-to-all-start.2 = ((bf16[16,16,576]{2,1,0:T(8,128)(2,1)}), bf16[16,16,576]{2,1,0:T(8,128)(2,1)S(1)}, u32[]{:S(2)}, u32[]{:S(2)}) async-start(bf16[16,16,576]{2,1,0:T(8,128)(2,1)} %bitcast.9), calls=%async_computation.2 | async-start | bytes 655360 | tf_op jit(solution)/shard_map/all_to_all | solution.py:391
  69.4 7.3 %collective-permute-start.6 = (bf16[256,288]{1,0:T(8,128)(2,1)S(1)}, bf16[256,288]{1,0:T(8,128)(2,1)S(1)}, u32[]{:S(2)}, u32[]{:S(2)}) collective-permute-start(bf16[256,288]{1,0:T(8,128)(2,1)S(1)} %dynamic-slice_bitcast_fusion), channel_id=1, source_target_pairs={{0,1},{1,0},{2,3},{3,2},{4,5},{5,4},{6,7},{7,6},{8,9},{9,8},{10,11... | collective-permute-start | bytes 442376 | tf_op jit(solution)/shard_map/ppermute | solution.py:288
  80.5 1.3 %copy-start.3 = (bf16[576,1152]{1,0:T(8,128)(2,1)S(1)}, bf16[576,1152]{1,0:T(8,128)(2,1)}, u32[]{:S(2)}) copy-start(bf16[576,1152]{1,0:T(8,128)(2,1)} %w_ref.1) | copy-start | bytes 3981316

commit v12 on v10

--- a/solution.py
+++ b/solution.py
@@ -16,6 +16,7 @@
 
 VMEM = pl.BlockSpec(memory_space=pltpu.VMEM)
 ANY = pl.BlockSpec(memory_space=pl.ANY)
+LARGE = pltpu.CompilerParams(vmem_limit_bytes=62 * 1024 * 1024)
 SMALL = pltpu.CompilerParams(vmem_limit_bytes=16 * 1024 * 1024)
 PARAMS = pltpu.CompilerParams(vmem_limit_bytes=63 * 1024 * 1024)
 
@@ -306,11 +307,10 @@
         ),
     )(tokens, w_spatial, w_temporal, out_spatial, modulation, bias_spatial)
 
-    (spread,) = after((tokens,), own)
-    spread = lax.all_to_all(spread.reshape(times, size, frames, width), "tm", 0, 0, tiled=True)
+    spread = lax.all_to_all(tokens.reshape(times, size, frames, width), "tm", 0, 0, tiled=True)
 
     other_bias = [across(bias_temporal, k) for k in range(1, spaces)]
-    (my_out,) = after((my_out,), *other_bias, *arrived)
+    (my_out,) = after((my_out,), own)
     arrived = [after((a,), own)[0] for a in arrived]
     direct_out = [across(my_out, k) for k in range(1, spaces)]
 
@@ -327,6 +327,7 @@
             pltpu.SemaphoreType.DMA((heads + 1,)),
         ],
         (0, 1),
+        params=LARGE,
     )(own, w_spatial, modulation, bias_spatial, *arrived)
 
     (my_heads,) = after((my_heads,), o_all, *direct_out)

time: 83.9 us -> 84.5 us (level)
  blocking collectives: 24.4 us -> 0 us
  waiting for transfers between devices: 12.1 us -> 31.6 us
  starting transfers between devices: 19.1 us -> 24.3 us
  local copies, waits for them, and re-layouts: 0.88 us -> 3.1 us
  Pallas kernels: 26.9 us -> 24.7 us
    all_to_all x1 -> x0, blocking collectives: 24.4 us -> none  [local(): lax.all_to_all(after((o_all,), spread, *out_pieces)[0].reshape(spaces * t...]
    ppermute x5, waiting for transfers between devices: 8.69 us -> 26.5 us  [across(): lax.ppermute(array, 'space', [(i, (i + k) % spaces) for i in range(spaces)])]
    all_to_all x1 -> x2, starting transfers between devices: 6.48 us -> 11.1 us  [the longest x1 5.98 us: local(): lax.all_to_all(tokens.reshape(times, size, frames, width), 'tm', 0, 0, ti...]
    unnamed x18 -> x24, local copies, waits for them, and re-layouts: 0.85 us -> 3.07 us
    ppermute x2, waiting for transfers between devices: 0.03 us -> 1.63 us  [beside(): return lax.ppermute(array, 'tm', [(i, i ^ 1) for i in range(times)])]
    pallas_call x1, Pallas kernels: 2.34 us -> 1.21 us  [local(): call(kernel_home, (rows, width), 4 + len(o_home) + len(out_pieces), 2 * r...]
    all_to_all x1, waiting for transfers between devices: 1.53 us -> 2.56 us  [local(): lax.all_to_all(o_t, 'tm', 0, 0, tiled=True).reshape(rows, spaces * cols)]
    ppermute x5, starting transfers between devices: 6.9 us -> 7.87 us  [across(): lax.ppermute(array, 'space', [(i, (i + k) % spaces) for i in range(spaces)])]
  transfers between devices with their start and end apart: 9 -> 10, of which waited for: 4 -> 6; matrix products, arithmetic and copies ran while one was open for 0% -> 0% of each run, Pallas kernels for 24% -> 22%
where the time goes in v12:
time: 84.5 us; the launch traced here: 83.9 us
  waiting for transfers between devices  31.6 us (37%)
  Pallas kernels  24.7 us (29%)
  starting transfers between devices  24.3 us (29%)
  local copies, waits for them, and re-layouts  3.1 us (4%)
    ppermute x5, waiting for transfers between devices, across(): lax.ppermute(array, 'space', [(i, (i + k) % spaces) for i in range(spaces)])  26.5 us
    ppermute x5, starting transfers between devices, across(): lax.ppermute(array, 'space', [(i, (i + k) % spaces) for i in range(spaces)])  7.87 us
    pallas_call x1, Pallas kernels, local(): call(kernel_spatial, (spaces, rows, cols), 4 + len(arrived), 10000000000....  7.51 us
    all_to_all x1, starting transfers between devices, local(): lax.all_to_all(tokens.reshape(times, size, frames, width), 'tm', 0, 0, ti...  5.98 us
    all_to_all x1, starting transfers between devices, local(): lax.all_to_all(o_t, 'tm', 0, 0, tiled=True).reshape(rows, spaces * cols)  5.25 us
    all_to_all x1, starting transfers between devices, local(): lax.all_to_all(after((o_all,), spread, *out_pieces)[0].reshape(spaces * t...  5.11 us
    pallas_call x1, Pallas kernels, local(): pl.pallas_call(kernel_qkv, out_shape=tuple((jax.ShapeDtypeStruct(a, BF) f...  4.83 us
    pallas_call x1, Pallas kernels, local(): call(functools.partial(kernel_rest, size=size, frames=frames, spaces=spac...  4.56 us
  transfers between devices with their start and end apart: 10, of which 6 were waited for; matrix products, arithmetic and copies ran while one was open for 0% of the time, Pallas kernels for 22%

profile of v12, /device:TPU:0, one launch (start us, length us, event | category | flops | bytes accessed | tf_op | source)
XLA Modules:
  0.0 83.9 jit_solution(13365577419430480974)
XLA Ops:
  0.0 2.9 %collective-permute-start = (bf16[128,2,1152]{2,1,0:T(2,128)(2,1)}, bf16[128,2,1152]{2,1,0:T(2,128)(2,1)}, u32[]{:S(2)}, u32[]{:S(2)}) collective-permute-start(bf16[128,2,1152]{2,1,0:T(2,128)(2,1)} %x_ref.3), channel_id=1, source_target_pairs={{0,1},{1,0},{2,3},{3,2},{4,5},{5,4},{6,7},{7,6},{8,9},{9,8},{10,11... | collective-permute-start | bytes 1769480 | tf_op jit(solution)/shard_map/ppermute | solution.py:286
  2.9 6.0 %all-to-all-start = ((bf16[16,8,2,1152]{3,2,1,0:T(2,128)(2,1)}), bf16[16,8,2,1152]{3,2,1,0:T(2,128)(2,1)}, u32[]{:S(2)}, u32[]{:S(2)}) async-start(bf16[16,8,2,1152]{3,2,1,0:T(2,128)(2,1)} %bitcast.16), calls=%async_computation | async-start | bytes 1179648 | tf_op jit(solution)/shard_map/all_to_all | solution.py:310
  8.9 4.8 %shard_map.100 = (bf16[4,3,72,256]{3,2,1,0:T(8,128)(2,1)}, bf16[2,216,1152]{2,1,0:T(8,128)(2,1)}, bf16[144,1152]{1,0:T(8,128)(2,1)}) custom-call(bf16[128,2,1152]{2,1,0:T(2,128)(2,1)} %x_ref.3, bf16[4,216,1152]{2,1,0:T(8,128)(2,1)} %bitcast.20, bf16[4,216,1152]{2,1,0:T(8,128)(2,1)} %bitcast.14, bf16[288,1152]{1,0:T(8,128)(2,1)} %refs_1_.1, ...), custom_call_target="tpu_custom_call" | custom-call | flops 509607936 | bytes 3000000 | tf_op jit(solution)/shard_map/pallas_call | solution.py:295
  13.8 0.0 copy-start.11
  13.8 0.0 copy-start.1
  13.8 0.0 copy-start.8
  13.8 0.0 copy-start.9
  13.8 0.6 collective-permute-start.1
  14.4 2.2 %collective-permute-done.refs_0_ = bf16[128,2,1152]{2,1,0:T(2,128)(2,1)} collective-permute-done((bf16[128,2,1152]{2,1,0:T(2,128)(2,1)}, bf16[128,2,1152]{2,1,0:T(2,128)(2,1)}, u32[]{:S(2)}, u32[]{:S(2)}) %collective-permute-start) | collective-permute-done | bytes 589856 | tf_op jit(solution)/shard_map/ppermute | solution.py:286
  16.6 7.5 %shard_map.101.o_own_ref = bf16[2,256,288]{2,1,0:T(8,128)(2,1)} custom-call(bf16[4,3,72,256]{3,2,1,0:T(8,128)(2,1)} %get-tuple-element.14.own_hbm, bf16[4,216,1152]{2,1,0:T(8,128)(2,1)} %bitcast.21, f32[6,1152]{1,0:T(8,128)} %mod_ref.9, f32[864]{0:T(1024)} %b_ref.4, bf16[128,2,1152]{2,1,0:T(2,128)(2,1)} %collective-permute-done.refs_0_), custom_call_target="tpu_custom_call" | custom-call | flops 10000000000 | bytes 4000000 | tf_op jit(solution)/shard_map/pallas_call | solution.py:317
  24.1 0.0 copy-start
  24.1 0.0 collective-permute-done.1.refs_1_.refs_2_
  24.1 2.4 %collective-permute-start.4 = (bf16[2,216,1152]{2,1,0:T(8,128)(2,1)}, bf16[2,216,1152]{2,1,0:T(8,128)(2,1)}, u32[]{:S(2)}, u32[]{:S(2)}) collective-permute-start(bf16[2,216,1152]{2,1,0:T(8,128)(2,1)} %get-tuple-element.21), channel_id=1, source_target_pairs={{0,1},{1,0},{2,3},{3,2},{4,5},{5,4},{6,7},{7,6},{8,9},{9,8},{10,11... | collective-permute-start | bytes 2985992 | tf_op jit(solution)/shard_map/ppermute | solution.py:286
  26.5 1.6 %collective-permute-done.2.refs_2_.refs_3_ = bf16[144,1152]{1,0:T(8,128)(2,1)S(1)} collective-permute-done((bf16[144,1152]{1,0:T(8,128)(2,1)S(1)}, bf16[144,1152]{1,0:T(8,128)(2,1)S(1)}, u32[]{:S(2)}, u32[]{:S(2)}) %collective-permute-start.2) | collective-permute-done | bytes 331808 | tf_op jit(solution)/shard_map/ppermute | solution.py:289
  28.1 0.7 copy-done.5
  28.9 5.1 %all-to-all-start.1 = ((bf16[32,16,288]{2,1,0:T(8,128)(2,1)}), bf16[32,16,288]{2,1,0:T(8,128)(2,1)S(1)}, u32[]{:S(2)}, u32[]{:S(2)}) async-start(bf16[32,16,288]{2,1,0:T(8,128)(2,1)} %bitcast.17), calls=%async_computation.1 | async-start | bytes 786432 | tf_op jit(solution)/shard_map/all_to_all | solution.py:339
  34.0 17.7 %collective-permute-done.4.refs_1_ = bf16[2,216,1152]{2,1,0:T(8,128)(2,1)} collective-permute-done((bf16[2,216,1152]{2,1,0:T(8,128)(2,1)}, bf16[2,216,1152]{2,1,0:T(8,128)(2,1)}, u32[]{:S(2)}, u32[]{:S(2)}) %collective-permute-start.4) | collective-permute-done | bytes 995360 | tf_op jit(solution)/shard_map/ppermute | solution.py:286
  51.7 0.9 %all-to-all-done.1 = bf16[32,16,288]{2,1,0:T(8,128)(2,1)S(1)} async-done(((bf16[32,16,288]{2,1,0:T(8,128)(2,1)}), bf16[32,16,288]{2,1,0:T(8,128)(2,1)S(1)}, u32[]{:S(2)}, u32[]{:S(2)}) %all-to-all-start.1) | async-done | bytes 294944 | tf_op jit(solution)/shard_map/all_to_all | solution.py:339
  52.6 0.1 collective-permute-start.5
  52.7 1.3 %collective-permute-start.3 = (f32[864]{0:T(1024)S(1)}, f32[864]{0:T(1024)S(1)}, u32[]{:S(2)}, u32[]{:S(2)}) collective-permute-start(f32[864]{0:T(1024)S(1)} %copy-done.11), channel_id=1, source_target_pairs={{0,1},{1,0},{2,3},{3,2},{4,5},{5,4},{6,7},{7,6},{8,9},{9,8},{10,11... | collective-permute-start | bytes 10376 | tf_op jit(solution)/shard_map/ppermute | solution.py:286
  54.1 1.0 %copy-done.6 = bf16[144,1152]{1,0:T(8,128)(2,1)S(1)} copy-done((bf16[144,1152]{1,0:T(8,128)(2,1)S(1)}, bf16[144,1152]{1,0:T(8,128)(2,1)}, u32[]{:S(2)}) %copy-start.6) | copy-done | bytes 331800
  55.0 2.7 %shard_map.102.h_ref = bf16[256,1152]{1,0:T(8,128)(2,1)S(1)} custom-call(bf16[2,256,288]{2,1,0:T(8,128)(2,1)S(1)} %bitcast.18, bf16[128,2,1152]{2,1,0:T(2,128)(2,1)} %bitcast.7.x_ref, f32[1152]{0:T(1024)S(1)} %copy-done.9, f32[6,1152]{1,0:T(8,128)S(1)} %copy-done.8, bf16[288,1152]{1,0:T(8,128)(2,1)S(1)} %copy-done.1, ...), custom_call_target="tpu_custom_call" | custom-call | flops 339738624 | bytes 3000000 | tf_op jit(solution)/shard_map/pallas_call | solution.py:360
  57.7 2.4 %shard_map.103.own_ref = f32[4,72,256]{2,1,0:T(8,128)S(1)} custom-call(bf16[256,1152]{1,0:T(8,128)(2,1)S(1)} %shard_map.102.h_ref, bf16[4,216,1152]{2,1,0:T(8,128)(2,1)S(1)} %bitcast.15, f32[864]{0:T(1024)S(1)} %copy-done.11), custom_call_target="tpu_custom_call" | custom-call | flops 509607936 | bytes 3000000 | tf_op jit(solution)/shard_map/pallas_call | solution.py:363
  60.1 0.0 copy-start.2
  60.1 4.6 %shard_map.104 = bf16[256,576]{1,0:T(8,128)(2,1)} custom-call(bf16[256,1152]{1,0:T(8,128)(2,1)S(1)} %shard_map.102.h_ref, f32[4,72,256]{2,1,0:T(8,128)S(1)} %shard_map.103.own_ref, f32[864]{0:T(1024)S(1)} %collective-permute-done.3.refs_0_, bf16[2,216,1152]{2,1,0:T(8,128)(2,1)} %collective-permute-done.4.refs_1_, ...), custom_call_target="tpu_custom_call" | custom-call | flops 509607936 | bytes 5000000 | tf_op jit(solution)/shard_map/pallas_call | solution.py:373
  64.7 5.2 %all-to-all-start.2 = ((bf16[16,16,576]{2,1,0:T(8,128)(2,1)}), bf16[16,16,576]{2,1,0:T(8,128)(2,1)S(1)}, u32[]{:S(2)}, u32[]{:S(2)}) async-start(bf16[16,16,576]{2,1,0:T(8,128)(2,1)} %bitcast.9), calls=%async_computation.2 | async-start | bytes 655360 | tf_op jit(solution)/shard_map/all_to_all | solution.py:385
  70.0 0.6 collective-permute-start.6
  70.7 6.6 %collective-permute-done.6.refs_0_ = bf16[256,288]{1,0:T(8,128)(2,1)S(1)} collective-permute-done((bf16[256,288]{1,0:T(8,128)(2,1)S(1)}, bf16[256,288]{1,0:T(8,128)(2,1)S(1)}, u32[]{:S(2)}, u32[]{:S(2)}) %collective-permute-start.6) | collective-permute-done | bytes 147488 | tf_op jit(solution)/shard_map/ppermute | solution.py:286
  77.3 1.2 %shard_map.105.y_ref = bf16[256,1152]{1,0:T(8,128)(2,1)S(1)} custom-call(bf16[2,256,288]{2,1,0:T(8,128)(2,1)S(1)} %copy-done.3, bf16[128,2,1152]{2,1,0:T(2,128)(2,1)S(1)} %copy-done.2, f32[1152]{0:T(1024)S(1)} %copy-done.9, f32[6,1152]{1,0:T(8,128)S(1)} %copy-done.8, bf16[256,288]{1,0:T(8,128)(2,1)S(1)} %collective-permute-done.6.refs_0_, ...), custom_call_target="tpu_custom_call" | custom-call | flops 339738624 | bytes 3000000 | tf_op jit(solution)/shard_map/pallas_call | solution.py:351
  78.5 2.6 %all-to-all-done.2 = bf16[16,16,576]{2,1,0:T(8,128)(2,1)S(1)} async-done(((bf16[16,16,576]{2,1,0:T(8,128)(2,1)}), bf16[16,16,576]{2,1,0:T(8,128)(2,1)S(1)}, u32[]{:S(2)}, u32[]{:S(2)}) %all-to-all-start.2) | async-done | bytes 294944 | tf_op jit(solution)/shard_map/all_to_all | solution.py:385
  81.1 1.3 %copy-done.4 = bf16[576,1152]{1,0:T(8,128)(2,1)S(1)} copy-done((bf16[576,1152]{1,0:T(8,128)(2,1)S(1)}, bf16[576,1152]{1,0:T(8,128)(2,1)}, u32[]{:S(2)}) %copy-start.4) | copy-done | bytes 1327128
  82.4 1.5 %shard_map.106 = bf16[128,2,1152]{2,1,0:T(2,128)(2,1)} custom-call(bf16[256,576]{1,0:T(8,128)(2,1)S(1)} %bitcast.19, bf16[256,1152]{1,0:T(8,128)(2,1)S(1)} %shard_map.105.y_ref, bf16[576,1152]{1,0:T(8,128)(2,1)S(1)} %copy-done.4, f32[1152]{0:T(1024)S(1)} %copy-done.10, f32[6,1152]{1,0:T(8,128)S(1)} %copy-done.8), custom_call_target="tpu_custom_call" | custom-call | flops 339738624 | bytes 3000000 | tf_op jit(solution)/shard_map/pallas_call | solution.py:387
  (20 shorter events, 0.1 us)
Async XLA Ops:
  0.0 16.6 %collective-permute-start = (bf16[128,2,1152]{2,1,0:T(2,128)(2,1)}, bf16[128,2,1152]{2,1,0:T(2,128)(2,1)}, u32[]{:S(2)}, u32[]{:S(2)}) collective-permute-start(bf16[128,2,1152]{2,1,0:T(2,128)(2,1)} %x_ref.3), channel_id=1, source_target_pairs={{0,1},{1,0},{2,3},{3,2},{4,5},{5,4},{6,7},{7,6},{8,9},{9,8},{10,11... | collective-permute-start | bytes 1769480 | tf_op jit(solution)/shard_map/ppermute | solution.py:286
  2.9 25.9 %all-to-all-start = ((bf16[16,8,2,1152]{3,2,1,0:T(2,128)(2,1)}), bf16[16,8,2,1152]{3,2,1,0:T(2,128)(2,1)}, u32[]{:S(2)}, u32[]{:S(2)}) async-start(bf16[16,8,2,1152]{3,2,1,0:T(2,128)(2,1)} %bitcast.16), calls=%async_computation | async-start | bytes 1179648 | tf_op jit(solution)/shard_map/all_to_all | solution.py:310
  13.8 39.0 %copy-start.11 = (f32[864]{0:T(1024)S(1)}, f32[864]{0:T(1024)}, u32[]{:S(2)}) copy-start(f32[864]{0:T(1024)} %b_ref.5) | copy-start | bytes 10372
  13.8 40.3 %copy-start.1 = (bf16[288,1152]{1,0:T(8,128)(2,1)S(1)}, bf16[288,1152]{1,0:T(8,128)(2,1)}, u32[]{:S(2)}) copy-start(bf16[288,1152]{1,0:T(8,128)(2,1)} %refs_1_.1) | copy-start | bytes 1990660
  13.8 40.3 %copy-start.8 = (f32[6,1152]{1,0:T(8,128)S(1)}, f32[6,1152]{1,0:T(8,128)}, u32[]{:S(2)}) copy-start(f32[6,1152]{1,0:T(8,128)} %mod_ref.9) | copy-start | bytes 82948
  13.8 40.3 %copy-start.9 = (f32[1152]{0:T(1024)S(1)}, f32[1152]{0:T(1024)}, u32[]{:S(2)}) copy-start(f32[1152]{0:T(1024)} %outbias_ref.4) | copy-start | bytes 13828
  13.8 10.3 %collective-permute-start.1 = (bf16[144,1152]{1,0:T(8,128)(2,1)}, bf16[144,1152]{1,0:T(8,128)(2,1)S(1)}, u32[]{:S(2)}, u32[]{:S(2)}) collective-permute-start(bf16[144,1152]{1,0:T(8,128)(2,1)} %get-tuple-element.17), channel_id=1, source_target_pairs={{0,1},{1,0},{2,3},{3,2},{4,5},{5,4},{6,7},{7,6},{8,9},{9,8},{10,11... | collective-permute-start | bytes 995336 | tf_op jit(solution)/shard_map/ppermute | solution.py:286
  24.1 33.6 %copy-start = (bf16[1152,864]{0,1:T(8,128)(2,1)S(1)}, bf16[1152,864]{0,1:T(8,128)(2,1)}, u32[]{:S(2)}) copy-start(bf16[1152,864]{0,1:T(8,128)(2,1)} %param.16) | copy-start | bytes 5971972
  24.1 27.6 %collective-permute-start.4 = (bf16[2,216,1152]{2,1,0:T(8,128)(2,1)}, bf16[2,216,1152]{2,1,0:T(8,128)(2,1)}, u32[]{:S(2)}, u32[]{:S(2)}) collective-permute-start(bf16[2,216,1152]{2,1,0:T(8,128)(2,1)} %get-tuple-element.21), channel_id=1, source_target_pairs={{0,1},{1,0},{2,3},{3,2},{4,5},{5,4},{6,7},{7,6},{8,9},{9,8},{10,11... | collective-permute-start | bytes 2985992 | tf_op jit(solution)/shard_map/ppermute | solution.py:286
  26.5 1.6 %collective-permute-start.2 = (bf16[144,1152]{1,0:T(8,128)(2,1)S(1)}, bf16[144,1152]{1,0:T(8,128)(2,1)S(1)}, u32[]{:S(2)}, u32[]{:S(2)}) collective-permute-start(bf16[144,1152]{1,0:T(8,128)(2,1)S(1)} %collective-permute-done.1.refs_1_.refs_2_), channel_id=1, source_target_pairs={{0,2},{2,0},{4,6},{6,4},{8,10},{10,8},{12,14},{14,12},{16,18},{18,... | collective-permute-start | bytes 995336 | tf_op jit(solution)/shard_map/ppermute | solution.py:289
  28.1 0.7 copy-start.5
  28.9 23.7 %all-to-all-start.1 = ((bf16[32,16,288]{2,1,0:T(8,128)(2,1)}), bf16[32,16,288]{2,1,0:T(8,128)(2,1)S(1)}, u32[]{:S(2)}, u32[]{:S(2)}) async-start(bf16[32,16,288]{2,1,0:T(8,128)(2,1)} %bitcast.17), calls=%async_computation.1 | async-start | bytes 786432 | tf_op jit(solution)/shard_map/all_to_all | solution.py:339
  52.6 7.5 %collective-permute-start.5 = (bf16[2,216,1152]{2,1,0:T(8,128)(2,1)}, bf16[2,216,1152]{2,1,0:T(8,128)(2,1)S(1)}, u32[]{:S(2)}, u32[]{:S(2)}) collective-permute-start(bf16[2,216,1152]{2,1,0:T(8,128)(2,1)} %collective-permute-done.4.refs_1_), channel_id=1, source_target_pairs={{0,2},{2,0},{4,6},{6,4},{8,10},{10,8},{12,14},{14,12},{16,18},{18,... | collective-permute-start | bytes 2985992 | tf_op jit(solution)/shard_map/ppermute | solution.py:289
  52.7 7.4 %collective-permute-start.3 = (f32[864]{0:T(1024)S(1)}, f32[864]{0:T(1024)S(1)}, u32[]{:S(2)}, u32[]{:S(2)}) collective-permute-start(f32[864]{0:T(1024)S(1)} %copy-done.11), channel_id=1, source_target_pairs={{0,1},{1,0},{2,3},{3,2},{4,5},{5,4},{6,7},{7,6},{8,9},{9,8},{10,11... | collective-permute-start | bytes 10376 | tf_op jit(solution)/shard_map/ppermute | solution.py:286
  54.1 1.0 %copy-start.6 = (bf16[144,1152]{1,0:T(8,128)(2,1)S(1)}, bf16[144,1152]{1,0:T(8,128)(2,1)}, u32[]{:S(2)}) copy-start(bf16[144,1152]{1,0:T(8,128)(2,1)} %copy-done.5) | copy-start | bytes 995332
  60.1 9.9 %copy-start.3 = (bf16[2,256,288]{2,1,0:T(8,128)(2,1)S(1)}, bf16[2,256,288]{2,1,0:T(8,128)(2,1)}, u32[]{:S(2)}) copy-start(bf16[2,256,288]{2,1,0:T(8,128)(2,1)} %shard_map.101.o_own_ref) | copy-start | bytes 884740
  60.1 17.2 %copy-start.2 = (bf16[128,2,1152]{2,1,0:T(2,128)(2,1)S(1)}, bf16[128,2,1152]{2,1,0:T(2,128)(2,1)}, u32[]{:S(2)}) copy-start(bf16[128,2,1152]{2,1,0:T(2,128)(2,1)} %x_ref.3) | copy-start | bytes 1769476
  60.1 17.2 %copy-start.7 = (bf16[144,1152]{1,0:T(8,128)(2,1)S(1)}, bf16[144,1152]{1,0:T(8,128)(2,1)}, u32[]{:S(2)}) copy-start(bf16[144,1152]{1,0:T(8,128)(2,1)} %copy-done.5) | copy-start | bytes 995332
  64.7 16.4 %copy-start.10 = (f32[1152]{0:T(1024)S(1)}, f32[1152]{0:T(1024)}, u32[]{:S(2)}) copy-start(f32[1152]{0:T(1024)} %outbias_ref.5) | copy-start | bytes 13828
  64.7 16.4 %all-to-all-start.2 = ((bf16[16,16,576]{2,1,0:T(8,128)(2,1)}), bf16[16,16,576]{2,1,0:T(8,128)(2,1)S(1)}, u32[]{:S(2)}, u32[]{:S(2)}) async-start(bf16[16,16,576]{2,1,0:T(8,128)(2,1)} %bitcast.9), calls=%async_computation.2 | async-start | bytes 655360 | tf_op jit(solution)/shard_map/all_to_all | solution.py:385
  70.0 7.3 %collective-permute-start.6 = (bf16[256,288]{1,0:T(8,128)(2,1)S(1)}, bf16[256,288]{1,0:T(8,128)(2,1)S(1)}, u32[]{:S(2)}, u32[]{:S(2)}) collective-permute-start(bf16[256,288]{1,0:T(8,128)(2,1)S(1)} %dynamic-slice_bitcast_fusion), channel_id=1, source_target_pairs={{0,1},{1,0},{2,3},{3,2},{4,5},{5,4},{6,7},{7,6},{8,9},{9,8},{10,11... | collective-permute-start | bytes 442376 | tf_op jit(solution)/shard_map/ppermute | solution.py:286
  81.1 1.3 %copy-start.4 = (bf16[576,1152]{1,0:T(8,128)(2,1)S(1)}, bf16[576,1152]{1,0:T(8,128)(2,1)}, u32[]{:S(2)}) copy-start(bf16[576,1152]{1,0:T(8,128)(2,1)} %w_ref.1) | copy-start | bytes 3981316

commit v13 on v12

--- a/solution.py
+++ b/solution.py
@@ -311,7 +311,7 @@
 
     other_bias = [across(bias_temporal, k) for k in range(1, spaces)]
     (my_out,) = after((my_out,), own)
-    arrived = [after((a,), own)[0] for a in arrived]
+    arrived = [after((a,), own, *other_bias)[0] for a in arrived]
     direct_out = [across(my_out, k) for k in range(1, spaces)]
 
     o_all = call(

time: 84.5 us -> 83.2 us (0.985)
  waiting for transfers between devices: 31.6 us -> 30 us
    ppermute x5, waiting for transfers between devices: 26.5 us -> 24.9 us  [across(): lax.ppermute(array, 'space', [(i, (i + k) % spaces) for i in range(spaces)])]
  transfers between devices with their start and end apart: 10 -> 10, of which waited for: 6 -> 7; matrix products, arithmetic and copies ran while one was open for 0% -> 0% of each run, Pallas kernels for 22% -> 22%
where the time goes in v13:
time: 83.2 us; the launch traced here: 82.7 us
  waiting for transfers between devices  30 us (36%)
  starting transfers between devices  24.7 us (30%)
  Pallas kernels  24.6 us (30%)
  local copies, waits for them, and re-layouts  3.09 us (4%)
    ppermute x5, waiting for transfers between devices, across(): lax.ppermute(array, 'space', [(i, (i + k) % spaces) for i in range(spaces)])  24.9 us
    ppermute x5, starting transfers between devices, across(): lax.ppermute(array, 'space', [(i, (i + k) % spaces) for i in range(spaces)])  8.29 us
    pallas_call x1, Pallas kernels, local(): call(kernel_spatial, (spaces, rows, cols), 4 + len(arrived), 10000000000....  7.52 us
    all_to_all x1, starting transfers between devices, local(): lax.all_to_all(tokens.reshape(times, size, frames, width), 'tm', 0, 0, ti...  5.98 us
    all_to_all x1, starting transfers between devices, local(): lax.all_to_all(o_t, 'tm', 0, 0, tiled=True).reshape(rows, spaces * cols)  5.39 us
    all_to_all x1, starting transfers between devices, local(): lax.all_to_all(after((o_all,), spread, *out_pieces)[0].reshape(spaces * t...  4.92 us
    pallas_call x1, Pallas kernels, local(): pl.pallas_call(kernel_qkv, out_shape=tuple((jax.ShapeDtypeStruct(a, BF) f...  4.8 us
    pallas_call x1, Pallas kernels, local(): call(functools.partial(kernel_rest, size=size, frames=frames, spaces=spac...  4.56 us
  transfers between devices with their start and end apart: 10, of which 7 were waited for; matrix products, arithmetic and copies ran while one was open for 0% of the time, Pallas kernels for 22%

profile of v13, /device:TPU:0, one launch (start us, length us, event | category | flops | bytes accessed | tf_op | source)
XLA Modules:
  0.0 82.7 jit_solution(4515625896123687374)
XLA Ops:
  0.0 2.9 %collective-permute-start = (bf16[128,2,1152]{2,1,0:T(2,128)(2,1)}, bf16[128,2,1152]{2,1,0:T(2,128)(2,1)}, u32[]{:S(2)}, u32[]{:S(2)}) collective-permute-start(bf16[128,2,1152]{2,1,0:T(2,128)(2,1)} %x_ref.3), channel_id=1, source_target_pairs={{0,1},{1,0},{2,3},{3,2},{4,5},{5,4},{6,7},{7,6},{8,9},{9,8},{10,11... | collective-permute-start | bytes 1769480 | tf_op jit(solution)/shard_map/ppermute | solution.py:286
  2.9 6.0 %all-to-all-start = ((bf16[16,8,2,1152]{3,2,1,0:T(2,128)(2,1)}), bf16[16,8,2,1152]{3,2,1,0:T(2,128)(2,1)}, u32[]{:S(2)}, u32[]{:S(2)}) async-start(bf16[16,8,2,1152]{3,2,1,0:T(2,128)(2,1)} %bitcast.16), calls=%async_computation | async-start | bytes 1179648 | tf_op jit(solution)/shard_map/all_to_all | solution.py:310
  8.9 0.6 collective-permute-start.1
  9.5 4.8 %shard_map.100 = (bf16[4,3,72,256]{3,2,1,0:T(8,128)(2,1)}, bf16[2,216,1152]{2,1,0:T(8,128)(2,1)}, bf16[144,1152]{1,0:T(8,128)(2,1)}) custom-call(bf16[128,2,1152]{2,1,0:T(2,128)(2,1)} %x_ref.3, bf16[4,216,1152]{2,1,0:T(8,128)(2,1)} %bitcast.20, bf16[4,216,1152]{2,1,0:T(8,128)(2,1)} %bitcast.14, bf16[288,1152]{1,0:T(8,128)(2,1)} %refs_1_.1, ...), custom_call_target="tpu_custom_call" | custom-call | flops 509607936 | bytes 3000000 | tf_op jit(solution)/shard_map/pallas_call | solution.py:295
  14.3 0.0 copy-start.1
  14.4 0.0 copy-start.8
  14.4 0.0 copy-start.9
  14.4 1.6 %collective-permute-start.2 = (bf16[144,1152]{1,0:T(8,128)(2,1)}, bf16[144,1152]{1,0:T(8,128)(2,1)S(1)}, u32[]{:S(2)}, u32[]{:S(2)}) collective-permute-start(bf16[144,1152]{1,0:T(8,128)(2,1)} %get-tuple-element.17), channel_id=1, source_target_pairs={{0,1},{1,0},{2,3},{3,2},{4,5},{5,4},{6,7},{7,6},{8,9},{9,8},{10,11... | collective-permute-start | bytes 995336 | tf_op jit(solution)/shard_map/ppermute | solution.py:286
  15.9 0.7 collective-permute-done.1.refs_0_
  16.6 7.5 %shard_map.101.o_own_ref = bf16[2,256,288]{2,1,0:T(8,128)(2,1)} custom-call(bf16[4,3,72,256]{3,2,1,0:T(8,128)(2,1)} %get-tuple-element.14.own_hbm, bf16[4,216,1152]{2,1,0:T(8,128)(2,1)} %bitcast.21, f32[6,1152]{1,0:T(8,128)} %mod_ref.9, f32[864]{0:T(1024)} %b_ref.4, bf16[128,2,1152]{2,1,0:T(2,128)(2,1)} %collective-permute-done.refs_0_), custom_call_target="tpu_custom_call" | custom-call | flops 10000000000 | bytes 4000000 | tf_op jit(solution)/shard_map/pallas_call | solution.py:317
  24.2 0.0 copy-start
  24.2 0.2 collective-permute-done.2.refs_1_.refs_2_
  24.4 1.6 %collective-permute-start.4 = (bf16[2,216,1152]{2,1,0:T(8,128)(2,1)}, bf16[2,216,1152]{2,1,0:T(8,128)(2,1)}, u32[]{:S(2)}, u32[]{:S(2)}) collective-permute-start(bf16[2,216,1152]{2,1,0:T(8,128)(2,1)} %get-tuple-element.21), channel_id=1, source_target_pairs={{0,1},{1,0},{2,3},{3,2},{4,5},{5,4},{6,7},{7,6},{8,9},{9,8},{10,11... | collective-permute-start | bytes 2985992 | tf_op jit(solution)/shard_map/ppermute | solution.py:286
  26.0 1.6 %collective-permute-done.3.refs_2_.refs_3_ = bf16[144,1152]{1,0:T(8,128)(2,1)S(1)} collective-permute-done((bf16[144,1152]{1,0:T(8,128)(2,1)S(1)}, bf16[144,1152]{1,0:T(8,128)(2,1)S(1)}, u32[]{:S(2)}, u32[]{:S(2)}) %collective-permute-start.3) | collective-permute-done | bytes 331808 | tf_op jit(solution)/shard_map/ppermute | solution.py:289
  27.6 0.7 copy-done.5
  28.4 4.9 %all-to-all-start.1 = ((bf16[32,16,288]{2,1,0:T(8,128)(2,1)}), bf16[32,16,288]{2,1,0:T(8,128)(2,1)S(1)}, u32[]{:S(2)}, u32[]{:S(2)}) async-start(bf16[32,16,288]{2,1,0:T(8,128)(2,1)} %bitcast.17), calls=%async_computation.1 | async-start | bytes 786432 | tf_op jit(solution)/shard_map/all_to_all | solution.py:339
  33.3 18.3 %collective-permute-done.4.refs_1_ = bf16[2,216,1152]{2,1,0:T(8,128)(2,1)} collective-permute-done((bf16[2,216,1152]{2,1,0:T(8,128)(2,1)}, bf16[2,216,1152]{2,1,0:T(8,128)(2,1)}, u32[]{:S(2)}, u32[]{:S(2)}) %collective-permute-start.4) | collective-permute-done | bytes 995360 | tf_op jit(solution)/shard_map/ppermute | solution.py:286
  51.6 0.9 %all-to-all-done.1 = bf16[32,16,288]{2,1,0:T(8,128)(2,1)S(1)} async-done(((bf16[32,16,288]{2,1,0:T(8,128)(2,1)}), bf16[32,16,288]{2,1,0:T(8,128)(2,1)S(1)}, u32[]{:S(2)}, u32[]{:S(2)}) %all-to-all-start.1) | async-done | bytes 294944 | tf_op jit(solution)/shard_map/all_to_all | solution.py:339
  52.5 0.1 collective-permute-start.5
  52.7 1.0 %copy-done.6 = bf16[144,1152]{1,0:T(8,128)(2,1)S(1)} copy-done((bf16[144,1152]{1,0:T(8,128)(2,1)S(1)}, bf16[144,1152]{1,0:T(8,128)(2,1)}, u32[]{:S(2)}) %copy-start.6) | copy-done | bytes 331800
  53.6 2.7 %shard_map.102.h_ref = bf16[256,1152]{1,0:T(8,128)(2,1)S(1)} custom-call(bf16[2,256,288]{2,1,0:T(8,128)(2,1)S(1)} %bitcast.18, bf16[128,2,1152]{2,1,0:T(2,128)(2,1)} %bitcast.7.x_ref, f32[1152]{0:T(1024)S(1)} %copy-done.9, f32[6,1152]{1,0:T(8,128)S(1)} %copy-done.8, bf16[288,1152]{1,0:T(8,128)(2,1)S(1)} %copy-done.1, ...), custom_call_target="tpu_custom_call" | custom-call | flops 339738624 | bytes 3000000 | tf_op jit(solution)/shard_map/pallas_call | solution.py:360
  56.3 2.4 %shard_map.103.own_ref = f32[4,72,256]{2,1,0:T(8,128)S(1)} custom-call(bf16[256,1152]{1,0:T(8,128)(2,1)S(1)} %shard_map.102.h_ref, bf16[4,216,1152]{2,1,0:T(8,128)(2,1)S(1)} %bitcast.15, f32[864]{0:T(1024)S(1)} %copy-done.11), custom_call_target="tpu_custom_call" | custom-call | flops 509607936 | bytes 3000000 | tf_op jit(solution)/shard_map/pallas_call | solution.py:363
  58.7 0.0 copy-start.2
  58.7 0.0 copy-start.7
  58.7 4.6 %shard_map.104 = bf16[256,576]{1,0:T(8,128)(2,1)} custom-call(bf16[256,1152]{1,0:T(8,128)(2,1)S(1)} %shard_map.102.h_ref, f32[4,72,256]{2,1,0:T(8,128)S(1)} %shard_map.103.own_ref, f32[864]{0:T(1024)S(1)} %collective-permute-done.1.refs_0_, bf16[2,216,1152]{2,1,0:T(8,128)(2,1)} %collective-permute-done.4.refs_1_, ...), custom_call_target="tpu_custom_call" | custom-call | flops 509607936 | bytes 5000000 | tf_op jit(solution)/shard_map/pallas_call | solution.py:373
  63.3 5.4 %all-to-all-start.2 = ((bf16[16,16,576]{2,1,0:T(8,128)(2,1)}), bf16[16,16,576]{2,1,0:T(8,128)(2,1)S(1)}, u32[]{:S(2)}, u32[]{:S(2)}) async-start(bf16[16,16,576]{2,1,0:T(8,128)(2,1)} %bitcast.9), calls=%async_computation.2 | async-start | bytes 655360 | tf_op jit(solution)/shard_map/all_to_all | solution.py:385
  68.8 1.6 %collective-permute-start.6 = (bf16[256,288]{1,0:T(8,128)(2,1)S(1)}, bf16[256,288]{1,0:T(8,128)(2,1)S(1)}, u32[]{:S(2)}, u32[]{:S(2)}) collective-permute-start(bf16[256,288]{1,0:T(8,128)(2,1)S(1)} %dynamic-slice_bitcast_fusion), channel_id=1, source_target_pairs={{0,1},{1,0},{2,3},{3,2},{4,5},{5,4},{6,7},{7,6},{8,9},{9,8},{10,11... | collective-permute-start | bytes 442376 | tf_op jit(solution)/shard_map/ppermute | solution.py:286
  70.3 5.7 %collective-permute-done.6.refs_0_ = bf16[256,288]{1,0:T(8,128)(2,1)S(1)} collective-permute-done((bf16[256,288]{1,0:T(8,128)(2,1)S(1)}, bf16[256,288]{1,0:T(8,128)(2,1)S(1)}, u32[]{:S(2)}, u32[]{:S(2)}) %collective-permute-start.6) | collective-permute-done | bytes 147488 | tf_op jit(solution)/shard_map/ppermute | solution.py:286
  76.0 1.2 %shard_map.105.y_ref = bf16[256,1152]{1,0:T(8,128)(2,1)S(1)} custom-call(bf16[2,256,288]{2,1,0:T(8,128)(2,1)S(1)} %copy-done.3, bf16[128,2,1152]{2,1,0:T(2,128)(2,1)S(1)} %copy-done.2, f32[1152]{0:T(1024)S(1)} %copy-done.9, f32[6,1152]{1,0:T(8,128)S(1)} %copy-done.8, bf16[256,288]{1,0:T(8,128)(2,1)S(1)} %collective-permute-done.6.refs_0_, ...), custom_call_target="tpu_custom_call" | custom-call | flops 339738624 | bytes 3000000 | tf_op jit(solution)/shard_map/pallas_call | solution.py:351
  77.2 2.6 %all-to-all-done.2 = bf16[16,16,576]{2,1,0:T(8,128)(2,1)S(1)} async-done(((bf16[16,16,576]{2,1,0:T(8,128)(2,1)}), bf16[16,16,576]{2,1,0:T(8,128)(2,1)S(1)}, u32[]{:S(2)}, u32[]{:S(2)}) %all-to-all-start.2) | async-done | bytes 294944 | tf_op jit(solution)/shard_map/all_to_all | solution.py:385
  79.8 1.3 %copy-done.4 = bf16[576,1152]{1,0:T(8,128)(2,1)S(1)} copy-done((bf16[576,1152]{1,0:T(8,128)(2,1)S(1)}, bf16[576,1152]{1,0:T(8,128)(2,1)}, u32[]{:S(2)}) %copy-start.4) | copy-done | bytes 1327128
  81.1 1.5 %shard_map.106 = bf16[128,2,1152]{2,1,0:T(2,128)(2,1)} custom-call(bf16[256,576]{1,0:T(8,128)(2,1)S(1)} %bitcast.19, bf16[256,1152]{1,0:T(8,128)(2,1)S(1)} %shard_map.105.y_ref, bf16[576,1152]{1,0:T(8,128)(2,1)S(1)} %copy-done.4, f32[1152]{0:T(1024)S(1)} %copy-done.10, f32[6,1152]{1,0:T(8,128)S(1)} %copy-done.8), custom_call_target="tpu_custom_call" | custom-call | flops 339738624 | bytes 3000000 | tf_op jit(solution)/shard_map/pallas_call | solution.py:387
  (20 shorter events, 0.1 us)
Async XLA Ops:
  0.0 16.6 %collective-permute-start = (bf16[128,2,1152]{2,1,0:T(2,128)(2,1)}, bf16[128,2,1152]{2,1,0:T(2,128)(2,1)}, u32[]{:S(2)}, u32[]{:S(2)}) collective-permute-start(bf16[128,2,1152]{2,1,0:T(2,128)(2,1)} %x_ref.3), channel_id=1, source_target_pairs={{0,1},{1,0},{2,3},{3,2},{4,5},{5,4},{6,7},{7,6},{8,9},{9,8},{10,11... | collective-permute-start | bytes 1769480 | tf_op jit(solution)/shard_map/ppermute | solution.py:286
  2.9 25.4 %all-to-all-start = ((bf16[16,8,2,1152]{3,2,1,0:T(2,128)(2,1)}), bf16[16,8,2,1152]{3,2,1,0:T(2,128)(2,1)}, u32[]{:S(2)}, u32[]{:S(2)}) async-start(bf16[16,8,2,1152]{3,2,1,0:T(2,128)(2,1)} %bitcast.16), calls=%async_computation | async-start | bytes 1179648 | tf_op jit(solution)/shard_map/all_to_all | solution.py:310
  8.9 7.7 %collective-permute-start.1 = (f32[864]{0:T(1024)}, f32[864]{0:T(1024)S(1)}, u32[]{:S(2)}, u32[]{:S(2)}) collective-permute-start(f32[864]{0:T(1024)} %b_ref.5), channel_id=1, source_target_pairs={{0,1},{1,0},{2,3},{3,2},{4,5},{5,4},{6,7},{7,6},{8,9},{9,8},{10,11... | collective-permute-start | bytes 10376 | tf_op jit(solution)/shard_map/ppermute | solution.py:286
  14.3 38.3 %copy-start.1 = (bf16[288,1152]{1,0:T(8,128)(2,1)S(1)}, bf16[288,1152]{1,0:T(8,128)(2,1)}, u32[]{:S(2)}) copy-start(bf16[288,1152]{1,0:T(8,128)(2,1)} %refs_1_.1) | copy-start | bytes 1990660
  14.4 38.3 %copy-start.8 = (f32[6,1152]{1,0:T(8,128)S(1)}, f32[6,1152]{1,0:T(8,128)}, u32[]{:S(2)}) copy-start(f32[6,1152]{1,0:T(8,128)} %mod_ref.9) | copy-start | bytes 82948
  14.4 38.3 %copy-start.9 = (f32[1152]{0:T(1024)S(1)}, f32[1152]{0:T(1024)}, u32[]{:S(2)}) copy-start(f32[1152]{0:T(1024)} %outbias_ref.4) | copy-start | bytes 13828
  14.4 10.0 %collective-permute-start.2 = (bf16[144,1152]{1,0:T(8,128)(2,1)}, bf16[144,1152]{1,0:T(8,128)(2,1)S(1)}, u32[]{:S(2)}, u32[]{:S(2)}) collective-permute-start(bf16[144,1152]{1,0:T(8,128)(2,1)} %get-tuple-element.17), channel_id=1, source_target_pairs={{0,1},{1,0},{2,3},{3,2},{4,5},{5,4},{6,7},{7,6},{8,9},{9,8},{10,11... | collective-permute-start | bytes 995336 | tf_op jit(solution)/shard_map/ppermute | solution.py:286
  16.6 39.7 %copy-start.11 = (f32[864]{0:T(1024)S(1)}, f32[864]{0:T(1024)}, u32[]{:S(2)}) copy-start(f32[864]{0:T(1024)} %b_ref.5) | copy-start | bytes 10372
  24.2 32.1 %copy-start = (bf16[1152,864]{0,1:T(8,128)(2,1)S(1)}, bf16[1152,864]{0,1:T(8,128)(2,1)}, u32[]{:S(2)}) copy-start(bf16[1152,864]{0,1:T(8,128)(2,1)} %param.16) | copy-start | bytes 5971972
  24.4 27.2 %collective-permute-start.4 = (bf16[2,216,1152]{2,1,0:T(8,128)(2,1)}, bf16[2,216,1152]{2,1,0:T(8,128)(2,1)}, u32[]{:S(2)}, u32[]{:S(2)}) collective-permute-start(bf16[2,216,1152]{2,1,0:T(8,128)(2,1)} %get-tuple-element.21), channel_id=1, source_target_pairs={{0,1},{1,0},{2,3},{3,2},{4,5},{5,4},{6,7},{7,6},{8,9},{9,8},{10,11... | collective-permute-start | bytes 2985992 | tf_op jit(solution)/shard_map/ppermute | solution.py:286
  26.0 1.6 %collective-permute-start.3 = (bf16[144,1152]{1,0:T(8,128)(2,1)S(1)}, bf16[144,1152]{1,0:T(8,128)(2,1)S(1)}, u32[]{:S(2)}, u32[]{:S(2)}) collective-permute-start(bf16[144,1152]{1,0:T(8,128)(2,1)S(1)} %collective-permute-done.2.refs_1_.refs_2_), channel_id=1, source_target_pairs={{0,2},{2,0},{4,6},{6,4},{8,10},{10,8},{12,14},{14,12},{16,18},{18,... | collective-permute-start | bytes 995336 | tf_op jit(solution)/shard_map/ppermute | solution.py:289
  27.6 0.7 copy-start.5
  28.4 24.2 %all-to-all-start.1 = ((bf16[32,16,288]{2,1,0:T(8,128)(2,1)}), bf16[32,16,288]{2,1,0:T(8,128)(2,1)S(1)}, u32[]{:S(2)}, u32[]{:S(2)}) async-start(bf16[32,16,288]{2,1,0:T(8,128)(2,1)} %bitcast.17), calls=%async_computation.1 | async-start | bytes 786432 | tf_op jit(solution)/shard_map/all_to_all | solution.py:339
  52.5 6.2 %collective-permute-start.5 = (bf16[2,216,1152]{2,1,0:T(8,128)(2,1)}, bf16[2,216,1152]{2,1,0:T(8,128)(2,1)S(1)}, u32[]{:S(2)}, u32[]{:S(2)}) collective-permute-start(bf16[2,216,1152]{2,1,0:T(8,128)(2,1)} %collective-permute-done.4.refs_1_), channel_id=1, source_target_pairs={{0,2},{2,0},{4,6},{6,4},{8,10},{10,8},{12,14},{14,12},{16,18},{18,... | collective-permute-start | bytes 2985992 | tf_op jit(solution)/shard_map/ppermute | solution.py:289
  52.7 1.0 %copy-start.6 = (bf16[144,1152]{1,0:T(8,128)(2,1)S(1)}, bf16[144,1152]{1,0:T(8,128)(2,1)}, u32[]{:S(2)}) copy-start(bf16[144,1152]{1,0:T(8,128)(2,1)} %copy-done.5) | copy-start | bytes 995332
  58.7 10.0 %copy-start.3 = (bf16[2,256,288]{2,1,0:T(8,128)(2,1)S(1)}, bf16[2,256,288]{2,1,0:T(8,128)(2,1)}, u32[]{:S(2)}) copy-start(bf16[2,256,288]{2,1,0:T(8,128)(2,1)} %shard_map.101.o_own_ref) | copy-start | bytes 884740
  58.7 17.3 %copy-start.2 = (bf16[128,2,1152]{2,1,0:T(2,128)(2,1)S(1)}, bf16[128,2,1152]{2,1,0:T(2,128)(2,1)}, u32[]{:S(2)}) copy-start(bf16[128,2,1152]{2,1,0:T(2,128)(2,1)} %x_ref.3) | copy-start | bytes 1769476
  58.7 17.3 %copy-start.7 = (bf16[144,1152]{1,0:T(8,128)(2,1)S(1)}, bf16[144,1152]{1,0:T(8,128)(2,1)}, u32[]{:S(2)}) copy-start(bf16[144,1152]{1,0:T(8,128)(2,1)} %copy-done.5) | copy-start | bytes 995332
  63.3 16.5 %copy-start.10 = (f32[1152]{0:T(1024)S(1)}, f32[1152]{0:T(1024)}, u32[]{:S(2)}) copy-start(f32[1152]{0:T(1024)} %outbias_ref.5) | copy-start | bytes 13828
  63.3 16.5 %all-to-all-start.2 = ((bf16[16,16,576]{2,1,0:T(8,128)(2,1)}), bf16[16,16,576]{2,1,0:T(8,128)(2,1)S(1)}, u32[]{:S(2)}, u32[]{:S(2)}) async-start(bf16[16,16,576]{2,1,0:T(8,128)(2,1)} %bitcast.9), calls=%async_computation.2 | async-start | bytes 655360 | tf_op jit(solution)/shard_map/all_to_all | solution.py:385
  68.8 7.3 %collective-permute-start.6 = (bf16[256,288]{1,0:T(8,128)(2,1)S(1)}, bf16[256,288]{1,0:T(8,128)(2,1)S(1)}, u32[]{:S(2)}, u32[]{:S(2)}) collective-permute-start(bf16[256,288]{1,0:T(8,128)(2,1)S(1)} %dynamic-slice_bitcast_fusion), channel_id=1, source_target_pairs={{0,1},{1,0},{2,3},{3,2},{4,5},{5,4},{6,7},{7,6},{8,9},{9,8},{10,11... | collective-permute-start | bytes 442376 | tf_op jit(solution)/shard_map/ppermute | solution.py:286
  79.8 1.3 %copy-start.4 = (bf16[576,1152]{1,0:T(8,128)(2,1)S(1)}, bf16[576,1152]{1,0:T(8,128)(2,1)}, u32[]{:S(2)}) copy-start(bf16[576,1152]{1,0:T(8,128)(2,1)} %w_ref.1) | copy-start | bytes 3981316

commit v14 on v13

--- a/solution.py
+++ b/solution.py
@@ -330,7 +330,7 @@
         params=LARGE,
     )(own, w_spatial, modulation, bias_spatial, *arrived)
 
-    (my_heads,) = after((my_heads,), o_all, *direct_out)
+    (my_heads,) = after((my_heads,), o_all, spread, *direct_out)
     direct_heads = [across(my_heads, k) for k in range(1, spaces)]
     out_pieces = [out_spatial]
     for a in direct_out:

time: 83.2 us -> 80.9 us (0.972)
  blocking collectives: 0 us -> 25.6 us
  waiting for transfers between devices: 30 us -> 10.9 us
  starting transfers between devices: 24.7 us -> 18.9 us
  local copies, waits for them, and re-layouts: 3.09 us -> 1.4 us
  Pallas kernels: 24.6 us -> 23.3 us
    all_to_all x0 -> x1, blocking collectives: none -> 25.6 us  [local(): lax.all_to_all(after((o_all,), spread, *out_pieces)[0].reshape(spaces * t...]
    ppermute x5, waiting for transfers between devices: 24.9 us -> 6.58 us  [across(): lax.ppermute(array, 'space', [(i, (i + k) % spaces) for i in range(spaces)])]
    all_to_all x1 -> x0, starting transfers between devices: 4.92 us -> none  [local(): lax.all_to_all(after((o_all,), spread, *out_pieces)[0].reshape(spaces * t...]
    unnamed x24 -> x18, local copies, waits for them, and re-layouts: 3.07 us -> 1.37 us
    pallas_call x1, Pallas kernels: 4.56 us -> 3.24 us  [local(): call(functools.partial(kernel_rest, size=size, frames=frames, spaces=spac...]
    all_to_all x1 -> x0, waiting for transfers between devices: 0.95 us -> none  [local(): lax.all_to_all(after((o_all,), spread, *out_pieces)[0].reshape(spaces * t...]
  transfers between devices with their start and end apart: 10 -> 9, of which waited for: 7 -> 6; matrix products, arithmetic and copies ran while one was open for 0% -> 0% of each run, Pallas kernels for 22% -> 23%
where the time goes in v14:
time: 80.9 us; the launch traced here: 80.4 us
  blocking collectives  25.6 us (32%)
  Pallas kernels  23.3 us (29%)
  starting transfers between devices  18.9 us (23%)
  waiting for transfers between devices  10.9 us (13%)
  local copies, waits for them, and re-layouts  1.4 us (2%)
    all_to_all x1, blocking collectives, local(): lax.all_to_all(after((o_all,), spread, *out_pieces)[0].reshape(spaces * t...  25.6 us
    ppermute x5, starting transfers between devices, across(): lax.ppermute(array, 'space', [(i, (i + k) % spaces) for i in range(spaces)])  8.14 us
    pallas_call x1, Pallas kernels, local(): call(kernel_spatial, (spaces, rows, cols), 4 + len(arrived), 10000000000....  7.52 us
    ppermute x5, waiting for transfers between devices, across(): lax.ppermute(array, 'space', [(i, (i + k) % spaces) for i in range(spaces)])  6.58 us
    all_to_all x1, starting transfers between devices, local(): lax.all_to_all(tokens.reshape(times, size, frames, width), 'tm', 0, 0, ti...  5.98 us
    pallas_call x1, Pallas kernels, local(): pl.pallas_call(kernel_qkv, out_shape=tuple((jax.ShapeDtypeStruct(a, BF) f...  4.82 us
    all_to_all x1, starting transfers between devices, local(): lax.all_to_all(o_t, 'tm', 0, 0, tiled=True).reshape(rows, spaces * cols)  4.67 us
    pallas_call x1, Pallas kernels, local(): call(functools.partial(kernel_rest, size=size, frames=frames, spaces=spac...  3.24 us
  transfers between devices with their start and end apart: 9, of which 6 were waited for; matrix products, arithmetic and copies ran while one was open for 0% of the time, Pallas kernels for 23%

profile of v14, /device:TPU:0, one launch (start us, length us, event | category | flops | bytes accessed | tf_op | source)
XLA Modules:
  0.0 80.4 jit_solution(9068099862401506984)
XLA Ops:
  0.0 2.9 %collective-permute-start = (bf16[128,2,1152]{2,1,0:T(2,128)(2,1)}, bf16[128,2,1152]{2,1,0:T(2,128)(2,1)}, u32[]{:S(2)}, u32[]{:S(2)}) collective-permute-start(bf16[128,2,1152]{2,1,0:T(2,128)(2,1)} %x_ref.3), channel_id=1, source_target_pairs={{0,1},{1,0},{2,3},{3,2},{4,5},{5,4},{6,7},{7,6},{8,9},{9,8},{10,11... | collective-permute-start | bytes 1769480 | tf_op jit(solution)/shard_map/ppermute | solution.py:286
  2.9 6.0 %all-to-all-start = ((bf16[16,8,2,1152]{3,2,1,0:T(2,128)(2,1)}), bf16[16,8,2,1152]{3,2,1,0:T(2,128)(2,1)}, u32[]{:S(2)}, u32[]{:S(2)}) async-start(bf16[16,8,2,1152]{3,2,1,0:T(2,128)(2,1)} %bitcast.16), calls=%async_computation | async-start | bytes 1179648 | tf_op jit(solution)/shard_map/all_to_all | solution.py:310
  8.9 0.6 collective-permute-start.1
  9.5 4.8 %shard_map.100 = (bf16[4,3,72,256]{3,2,1,0:T(8,128)(2,1)}, bf16[2,216,1152]{2,1,0:T(8,128)(2,1)}, bf16[144,1152]{1,0:T(8,128)(2,1)}) custom-call(bf16[128,2,1152]{2,1,0:T(2,128)(2,1)} %x_ref.3, bf16[4,216,1152]{2,1,0:T(8,128)(2,1)} %bitcast.20, bf16[4,216,1152]{2,1,0:T(8,128)(2,1)} %bitcast.14, bf16[288,1152]{1,0:T(8,128)(2,1)} %refs_1_.1, ...), custom_call_target="tpu_custom_call" | custom-call | flops 509607936 | bytes 3000000 | tf_op jit(solution)/shard_map/pallas_call | solution.py:295
  14.4 0.0 copy-start.1
  14.4 0.0 copy-start.5
  14.4 0.0 copy-start.6
  14.4 1.6 %collective-permute-start.2 = (bf16[144,1152]{1,0:T(8,128)(2,1)}, bf16[144,1152]{1,0:T(8,128)(2,1)S(1)}, u32[]{:S(2)}, u32[]{:S(2)}) collective-permute-start(bf16[144,1152]{1,0:T(8,128)(2,1)} %get-tuple-element.17), channel_id=1, source_target_pairs={{0,1},{1,0},{2,3},{3,2},{4,5},{5,4},{6,7},{7,6},{8,9},{9,8},{10,11... | collective-permute-start | bytes 995336 | tf_op jit(solution)/shard_map/ppermute | solution.py:286
  15.9 0.7 collective-permute-done.1.refs_0_
  16.6 0.0 collective-permute-done.refs_0_
  16.6 7.5 %shard_map.101.o_own_ref = bf16[2,256,288]{2,1,0:T(8,128)(2,1)} custom-call(bf16[4,3,72,256]{3,2,1,0:T(8,128)(2,1)} %get-tuple-element.14.own_hbm, bf16[4,216,1152]{2,1,0:T(8,128)(2,1)} %bitcast.21, f32[6,1152]{1,0:T(8,128)} %mod_ref.9, f32[864]{0:T(1024)} %b_ref.4, bf16[128,2,1152]{2,1,0:T(2,128)(2,1)} %collective-permute-done.refs_0_), custom_call_target="tpu_custom_call" | custom-call | flops 10000000000 | bytes 4000000 | tf_op jit(solution)/shard_map/pallas_call | solution.py:317
  24.2 0.0 copy-start
  24.2 0.0 copy-start.8
  24.2 0.2 collective-permute-done.2.refs_1_.refs_2_
  24.4 0.1 all-to-all-done
  24.5 1.5 %collective-permute-start.4 = (bf16[2,216,1152]{2,1,0:T(8,128)(2,1)}, bf16[2,216,1152]{2,1,0:T(8,128)(2,1)S(1)}, u32[]{:S(2)}, u32[]{:S(2)}) collective-permute-start(bf16[2,216,1152]{2,1,0:T(8,128)(2,1)} %get-tuple-element.21), channel_id=1, source_target_pairs={{0,1},{1,0},{2,3},{3,2},{4,5},{5,4},{6,7},{7,6},{8,9},{9,8},{10,11... | collective-permute-start | bytes 2985992 | tf_op jit(solution)/shard_map/ppermute | solution.py:286
  26.0 0.0 collective-permute-start.3
  26.0 1.6 %collective-permute-done.3.refs_2_.refs_3_ = bf16[144,1152]{1,0:T(8,128)(2,1)S(1)} collective-permute-done((bf16[144,1152]{1,0:T(8,128)(2,1)S(1)}, bf16[144,1152]{1,0:T(8,128)(2,1)S(1)}, u32[]{:S(2)}, u32[]{:S(2)}) %collective-permute-start.3) | collective-permute-done | bytes 331808 | tf_op jit(solution)/shard_map/ppermute | solution.py:289
  27.6 25.6 %all_to_all.15 = bf16[32,16,288]{2,1,0:T(8,128)(2,1)S(1)} all-to-all(bf16[32,16,288]{2,1,0:T(8,128)(2,1)} %bitcast.17), channel_id=1, replica_groups=mesh['grp'=1,'tm'=16,'space'=2] {'space','tm'}, dimensions={0} | all-to-all | bytes 589824 | tf_op jit(solution)/shard_map/all_to_all | solution.py:339
  53.3 0.0 collective-permute-done.4.refs_1_
  53.3 0.1 collective-permute-start.5
  53.4 2.7 %shard_map.102.h_ref = bf16[256,1152]{1,0:T(8,128)(2,1)S(1)} custom-call(bf16[2,256,288]{2,1,0:T(8,128)(2,1)S(1)} %bitcast.18, bf16[128,2,1152]{2,1,0:T(2,128)(2,1)} %bitcast.7.x_ref, f32[1152]{0:T(1024)S(1)} %copy-done.6, f32[6,1152]{1,0:T(8,128)S(1)} %copy-done.5, bf16[288,1152]{1,0:T(8,128)(2,1)S(1)} %copy-done.1, ...), custom_call_target="tpu_custom_call" | custom-call | flops 339738624 | bytes 3000000 | tf_op jit(solution)/shard_map/pallas_call | solution.py:360
  56.1 2.4 %shard_map.103.own_ref = f32[4,72,256]{2,1,0:T(8,128)S(1)} custom-call(bf16[256,1152]{1,0:T(8,128)(2,1)S(1)} %shard_map.102.h_ref, bf16[4,216,1152]{2,1,0:T(8,128)(2,1)S(1)} %bitcast.15, f32[864]{0:T(1024)S(1)} %copy-done.8), custom_call_target="tpu_custom_call" | custom-call | flops 509607936 | bytes 3000000 | tf_op jit(solution)/shard_map/pallas_call | solution.py:363
  58.5 0.0 copy-start.2
  58.5 3.2 %shard_map.104 = bf16[256,576]{1,0:T(8,128)(2,1)} custom-call(bf16[256,1152]{1,0:T(8,128)(2,1)S(1)} %shard_map.102.h_ref, f32[4,72,256]{2,1,0:T(8,128)S(1)} %shard_map.103.own_ref, f32[864]{0:T(1024)S(1)} %collective-permute-done.1.refs_0_, bf16[2,216,1152]{2,1,0:T(8,128)(2,1)S(1)} %collective-permute-done.4.refs_1_, ...), custom_call_target="tpu_custom_call" | custom-call | flops 509607936 | bytes 5000000 | tf_op jit(solution)/shard_map/pallas_call | solution.py:373
  61.7 4.7 %all-to-all-start.2 = ((bf16[16,16,576]{2,1,0:T(8,128)(2,1)}), bf16[16,16,576]{2,1,0:T(8,128)(2,1)S(1)}, u32[]{:S(2)}, u32[]{:S(2)}) async-start(bf16[16,16,576]{2,1,0:T(8,128)(2,1)} %bitcast.9), calls=%async_computation.2 | async-start | bytes 655360 | tf_op jit(solution)/shard_map/all_to_all | solution.py:385
  66.5 1.6 %collective-permute-start.6 = (bf16[256,288]{1,0:T(8,128)(2,1)S(1)}, bf16[256,288]{1,0:T(8,128)(2,1)S(1)}, u32[]{:S(2)}, u32[]{:S(2)}) collective-permute-start(bf16[256,288]{1,0:T(8,128)(2,1)S(1)} %dynamic-slice_bitcast_fusion), channel_id=1, source_target_pairs={{0,1},{1,0},{2,3},{3,2},{4,5},{5,4},{6,7},{7,6},{8,9},{9,8},{10,11... | collective-permute-start | bytes 442376 | tf_op jit(solution)/shard_map/ppermute | solution.py:286
  68.1 5.7 %collective-permute-done.6.refs_0_ = bf16[256,288]{1,0:T(8,128)(2,1)S(1)} collective-permute-done((bf16[256,288]{1,0:T(8,128)(2,1)S(1)}, bf16[256,288]{1,0:T(8,128)(2,1)S(1)}, u32[]{:S(2)}, u32[]{:S(2)}) %collective-permute-start.6) | collective-permute-done | bytes 147488 | tf_op jit(solution)/shard_map/ppermute | solution.py:286
  73.7 1.2 %shard_map.105.y_ref = bf16[256,1152]{1,0:T(8,128)(2,1)S(1)} custom-call(bf16[2,256,288]{2,1,0:T(8,128)(2,1)S(1)} %copy-done.3, bf16[128,2,1152]{2,1,0:T(2,128)(2,1)S(1)} %copy-done.2, f32[1152]{0:T(1024)S(1)} %copy-done.6, f32[6,1152]{1,0:T(8,128)S(1)} %copy-done.5, bf16[256,288]{1,0:T(8,128)(2,1)S(1)} %collective-permute-done.6.refs_0_, ...), custom_call_target="tpu_custom_call" | custom-call | flops 339738624 | bytes 3000000 | tf_op jit(solution)/shard_map/pallas_call | solution.py:351
  75.0 2.6 %all-to-all-done.2 = bf16[16,16,576]{2,1,0:T(8,128)(2,1)S(1)} async-done(((bf16[16,16,576]{2,1,0:T(8,128)(2,1)}), bf16[16,16,576]{2,1,0:T(8,128)(2,1)S(1)}, u32[]{:S(2)}, u32[]{:S(2)}) %all-to-all-start.2) | async-done | bytes 294944 | tf_op jit(solution)/shard_map/all_to_all | solution.py:385
  77.5 1.3 %copy-done.4 = bf16[576,1152]{1,0:T(8,128)(2,1)S(1)} copy-done((bf16[576,1152]{1,0:T(8,128)(2,1)S(1)}, bf16[576,1152]{1,0:T(8,128)(2,1)}, u32[]{:S(2)}) %copy-start.4) | copy-done | bytes 1327128
  78.8 1.5 %shard_map.106 = bf16[128,2,1152]{2,1,0:T(2,128)(2,1)} custom-call(bf16[256,576]{1,0:T(8,128)(2,1)S(1)} %bitcast.19, bf16[256,1152]{1,0:T(8,128)(2,1)S(1)} %shard_map.105.y_ref, bf16[576,1152]{1,0:T(8,128)(2,1)S(1)} %copy-done.4, f32[1152]{0:T(1024)S(1)} %copy-done.7, f32[6,1152]{1,0:T(8,128)S(1)} %copy-done.5), custom_call_target="tpu_custom_call" | custom-call | flops 339738624 | bytes 3000000 | tf_op jit(solution)/shard_map/pallas_call | solution.py:387
  (13 shorter events, 0.1 us)
Async XLA Ops:
  0.0 16.6 %collective-permute-start = (bf16[128,2,1152]{2,1,0:T(2,128)(2,1)}, bf16[128,2,1152]{2,1,0:T(2,128)(2,1)}, u32[]{:S(2)}, u32[]{:S(2)}) collective-permute-start(bf16[128,2,1152]{2,1,0:T(2,128)(2,1)} %x_ref.3), channel_id=1, source_target_pairs={{0,1},{1,0},{2,3},{3,2},{4,5},{5,4},{6,7},{7,6},{8,9},{9,8},{10,11... | collective-permute-start | bytes 1769480 | tf_op jit(solution)/shard_map/ppermute | solution.py:286
  2.9 21.6 %all-to-all-start = ((bf16[16,8,2,1152]{3,2,1,0:T(2,128)(2,1)}), bf16[16,8,2,1152]{3,2,1,0:T(2,128)(2,1)}, u32[]{:S(2)}, u32[]{:S(2)}) async-start(bf16[16,8,2,1152]{3,2,1,0:T(2,128)(2,1)} %bitcast.16), calls=%async_computation | async-start | bytes 1179648 | tf_op jit(solution)/shard_map/all_to_all | solution.py:310
  8.9 7.7 %collective-permute-start.1 = (f32[864]{0:T(1024)}, f32[864]{0:T(1024)S(1)}, u32[]{:S(2)}, u32[]{:S(2)}) collective-permute-start(f32[864]{0:T(1024)} %b_ref.5), channel_id=1, source_target_pairs={{0,1},{1,0},{2,3},{3,2},{4,5},{5,4},{6,7},{7,6},{8,9},{9,8},{10,11... | collective-permute-start | bytes 10376 | tf_op jit(solution)/shard_map/ppermute | solution.py:286
  14.4 39.0 %copy-start.1 = (bf16[288,1152]{1,0:T(8,128)(2,1)S(1)}, bf16[288,1152]{1,0:T(8,128)(2,1)}, u32[]{:S(2)}) copy-start(bf16[288,1152]{1,0:T(8,128)(2,1)} %refs_1_.1) | copy-start | bytes 1990660
  14.4 39.0 %copy-start.5 = (f32[6,1152]{1,0:T(8,128)S(1)}, f32[6,1152]{1,0:T(8,128)}, u32[]{:S(2)}) copy-start(f32[6,1152]{1,0:T(8,128)} %mod_ref.9) | copy-start | bytes 82948
  14.4 39.0 %copy-start.6 = (f32[1152]{0:T(1024)S(1)}, f32[1152]{0:T(1024)}, u32[]{:S(2)}) copy-start(f32[1152]{0:T(1024)} %outbias_ref.4) | copy-start | bytes 13828
  14.4 10.0 %collective-permute-start.2 = (bf16[144,1152]{1,0:T(8,128)(2,1)}, bf16[144,1152]{1,0:T(8,128)(2,1)S(1)}, u32[]{:S(2)}, u32[]{:S(2)}) collective-permute-start(bf16[144,1152]{1,0:T(8,128)(2,1)} %get-tuple-element.17), channel_id=1, source_target_pairs={{0,1},{1,0},{2,3},{3,2},{4,5},{5,4},{6,7},{7,6},{8,9},{9,8},{10,11... | collective-permute-start | bytes 995336 | tf_op jit(solution)/shard_map/ppermute | solution.py:286
  24.2 31.9 %copy-start = (bf16[1152,864]{0,1:T(8,128)(2,1)S(1)}, bf16[1152,864]{0,1:T(8,128)(2,1)}, u32[]{:S(2)}) copy-start(bf16[1152,864]{0,1:T(8,128)(2,1)} %param.16) | copy-start | bytes 5971972
  24.2 31.9 %copy-start.8 = (f32[864]{0:T(1024)S(1)}, f32[864]{0:T(1024)}, u32[]{:S(2)}) copy-start(f32[864]{0:T(1024)} %b_ref.5) | copy-start | bytes 10372
  24.5 28.7 %collective-permute-start.4 = (bf16[2,216,1152]{2,1,0:T(8,128)(2,1)}, bf16[2,216,1152]{2,1,0:T(8,128)(2,1)S(1)}, u32[]{:S(2)}, u32[]{:S(2)}) collective-permute-start(bf16[2,216,1152]{2,1,0:T(8,128)(2,1)} %get-tuple-element.21), channel_id=1, source_target_pairs={{0,1},{1,0},{2,3},{3,2},{4,5},{5,4},{6,7},{7,6},{8,9},{9,8},{10,11... | collective-permute-start | bytes 2985992 | tf_op jit(solution)/shard_map/ppermute | solution.py:286
  26.0 1.6 %collective-permute-start.3 = (bf16[144,1152]{1,0:T(8,128)(2,1)S(1)}, bf16[144,1152]{1,0:T(8,128)(2,1)S(1)}, u32[]{:S(2)}, u32[]{:S(2)}) collective-permute-start(bf16[144,1152]{1,0:T(8,128)(2,1)S(1)} %collective-permute-done.2.refs_1_.refs_2_), channel_id=1, source_target_pairs={{0,2},{2,0},{4,6},{6,4},{8,10},{10,8},{12,14},{14,12},{16,18},{18,... | collective-permute-start | bytes 995336 | tf_op jit(solution)/shard_map/ppermute | solution.py:289
  53.3 5.2 %collective-permute-start.5 = (bf16[2,216,1152]{2,1,0:T(8,128)(2,1)S(1)}, bf16[2,216,1152]{2,1,0:T(8,128)(2,1)S(1)}, u32[]{:S(2)}, u32[]{:S(2)}) collective-permute-start(bf16[2,216,1152]{2,1,0:T(8,128)(2,1)S(1)} %collective-permute-done.4.refs_1_), channel_id=1, source_target_pairs={{0,2},{2,0},{4,6},{6,4},{8,10},{10,8},{12,14},{14,12},{16,18},{18,... | collective-permute-start | bytes 2985992 | tf_op jit(solution)/shard_map/ppermute | solution.py:289
  58.5 8.0 %copy-start.3 = (bf16[2,256,288]{2,1,0:T(8,128)(2,1)S(1)}, bf16[2,256,288]{2,1,0:T(8,128)(2,1)}, u32[]{:S(2)}) copy-start(bf16[2,256,288]{2,1,0:T(8,128)(2,1)} %shard_map.101.o_own_ref) | copy-start | bytes 884740
  58.5 15.3 %copy-start.2 = (bf16[128,2,1152]{2,1,0:T(2,128)(2,1)S(1)}, bf16[128,2,1152]{2,1,0:T(2,128)(2,1)}, u32[]{:S(2)}) copy-start(bf16[128,2,1152]{2,1,0:T(2,128)(2,1)} %x_ref.3) | copy-start | bytes 1769476
  61.7 15.8 %copy-start.7 = (f32[1152]{0:T(1024)S(1)}, f32[1152]{0:T(1024)}, u32[]{:S(2)}) copy-start(f32[1152]{0:T(1024)} %outbias_ref.5) | copy-start | bytes 13828
  61.7 15.8 %all-to-all-start.2 = ((bf16[16,16,576]{2,1,0:T(8,128)(2,1)}), bf16[16,16,576]{2,1,0:T(8,128)(2,1)S(1)}, u32[]{:S(2)}, u32[]{:S(2)}) async-start(bf16[16,16,576]{2,1,0:T(8,128)(2,1)} %bitcast.9), calls=%async_computation.2 | async-start | bytes 655360 | tf_op jit(solution)/shard_map/all_to_all | solution.py:385
  66.5 7.3 %collective-permute-start.6 = (bf16[256,288]{1,0:T(8,128)(2,1)S(1)}, bf16[256,288]{1,0:T(8,128)(2,1)S(1)}, u32[]{:S(2)}, u32[]{:S(2)}) collective-permute-start(bf16[256,288]{1,0:T(8,128)(2,1)S(1)} %dynamic-slice_bitcast_fusion), channel_id=1, source_target_pairs={{0,1},{1,0},{2,3},{3,2},{4,5},{5,4},{6,7},{7,6},{8,9},{9,8},{10,11... | collective-permute-start | bytes 442376 | tf_op jit(solution)/shard_map/ppermute | solution.py:286
  77.5 1.3 %copy-start.4 = (bf16[576,1152]{1,0:T(8,128)(2,1)S(1)}, bf16[576,1152]{1,0:T(8,128)(2,1)}, u32[]{:S(2)}) copy-start(bf16[576,1152]{1,0:T(8,128)(2,1)} %w_ref.1) | copy-start | bytes 3981316

commit v15 on v14

--- a/solution.py
+++ b/solution.py
@@ -385,7 +385,7 @@
     o_final = lax.all_to_all(o_t, "tm", 0, 0, tiled=True).reshape(rows, spaces * cols)
 
     return call(
-        kernel_final, (patches, frames, width), 5, 2 * rows * width * cols * spaces, 3e6, params=SMALL
+        kernel_final, (patches, frames, width), 5, 2 * rows * width * cols * spaces, 3e6
     )(o_final, y_home, out_temporal, outbias_temporal, modulation)
 
 

time: 80.9 us -> 81.1 us (level)
  Pallas kernels: 23.3 us -> 25 us
    pallas_call x1, Pallas kernels: 1.52 us -> 3.13 us  [local(): call(kernel_final, (patches, frames, width), 5, 2 * rows * width * cols *...]
where the time goes in v15:
time: 81.1 us; the launch traced here: 80.6 us
  blocking collectives  25.6 us (32%)
  Pallas kernels  25 us (31%)
  starting transfers between devices  18.8 us (23%)
  waiting for transfers between devices  10.2 us (13%)
  local copies, waits for them, and re-layouts  0.88 us (1%)
    all_to_all x1, blocking collectives, local(): lax.all_to_all(after((o_all,), spread, *out_pieces)[0].reshape(spaces * t...  25.6 us
    ppermute x5, starting transfers between devices, across(): lax.ppermute(array, 'space', [(i, (i + k) % spaces) for i in range(spaces)])  8.11 us
    pallas_call x1, Pallas kernels, local(): call(kernel_spatial, (spaces, rows, cols), 4 + len(arrived), 10000000000....  7.52 us
    ppermute x5, waiting for transfers between devices, across(): lax.ppermute(array, 'space', [(i, (i + k) % spaces) for i in range(spaces)])  6.57 us
    all_to_all x1, starting transfers between devices, local(): lax.all_to_all(tokens.reshape(times, size, frames, width), 'tm', 0, 0, ti...  5.98 us
    pallas_call x1, Pallas kernels, local(): pl.pallas_call(kernel_qkv, out_shape=tuple((jax.ShapeDtypeStruct(a, BF) f...  4.82 us
    all_to_all x1, starting transfers between devices, local(): lax.all_to_all(o_t, 'tm', 0, 0, tiled=True).reshape(rows, spaces * cols)  4.58 us
    pallas_call x1, Pallas kernels, local(): call(functools.partial(kernel_rest, size=size, frames=frames, spaces=spac...  3.24 us
  transfers between devices with their start and end apart: 9, of which 6 were waited for; matrix products, arithmetic and copies ran while one was open for 0% of the time, Pallas kernels for 23%

profile of v15, /device:TPU:0, one launch (start us, length us, event | category | flops | bytes accessed | tf_op | source)
XLA Modules:
  0.0 80.6 jit_solution(855806854888556045)
XLA Ops:
  0.0 2.9 %collective-permute-start = (bf16[128,2,1152]{2,1,0:T(2,128)(2,1)}, bf16[128,2,1152]{2,1,0:T(2,128)(2,1)}, u32[]{:S(2)}, u32[]{:S(2)}) collective-permute-start(bf16[128,2,1152]{2,1,0:T(2,128)(2,1)} %x_ref.3), channel_id=1, source_target_pairs={{0,1},{1,0},{2,3},{3,2},{4,5},{5,4},{6,7},{7,6},{8,9},{9,8},{10,11... | collective-permute-start | bytes 1769480 | tf_op jit(solution)/shard_map/ppermute | solution.py:286
  2.9 6.0 %all-to-all-start = ((bf16[16,8,2,1152]{3,2,1,0:T(2,128)(2,1)}), bf16[16,8,2,1152]{3,2,1,0:T(2,128)(2,1)}, u32[]{:S(2)}, u32[]{:S(2)}) async-start(bf16[16,8,2,1152]{3,2,1,0:T(2,128)(2,1)} %bitcast.16), calls=%async_computation | async-start | bytes 1179648 | tf_op jit(solution)/shard_map/all_to_all | solution.py:310
  8.9 0.6 collective-permute-start.1
  9.5 4.8 %shard_map.100 = (bf16[4,3,72,256]{3,2,1,0:T(8,128)(2,1)}, bf16[2,216,1152]{2,1,0:T(8,128)(2,1)}, bf16[144,1152]{1,0:T(8,128)(2,1)}) custom-call(bf16[128,2,1152]{2,1,0:T(2,128)(2,1)} %x_ref.3, bf16[4,216,1152]{2,1,0:T(8,128)(2,1)} %bitcast.19, bf16[4,216,1152]{2,1,0:T(8,128)(2,1)} %bitcast.14, bf16[288,1152]{1,0:T(8,128)(2,1)} %refs_1_.1, ...), custom_call_target="tpu_custom_call" | custom-call | flops 509607936 | bytes 3000000 | tf_op jit(solution)/shard_map/pallas_call | solution.py:295
  14.4 0.0 copy-start.1
  14.4 0.0 copy-start.5
  14.4 0.0 copy-start.6
  14.4 1.6 %collective-permute-start.2 = (bf16[144,1152]{1,0:T(8,128)(2,1)}, bf16[144,1152]{1,0:T(8,128)(2,1)S(1)}, u32[]{:S(2)}, u32[]{:S(2)}) collective-permute-start(bf16[144,1152]{1,0:T(8,128)(2,1)} %get-tuple-element.17), channel_id=1, source_target_pairs={{0,1},{1,0},{2,3},{3,2},{4,5},{5,4},{6,7},{7,6},{8,9},{9,8},{10,11... | collective-permute-start | bytes 995336 | tf_op jit(solution)/shard_map/ppermute | solution.py:286
  15.9 0.7 collective-permute-done.1.refs_0_
  16.6 0.0 collective-permute-done.refs_0_
  16.6 7.5 %shard_map.101.o_own_ref = bf16[2,256,288]{2,1,0:T(8,128)(2,1)} custom-call(bf16[4,3,72,256]{3,2,1,0:T(8,128)(2,1)} %get-tuple-element.14.own_hbm, bf16[4,216,1152]{2,1,0:T(8,128)(2,1)} %bitcast.20, f32[6,1152]{1,0:T(8,128)} %mod_ref.9, f32[864]{0:T(1024)} %b_ref.4, bf16[128,2,1152]{2,1,0:T(2,128)(2,1)} %collective-permute-done.refs_0_), custom_call_target="tpu_custom_call" | custom-call | flops 10000000000 | bytes 4000000 | tf_op jit(solution)/shard_map/pallas_call | solution.py:317
  24.2 0.0 copy-start
  24.2 0.0 copy-start.7
  24.2 0.2 collective-permute-done.2.refs_1_.refs_2_
  24.4 0.1 all-to-all-done
  24.5 1.5 %collective-permute-start.4 = (bf16[2,216,1152]{2,1,0:T(8,128)(2,1)}, bf16[2,216,1152]{2,1,0:T(8,128)(2,1)S(1)}, u32[]{:S(2)}, u32[]{:S(2)}) collective-permute-start(bf16[2,216,1152]{2,1,0:T(8,128)(2,1)} %get-tuple-element.21), channel_id=1, source_target_pairs={{0,1},{1,0},{2,3},{3,2},{4,5},{5,4},{6,7},{7,6},{8,9},{9,8},{10,11... | collective-permute-start | bytes 2985992 | tf_op jit(solution)/shard_map/ppermute | solution.py:286
  26.0 1.6 %collective-permute-done.3.refs_2_.refs_3_ = bf16[144,1152]{1,0:T(8,128)(2,1)S(1)} collective-permute-done((bf16[144,1152]{1,0:T(8,128)(2,1)S(1)}, bf16[144,1152]{1,0:T(8,128)(2,1)S(1)}, u32[]{:S(2)}, u32[]{:S(2)}) %collective-permute-start.3) | collective-permute-done | bytes 331808 | tf_op jit(solution)/shard_map/ppermute | solution.py:289
  27.6 25.6 %all_to_all.15 = bf16[32,16,288]{2,1,0:T(8,128)(2,1)S(1)} all-to-all(bf16[32,16,288]{2,1,0:T(8,128)(2,1)} %bitcast.17), channel_id=1, replica_groups=mesh['grp'=1,'tm'=16,'space'=2] {'space','tm'}, dimensions={0} | all-to-all | bytes 589824 | tf_op jit(solution)/shard_map/all_to_all | solution.py:339
  53.3 0.0 collective-permute-done.4.refs_1_
  53.3 0.1 collective-permute-start.5
  53.4 2.7 %shard_map.102.h_ref = bf16[256,1152]{1,0:T(8,128)(2,1)S(1)} custom-call(bf16[2,256,288]{2,1,0:T(8,128)(2,1)S(1)} %bitcast.18, bf16[128,2,1152]{2,1,0:T(2,128)(2,1)} %bitcast.7.x_ref, f32[1152]{0:T(1024)S(1)} %copy-done.6, f32[6,1152]{1,0:T(8,128)S(1)} %copy-done.5, bf16[288,1152]{1,0:T(8,128)(2,1)S(1)} %copy-done.1, ...), custom_call_target="tpu_custom_call" | custom-call | flops 339738624 | bytes 3000000 | tf_op jit(solution)/shard_map/pallas_call | solution.py:360
  56.1 2.4 %shard_map.103.own_ref = f32[4,72,256]{2,1,0:T(8,128)S(1)} custom-call(bf16[256,1152]{1,0:T(8,128)(2,1)S(1)} %shard_map.102.h_ref, bf16[4,216,1152]{2,1,0:T(8,128)(2,1)S(1)} %bitcast.15, f32[864]{0:T(1024)S(1)} %copy-done.7), custom_call_target="tpu_custom_call" | custom-call | flops 509607936 | bytes 3000000 | tf_op jit(solution)/shard_map/pallas_call | solution.py:363
  58.5 0.0 copy-start.2
  58.5 0.0 collective-permute-done.5.refs_2_
  58.5 3.2 %shard_map.104 = bf16[256,576]{1,0:T(8,128)(2,1)} custom-call(bf16[256,1152]{1,0:T(8,128)(2,1)S(1)} %shard_map.102.h_ref, f32[4,72,256]{2,1,0:T(8,128)S(1)} %shard_map.103.own_ref, f32[864]{0:T(1024)S(1)} %collective-permute-done.1.refs_0_, bf16[2,216,1152]{2,1,0:T(8,128)(2,1)S(1)} %collective-permute-done.4.refs_1_, ...), custom_call_target="tpu_custom_call" | custom-call | flops 509607936 | bytes 5000000 | tf_op jit(solution)/shard_map/pallas_call | solution.py:373
  61.7 4.6 %all-to-all-start.2 = ((bf16[16,16,576]{2,1,0:T(8,128)(2,1)}), bf16[16,16,576]{2,1,0:T(8,128)(2,1)}, u32[]{:S(2)}, u32[]{:S(2)}) async-start(bf16[16,16,576]{2,1,0:T(8,128)(2,1)} %bitcast.9), calls=%async_computation.2 | async-start | bytes 655360 | tf_op jit(solution)/shard_map/all_to_all | solution.py:385
  66.4 1.5 %collective-permute-start.6 = (bf16[256,288]{1,0:T(8,128)(2,1)S(1)}, bf16[256,288]{1,0:T(8,128)(2,1)S(1)}, u32[]{:S(2)}, u32[]{:S(2)}) collective-permute-start(bf16[256,288]{1,0:T(8,128)(2,1)S(1)} %dynamic-slice_bitcast_fusion), channel_id=1, source_target_pairs={{0,1},{1,0},{2,3},{3,2},{4,5},{5,4},{6,7},{7,6},{8,9},{9,8},{10,11... | collective-permute-start | bytes 442376 | tf_op jit(solution)/shard_map/ppermute | solution.py:286
  67.9 5.7 %collective-permute-done.6.refs_0_ = bf16[256,288]{1,0:T(8,128)(2,1)S(1)} collective-permute-done((bf16[256,288]{1,0:T(8,128)(2,1)S(1)}, bf16[256,288]{1,0:T(8,128)(2,1)S(1)}, u32[]{:S(2)}, u32[]{:S(2)}) %collective-permute-start.6) | collective-permute-done | bytes 147488 | tf_op jit(solution)/shard_map/ppermute | solution.py:286
  73.6 1.2 %shard_map.105.y_ref = bf16[256,1152]{1,0:T(8,128)(2,1)S(1)} custom-call(bf16[2,256,288]{2,1,0:T(8,128)(2,1)S(1)} %copy-done.3, bf16[128,2,1152]{2,1,0:T(2,128)(2,1)S(1)} %copy-done.2, f32[1152]{0:T(1024)S(1)} %copy-done.6, f32[6,1152]{1,0:T(8,128)S(1)} %copy-done.5, bf16[256,288]{1,0:T(8,128)(2,1)S(1)} %collective-permute-done.6.refs_0_, ...), custom_call_target="tpu_custom_call" | custom-call | flops 339738624 | bytes 3000000 | tf_op jit(solution)/shard_map/pallas_call | solution.py:351
  74.8 0.8 %copy-done.4 = bf16[256,1152]{1,0:T(8,128)(2,1)} copy-done((bf16[256,1152]{1,0:T(8,128)(2,1)}, bf16[256,1152]{1,0:T(8,128)(2,1)S(1)}, u32[]{:S(2)}) %copy-start.4) | copy-done | bytes 589848
  75.7 1.8 %all-to-all-done.2 = bf16[16,16,576]{2,1,0:T(8,128)(2,1)} async-done(((bf16[16,16,576]{2,1,0:T(8,128)(2,1)}), bf16[16,16,576]{2,1,0:T(8,128)(2,1)}, u32[]{:S(2)}, u32[]{:S(2)}) %all-to-all-start.2) | async-done | bytes 294944 | tf_op jit(solution)/shard_map/all_to_all | solution.py:385
  77.5 3.1 %shard_map.106 = bf16[128,2,1152]{2,1,0:T(2,128)(2,1)} custom-call(bf16[256,576]{1,0:T(8,128)(2,1)} %bitcast.10.o_ref, bf16[256,1152]{1,0:T(8,128)(2,1)} %copy-done.4, bf16[576,1152]{1,0:T(8,128)(2,1)} %w_ref.1, f32[1152]{0:T(1024)} %outbias_ref.5, f32[6,1152]{1,0:T(8,128)} %mod_ref.9), custom_call_target="tpu_custom_call" | custom-call | flops 339738624 | bytes 3000000 | tf_op jit(solution)/shard_map/pallas_call | solution.py:387
  (11 shorter events, 0.0 us)
Async XLA Ops:
  0.0 16.6 %collective-permute-start = (bf16[128,2,1152]{2,1,0:T(2,128)(2,1)}, bf16[128,2,1152]{2,1,0:T(2,128)(2,1)}, u32[]{:S(2)}, u32[]{:S(2)}) collective-permute-start(bf16[128,2,1152]{2,1,0:T(2,128)(2,1)} %x_ref.3), channel_id=1, source_target_pairs={{0,1},{1,0},{2,3},{3,2},{4,5},{5,4},{6,7},{7,6},{8,9},{9,8},{10,11... | collective-permute-start | bytes 1769480 | tf_op jit(solution)/shard_map/ppermute | solution.py:286
  2.9 21.6 %all-to-all-start = ((bf16[16,8,2,1152]{3,2,1,0:T(2,128)(2,1)}), bf16[16,8,2,1152]{3,2,1,0:T(2,128)(2,1)}, u32[]{:S(2)}, u32[]{:S(2)}) async-start(bf16[16,8,2,1152]{3,2,1,0:T(2,128)(2,1)} %bitcast.16), calls=%async_computation | async-start | bytes 1179648 | tf_op jit(solution)/shard_map/all_to_all | solution.py:310
  8.9 7.7 %collective-permute-start.1 = (f32[864]{0:T(1024)}, f32[864]{0:T(1024)S(1)}, u32[]{:S(2)}, u32[]{:S(2)}) collective-permute-start(f32[864]{0:T(1024)} %b_ref.5), channel_id=1, source_target_pairs={{0,1},{1,0},{2,3},{3,2},{4,5},{5,4},{6,7},{7,6},{8,9},{9,8},{10,11... | collective-permute-start | bytes 10376 | tf_op jit(solution)/shard_map/ppermute | solution.py:286
  14.4 39.0 %copy-start.1 = (bf16[288,1152]{1,0:T(8,128)(2,1)S(1)}, bf16[288,1152]{1,0:T(8,128)(2,1)}, u32[]{:S(2)}) copy-start(bf16[288,1152]{1,0:T(8,128)(2,1)} %refs_1_.1) | copy-start | bytes 1990660
  14.4 39.0 %copy-start.5 = (f32[6,1152]{1,0:T(8,128)S(1)}, f32[6,1152]{1,0:T(8,128)}, u32[]{:S(2)}) copy-start(f32[6,1152]{1,0:T(8,128)} %mod_ref.9) | copy-start | bytes 82948
  14.4 39.0 %copy-start.6 = (f32[1152]{0:T(1024)S(1)}, f32[1152]{0:T(1024)}, u32[]{:S(2)}) copy-start(f32[1152]{0:T(1024)} %outbias_ref.4) | copy-start | bytes 13828
  14.4 10.0 %collective-permute-start.2 = (bf16[144,1152]{1,0:T(8,128)(2,1)}, bf16[144,1152]{1,0:T(8,128)(2,1)S(1)}, u32[]{:S(2)}, u32[]{:S(2)}) collective-permute-start(bf16[144,1152]{1,0:T(8,128)(2,1)} %get-tuple-element.17), channel_id=1, source_target_pairs={{0,1},{1,0},{2,3},{3,2},{4,5},{5,4},{6,7},{7,6},{8,9},{9,8},{10,11... | collective-permute-start | bytes 995336 | tf_op jit(solution)/shard_map/ppermute | solution.py:286
  24.2 31.9 %copy-start = (bf16[1152,864]{0,1:T(8,128)(2,1)S(1)}, bf16[1152,864]{0,1:T(8,128)(2,1)}, u32[]{:S(2)}) copy-start(bf16[1152,864]{0,1:T(8,128)(2,1)} %param.16) | copy-start | bytes 5971972
  24.2 31.9 %copy-start.7 = (f32[864]{0:T(1024)S(1)}, f32[864]{0:T(1024)}, u32[]{:S(2)}) copy-start(f32[864]{0:T(1024)} %b_ref.5) | copy-start | bytes 10372
  24.5 28.7 %collective-permute-start.4 = (bf16[2,216,1152]{2,1,0:T(8,128)(2,1)}, bf16[2,216,1152]{2,1,0:T(8,128)(2,1)S(1)}, u32[]{:S(2)}, u32[]{:S(2)}) collective-permute-start(bf16[2,216,1152]{2,1,0:T(8,128)(2,1)} %get-tuple-element.21), channel_id=1, source_target_pairs={{0,1},{1,0},{2,3},{3,2},{4,5},{5,4},{6,7},{7,6},{8,9},{9,8},{10,11... | collective-permute-start | bytes 2985992 | tf_op jit(solution)/shard_map/ppermute | solution.py:286
  26.0 1.6 %collective-permute-start.3 = (bf16[144,1152]{1,0:T(8,128)(2,1)S(1)}, bf16[144,1152]{1,0:T(8,128)(2,1)S(1)}, u32[]{:S(2)}, u32[]{:S(2)}) collective-permute-start(bf16[144,1152]{1,0:T(8,128)(2,1)S(1)} %collective-permute-done.2.refs_1_.refs_2_), channel_id=1, source_target_pairs={{0,2},{2,0},{4,6},{6,4},{8,10},{10,8},{12,14},{14,12},{16,18},{18,... | collective-permute-start | bytes 995336 | tf_op jit(solution)/shard_map/ppermute | solution.py:289
  53.3 5.2 %collective-permute-start.5 = (bf16[2,216,1152]{2,1,0:T(8,128)(2,1)S(1)}, bf16[2,216,1152]{2,1,0:T(8,128)(2,1)S(1)}, u32[]{:S(2)}, u32[]{:S(2)}) collective-permute-start(bf16[2,216,1152]{2,1,0:T(8,128)(2,1)S(1)} %collective-permute-done.4.refs_1_), channel_id=1, source_target_pairs={{0,2},{2,0},{4,6},{6,4},{8,10},{10,8},{12,14},{14,12},{16,18},{18,... | collective-permute-start | bytes 2985992 | tf_op jit(solution)/shard_map/ppermute | solution.py:289
  58.5 7.9 %copy-start.3 = (bf16[2,256,288]{2,1,0:T(8,128)(2,1)S(1)}, bf16[2,256,288]{2,1,0:T(8,128)(2,1)}, u32[]{:S(2)}) copy-start(bf16[2,256,288]{2,1,0:T(8,128)(2,1)} %shard_map.101.o_own_ref) | copy-start | bytes 884740
  58.5 15.1 %copy-start.2 = (bf16[128,2,1152]{2,1,0:T(2,128)(2,1)S(1)}, bf16[128,2,1152]{2,1,0:T(2,128)(2,1)}, u32[]{:S(2)}) copy-start(bf16[128,2,1152]{2,1,0:T(2,128)(2,1)} %x_ref.3) | copy-start | bytes 1769476
  61.7 15.7 %all-to-all-start.2 = ((bf16[16,16,576]{2,1,0:T(8,128)(2,1)}), bf16[16,16,576]{2,1,0:T(8,128)(2,1)}, u32[]{:S(2)}, u32[]{:S(2)}) async-start(bf16[16,16,576]{2,1,0:T(8,128)(2,1)} %bitcast.9), calls=%async_computation.2 | async-start | bytes 655360 | tf_op jit(solution)/shard_map/all_to_all | solution.py:385
  66.4 7.2 %collective-permute-start.6 = (bf16[256,288]{1,0:T(8,128)(2,1)S(1)}, bf16[256,288]{1,0:T(8,128)(2,1)S(1)}, u32[]{:S(2)}, u32[]{:S(2)}) collective-permute-start(bf16[256,288]{1,0:T(8,128)(2,1)S(1)} %dynamic-slice_bitcast_fusion), channel_id=1, source_target_pairs={{0,1},{1,0},{2,3},{3,2},{4,5},{5,4},{6,7},{7,6},{8,9},{9,8},{10,11... | collective-permute-start | bytes 442376 | tf_op jit(solution)/shard_map/ppermute | solution.py:286
  74.8 0.8 %copy-start.4 = (bf16[256,1152]{1,0:T(8,128)(2,1)}, bf16[256,1152]{1,0:T(8,128)(2,1)S(1)}, u32[]{:S(2)}) copy-start(bf16[256,1152]{1,0:T(8,128)(2,1)S(1)} %shard_map.105.y_ref) | copy-start | bytes 1769476
